TPU v7x, 32 devices: a whole 2x2x4 slice. The times are simulated.
32 devices in a mesh: groups: 2 (over y), pool: 4 (over z), tensor: 4 (over x, core).
Axes of the slice: x: 2, y: 2, z: 4, core: 2. Of those that a mesh axis runs over, the one named last changes fastest.
Arguments:
- hidden_in: bfloat16 [128, 16384], P('groups', 'pool'), parts along dimension 0, may hold values from -750 to 750
- norm_gain: bfloat16 [16384], P('pool'), may hold values from 0.099609375 to 1.8984375
- w_query: bfloat16 [16384, 16384], P('pool', 'tensor'), may hold values from -0.046875 to 0.046875
- w_key: bfloat16 [16384, 1024], P('pool', 'tensor'), may hold values from -0.046875 to 0.046875
- w_value: bfloat16 [16384, 1024], P('pool', 'tensor'), may hold values from -0.046875 to 0.046875
- cache_keys: bfloat16 [8192, 1024], P(('groups', 'pool'), 'tensor'), parts along dimension 0, may hold values from -110 to 110
- cache_values: bfloat16 [8192, 1024], P(('groups', 'pool'), 'tensor'), parts along dimension 0, may hold values from -6 to 6
- send_row: int32 [8, 4, 4], P('groups'), parts along dimension 0, may hold values from -1 to 15, as said below
- piece_len: int32 [8, 4, 4], P(('groups', 'pool')), parts along dimension 0, may hold values from 0 to 64, as said below
- row_len: int32 [128], P('groups'), parts along dimension 0, may hold values from 1 to 64, as said below
Outputs:
- attention: bfloat16 [128, 16384], P(('groups', 'pool'), 'tensor'), parts along dimension 0
There are 2 independent parts, one for each index of `groups`. A program takes and returns all parts, laid end to end along the dimension named above; an argument that names none is the same for every part. Nothing has to cross between parts.
Inputs may be any that keep to these rules, and one draw needn't show every extreme that they name: `send_row`: each entry is -1 or a row of 0 to 15; every row of every home is named at least once; entry [h, p, c] is live exactly when piece_len[p, h, c] > 0. `piece_len`: 0 exactly at empty slots. `row_len`: the sum of piece_len over the slots that name the row.
All inputs are finite; a program needn't handle non-finite values.
Results may differ from a plain program's by a relative error of at most 0.012.
Values may be sent and summed in bfloat16 or wider, within the bound.
No kernel may reach another device: no remote copies, remote signals or barrier semaphores. Data moves between devices by JAX's collectives and lax.ppermute only.
A program may use at most 128 MiB of HBM per device.

v0:
```python
import jax
import jax.numpy as jnp
from jax import lax
from jax.sharding import PartitionSpec as P

D = 16384
HD = 128
SEG = 64


EPS = 1e-05
THETA = 500000.0


def rotate(vectors, positions):
    head_size = vectors.shape[-1]
    half_dim = head_size // 2
    inverse_freq = THETA ** (-(jnp.arange(half_dim, dtype=jnp.float32) * 2.0) / head_size)
    angles = positions.astype(jnp.float32)[:, None] * inverse_freq[None, :]
    cosines = jnp.cos(angles)[:, None, :]
    sines = jnp.sin(angles)[:, None, :]
    front_half = vectors[..., :half_dim]
    back_half = vectors[..., half_dim:]
    return jnp.concatenate(
        [front_half * cosines - back_half * sines, back_half * cosines + front_half * sines], -1
    )


def partial_attention(queries, key_block, value_block, lengths):
    score = jnp.einsum(
        "rkgd,rtkd->rkgt", queries, key_block, preferred_element_type=jnp.float32
    ) * HD ** (-0.5)
    usable = (jnp.arange(key_block.shape[1], dtype=jnp.int32)[None, :] < lengths[:, None])[
        :, None, None, :
    ]
    peak_score = jnp.max(jnp.where(usable, score, -1e30), axis=-1)
    weight = jnp.where(usable, jnp.exp(score - peak_score[..., None]), 0.0)
    totals = jnp.sum(weight, axis=-1)
    blended = jnp.einsum(
        "rkgt,rtkd->rkgd",
        weight.astype(jnp.bfloat16),
        value_block,
        preferred_element_type=jnp.float32,
    )
    slot_total = queries.shape[0]
    return (
        blended.reshape(slot_total, -1),
        peak_score.reshape(slot_total, -1),
        totals.reshape(slot_total, -1),
    )


def body(
    hidden_in,
    norm_gain,
    w_query,
    w_key,
    w_value,
    cache_keys,
    cache_values,
    send_row,
    piece_len,
    row_len,
):
    pool_size = lax.axis_size("pool")
    pool_index = lax.axis_index("pool")
    row_count = hidden_in.shape[0]
    rows_local = row_count // pool_size
    slot_count = send_row.shape[2]
    query_heads = w_query.shape[1] // HD
    value_heads = w_key.shape[1] // HD
    group = query_heads // value_heads
    query_cols = query_heads * HD
    value_cols = value_heads * HD
    x_float = hidden_in.astype(jnp.float32)
    scaled = (x_float * norm_gain.astype(jnp.float32)).astype(jnp.bfloat16)
    home_start = pool_index * rows_local
    power_all = lax.psum(jnp.sum(x_float * x_float, axis=1), "pool")
    parts_list = [
        jnp.dot(scaled, weights, preferred_element_type=jnp.float32)
        for weights in (w_query, w_key, w_value)
    ]
    power_rows = lax.dynamic_slice_in_dim(power_all, home_start, rows_local, 0)
    home_sums = (
        lax.psum_scatter(jnp.concatenate(parts_list, 1), "pool", scatter_dimension=0, tiled=True)
        * lax.rsqrt(power_rows / D + EPS)[:, None]
    )
    positions = lax.dynamic_slice_in_dim(row_len, home_start, rows_local, 0)
    home_query = rotate(
        home_sums[:, :query_cols].reshape(rows_local, query_heads, HD), positions
    ).astype(jnp.bfloat16)
    outgoing_rows = lax.dynamic_index_in_dim(send_row, pool_index, 0, keepdims=False)
    outgoing = home_query.reshape(rows_local, query_cols)[jnp.maximum(outgoing_rows, 0)]
    outgoing = jnp.where((outgoing_rows >= 0)[..., None], outgoing, jnp.zeros_like(outgoing))
    incoming = lax.all_to_all(outgoing, "pool", split_axis=0, concat_axis=0, tiled=True)
    key_b = rotate(
        home_sums[:, query_cols : query_cols + value_cols].reshape(rows_local, value_heads, HD),
        positions,
    ).astype(jnp.bfloat16)
    value_b = (
        home_sums[:, query_cols + value_cols :]
        .astype(jnp.bfloat16)
        .reshape(rows_local, value_heads, HD)
    )
    request_total = pool_size * slot_count
    queries = incoming.reshape(request_total, value_heads, group, HD)
    key_block = cache_keys.reshape(request_total, SEG, value_heads, HD)
    value_block = cache_values.reshape(request_total, SEG, value_heads, HD)
    blended, peaks, totals = partial_attention(
        queries, key_block, value_block, piece_len.reshape(request_total)
    )
    blended = blended.reshape(pool_size, slot_count, query_cols)
    peaks = peaks.reshape(pool_size, slot_count, query_heads)
    totals = totals.reshape(pool_size, slot_count, query_heads)
    blended, peaks, totals = (
        lax.all_to_all(blended, "pool", split_axis=0, concat_axis=0, tiled=True),
        lax.all_to_all(peaks, "pool", split_axis=0, concat_axis=0, tiled=True),
        lax.all_to_all(totals, "pool", split_axis=0, concat_axis=0, tiled=True),
    )
    blended = blended.reshape(request_total, query_heads, HD)
    peaks = peaks.reshape(request_total, query_heads)
    totals = totals.reshape(request_total, query_heads)
    grouped = home_query.reshape(rows_local, value_heads, group, HD)
    self_peak = (
        jnp.einsum("rkgd,rkd->rkg", grouped, key_b, preferred_element_type=jnp.float32)
        * HD ** (-0.5)
    ).reshape(rows_local, query_heads)
    self_value = jnp.repeat(value_b.astype(jnp.float32), group, axis=1)
    slot_rows = lax.dynamic_index_in_dim(send_row, pool_index, 0, keepdims=False).reshape(
        request_total
    )
    matches = slot_rows[None, :] == jnp.arange(rows_local, dtype=jnp.int32)[:, None]
    highest = jnp.maximum(
        self_peak, jnp.max(jnp.where(matches[:, :, None], peaks[None], -1e30), axis=1)
    )
    factor = jnp.where(matches[:, :, None], jnp.exp(peaks[None] - highest[:, None, :]), 0.0)
    self_weight = jnp.exp(self_peak - highest)
    denominator = self_weight + jnp.sum(factor * totals[None], axis=1)
    numerator = self_weight[..., None] * self_value + jnp.einsum("jsh,shd->jhd", factor, blended)
    return (numerator / denominator[..., None]).astype(jnp.bfloat16).reshape(rows_local, query_cols)


def solution(mesh):
    return jax.shard_map(
        body,
        mesh=mesh,
        in_specs=(
            P("groups", "pool"),
            P("pool"),
            P("pool", "tensor"),
            P("pool", "tensor"),
            P("pool", "tensor"),
            P(("groups", "pool"), "tensor"),
            P(("groups", "pool"), "tensor"),
            P("groups", None, None),
            P(("groups", "pool"), None, None),
            P("groups"),
        ),
        out_specs=P(("groups", "pool"), "tensor"),
        check_vma=False,
    )
```

profile of v0, /device:TPU:0, one launch (start us, length us, event | category | flops | bytes accessed | tf_op | source)
XLA Modules:
  0.0 105.5 jit_solution(14639199252359104488)
XLA Ops:
  6.5 0.0 copy-start
  6.5 0.9 convert_element_type.34
  7.4 0.7 copy-done
  8.1 1.5 %fusion.9 = f32[64,256]{1,0:T(8,128)S(1)} fusion(bf16[4096,256]{1,0:T(8,128)(2,1)S(1)} %copy-done, bf16[64,4096]{1,0:T(8,128)(2,1)} %param.10, f32[4096]{0:T(1024)S(1)} %convert_element_type.34), kind=kOutput, calls=%fused_computation.15 | convolution fusion | flops 135004160 | bytes 2703360 | tf_op jit(solution)/shard_map/dot_general | solution.py:80
  9.7 0.5 fusion.11
  10.1 13.6 %fusion.13 = f32[64,4096]{1,0:T(8,128)S(1)} fusion(bf16[4096,4096]{1,0:T(8,128)(2,1)} %param.12, bf16[64,4096]{1,0:T(8,128)(2,1)S(1)} %copy-done.1, f32[4096]{0:T(1024)S(1)} %convert_element_type.34), kind=kOutput, calls=%fused_computation.17 | convolution fusion | flops 2148270080 | bytes 35143680 | tf_op jit(solution)/shard_map/dot_general | solution.py:80
  23.7 0.0 copy-start.3
  23.7 1.1 %pad_maximum_fusion = f32[64,4608]{1,0:T(8,128)} fusion(f32[64,256]{1,0:T(8,128)S(1)} %fusion.9, f32[64,256]{1,0:T(8,128)S(1)} %fusion.11, f32[64,4096]{1,0:T(8,128)S(1)} %fusion.13), kind=kLoop, calls=%fused_computation.3 | loop fusion | flops 589824 | bytes 2359296 | tf_op jit(solution)/shard_map/concatenate | solution.py:85
  24.8 0.0 reduce-scatter.2.cloned.1.call-update
  24.9 0.1 lt.32
  24.9 0.7 compare_bitcast_fusion
  25.6 0.1 eq.19
  25.7 0.1 reshape.197
  25.8 1.2 %reshape.189 = bf16[16,64,2,128]{3,2,1,0:T(2,128)(2,1)S(1)} reshape(bf16[1024,256]{1,0:T(8,128)(2,1)} %param.15) | data formatting | bytes 1048576 | tf_op jit(solution)/shard_map/reshape | solution.py:107
  27.0 2.0 %reshape.191 = bf16[16,64,2,128]{3,2,1,0:T(2,128)(2,1)} reshape(bf16[1024,256]{1,0:T(8,128)(2,1)} %param.16) | data formatting | bytes 1048576 | tf_op jit(solution)/shard_map/reshape | solution.py:108
  29.0 0.2 fusion.5
  29.2 13.8 %psum.7 = f32[64]{0:T(128)S(1)} all-reduce(f32[64]{0:T(128)S(1)} %fusion.5), channel_id=1, replica_groups=mesh['groups'=2,'pool'=4,'tensor'=4] {'pool'}, use_global_device_ids=true, to_apply=%region_2.0 | all-reduce | flops 64 | bytes 512 | tf_op jit(solution)/shard_map/psum | solution.py:78
  43.0 0.1 add_rsqrt_fusion
  43.1 0.1 dynamic-slice_convert_fusion
  43.1 0.1 iota_compare_fusion
  43.2 0.1 multiply_cosine_fusion
  43.3 13.6 %reduce-scatter.2.cloned.1.call-done = f32[16,4608]{1,0:T(8,128)} async-done(((f32[64,4608]{1,0:T(8,128)}), f32[16,4608]{1,0:T(8,128)}) %reduce-scatter.2.cloned.1.call-update) | async-done | bytes 294928 | tf_op jit(solution)/shard_map/reduce_scatter | solution.py:85
  57.0 1.0 broadcast_multiply_fusion
  58.1 0.1 copy.26
  58.1 0.1 subtract_convert_fusion
  58.3 0.1 pad_maximum_fusion.1
  58.4 0.1 copy.41
  58.5 0.6 gather_fusion
  59.1 0.1 reshape.196
  59.2 0.8 broadcast_select_fusion
  59.9 3.3 %all-to-all-start = ((bf16[4,4,4096]{2,1,0:T(4,128)(2,1)}), bf16[4,4,4096]{2,1,0:T(4,128)(2,1)S(1)}, u32[]{:S(2)}, u32[]{:S(2)}) async-start(bf16[4,4,4096]{2,1,0:T(4,128)(2,1)} %broadcast_select_fusion), calls=%async_computation.1 | async-start | bytes 262144 | tf_op jit(solution)/shard_map/all_to_all | solution.py:95
  63.3 0.1 subtract_convert_fusion.1
  63.4 0.1 maximum_bitcast_fusion
  63.5 0.2 fusion.19
  63.7 0.1 copy.23
  63.8 5.6 %all-to-all-done = bf16[4,4,4096]{2,1,0:T(4,128)(2,1)S(1)} async-done(((bf16[4,4,4096]{2,1,0:T(4,128)(2,1)}), bf16[4,4,4096]{2,1,0:T(4,128)(2,1)S(1)}, u32[]{:S(2)}, u32[]{:S(2)}) %all-to-all-start) | async-done | bytes 131104 | tf_op jit(solution)/shard_map/all_to_all | solution.py:95
  69.4 0.2 reshape.188
  69.6 0.5 select_reduce_fusion.1
  70.0 0.3 fusion.16
  70.3 0.1 reshape_reshape.11
  70.4 0.7 reshape.209
  71.1 3.2 %all-to-all-start.3 = ((f32[4,1,128]{2,1,0:T(1,128)}), f32[4,1,128]{2,1,0:T(1,128)S(1)}, u32[]{:S(2)}, u32[]{:S(2)}) async-start(f32[4,1,128]{2,1,0:T(1,128)} %reshape.209), calls=%async_computation.4 | async-start | bytes 4096 | tf_op jit(solution)/shard_map/all_to_all | solution.py:118
  74.3 0.1 reshape_reshape.9
  74.4 0.7 reshape.207
  75.1 4.7 %all-to-all-done.3 = f32[4,1,128]{2,1,0:T(1,128)S(1)} async-done(((f32[4,1,128]{2,1,0:T(1,128)}), f32[4,1,128]{2,1,0:T(1,128)S(1)}, u32[]{:S(2)}, u32[]{:S(2)}) %all-to-all-start.3) | async-done | bytes 2080 | tf_op jit(solution)/shard_map/all_to_all | solution.py:118
  79.8 3.2 %all-to-all-start.1 = ((f32[4,1,128]{2,1,0:T(1,128)}), f32[4,1,128]{2,1,0:T(1,128)S(1)}, u32[]{:S(2)}, u32[]{:S(2)}) async-start(f32[4,1,128]{2,1,0:T(1,128)} %reshape.207), calls=%async_computation.2 | async-start | bytes 4096 | tf_op jit(solution)/shard_map/all_to_all | solution.py:117
  83.0 1.4 %fusion.6 = bf16[16,2,16,128]{3,2,1,0:T(8,128)(2,1)S(1)} fusion(bf16[16,64,2,128]{3,2,1,0:T(2,128)(2,1)} %reshape.191, f32[16,2,16,64]{3,2,1,0:T(8,128)S(1)} %get-tuple-element.16, f32[16,2,16]{2,1,0:T(2,128)S(1)} %get-tuple-element.15, pred[16,64]{1,0:T(8,128)(4,1)S(1)} %iota_compare_fusion), kind=kOutput, calls=%fused_computation.12 | convolution fusion | flops 8486912 | bytes 789504 | tf_op jit(solution)/shard_map/rkgt,rtkd->rkgd/dot_general | solution.py:39
  84.4 0.7 reshape_reshape.10
  85.1 0.5 broadcast.114
  85.6 0.6 reduce
  86.2 0.1 reshape.210
  86.3 0.1 copy.20
  86.3 2.0 %all-to-all-done.1 = f32[4,1,128]{2,1,0:T(1,128)S(1)} async-done(((f32[4,1,128]{2,1,0:T(1,128)}), f32[4,1,128]{2,1,0:T(1,128)S(1)}, u32[]{:S(2)}, u32[]{:S(2)}) %all-to-all-start.1) | async-done | bytes 2080 | tf_op jit(solution)/shard_map/all_to_all | solution.py:117
  88.4 3.3 %all-to-all-start.2 = ((bf16[4,4,4096]{2,1,0:T(4,128)(2,1)}), bf16[4,4,4096]{2,1,0:T(4,128)(2,1)S(1)}, u32[]{:S(2)}, u32[]{:S(2)}) async-start(bf16[4,4,4096]{2,1,0:T(4,128)(2,1)} %reshape_reshape.10), calls=%async_computation.3 | async-start | bytes 262144 | tf_op jit(solution)/shard_map/all_to_all | solution.py:116
  91.7 0.6 reduce.1
  92.3 0.1 reshape.208
  92.4 0.1 copy.16
  92.5 0.1 select_reduce_fusion
  92.6 0.2 multiply_reduce_fusion
  92.9 0.1 bitcast_multiply_fusion
  93.0 4.6 %all-to-all-done.2 = bf16[4,4,4096]{2,1,0:T(4,128)(2,1)S(1)} async-done(((bf16[4,4,4096]{2,1,0:T(4,128)(2,1)}), bf16[4,4,4096]{2,1,0:T(4,128)(2,1)S(1)}, u32[]{:S(2)}, u32[]{:S(2)}) %all-to-all-start.2) | async-done | bytes 131104 | tf_op jit(solution)/shard_map/all_to_all | solution.py:116
  97.6 0.2 reshape.192
  97.8 0.3 fusion.3
  98.0 0.7 copy.42
  (19 shorter events, 0.1 us)
Async XLA Ops:
  6.5 1.6 %copy-start = (bf16[4096,256]{1,0:T(8,128)(2,1)S(1)}, bf16[4096,256]{1,0:T(8,128)(2,1)}, u32[]{:S(2)}) copy-start(bf16[4096,256]{1,0:T(8,128)(2,1)} %param.14) | copy-start | bytes 6291460
  6.5 3.1 %copy-start.1 = (bf16[64,4096]{1,0:T(8,128)(2,1)S(1)}, bf16[64,4096]{1,0:T(8,128)(2,1)}, u32[]{:S(2)}) copy-start(bf16[64,4096]{1,0:T(8,128)(2,1)} %param.10) | copy-start | bytes 1572868
  6.5 50.4 %reduce-scatter.2.cloned.1.call-start = ((), (), s32[]{:S(2)}) async-start(), calls=%async_computation.5 | async-start | bytes 1474560 | tf_op jit(solution)/shard_map/reduce_scatter | solution.py:85
  6.5 3.1 %copy-start.2 = (bf16[4096,256]{1,0:T(8,128)(2,1)S(1)}, bf16[4096,256]{1,0:T(8,128)(2,1)}, u32[]{:S(2)}) copy-start(bf16[4096,256]{1,0:T(8,128)(2,1)} %param.13) | copy-start | bytes 6291460
  23.7 1.1 %copy-start.3 = (s32[1,4,4]{2,1,0:T(4,128)S(1)}, s32[1,4,4]{2,1,0:T(4,128)}, u32[]{:S(2)}) copy-start(s32[1,4,4]{2,1,0:T(4,128)} %param.18) | copy-start | bytes 196
  24.8 18.2 %copy-start.4 = (s32[64]{0:T(128)S(1)}, s32[64]{0:T(128)}, u32[]{:S(2)}) copy-start(s32[64]{0:T(128)} %param.19) | copy-start | bytes 772
  59.9 9.5 %all-to-all-start = ((bf16[4,4,4096]{2,1,0:T(4,128)(2,1)}), bf16[4,4,4096]{2,1,0:T(4,128)(2,1)S(1)}, u32[]{:S(2)}, u32[]{:S(2)}) async-start(bf16[4,4,4096]{2,1,0:T(4,128)(2,1)} %broadcast_select_fusion), calls=%async_computation.1 | async-start | bytes 262144 | tf_op jit(solution)/shard_map/all_to_all | solution.py:95
  71.1 8.7 %all-to-all-start.3 = ((f32[4,1,128]{2,1,0:T(1,128)}), f32[4,1,128]{2,1,0:T(1,128)S(1)}, u32[]{:S(2)}, u32[]{:S(2)}) async-start(f32[4,1,128]{2,1,0:T(1,128)} %reshape.209), calls=%async_computation.4 | async-start | bytes 4096 | tf_op jit(solution)/shard_map/all_to_all | solution.py:118
  79.8 8.6 %all-to-all-start.1 = ((f32[4,1,128]{2,1,0:T(1,128)}), f32[4,1,128]{2,1,0:T(1,128)S(1)}, u32[]{:S(2)}, u32[]{:S(2)}) async-start(f32[4,1,128]{2,1,0:T(1,128)} %reshape.207), calls=%async_computation.2 | async-start | bytes 4096 | tf_op jit(solution)/shard_map/all_to_all | solution.py:117
  88.4 9.2 %all-to-all-start.2 = ((bf16[4,4,4096]{2,1,0:T(4,128)(2,1)}), bf16[4,4,4096]{2,1,0:T(4,128)(2,1)S(1)}, u32[]{:S(2)}, u32[]{:S(2)}) async-start(bf16[4,4,4096]{2,1,0:T(4,128)(2,1)} %reshape_reshape.10), calls=%async_computation.3 | async-start | bytes 262144 | tf_op jit(solution)/shard_map/all_to_all | solution.py:116
Sparse Core Ops, SparseCore 0:
  25.0 31.9 reduce-scatter.1
where the time goes:
time: 106 us
  waiting for transfers between devices  30.5 us (29%)
  matrix products  17.9 us (17%)
  blocking collectives  13.8 us (13%)
  between operations  13.7 us (13%)
  starting transfers between devices  13.1 us (12%)
  local copies, waits for them, and re-layouts  9.09 us (9%)
  other arithmetic  7.47 us (7%)
    dot_general x3, matrix products, body(): jnp.dot(scaled, weights, preferred_element_type=jnp.float32)  15.5 us
    psum x1, blocking collectives, body(): power_all = lax.psum(jnp.sum(x_float * x_float, axis=1), 'pool')  13.8 us
    reduce_scatter x1, waiting for transfers between devices, body(): lax.psum_scatter(jnp.concatenate(parts_list, 1), 'pool', scatter_dimensio...  13.6 us
    all_to_all x1, waiting for transfers between devices, body(): lax.all_to_all(outgoing, 'pool', split_axis=0, concat_axis=0, tiled=True)  5.59 us
    all_to_all x1, waiting for transfers between devices, body(): lax.all_to_all(totals, 'pool', split_axis=0, concat_axis=0, tiled=True)  4.66 us
    all_to_all x1, waiting for transfers between devices, body(): lax.all_to_all(blended, 'pool', split_axis=0, concat_axis=0, tiled=True)  4.57 us
    all_to_all x1, starting transfers between devices, body(): lax.all_to_all(blended, 'pool', split_axis=0, concat_axis=0, tiled=True)  3.33 us
    all_to_all x1, starting transfers between devices, body(): lax.all_to_all(outgoing, 'pool', split_axis=0, concat_axis=0, tiled=True)  3.33 us
  transfers between devices with their start and end apart: 5, of which 5 were waited for; matrix products, arithmetic and copies ran while one was open for 10% of the time, Pallas kernels for 0%

commit v1 on v0

v1 whole, which is shorter than its diff:
```python
import functools

import jax
import jax.numpy as jnp
import numpy as np
from jax import lax
from jax.experimental import pallas as pl
from jax.experimental.pallas import tpu as pltpu
from jax.sharding import PartitionSpec as P

HD = 128
EPS = 1e-05
THETA = 500000.0
LOW = -1e30
WINDOW = 6


def divides(width, limit):
    while width % limit:
        limit //= 2
    return limit


def split3(x):
    a = x.astype(jnp.bfloat16).astype(jnp.float32)
    r = x - a
    b = r.astype(jnp.bfloat16).astype(jnp.float32)
    return a, b, (r - b).astype(jnp.bfloat16).astype(jnp.float32)


def project_kernel(pool, slots, rows_local, meta, row_len, hidden, gain, *rest):
    n_w = 3
    weights, rest = rest[:n_w], rest[n_w:]
    outs, rest = rest[:pool], rest[pool:]
    pos_out, x_buf, g_buf, pick, lhs, *bufs, in_sem, sems = rest
    per = pool * slots
    n_slots = pool * per
    tiles = []
    for n, (w, buf) in enumerate(zip(weights, bufs)):
        width = buf.shape[2]
        for t in range(buf.shape[0]):
            tiles.append((n, t, width))

    def copy(i):
        n, t, width = tiles[i]
        return pltpu.make_async_copy(
            weights[n].at[:, t * width : (t + 1) * width], bufs[n].at[t], sems.at[i]
        )

    x_copy = pltpu.make_async_copy(hidden, x_buf, in_sem.at[0])
    g_copy = pltpu.make_async_copy(gain, g_buf, in_sem.at[1])
    x_copy.start()
    g_copy.start()
    for i in range(min(WINDOW, len(tiles))):
        copy(i).start()

    me = meta[0]
    n_rows = x_buf.shape[0]
    lane = lax.broadcasted_iota(jnp.int32, (1, n_rows), 1)

    def slot_row(k, j, c):
        owner = lax.rem(me + k, pool)
        home = lax.rem(owner + j, pool)
        r = meta[1 + home * per + owner * slots + c]
        return jnp.where(r >= 0, home * rows_local + r, -1)

    def fill(i, carry):
        k, s = i // per, lax.rem(i, per)
        row = slot_row(k, s // slots, lax.rem(s, slots))
        pick[pl.ds(i, 1), :] = (lane == row).astype(jnp.float32)
        return carry

    lax.fori_loop(0, n_slots, fill, 0)

    def fill_pos(s, carry):
        row = slot_row(0, s // slots, lax.rem(s, slots))
        at = row_len[jnp.maximum(row, 0)].astype(jnp.float32)
        pos_out[pl.ds(s, 1), :] = jnp.full((1, HD), at, jnp.float32)
        return carry

    lax.fori_loop(0, per, fill_pos, 0)

    x_copy.wait()
    g_copy.wait()
    x = x_buf[...].astype(jnp.float32)
    power = jnp.sum(x * x, axis=1, keepdims=True)
    scaled = (x * g_buf[...].astype(jnp.float32)).astype(jnp.bfloat16)
    chosen = pick[...].astype(jnp.bfloat16)
    lhs[...] = jnp.dot(chosen, scaled, preferred_element_type=jnp.float32).astype(jnp.bfloat16)
    at = lax.broadcasted_iota(jnp.int32, (n_rows, HD), 1)
    a, b, c = split3(power)
    aux = jnp.where(at == 0, a, jnp.where(at == 1, b, jnp.where(at == 2, c, 0.0)))
    aux = jnp.dot(chosen, aux.astype(jnp.bfloat16), preferred_element_type=jnp.float32)
    tail = outs[0].shape[1] - HD
    for k in range(pool):
        outs[k][:, tail:] = aux[k * per : (k + 1) * per].astype(outs[k].dtype)

    start = 0
    first = 0
    for n in range(n_w):
        count, width = bufs[n].shape[0], bufs[n].shape[2]

        def column(t, carry, n=n, first=first, start=start, width=width):
            i = first + t
            pltpu.make_async_copy(
                weights[n].at[:, pl.ds(pl.multiple_of(t * width, width), width)],
                bufs[n].at[t],
                sems.at[i],
            ).wait()
            part = jnp.dot(lhs[...], bufs[n][t], preferred_element_type=jnp.float32)
            for k in range(pool):
                outs[k][:, pl.ds(pl.multiple_of(start + t * width, width), width)] = part[
                    k * per : (k + 1) * per
                ].astype(outs[k].dtype)
            return carry

        t = 0
        while t < count:
            ahead = first + t + WINDOW
            if ahead < len(tiles):
                m, u, w_ahead = tiles[ahead]
                run = 1
                while (
                    t + run < count
                    and ahead + run < len(tiles)
                    and tiles[ahead + run][0] == m
                ):
                    run += 1

                def step(q, carry, m=m, u=u, w=w_ahead, t=t, ahead=ahead):
                    pltpu.make_async_copy(
                        weights[m].at[:, pl.ds(pl.multiple_of((u + q) * w, w), w)],
                        bufs[m].at[u + q],
                        sems.at[ahead + q],
                    ).start()
                    return column(t + q, carry)

                lax.fori_loop(0, run, step, 0)
            else:
                run = count - t
                lax.fori_loop(t, count, column, 0)
            t += run
        start += count * width
        first += count


def attend_kernel(pool, slots, seg, width_d, q_heads, kv_heads, meta, first, lens, *rest):
    parts, rest = rest[:pool], rest[pool:]
    cos, sin, keys, values = rest[:4]
    outs, rest = rest[4 : 4 + pool], rest[4 + pool :]
    q_buf, k_buf, v_buf = rest
    per = pool * slots
    group = q_heads // kv_heads
    scale = HD ** (-0.5)

    def total(at):
        got = parts[0][:, at : at + HD].astype(jnp.float32)
        for part in parts[1:]:
            got = got + part[:, at : at + HD].astype(jnp.float32)
        return got

    power = jnp.sum(total((q_heads + 2 * kv_heads) * HD), axis=1, keepdims=True)
    factor = lax.rsqrt(power * (1.0 / width_d) + EPS)
    cosines, sines = cos[...], sin[...]

    def rounded(x):
        return x.astype(jnp.bfloat16).astype(jnp.float32)

    def rotated(x):
        return rounded(x * cosines + pltpu.roll(x, HD // 2, axis=1) * sines)

    for i in range(q_heads):
        q_buf[i * per : (i + 1) * per, :] = rotated(total(i * HD) * factor)
    for g in range(kv_heads):
        k_buf[g * per : (g + 1) * per, :] = rotated(total((q_heads + g) * HD) * factor)
        v_buf[g * per : (g + 1) * per, :] = rounded(
            total((q_heads + kv_heads + g) * HD) * factor
        )

    me = meta[0]
    lane = lax.broadcasted_iota(jnp.int32, (group, HD), 1)
    at = lax.broadcasted_iota(jnp.int32, (group, seg), 1)
    for j in range(pool):
        home = lax.rem(me + j, pool)
        marks = [jnp.zeros((group, HD), jnp.float32) for _ in range(kv_heads)]
        for c in range(slots):
            s = j * slots + c
            cell = home * slots + c
            base = pl.multiple_of(cell * seg, seg)
            length = lens[cell]
            own = first[cell]
            usable = at < length
            for g in range(kv_heads):
                query = q_buf[pl.ds(g * group * per + s, group, stride=per), :]
                key_block = keys[pl.ds(base, seg), g * HD : (g + 1) * HD]
                value_block = values[pl.ds(base, seg), g * HD : (g + 1) * HD]
                score = (
                    lax.dot_general(
                        query.astype(jnp.bfloat16),
                        key_block,
                        (((1,), (1,)), ((), ())),
                        preferred_element_type=jnp.float32,
                    )
                    * scale
                )
                key_own = k_buf[g * per + s : g * per + s + 1, :]
                value_own = v_buf[g * per + s : g * per + s + 1, :]
                score_own = jnp.sum(query * key_own, axis=1, keepdims=True) * scale
                score_own = jnp.where(own > 0, score_own, LOW)
                top = jnp.maximum(
                    jnp.max(jnp.where(usable, score, LOW), axis=1, keepdims=True), score_own
                )
                weight = jnp.where(usable, jnp.exp(score - top), 0.0)
                weight_own = jnp.where(own > 0, jnp.exp(score_own - top), 0.0)
                sums = jnp.sum(weight, axis=1, keepdims=True) + weight_own
                sums = jnp.where(length > 0, sums, 1.0)
                mixed = (
                    jnp.dot(
                        weight.astype(jnp.bfloat16),
                        value_block,
                        preferred_element_type=jnp.float32,
                    )
                    + weight_own * value_own
                )
                to = c * q_heads + g * group
                outs[j][to : to + group, :] = (mixed / sums).astype(jnp.bfloat16)
                level = split3(top + jnp.log(sums))
                for piece in range(3):
                    marks[g] = jnp.where(lane == piece * slots + c, level[piece], marks[g])
        for g in range(kv_heads):
            to = slots * q_heads + g * group
            outs[j][to : to + group, :] = marks[g].astype(jnp.bfloat16)


def merge_kernel(pool, slots, rows_local, q_heads, meta, *rest):
    parts, (out, o_buf, f_buf) = rest[:pool], rest[pool:]
    per = pool * slots
    block = slots * q_heads
    me = meta[0]
    lane = lax.broadcasted_iota(jnp.int32, (q_heads, HD), 1)
    level = jnp.zeros((q_heads, HD), jnp.float32)
    slot_rows = jnp.full((1, HD), -1, jnp.int32)
    for k in range(pool):
        o_buf[k * block : (k + 1) * block, :] = parts[k][:block, :].astype(jnp.float32)
        marks = parts[k][block:, :].astype(jnp.float32)
        marks = (
            marks + pltpu.roll(marks, HD - slots, axis=1) + pltpu.roll(marks, HD - 2 * slots, axis=1)
        )
        if k:
            marks = pltpu.roll(marks, k * slots, axis=1)
        level = jnp.where((lane >= k * slots) & (lane < (k + 1) * slots), marks, level)
        owner = lax.rem(me + pool - k, pool)
        for c in range(slots):
            r = meta[1 + me * per + owner * slots + c]
            slot_rows = jnp.where(lane[:1] == k * slots + c, r, slot_rows)
    for r in range(rows_local):
        match = slot_rows == r
        top = jnp.max(jnp.where(match, level, LOW), axis=1, keepdims=True)
        factor = jnp.where(match, jnp.exp(level - top), 0.0)
        factor = factor / jnp.sum(factor, axis=1, keepdims=True)
        high = factor.astype(jnp.bfloat16).astype(jnp.float32)
        low = pltpu.roll(factor - high, per, axis=1)
        f_buf[pl.ds(r, q_heads, stride=rows_local), :] = high + low
    for i in range(q_heads):
        o = o_buf[pl.ds(i, per, stride=q_heads), :].astype(jnp.bfloat16)
        f = f_buf[i * rows_local : (i + 1) * rows_local, : 2 * per].astype(jnp.bfloat16)
        out[:, i * HD : (i + 1) * HD] = jnp.dot(
            f, jnp.concatenate([o, o], axis=0), preferred_element_type=jnp.float32
        ).astype(jnp.bfloat16)


def exchange(parts):
    pool = len(parts)
    return [parts[0]] + [
        lax.ppermute(parts[k], "pool", [(i, (i + k) % pool) for i in range(pool)])
        for k in range(1, pool)
    ]


SMEM = pl.BlockSpec(memory_space=pltpu.SMEM)
VMEM = pl.BlockSpec(memory_space=pltpu.VMEM)
ANY = pl.BlockSpec(memory_space=pl.ANY)


def body(
    hidden_in,
    norm_gain,
    w_query,
    w_key,
    w_value,
    cache_keys,
    cache_values,
    send_row,
    piece_len,
    row_len,
):
    pool = lax.axis_size("pool")
    me = lax.axis_index("pool")
    n_rows, depth = hidden_in.shape
    width_d = depth * pool
    rows_local = n_rows // pool
    slots = send_row.shape[2]
    per = pool * slots
    seg = cache_keys.shape[0] // per
    q_cols, kv_cols = w_query.shape[1], w_key.shape[1]
    q_heads, kv_heads = q_cols // HD, kv_cols // HD
    cols = q_cols + 2 * kv_cols + HD

    meta = jnp.concatenate([me[None].astype(jnp.int32), send_row.reshape(-1)])
    lens = piece_len.reshape(-1)

    weights = (w_query, w_key, w_value)
    bufs = []
    n_tiles = 0
    for w in weights:
        width = divides(w.shape[1], 256)
        bufs.append(pltpu.VMEM((w.shape[1] // width, depth, width), jnp.bfloat16))
        n_tiles += w.shape[1] // width
    *terms, positions = pl.pallas_call(
        functools.partial(project_kernel, pool, slots, rows_local),
        out_shape=[jax.ShapeDtypeStruct((per, cols), jnp.float32)]
        + [jax.ShapeDtypeStruct((per, cols), jnp.bfloat16)] * (pool - 1)
        + [jax.ShapeDtypeStruct((per, HD), jnp.float32)],
        in_specs=[SMEM, SMEM] + [ANY] * 5,
        out_specs=[VMEM] * (pool + 1),
        scratch_shapes=[
            pltpu.VMEM((n_rows, depth), jnp.bfloat16),
            pltpu.VMEM((1, depth), jnp.bfloat16),
            pltpu.VMEM((pool * per, n_rows), jnp.float32),
            pltpu.VMEM((pool * per, depth), jnp.bfloat16),
            *bufs,
            pltpu.SemaphoreType.DMA((2,)),
            pltpu.SemaphoreType.DMA((n_tiles,)),
        ],
        compiler_params=pltpu.CompilerParams(vmem_limit_bytes=50 * 2**20),
        name="project",
    )(meta, row_len, hidden_in, norm_gain.reshape(1, depth), *weights)

    terms = exchange(terms)

    named = send_row.reshape(pool, per)
    mine = lax.dynamic_slice_in_dim(send_row, me, 1, 1)[:, 0, :]
    order = me * slots + jnp.arange(slots, dtype=jnp.int32)
    earlier = (named[:, None, :] == mine[:, :, None]) & (
        jnp.arange(per, dtype=jnp.int32)[None, None, :] < order[None, :, None]
    )
    first = ((mine >= 0) & ~jnp.any(earlier, axis=2)).astype(jnp.int32).reshape(-1)

    half = HD // 2
    freq = THETA ** (-(np.arange(half) * 2.0) / HD)
    angles = positions * np.concatenate([freq, freq]).astype(np.float32)[None, :]
    sign = np.concatenate([-np.ones(half), np.ones(half)]).astype(np.float32)[None, :]
    cosines, sines = jnp.cos(angles), jnp.sin(angles) * sign

    found = pl.pallas_call(
        functools.partial(attend_kernel, pool, slots, seg, width_d, q_heads, kv_heads),
        out_shape=[jax.ShapeDtypeStruct(((slots + 1) * q_heads, HD), jnp.bfloat16)] * pool,
        in_specs=[SMEM] * 3 + [VMEM] * (pool + 4),
        out_specs=[VMEM] * pool,
        scratch_shapes=[
            pltpu.VMEM((q_heads * per, HD), jnp.float32),
            pltpu.VMEM((kv_heads * per, HD), jnp.float32),
            pltpu.VMEM((kv_heads * per, HD), jnp.float32),
        ],
        compiler_params=pltpu.CompilerParams(vmem_limit_bytes=24 * 2**20),
        name="attend",
    )(meta, first, lens, *terms, cosines, sines, cache_keys, cache_values)

    found = exchange(found)

    return pl.pallas_call(
        functools.partial(merge_kernel, pool, slots, rows_local, q_heads),
        out_shape=jax.ShapeDtypeStruct((rows_local, q_cols), jnp.bfloat16),
        in_specs=[SMEM] + [VMEM] * pool,
        out_specs=VMEM,
        scratch_shapes=[
            pltpu.VMEM((per * q_heads, HD), jnp.float32),
            pltpu.VMEM((rows_local * q_heads, HD), jnp.float32),
        ],
        compiler_params=pltpu.CompilerParams(vmem_limit_bytes=24 * 2**20),
        name="merge",
    )(meta, *found)


def solution(mesh):
    return jax.shard_map(
        body,
        mesh=mesh,
        in_specs=(
            P("groups", "pool"),
            P("pool"),
            P("pool", "tensor"),
            P("pool", "tensor"),
            P("pool", "tensor"),
            P(("groups", "pool"), "tensor"),
            P(("groups", "pool"), "tensor"),
            P("groups", None, None),
            P(("groups", "pool"), None, None),
            P("groups"),
        ),
        out_specs=P(("groups", "pool"), "tensor"),
        check_vma=False,
    )
```

time: 106 us -> 54 us (0.51)
  Pallas kernels: 0 us -> 23.7 us
  waiting for transfers between devices: 30.5 us -> 11.1 us
  matrix products: 17.9 us -> 0 us
  blocking collectives: 13.8 us -> 0 us
  between operations: 13.7 us -> 0.08 us
  other arithmetic: 7.47 us -> 0.47 us
  local copies, waits for them, and re-layouts: 9.09 us -> 5.15 us
    pallas_call x0 -> x3, Pallas kernels: none -> 23.7 us  [the longest x1 13.8 us: body(): pl.pallas_call(functools.partial(project_kernel, pool, slots, rows_local)...]
    dot_general x7 -> x0, matrix products: 17.9 us -> none  [the longest x3 15.5 us: body(): jnp.dot(scaled, weights, preferred_element_type=jnp.float32)]
    all_to_all x4 -> x0, waiting for transfers between devices: 16.9 us -> none  [the longest x1 5.59 us: body(): lax.all_to_all(outgoing, 'pool', split_axis=0, concat_axis=0, tiled=True)]
    psum x1 -> x0, blocking collectives: 13.8 us -> none  [body(): power_all = lax.psum(jnp.sum(x_float * x_float, axis=1), 'pool')]
    reduce_scatter x1 -> x0, waiting for transfers between devices: 13.6 us -> none  [body(): lax.psum_scatter(jnp.concatenate(parts_list, 1), 'pool', scatter_dimensio...]
    ppermute x0 -> x6, starting transfers between devices: none -> 13.2 us  [exchange(): lax.ppermute(parts[k], 'pool', [(i, (i + k) % pool) for i in range(pool)])]
    all_to_all x4 -> x0, starting transfers between devices: 13.1 us -> none  [the longest x1 3.33 us: body(): lax.all_to_all(blended, 'pool', split_axis=0, concat_axis=0, tiled=True)]
    ppermute x0 -> x6, waiting for transfers between devices: none -> 11.1 us  [exchange(): lax.ppermute(parts[k], 'pool', [(i, (i + k) % pool) for i in range(pool)])]
  transfers between devices with their start and end apart: 5 -> 6, of which waited for: 5 -> 5; matrix products, arithmetic and copies ran while one was open for 10% -> 1% of each run, Pallas kernels for 0% -> 0%
where the time goes in v1:
time: 54 us; the launch traced here: 53.7 us
  Pallas kernels  23.7 us (44%)
  starting transfers between devices  13.2 us (24%)
  waiting for transfers between devices  11.1 us (21%)
  local copies, waits for them, and re-layouts  5.15 us (10%)
    pallas_call x1, Pallas kernels, body(): pl.pallas_call(functools.partial(project_kernel, pool, slots, rows_local)...  13.8 us
    ppermute x6, starting transfers between devices, exchange(): lax.ppermute(parts[k], 'pool', [(i, (i + k) % pool) for i in range(pool)])  13.2 us
    ppermute x6, waiting for transfers between devices, exchange(): lax.ppermute(parts[k], 'pool', [(i, (i + k) % pool) for i in range(pool)])  11.1 us
    pallas_call x1, Pallas kernels, body(): pl.pallas_call(functools.partial(attend_kernel, pool, slots, seg, width_d...  7.91 us
    unnamed x18, local copies, waits for them, and re-layouts  3.31 us
    pallas_call x1, Pallas kernels, body(): pl.pallas_call(functools.partial(merge_kernel, pool, slots, rows_local, q...  1.96 us
  transfers between devices with their start and end apart: 6, of which 5 were waited for; matrix products, arithmetic and copies ran while one was open for 1% of the time, Pallas kernels for 0%

profile of v1, /device:TPU:0, one launch (start us, length us, event | category | flops | bytes accessed | tf_op | source)
XLA Modules:
  0.0 53.7 jit_solution(16470338093280838608)
XLA Ops:
  0.0 0.8 %reshape.44 = s32[64]{0:T(128)S(1)} reshape(s32[4,4,4]{2,1,0:T(4,128)} %param.19) | data formatting | bytes 512 | tf_op jit(solution)/shard_map/reshape | solution.py:309
  0.8 0.7 %reshape.46.gain = bf16[1,4096]{1,0:T(2,128)(2,1)S(1)} reshape(bf16[4096]{0:T(1024)(128)(2,1)} %param.13) | data formatting | bytes 16384 | tf_op jit(solution)/shard_map/reshape | solution.py:337
  1.5 0.1 pad_add_fusion.meta
  1.6 0.0 copy-start
  1.6 1.6 %copy-done = bf16[4096,256]{1,0:T(8,128)(2,1)S(1)} copy-done((bf16[4096,256]{1,0:T(8,128)(2,1)S(1)}, bf16[4096,256]{1,0:T(8,128)(2,1)}, u32[]{:S(2)}) %copy-start) | copy-done | bytes 2097176
  3.2 0.0 copy-start.1
  3.2 1.0 %copy-done.1 = bf16[64,4096]{1,0:T(8,128)(2,1)S(1)} copy-done((bf16[64,4096]{1,0:T(8,128)(2,1)S(1)}, bf16[64,4096]{1,0:T(8,128)(2,1)}, u32[]{:S(2)}) %copy-start.1) | copy-done | bytes 524312
  4.2 0.0 copy-start.4
  4.2 0.7 %copy-done.4 = s32[64]{0:T(128)S(1)} copy-done((s32[64]{0:T(128)S(1)}, s32[64]{0:T(128)}, u32[]{:S(2)}) %copy-start.4) | copy-done | bytes 280
  4.9 0.0 copy-start.5
  4.9 0.0 copy-start.6
  4.9 0.0 copy-start.7
  4.9 0.0 copy-start.8
  4.9 0.0 copy-start.2
  4.9 0.0 copy-start.3
  4.9 13.8 %project.1 = (f32[16,4736]{1,0:T(8,128)S(1)}, bf16[16,4736]{1,0:T(8,128)(2,1)S(1)}, bf16[16,4736]{1,0:T(8,128)(2,1)S(1)}, bf16[16,4736]{1,0:T(8,128)(2,1)S(1)}, f32[16,128]{1,0:T(8,128)S(1)}) custom-call(s32[65]{0:T(128)S(1)} %pad_add_fusion.meta, s32[64]{0:T(128)S(1)} %copy-done.4, bf16[64,4096]{1,0:T(8,128)(2,1)S(1)} %copy-done.1, ...), custom_call_target="tpu_custom_call" | custom-call | tf_op jit(solution)/shard_map/project/pallas_call | solution.py:319
  18.7 3.1 %collective-permute-start = (bf16[16,4736]{1,0:T(8,128)(2,1)S(1)}, bf16[16,4736]{1,0:T(8,128)(2,1)S(1)}, u32[]{:S(2)}, u32[]{:S(2)}) collective-permute-start(bf16[16,4736]{1,0:T(8,128)(2,1)S(1)} %get-tuple-element.15), channel_id=1, source_target_pairs={{0,4},{4,8},{8,12},{12,0},{1,5},{5,9},{9,13},{13,1},{2,6},{6,10},{... | collective-permute-start | bytes 454664 | tf_op jit(solution)/shard_map/ppermute | solution.py:275
  21.8 2.6 %collective-permute-start.1 = (bf16[16,4736]{1,0:T(8,128)(2,1)S(1)}, bf16[16,4736]{1,0:T(8,128)(2,1)S(1)}, u32[]{:S(2)}, u32[]{:S(2)}) collective-permute-start(bf16[16,4736]{1,0:T(8,128)(2,1)S(1)} %get-tuple-element.16), channel_id=1, source_target_pairs={{0,8},{4,12},{8,0},{12,4},{1,9},{5,13},{9,1},{13,5},{2,10},{6,14},... | collective-permute-start | bytes 454664 | tf_op jit(solution)/shard_map/ppermute | solution.py:275
  24.4 1.3 %collective-permute-start.2 = (bf16[16,4736]{1,0:T(8,128)(2,1)S(1)}, bf16[16,4736]{1,0:T(8,128)(2,1)S(1)}, u32[]{:S(2)}, u32[]{:S(2)}) collective-permute-start(bf16[16,4736]{1,0:T(8,128)(2,1)S(1)} %get-tuple-element.17), channel_id=1, source_target_pairs={{0,12},{4,0},{8,4},{12,8},{1,13},{5,1},{9,5},{13,9},{2,14},{6,2},{... | collective-permute-start | bytes 454664 | tf_op jit(solution)/shard_map/ppermute | solution.py:275
  25.7 0.0 copy-done.5
  25.7 0.1 eq.17
  25.8 0.1 iota_compare_fusion
  25.9 0.0 copy-done.6
  25.9 0.1 reshape.45.lens
  26.0 0.1 ge.8
  26.1 0.2 and_reduce_fusion
  26.3 0.1 not.8
  26.4 0.0 copy-done.7
  26.4 0.0 copy-done.8
  26.4 0.1 sine_multiply_fusion
  26.5 2.2 %collective-permute-done.rest_1_ = bf16[16,4736]{1,0:T(8,128)(2,1)S(1)} collective-permute-done((bf16[16,4736]{1,0:T(8,128)(2,1)S(1)}, bf16[16,4736]{1,0:T(8,128)(2,1)S(1)}, u32[]{:S(2)}, u32[]{:S(2)}) %collective-permute-start) | collective-permute-done | bytes 151584 | tf_op jit(solution)/shard_map/ppermute | solution.py:275
  28.7 5.7 %collective-permute-done.1.rest_2_ = bf16[16,4736]{1,0:T(8,128)(2,1)S(1)} collective-permute-done((bf16[16,4736]{1,0:T(8,128)(2,1)S(1)}, bf16[16,4736]{1,0:T(8,128)(2,1)S(1)}, u32[]{:S(2)}, u32[]{:S(2)}) %collective-permute-start.1) | collective-permute-done | bytes 151584 | tf_op jit(solution)/shard_map/ppermute | solution.py:275
  34.4 0.0 collective-permute-done.2.rest_3_
  34.4 0.0 copy-done.2
  34.4 0.0 copy-done.3
  34.4 7.9 %attend.1 = (bf16[160,128]{1,0:T(8,128)(2,1)S(1)}, bf16[160,128]{1,0:T(8,128)(2,1)S(1)}, bf16[160,128]{1,0:T(8,128)(2,1)S(1)}, bf16[160,128]{1,0:T(8,128)(2,1)S(1)}) custom-call(s32[65]{0:T(128)S(1)} %pad_add_fusion.meta, s32[16]{0:T(128)S(1)} %and_convert_fusion.first, s32[16]{0:T(128)S(1)} %reshape.45.lens, f32[16,4736]{1,0:T(8,128)S(1)} %get-tuple-element.14.rest_0_, ...), custom_call_target="tpu_custom_call" | custom-call | tf_op jit(solution)/shard_map/attend/pallas_call | solution.py:355
  42.3 3.8 %collective-permute-start.3 = (bf16[160,128]{1,0:T(8,128)(2,1)S(1)}, bf16[160,128]{1,0:T(8,128)(2,1)S(1)}, u32[]{:S(2)}, u32[]{:S(2)}) collective-permute-start(bf16[160,128]{1,0:T(8,128)(2,1)S(1)} %get-tuple-element.20), channel_id=1, source_target_pairs={{0,4},{4,8},{8,12},{12,0},{1,5},{5,9},{9,13},{13,1},{2,6},{6,10},{... | collective-permute-start | bytes 122888 | tf_op jit(solution)/shard_map/ppermute | solution.py:275
  46.0 1.6 %collective-permute-start.4 = (bf16[160,128]{1,0:T(8,128)(2,1)S(1)}, bf16[160,128]{1,0:T(8,128)(2,1)S(1)}, u32[]{:S(2)}, u32[]{:S(2)}) collective-permute-start(bf16[160,128]{1,0:T(8,128)(2,1)S(1)} %get-tuple-element.21), channel_id=1, source_target_pairs={{0,8},{4,12},{8,0},{12,4},{1,9},{5,13},{9,1},{13,5},{2,10},{6,14},... | collective-permute-start | bytes 122888 | tf_op jit(solution)/shard_map/ppermute | solution.py:275
  47.7 0.8 %collective-permute-start.5 = (bf16[160,128]{1,0:T(8,128)(2,1)S(1)}, bf16[160,128]{1,0:T(8,128)(2,1)S(1)}, u32[]{:S(2)}, u32[]{:S(2)}) collective-permute-start(bf16[160,128]{1,0:T(8,128)(2,1)S(1)} %get-tuple-element.22), channel_id=1, source_target_pairs={{0,12},{4,0},{8,4},{12,8},{1,13},{5,1},{9,5},{13,9},{2,14},{6,2},{... | collective-permute-start | bytes 122888 | tf_op jit(solution)/shard_map/ppermute | solution.py:275
  48.5 0.7 %collective-permute-done.3.rest_1_ = bf16[160,128]{1,0:T(8,128)(2,1)S(1)} collective-permute-done((bf16[160,128]{1,0:T(8,128)(2,1)S(1)}, bf16[160,128]{1,0:T(8,128)(2,1)S(1)}, u32[]{:S(2)}, u32[]{:S(2)}) %collective-permute-start.3) | collective-permute-done | bytes 40992 | tf_op jit(solution)/shard_map/ppermute | solution.py:275
  49.2 2.1 %collective-permute-done.4.rest_2_ = bf16[160,128]{1,0:T(8,128)(2,1)S(1)} collective-permute-done((bf16[160,128]{1,0:T(8,128)(2,1)S(1)}, bf16[160,128]{1,0:T(8,128)(2,1)S(1)}, u32[]{:S(2)}, u32[]{:S(2)}) %collective-permute-start.4) | collective-permute-done | bytes 40992 | tf_op jit(solution)/shard_map/ppermute | solution.py:275
  51.3 0.4 collective-permute-done.5.rest_3_
  51.7 2.0 %merge.1 = bf16[16,4096]{1,0:T(8,128)(2,1)} custom-call(s32[65]{0:T(128)S(1)} %pad_add_fusion.meta, bf16[160,128]{1,0:T(8,128)(2,1)S(1)} %get-tuple-element.19.rest_0_, bf16[160,128]{1,0:T(8,128)(2,1)S(1)} %collective-permute-done.3.rest_1_, bf16[160,128]{1,0:T(8,128)(2,1)S(1)} %collective-permute-done.4.rest_2_, ...), custom_call_target="tpu_custom_call" | custom-call | tf_op jit(solution)/shard_map/merge/pallas_call | solution.py:371
  (4 shorter events, 0.0 us)
Async XLA Ops:
  1.6 1.6 %copy-start = (bf16[4096,256]{1,0:T(8,128)(2,1)S(1)}, bf16[4096,256]{1,0:T(8,128)(2,1)}, u32[]{:S(2)}) copy-start(bf16[4096,256]{1,0:T(8,128)(2,1)} %rest_1_.1) | copy-start | bytes 6291460
  3.2 1.0 %copy-start.1 = (bf16[64,4096]{1,0:T(8,128)(2,1)S(1)}, bf16[64,4096]{1,0:T(8,128)(2,1)}, u32[]{:S(2)}) copy-start(bf16[64,4096]{1,0:T(8,128)(2,1)} %hidden.1) | copy-start | bytes 1572868
  4.2 0.7 %copy-start.4 = (s32[64]{0:T(128)S(1)}, s32[64]{0:T(128)}, u32[]{:S(2)}) copy-start(s32[64]{0:T(128)} %row_len.1) | copy-start | bytes 772
  4.9 20.9 %copy-start.5 = (s32[4,4,4]{2,1,0:T(4,128)S(1)}, s32[4,4,4]{2,1,0:T(4,128)}, u32[]{:S(2)}) copy-start(s32[4,4,4]{2,1,0:T(4,128)} %param.19) | copy-start | bytes 772
  4.9 21.0 %copy-start.6 = (s32[1,4,4]{2,1,0:T(4,128)S(1)}, s32[1,4,4]{2,1,0:T(4,128)}, u32[]{:S(2)}) copy-start(s32[1,4,4]{2,1,0:T(4,128)} %param.20) | copy-start | bytes 196
  4.9 21.6 %copy-start.7 = (f32[128]{0:T(128)S(1)}, f32[128]{0:T(128)}, u32[]{:S(2)}) copy-start(f32[128]{0:T(128)} %constant.20) | copy-start | bytes 1540
  4.9 21.6 %copy-start.8 = (f32[128]{0:T(128)S(1)}, f32[128]{0:T(128)}, u32[]{:S(2)}) copy-start(f32[128]{0:T(128)} %constant.19) | copy-start | bytes 1540
  4.9 29.5 %copy-start.2 = (bf16[1024,256]{1,0:T(8,128)(2,1)S(1)}, bf16[1024,256]{1,0:T(8,128)(2,1)}, u32[]{:S(2)}) copy-start(bf16[1024,256]{1,0:T(8,128)(2,1)} %rest_6_.1) | copy-start | bytes 1572868
  4.9 29.5 %copy-start.3 = (bf16[1024,256]{1,0:T(8,128)(2,1)S(1)}, bf16[1024,256]{1,0:T(8,128)(2,1)}, u32[]{:S(2)}) copy-start(bf16[1024,256]{1,0:T(8,128)(2,1)} %rest_7_.1) | copy-start | bytes 1572868
  18.7 10.0 %collective-permute-start = (bf16[16,4736]{1,0:T(8,128)(2,1)S(1)}, bf16[16,4736]{1,0:T(8,128)(2,1)S(1)}, u32[]{:S(2)}, u32[]{:S(2)}) collective-permute-start(bf16[16,4736]{1,0:T(8,128)(2,1)S(1)} %get-tuple-element.15), channel_id=1, source_target_pairs={{0,4},{4,8},{8,12},{12,0},{1,5},{5,9},{9,13},{13,1},{2,6},{6,10},{... | collective-permute-start | bytes 454664 | tf_op jit(solution)/shard_map/ppermute | solution.py:275
  21.8 12.6 %collective-permute-start.1 = (bf16[16,4736]{1,0:T(8,128)(2,1)S(1)}, bf16[16,4736]{1,0:T(8,128)(2,1)S(1)}, u32[]{:S(2)}, u32[]{:S(2)}) collective-permute-start(bf16[16,4736]{1,0:T(8,128)(2,1)S(1)} %get-tuple-element.16), channel_id=1, source_target_pairs={{0,8},{4,12},{8,0},{12,4},{1,9},{5,13},{9,1},{13,5},{2,10},{6,14},... | collective-permute-start | bytes 454664 | tf_op jit(solution)/shard_map/ppermute | solution.py:275
  24.4 10.0 %collective-permute-start.2 = (bf16[16,4736]{1,0:T(8,128)(2,1)S(1)}, bf16[16,4736]{1,0:T(8,128)(2,1)S(1)}, u32[]{:S(2)}, u32[]{:S(2)}) collective-permute-start(bf16[16,4736]{1,0:T(8,128)(2,1)S(1)} %get-tuple-element.17), channel_id=1, source_target_pairs={{0,12},{4,0},{8,4},{12,8},{1,13},{5,1},{9,5},{13,9},{2,14},{6,2},{... | collective-permute-start | bytes 454664 | tf_op jit(solution)/shard_map/ppermute | solution.py:275
  42.3 6.9 %collective-permute-start.3 = (bf16[160,128]{1,0:T(8,128)(2,1)S(1)}, bf16[160,128]{1,0:T(8,128)(2,1)S(1)}, u32[]{:S(2)}, u32[]{:S(2)}) collective-permute-start(bf16[160,128]{1,0:T(8,128)(2,1)S(1)} %get-tuple-element.20), channel_id=1, source_target_pairs={{0,4},{4,8},{8,12},{12,0},{1,5},{5,9},{9,13},{13,1},{2,6},{6,10},{... | collective-permute-start | bytes 122888 | tf_op jit(solution)/shard_map/ppermute | solution.py:275
  46.0 5.2 %collective-permute-start.4 = (bf16[160,128]{1,0:T(8,128)(2,1)S(1)}, bf16[160,128]{1,0:T(8,128)(2,1)S(1)}, u32[]{:S(2)}, u32[]{:S(2)}) collective-permute-start(bf16[160,128]{1,0:T(8,128)(2,1)S(1)} %get-tuple-element.21), channel_id=1, source_target_pairs={{0,8},{4,12},{8,0},{12,4},{1,9},{5,13},{9,1},{13,5},{2,10},{6,14},... | collective-permute-start | bytes 122888 | tf_op jit(solution)/shard_map/ppermute | solution.py:275
  47.7 4.1 %collective-permute-start.5 = (bf16[160,128]{1,0:T(8,128)(2,1)S(1)}, bf16[160,128]{1,0:T(8,128)(2,1)S(1)}, u32[]{:S(2)}, u32[]{:S(2)}) collective-permute-start(bf16[160,128]{1,0:T(8,128)(2,1)S(1)} %get-tuple-element.22), channel_id=1, source_target_pairs={{0,12},{4,0},{8,4},{12,8},{1,13},{5,1},{9,5},{13,9},{2,14},{6,2},{... | collective-permute-start | bytes 122888 | tf_op jit(solution)/shard_map/ppermute | solution.py:275

commit v2 on v1

v2 whole, which is shorter than its diff:
```python
import functools

import jax
import jax.numpy as jnp
import numpy as np
from jax import lax
from jax.experimental import pallas as pl
from jax.experimental.pallas import tpu as pltpu
from jax.sharding import PartitionSpec as P

HD = 128
EPS = 1e-05
THETA = 500000.0
LOW = -1e30
WINDOW = 8
TILE = 256
MARKS = 72


def divides(width, limit):
    while width % limit:
        limit //= 2
    return limit


def split3(x):
    a = x.astype(jnp.bfloat16).astype(jnp.float32)
    r = x - a
    b = r.astype(jnp.bfloat16).astype(jnp.float32)
    return a, b, (r - b).astype(jnp.bfloat16).astype(jnp.float32)


def project_kernel(pool, slots, rows_local, me_ref, send, row_len, hidden, gain, *rest):
    n_w = 3
    weights, rest = rest[:n_w], rest[n_w:]
    out, pos_out, send_buf, len_buf, x_buf, g_buf, pick, lhs, *bufs, in_sem, sems = rest
    per = pool * slots
    n_slots = pool * per
    tiles = []
    for n, buf in enumerate(bufs):
        for t in range(buf.shape[0]):
            tiles.append((n, t))

    def copy(n, t, i):
        width = bufs[n].shape[2]
        at = t * width if isinstance(t, int) else pl.multiple_of(t * width, width)
        return pltpu.make_async_copy(
            weights[n].at[:, pl.ds(at, width)], bufs[n].at[t], sems.at[i]
        )

    inputs = [
        pltpu.make_async_copy(source, target, in_sem.at[i])
        for i, (source, target) in enumerate(
            ((send, send_buf), (row_len, len_buf), (hidden, x_buf), (gain, g_buf))
        )
    ]
    for one in inputs:
        one.start()
    for i in range(min(WINDOW, len(tiles))):
        copy(*tiles[i], i).start()

    n_rows = x_buf.shape[0]
    lane = lax.broadcasted_iota(jnp.int32, (1, n_rows), 1)
    inputs[0].wait()
    inputs[1].wait()

    def slot_row(owner, home, c):
        r = send_buf[home, owner, c] if len(send_buf.shape) == 3 else send_buf[
            home * per + owner * slots + c
        ]
        return jnp.where(r >= 0, home * rows_local + r, -1)

    def fill(i, carry):
        for c in range(slots):
            row = slot_row(i // pool, lax.rem(i, pool), c)
            pick[pl.ds(i * slots + c, 1), :] = (lane == row).astype(jnp.float32)
        return carry

    lax.fori_loop(0, pool * pool, fill, 0)
    me = me_ref[0]

    def fill_pos(home, carry):
        for c in range(slots):
            row = slot_row(me, home, c)
            at = len_buf[jnp.maximum(row, 0)].astype(jnp.float32)
            pos_out[pl.ds(home * slots + c, 1), :] = jnp.full((1, HD), at, jnp.float32)
        return carry

    lax.fori_loop(0, pool, fill_pos, 0)

    inputs[2].wait()
    inputs[3].wait()
    x = x_buf[...].astype(jnp.float32)
    power = jnp.sum(x * x, axis=1, keepdims=True)
    gains = g_buf[...].astype(jnp.float32).reshape(1, x.shape[1])
    scaled = (x * gains).astype(jnp.bfloat16)
    chosen = pick[...].astype(jnp.bfloat16)
    lhs[...] = jnp.dot(chosen, scaled, preferred_element_type=jnp.float32).astype(jnp.bfloat16)
    at = lax.broadcasted_iota(jnp.int32, (n_rows, HD), 1)
    a, b, c = split3(power)
    aux = jnp.where(at == 0, a, jnp.where(at == 1, b, jnp.where(at == 2, c, 0.0)))
    aux = jnp.dot(chosen, aux.astype(jnp.bfloat16), preferred_element_type=jnp.float32)
    tail = out.shape[1] - HD
    out[:, tail:] = aux.astype(jnp.bfloat16)

    start = 0
    first = 0
    for n in range(n_w):
        count, width = bufs[n].shape[0], bufs[n].shape[2]

        def column(t, carry, n=n, first=first, start=start, width=width):
            copy(n, t, first + t).wait()
            part = jnp.dot(lhs[...], bufs[n][t], preferred_element_type=jnp.float32)
            out[:, pl.ds(pl.multiple_of(start + t * width, width), width)] = part.astype(
                jnp.bfloat16
            )
            return carry

        t = 0
        while t < count:
            ahead = first + t + WINDOW
            if ahead < len(tiles):
                m, u = tiles[ahead]
                run = 1
                while (
                    t + run < count
                    and ahead + run < len(tiles)
                    and tiles[ahead + run][0] == m
                ):
                    run += 1

                def step(q, carry, m=m, u=u, t=t, ahead=ahead):
                    copy(m, u + q, ahead + q).start()
                    return column(t + q, carry)

                lax.fori_loop(0, run, step, 0)
            else:
                run = count - t
                lax.fori_loop(t, count, column, 0)
            t += run
        start += count * width
        first += count


def attend_kernel(pool, slots, seg, width_d, q_heads, kv_heads, terms, cos, sin, marks, keys, values, out, q_buf):
    per = pool * slots
    group = q_heads // kv_heads
    step = HD // group
    scale = HD ** (-0.5)

    def total(at):
        got = terms[:per, at : at + HD].astype(jnp.float32)
        for p in range(1, pool):
            got = got + terms[p * per : (p + 1) * per, at : at + HD].astype(jnp.float32)
        return got

    power = jnp.sum(total((q_heads + 2 * kv_heads) * HD), axis=1, keepdims=True)
    factor = lax.rsqrt(power * (1.0 / width_d) + EPS)
    cosines, sines = cos[...], sin[...]

    def rounded(x):
        return x.astype(jnp.bfloat16).astype(jnp.float32)

    def rotated(x):
        return rounded(x * cosines + pltpu.roll(x, HD // 2, axis=1) * sines)

    for i in range(q_heads):
        q_buf[i * per : (i + 1) * per, :] = rotated(total((2 * kv_heads + i) * HD) * factor)
    keys_own = [rotated(total(g * HD) * factor) for g in range(kv_heads)]
    values_own = [
        rounded(total((kv_heads + g) * HD) * factor) for g in range(kv_heads)
    ]

    lane = lax.broadcasted_iota(jnp.int32, (1, HD), 1)
    slot_of = lane // group
    at = lax.broadcasted_iota(jnp.int32, (seg, HD), 0)
    at_own = lax.broadcasted_iota(jnp.int32, (step, HD), 0)
    blocks = [(g, s) for s in range(0, per, step) for g in range(kv_heads)]
    columns = []
    for g, s in blocks:
        query = jnp.concatenate(
            [q_buf[pl.ds(g * group * per + s + u, group, stride=per), :] for u in range(step)], 0
        )
        columns.append(query.T.astype(jnp.bfloat16))
    scores = []
    for (g, s), query in zip(blocks, columns):
        wide = jnp.dot(
            keys[s * seg : (s + step) * seg, g * HD : (g + 1) * HD],
            query,
            preferred_element_type=jnp.float32,
        )
        score = wide[:seg]
        for u in range(1, step):
            score = jnp.where(slot_of == u, wide[u * seg : (u + 1) * seg], score)
        own = jnp.dot(
            keys_own[g][s : s + step].astype(jnp.bfloat16),
            query,
            preferred_element_type=jnp.float32,
        )
        own = jnp.sum(jnp.where(at_own == slot_of, own, 0.0), axis=0, keepdims=True)
        scores.append((score * scale, own * scale))
    turned = []
    for (g, s), (score, own) in zip(blocks, scores):
        length = marks[0:1, s * group : s * group + HD]
        with_own = marks[1:2, s * group : s * group + HD] > 0
        usable = at < length
        own = jnp.where(with_own, own, LOW)
        top = jnp.maximum(jnp.max(jnp.where(usable, score, LOW), axis=0, keepdims=True), own)
        weight = jnp.where(usable, jnp.exp(score - top), 0.0)
        weight_own = jnp.where(with_own, jnp.exp(own - top), 0.0)
        sums = jnp.sum(weight, axis=0, keepdims=True) + weight_own
        sums = jnp.where(length > 0, sums, 1.0)
        level = split3(top + jnp.log(sums))
        rows = [weight_own, 1.0 / sums] + [jnp.zeros((1, HD), jnp.float32)] * (MARKS - seg - 2)
        for piece in range(3):
            for c in range(slots):
                rows.append(jnp.where(lax.rem(slot_of, slots) == c, level[piece], 0.0))
        rows.append(jnp.zeros((HD - MARKS - 3 * slots, HD), jnp.float32))
        turned.append(jnp.concatenate([weight] + rows, 0).T)
    place = lax.broadcasted_iota(jnp.int32, (group, HD), 1)
    kept = (place >= MARKS) & (place < MARKS + 3 * slots)
    levels = {}
    for (g, s), block in zip(blocks, turned):
        for u in range(step):
            home, c = (s + u) // slots, (s + u) % slots
            rows = block[u * group : (u + 1) * group]
            mixed = jnp.dot(
                rows[:, :seg].astype(jnp.bfloat16),
                values[(s + u) * seg : (s + u + 1) * seg, g * HD : (g + 1) * HD],
                preferred_element_type=jnp.float32,
            )
            mixed = mixed + rows[:, seg : seg + 1] * values_own[g][s + u : s + u + 1]
            to = (home * (slots + 1) + c) * q_heads + g * group
            out[to : to + group, :] = (mixed * rows[:, seg + 1 : seg + 2]).astype(jnp.bfloat16)
            levels[home, g] = levels.get((home, g), 0.0) + jnp.where(kept, rows, 0.0)
    for (home, g), level in levels.items():
        to = (home * (slots + 1) + slots) * q_heads + g * group
        out[to : to + group, :] = level.astype(jnp.bfloat16)


def merge_kernel(pool, slots, rows_local, q_heads, slot_row, found, out, o_buf, f_buf):
    per = pool * slots
    block = slots * q_heads
    lane = lax.broadcasted_iota(jnp.int32, (q_heads, HD), 1)
    level = jnp.zeros((q_heads, HD), jnp.float32)
    for p in range(pool):
        at = p * (block + q_heads)
        o_buf[p * block : (p + 1) * block, :] = found[at : at + block, :].astype(jnp.float32)
        got = found[at + block : at + block + q_heads, :].astype(jnp.float32)
        got = sum(
            pltpu.roll(got, (p * slots - MARKS - piece * slots) % HD, axis=1) for piece in range(3)
        )
        level = jnp.where((lane >= p * slots) & (lane < (p + 1) * slots), got, level)
    rows = slot_row[...]
    for r in range(rows_local):
        match = rows == r
        top = jnp.max(jnp.where(match, level, LOW), axis=1, keepdims=True)
        factor = jnp.where(match, jnp.exp(level - top), 0.0)
        factor = factor / jnp.sum(factor, axis=1, keepdims=True)
        high = factor.astype(jnp.bfloat16).astype(jnp.float32)
        low = pltpu.roll(factor - high, per, axis=1)
        f_buf[pl.ds(r, q_heads, stride=rows_local), :] = high + low
    for i in range(q_heads):
        o = o_buf[pl.ds(i, per, stride=q_heads), :].astype(jnp.bfloat16)
        f = f_buf[i * rows_local : (i + 1) * rows_local, : 2 * per].astype(jnp.bfloat16)
        out[:, i * HD : (i + 1) * HD] = jnp.dot(
            f, jnp.concatenate([o, o], axis=0), preferred_element_type=jnp.float32
        ).astype(jnp.bfloat16)


def exchange(x):
    return lax.all_to_all(x, "pool", split_axis=0, concat_axis=0, tiled=True)


def in_hbm(x):
    return pltpu.with_memory_space_constraint(x, pltpu.HBM)


SMEM = pl.BlockSpec(memory_space=pltpu.SMEM)
VMEM = pl.BlockSpec(memory_space=pltpu.VMEM)
HBM = pl.BlockSpec(memory_space=pltpu.HBM)


def body(
    hidden_in,
    norm_gain,
    w_query,
    w_key,
    w_value,
    cache_keys,
    cache_values,
    send_row,
    piece_len,
    row_len,
):
    pool = lax.axis_size("pool")
    me = lax.axis_index("pool").astype(jnp.int32)
    n_rows, depth = hidden_in.shape
    width_d = depth * pool
    rows_local = n_rows // pool
    slots = send_row.shape[2]
    per = pool * slots
    seg = cache_keys.shape[0] // per
    q_cols, kv_cols = w_query.shape[1], w_key.shape[1]
    q_heads, kv_heads = q_cols // HD, kv_cols // HD
    group = q_heads // kv_heads
    cols = q_cols + 2 * kv_cols + HD

    sends = send_row if pool <= 8 else send_row.reshape(-1)
    weights = (w_key, w_value, w_query)
    bufs = []
    n_tiles = 0
    for w in weights:
        width = divides(w.shape[1], TILE)
        bufs.append(pltpu.VMEM((w.shape[1] // width, depth, width), jnp.bfloat16))
        n_tiles += w.shape[1] // width
    operands = [in_hbm(x) for x in (sends, row_len, hidden_in, norm_gain, *weights)]
    terms, positions = pl.pallas_call(
        functools.partial(project_kernel, pool, slots, rows_local),
        out_shape=[
            jax.ShapeDtypeStruct((pool * per, cols), jnp.bfloat16),
            jax.ShapeDtypeStruct((per, HD), jnp.float32),
        ],
        in_specs=[SMEM] + [HBM] * 7,
        out_specs=[VMEM] * 2,
        scratch_shapes=[
            pltpu.SMEM(sends.shape, jnp.int32),
            pltpu.SMEM(row_len.shape, jnp.int32),
            pltpu.VMEM((n_rows, depth), jnp.bfloat16),
            pltpu.VMEM((depth,), jnp.bfloat16),
            pltpu.VMEM((pool * per, n_rows), jnp.float32),
            pltpu.VMEM((pool * per, depth), jnp.bfloat16),
            *bufs,
            pltpu.SemaphoreType.DMA((4,)),
            pltpu.SemaphoreType.DMA((n_tiles,)),
        ],
        compiler_params=pltpu.CompilerParams(vmem_limit_bytes=46 * 2**20),
        name="project",
    )(me[None], *operands)

    terms = exchange(terms)

    named = send_row.reshape(pool, per)
    mine = lax.dynamic_slice_in_dim(send_row, me, 1, 1)[:, 0, :]
    order = me * slots + jnp.arange(slots, dtype=jnp.int32)
    earlier = (named[:, None, :] == mine[:, :, None]) & (
        jnp.arange(per, dtype=jnp.int32)[None, None, :] < order[None, :, None]
    )
    first = ((mine >= 0) & ~jnp.any(earlier, axis=2)).astype(jnp.int32).reshape(-1)
    marks = jnp.stack([piece_len.reshape(-1), first])
    marks = jnp.broadcast_to(marks[:, :, None], (2, per, group)).reshape(2, per * group)
    slot_row = lax.dynamic_slice_in_dim(named, me, 1, 0)
    slot_row = jnp.concatenate([slot_row, jnp.full((1, HD - per), -1, jnp.int32)], 1)

    half = HD // 2
    freq = THETA ** (-(np.arange(half) * 2.0) / HD)
    angles = positions * np.concatenate([freq, freq]).astype(np.float32)[None, :]
    sign = np.concatenate([-np.ones(half), np.ones(half)]).astype(np.float32)[None, :]
    cosines, sines = jnp.cos(angles), jnp.sin(angles) * sign

    found = pl.pallas_call(
        functools.partial(attend_kernel, pool, slots, seg, width_d, q_heads, kv_heads),
        out_shape=jax.ShapeDtypeStruct((pool * (slots + 1) * q_heads, HD), jnp.bfloat16),
        in_specs=[VMEM] * 6,
        out_specs=VMEM,
        scratch_shapes=[pltpu.VMEM((q_heads * per, HD), jnp.float32)],
        compiler_params=pltpu.CompilerParams(vmem_limit_bytes=24 * 2**20),
        name="attend",
    )(terms, cosines, sines, marks, cache_keys, cache_values)

    found = exchange(found)

    return pl.pallas_call(
        functools.partial(merge_kernel, pool, slots, rows_local, q_heads),
        out_shape=jax.ShapeDtypeStruct((rows_local, q_cols), jnp.bfloat16),
        in_specs=[VMEM] * 2,
        out_specs=VMEM,
        scratch_shapes=[
            pltpu.VMEM((per * q_heads, HD), jnp.float32),
            pltpu.VMEM((rows_local * q_heads, HD), jnp.float32),
        ],
        compiler_params=pltpu.CompilerParams(vmem_limit_bytes=24 * 2**20),
        name="merge",
    )(slot_row, found)


def solution(mesh):
    return jax.shard_map(
        body,
        mesh=mesh,
        in_specs=(
            P("groups", "pool"),
            P("pool"),
            P("pool", "tensor"),
            P("pool", "tensor"),
            P("pool", "tensor"),
            P(("groups", "pool"), "tensor"),
            P(("groups", "pool"), "tensor"),
            P("groups", None, None),
            P(("groups", "pool"), None, None),
            P("groups"),
        ),
        out_specs=P(("groups", "pool"), "tensor"),
        check_vma=False,
    )
```

time: 54 us -> 51.7 us (0.957)
  waiting for transfers between devices: 11.1 us -> 21.5 us
  local copies, waits for them, and re-layouts: 5.15 us -> 0.53 us
  Pallas kernels: 23.7 us -> 19.2 us
  starting transfers between devices: 13.2 us -> 9.69 us
    all_to_all x0 -> x2, waiting for transfers between devices: none -> 21.5 us  [exchange(): return lax.all_to_all(x, 'pool', split_axis=0, concat_axis=0, tiled=True)]
    ppermute x6 -> x0, starting transfers between devices: 13.2 us -> none  [exchange(): lax.ppermute(parts[k], 'pool', [(i, (i + k) % pool) for i in range(pool)])]
    ppermute x6 -> x0, waiting for transfers between devices: 11.1 us -> none  [exchange(): lax.ppermute(parts[k], 'pool', [(i, (i + k) % pool) for i in range(pool)])]
    all_to_all x0 -> x2, starting transfers between devices: none -> 9.69 us  [exchange(): return lax.all_to_all(x, 'pool', split_axis=0, concat_axis=0, tiled=True)]
    pallas_call x1, Pallas kernels: 7.91 us -> 1.64 us  [body(): pl.pallas_call(functools.partial(attend_kernel, pool, slots, seg, width_d...]
    unnamed x18 -> x12, local copies, waits for them, and re-layouts: 3.31 us -> 0.02 us
    pallas_call x1, Pallas kernels: 13.8 us -> 16.1 us  [body(): pl.pallas_call(functools.partial(project_kernel, pool, slots, rows_local)...]
    reshape x3 -> x2, local copies, waits for them, and re-layouts: 1.58 us -> 0.17 us  [the longest x1 0.09 us: body(): jnp.broadcast_to(marks[:, :, None], (2, per, group)).reshape(2, per * group)]
  transfers between devices with their start and end apart: 6 -> 2, of which waited for: 5 -> 2; matrix products, arithmetic and copies ran while one was open for 1% -> 2% of each run, Pallas kernels for 0% -> 0%
where the time goes in v2:
time: 51.7 us; the launch traced here: 51.4 us
  waiting for transfers between devices  21.5 us (42%)
  Pallas kernels  19.2 us (37%)
  starting transfers between devices  9.69 us (19%)
  local copies, waits for them, and re-layouts  0.53 us (1%)
    all_to_all x2, waiting for transfers between devices, exchange(): return lax.all_to_all(x, 'pool', split_axis=0, concat_axis=0, tiled=True)  21.5 us
    pallas_call x1, Pallas kernels, body(): pl.pallas_call(functools.partial(project_kernel, pool, slots, rows_local)...  16.1 us
    all_to_all x2, starting transfers between devices, exchange(): return lax.all_to_all(x, 'pool', split_axis=0, concat_axis=0, tiled=True)  9.69 us
    pallas_call x1, Pallas kernels, body(): pl.pallas_call(functools.partial(attend_kernel, pool, slots, seg, width_d...  1.64 us
    pallas_call x1, Pallas kernels, body(): pl.pallas_call(functools.partial(merge_kernel, pool, slots, rows_local, q...  1.41 us
  transfers between devices with their start and end apart: 2, of which 2 were waited for; matrix products, arithmetic and copies ran while one was open for 2% of the time, Pallas kernels for 0%

profile of v2, /device:TPU:0, one launch (start us, length us, event | category | flops | bytes accessed | tf_op | source)
XLA Modules:
  0.0 51.4 jit_solution(5793933057236065163)
XLA Ops:
  0.0 0.0 copy-start.2
  0.0 0.0 copy-start.3
  0.0 0.0 copy-start.4
  0.0 0.0 copy-start.5
  0.0 0.0 copy-start
  0.0 0.0 copy-start.1
  0.0 16.1 %project.1 = (bf16[64,4736]{1,0:T(8,128)(2,1)}, f32[16,128]{1,0:T(8,128)S(1)}) custom-call(s32[1]{0:T(128)} %bitcast.me_ref, s32[4,4,4]{2,1,0:T(4,128)} %send.1, s32[64]{0:T(128)} %row_len.1, bf16[64,4096]{1,0:T(8,128)(2,1)} %hidden.1, bf16[4096]{0:T(1024)(128)(2,1)} %gain.1, bf16[4096,256]{1,0:T(8,128)(2,1)} %rest_0_.1, bf16[4096,256]{1,0:T(8,128)(2,1)} %rest_1_.1, ...), custom_call_target="tpu_custom_call" | custom-call | tf_op jit(solution)/shard_map/project/pallas_call | solution.py:318
  16.1 6.3 %all-to-all-start = ((bf16[4,16,4736]{2,1,0:T(8,128)(2,1)}), bf16[4,16,4736]{2,1,0:T(8,128)(2,1)S(1)}, u32[]{:S(2)}, u32[]{:S(2)}) async-start(bf16[4,16,4736]{2,1,0:T(8,128)(2,1)} %bitcast.1), calls=%async_computation | async-start | bytes 1212416 | tf_op jit(solution)/shard_map/all_to_all | solution.py:272
  22.5 0.0 copy-done.2
  22.5 0.1 reshape.69
  22.6 0.0 copy-done.3
  22.6 0.1 stack_reshape.4
  22.7 0.1 ge.14
  22.8 0.1 iota_compare_fusion
  22.9 0.2 and_reduce_fusion
  23.1 0.1 not.14
  23.2 0.1 broadcast_in_dim.5
  23.3 0.1 reshape.70.marks
  23.4 0.0 copy-done.4
  23.4 0.0 copy-done.5
  23.4 0.1 sine_multiply_fusion
  23.4 15.3 %all-to-all-done = bf16[4,16,4736]{2,1,0:T(8,128)(2,1)S(1)} async-done(((bf16[4,16,4736]{2,1,0:T(8,128)(2,1)}), bf16[4,16,4736]{2,1,0:T(8,128)(2,1)S(1)}, u32[]{:S(2)}, u32[]{:S(2)}) %all-to-all-start) | async-done | bytes 606240 | tf_op jit(solution)/shard_map/all_to_all | solution.py:272
  38.7 0.0 copy-done
  38.7 0.0 copy-done.1
  38.7 1.6 %attend.1 = bf16[640,128]{1,0:T(8,128)(2,1)} custom-call(bf16[64,4736]{1,0:T(8,128)(2,1)S(1)} %bitcast.6, f32[16,128]{1,0:T(8,128)S(1)} %get-tuple-element.12.cos, f32[16,128]{1,0:T(8,128)S(1)} %get-tuple-element.11.sin, s32[2,256]{1,0:T(2,128)S(1)} %reshape.70.marks, bf16[1024,256]{1,0:T(8,128)(2,1)S(1)} %copy-done, bf16[1024,256]{1,0:T(8,128)(2,1)S(1)} %copy-done.1), custom_call_target="tpu_custom_call" | custom-call | tf_op jit(solution)/shard_map/attend/pallas_call | solution.py:361
  40.4 3.3 %all-to-all-start.1 = ((bf16[4,160,128]{2,1,0:T(8,128)(2,1)}), bf16[4,160,128]{2,1,0:T(8,128)(2,1)S(1)}, u32[]{:S(2)}, u32[]{:S(2)}) async-start(bf16[4,160,128]{2,1,0:T(8,128)(2,1)} %bitcast.4), calls=%async_computation.1 | async-start | bytes 327680 | tf_op jit(solution)/shard_map/all_to_all | solution.py:272
  43.8 6.2 %all-to-all-done.1 = bf16[4,160,128]{2,1,0:T(8,128)(2,1)S(1)} async-done(((bf16[4,160,128]{2,1,0:T(8,128)(2,1)}), bf16[4,160,128]{2,1,0:T(8,128)(2,1)S(1)}, u32[]{:S(2)}, u32[]{:S(2)}) %all-to-all-start.1) | async-done | bytes 163872 | tf_op jit(solution)/shard_map/all_to_all | solution.py:272
  50.0 1.4 %merge.1 = bf16[16,4096]{1,0:T(8,128)(2,1)} custom-call(s32[1,128]{1,0:T(1,128)S(1)} %concatenate.3.slot_row, bf16[640,128]{1,0:T(8,128)(2,1)S(1)} %bitcast.7), custom_call_target="tpu_custom_call" | custom-call | tf_op jit(solution)/shard_map/merge/pallas_call | solution.py:373
  (7 shorter events, 0.1 us)
Async XLA Ops:
  0.0 22.5 %copy-start.2 = (s32[4,4,4]{2,1,0:T(4,128)S(1)}, s32[4,4,4]{2,1,0:T(4,128)}, u32[]{:S(2)}) copy-start(s32[4,4,4]{2,1,0:T(4,128)} %send.1) | copy-start | bytes 772
  0.0 22.6 %copy-start.3 = (s32[1,4,4]{2,1,0:T(4,128)S(1)}, s32[1,4,4]{2,1,0:T(4,128)}, u32[]{:S(2)}) copy-start(s32[1,4,4]{2,1,0:T(4,128)} %param.20) | copy-start | bytes 196
  0.0 23.4 %copy-start.4 = (f32[128]{0:T(128)S(1)}, f32[128]{0:T(128)}, u32[]{:S(2)}) copy-start(f32[128]{0:T(128)} %constant.24) | copy-start | bytes 1540
  0.0 23.4 %copy-start.5 = (f32[128]{0:T(128)S(1)}, f32[128]{0:T(128)}, u32[]{:S(2)}) copy-start(f32[128]{0:T(128)} %constant.23) | copy-start | bytes 1540
  0.0 38.7 %copy-start = (bf16[1024,256]{1,0:T(8,128)(2,1)S(1)}, bf16[1024,256]{1,0:T(8,128)(2,1)}, u32[]{:S(2)}) copy-start(bf16[1024,256]{1,0:T(8,128)(2,1)} %keys.1) | copy-start | bytes 1572868
  0.0 38.7 %copy-start.1 = (bf16[1024,256]{1,0:T(8,128)(2,1)S(1)}, bf16[1024,256]{1,0:T(8,128)(2,1)}, u32[]{:S(2)}) copy-start(bf16[1024,256]{1,0:T(8,128)(2,1)} %values.1) | copy-start | bytes 1572868
  16.1 22.6 %all-to-all-start = ((bf16[4,16,4736]{2,1,0:T(8,128)(2,1)}), bf16[4,16,4736]{2,1,0:T(8,128)(2,1)S(1)}, u32[]{:S(2)}, u32[]{:S(2)}) async-start(bf16[4,16,4736]{2,1,0:T(8,128)(2,1)} %bitcast.1), calls=%async_computation | async-start | bytes 1212416 | tf_op jit(solution)/shard_map/all_to_all | solution.py:272
  40.4 9.6 %all-to-all-start.1 = ((bf16[4,160,128]{2,1,0:T(8,128)(2,1)}), bf16[4,160,128]{2,1,0:T(8,128)(2,1)S(1)}, u32[]{:S(2)}, u32[]{:S(2)}) async-start(bf16[4,160,128]{2,1,0:T(8,128)(2,1)} %bitcast.4), calls=%async_computation.1 | async-start | bytes 327680 | tf_op jit(solution)/shard_map/all_to_all | solution.py:272

commit v3 on v2

v3 whole, which is shorter than its diff:
```python
import functools

import jax
import jax.numpy as jnp
import numpy as np
from jax import lax
from jax.experimental import pallas as pl
from jax.experimental.pallas import tpu as pltpu
from jax.sharding import PartitionSpec as P

HD = 128
EPS = 1e-05
THETA = 500000.0
LOW = -1e30
WINDOW = 6
DEEP = 512
MARKS = 72


def divides(width, limit):
    while width % limit:
        limit //= 2
    return limit


def split3(x):
    a = x.astype(jnp.bfloat16).astype(jnp.float32)
    r = x - a
    b = r.astype(jnp.bfloat16).astype(jnp.float32)
    return a, b, (r - b).astype(jnp.bfloat16).astype(jnp.float32)


def slot_row(send, per, slots, rows_local, owner, home, c):
    if len(send.shape) == 3:
        r = send[home, owner, c]
    else:
        r = send[home * per + owner * slots + c]
    return jnp.where(r >= 0, home * rows_local + r, -1)


def project_blocks(plan, lhs, sems):
    blocks = [(n, t) for n, entry in enumerate(plan) for t in range(entry[2].shape[0])]

    def copy(n, t, i):
        w, column, buf, _, _ = plan[n]
        _, deep, width = buf.shape
        at = t * deep if isinstance(t, int) else pl.multiple_of(t * deep, deep)
        return pltpu.make_async_copy(
            w.at[pl.ds(at, deep), column : column + width], buf.at[t], sems.at[i]
        )

    def begin():
        for i in range(min(WINDOW, len(blocks))):
            copy(*blocks[i], i).start()

    def finish():
        first = 0
        for n, (w, column, buf, sums, to) in enumerate(plan):
            count, deep, width = buf.shape
            tile = divides(width, 512)

            def work(t, carry, n=n, first=first, buf=buf, sums=sums, to=to, tile=tile, width=width):
                copy(n, t, first + t).wait()
                left = lhs[t] if count > 1 else None
                for at in range(0, width, tile):
                    if count > 1:
                        part = jnp.dot(
                            left, buf[t, :, at : at + tile], preferred_element_type=jnp.float32
                        )
                        sums[:, to + at : to + at + tile] += part
                    else:
                        part = 0.0
                        for k in range(lhs.shape[0]):
                            each = lhs.shape[2]
                            part = part + jnp.dot(
                                lhs[k],
                                buf[0, k * each : (k + 1) * each, at : at + tile],
                                preferred_element_type=jnp.float32,
                            )
                        sums[:, to + at : to + at + tile] = part
                return carry

            if count > 1:
                sums[:, to : to + width] = jnp.zeros((sums.shape[0], width), jnp.float32)
            t = 0
            while t < count:
                ahead = first + t + WINDOW
                if ahead < len(blocks):
                    m, u = blocks[ahead]
                    run = 1
                    while (
                        t + run < count
                        and ahead + run < len(blocks)
                        and blocks[ahead + run][0] == m
                    ):
                        run += 1

                    def step(q, carry, m=m, u=u, t=t, ahead=ahead, work=work):
                        copy(m, u + q, ahead + q).start()
                        return work(t + q, carry)

                    lax.fori_loop(0, run, step, 0)
                else:
                    run = count - t
                    lax.fori_loop(t, count, work, 0)
                t += run
            first += count

    return begin, finish


def project_kernel(pool, slots, rows_local, columns, me_ref, send, row_len, hidden, gain, *rest):
    w_key, w_value, w_query, *rest = rest
    outs, rest = rest[:pool], rest[pool:]
    lhs, pos_out, send_buf, len_buf, x_buf, g_buf, pick, *rest = rest
    key_buf, value_buf, query_buf, sums, in_sem, sems = rest
    per = pool * slots
    kv_cols = w_key.shape[1]
    begin, finish = project_blocks(
        [
            (w_key, 0, key_buf, sums, 0),
            (w_value, 0, value_buf, sums, kv_cols),
            (w_query, 0, query_buf, sums, 2 * kv_cols),
        ],
        lhs,
        sems,
    )
    inputs = [
        pltpu.make_async_copy(source, target, in_sem.at[i])
        for i, (source, target) in enumerate(
            ((send, send_buf), (row_len, len_buf), (hidden, x_buf), (gain, g_buf))
        )
    ]
    for one in inputs:
        one.start()
    begin()

    n_rows = x_buf.shape[0]
    lane = lax.broadcasted_iota(jnp.int32, (1, n_rows), 1)
    me = me_ref[0]
    row_of = functools.partial(slot_row, send_buf, per, slots, rows_local)
    inputs[0].wait()
    inputs[1].wait()

    def fill(i, carry):
        owner = lax.rem(me + i // pool, pool)
        home = lax.rem(owner + lax.rem(i, pool), pool)
        for c in range(slots):
            row = row_of(owner, home, c)
            pick[pl.ds(i * slots + c, 1), :] = (lane == row).astype(jnp.float32)
        return carry

    lax.fori_loop(0, pool * pool, fill, 0)

    def fill_pos(j, carry):
        for c in range(slots):
            row = row_of(me, lax.rem(me + j, pool), c)
            at = len_buf[jnp.maximum(row, 0)].astype(jnp.float32)
            pos_out[pl.ds(j * slots + c, 1), :] = jnp.full((1, HD), at, jnp.float32)
        return carry

    lax.fori_loop(0, pool, fill_pos, 0)

    inputs[2].wait()
    inputs[3].wait()
    x = x_buf[...].astype(jnp.float32)
    power = jnp.sum(x * x, axis=1, keepdims=True)
    gains = g_buf[...].astype(jnp.float32).reshape(1, x.shape[1])
    scaled = (x * gains).astype(jnp.bfloat16)
    chosen = pick[...].astype(jnp.bfloat16)
    each = lhs.shape[2]
    for k in range(lhs.shape[0]):
        lhs[k] = jnp.dot(
            chosen, scaled[:, k * each : (k + 1) * each], preferred_element_type=jnp.float32
        ).astype(jnp.bfloat16)
    at = lax.broadcasted_iota(jnp.int32, (n_rows, HD), 1)
    a, b, c = split3(power)
    aux = jnp.where(at == 0, a, jnp.where(at == 1, b, jnp.where(at == 2, c, 0.0)))
    aux = jnp.dot(chosen, aux.astype(jnp.bfloat16), preferred_element_type=jnp.float32)
    finish()
    cols = sums.shape[1]
    for k in range(pool):
        outs[k][:, :cols] = sums[k * per : (k + 1) * per, :].astype(jnp.bfloat16)
        outs[k][:, cols:] = aux[k * per : (k + 1) * per].astype(jnp.bfloat16)


def project_rest_kernel(pool, column, lhs, w_query, *rest):
    outs, (query_buf, sums, sems) = rest[:pool], rest[pool:]
    begin, finish = project_blocks([(w_query, column, query_buf, sums, 0)], lhs, sems)
    begin()
    finish()
    per = sums.shape[0] // pool
    for k in range(pool):
        outs[k][...] = sums[k * per : (k + 1) * per, :].astype(jnp.bfloat16)


def attend_kernel(pool, slots, seg, width_d, q_heads, kv_heads, batches, me_ref, *rest):
    terms, rest = rest[: pool * batches], rest[pool * batches :]
    cos, sin, marks, keys, values = rest[:5]
    outs, (q_buf,) = rest[5 : 5 + pool], rest[5 + pool :]
    per = pool * slots
    group = q_heads // kv_heads
    step = HD // group
    scale = HD ** (-0.5)

    def total(batch, at):
        got = terms[batch * pool][:, at : at + HD].astype(jnp.float32)
        for p in range(1, pool):
            got = got + terms[batch * pool + p][:, at : at + HD].astype(jnp.float32)
        return got

    heads = [(0, at) for at in range(2 * kv_heads * HD, terms[0].shape[1] - HD, HD)]
    for batch in range(1, batches):
        heads += [(batch, at) for at in range(0, terms[batch * pool].shape[1], HD)]
    power = jnp.sum(total(0, terms[0].shape[1] - HD), axis=1, keepdims=True)
    factor = lax.rsqrt(power * (1.0 / width_d) + EPS)
    cosines, sines = cos[...], sin[...]

    def rounded(x):
        return x.astype(jnp.bfloat16).astype(jnp.float32)

    def rotated(x):
        return rounded(x * cosines + pltpu.roll(x, HD // 2, axis=1) * sines)

    for i in range(q_heads):
        q_buf[i * per : (i + 1) * per, :] = rotated(total(*heads[i]) * factor)
    keys_own = [rotated(total(0, g * HD) * factor) for g in range(kv_heads)]
    values_own = [
        rounded(total(0, (kv_heads + g) * HD) * factor) for g in range(kv_heads)
    ]

    me = me_ref[0]

    def base(j):
        return pl.multiple_of(lax.rem(me + j, pool) * (slots * seg), slots * seg)

    lane = lax.broadcasted_iota(jnp.int32, (1, HD), 1)
    slot_of = lane // group
    at = lax.broadcasted_iota(jnp.int32, (seg, HD), 0)
    at_own = lax.broadcasted_iota(jnp.int32, (step, HD), 0)
    blocks = [(g, s) for s in range(0, per, step) for g in range(kv_heads)]
    columns = []
    for g, s in blocks:
        query = jnp.concatenate(
            [q_buf[pl.ds(g * group * per + s + u, group, stride=per), :] for u in range(step)], 0
        )
        columns.append(query.T.astype(jnp.bfloat16))
    scores = []
    for (g, s), query in zip(blocks, columns):
        score = None
        for u in range(0, step, slots):
            wide = jnp.dot(
                keys[pl.ds(base((s + u) // slots), slots * seg), g * HD : (g + 1) * HD],
                query,
                preferred_element_type=jnp.float32,
            )
            for c in range(slots):
                each = wide[c * seg : (c + 1) * seg]
                score = each if score is None else jnp.where(slot_of == u + c, each, score)
        own = jnp.dot(
            keys_own[g][s : s + step].astype(jnp.bfloat16),
            query,
            preferred_element_type=jnp.float32,
        )
        own = jnp.sum(jnp.where(at_own == slot_of, own, 0.0), axis=0, keepdims=True)
        scores.append((score * scale, own * scale))
    turned = []
    for (g, s), (score, own) in zip(blocks, scores):
        length = marks[0:1, s * group : s * group + HD]
        with_own = marks[1:2, s * group : s * group + HD] > 0
        usable = at < length
        own = jnp.where(with_own, own, LOW)
        top = jnp.maximum(jnp.max(jnp.where(usable, score, LOW), axis=0, keepdims=True), own)
        weight = jnp.where(usable, jnp.exp(score - top), 0.0)
        weight_own = jnp.where(with_own, jnp.exp(own - top), 0.0)
        sums = jnp.sum(weight, axis=0, keepdims=True) + weight_own
        sums = jnp.where(length > 0, sums, 1.0)
        level = split3(top + jnp.log(sums))
        rows = [weight_own, 1.0 / sums] + [jnp.zeros((1, HD), jnp.float32)] * (MARKS - seg - 2)
        for piece in range(3):
            for c in range(slots):
                rows.append(jnp.where(lax.rem(slot_of, slots) == c, level[piece], 0.0))
        rows.append(jnp.zeros((HD - MARKS - 3 * slots, HD), jnp.float32))
        turned.append(jnp.concatenate([weight] + rows, 0).T)
    place = lax.broadcasted_iota(jnp.int32, (group, HD), 1)
    kept = (place >= MARKS) & (place < MARKS + 3 * slots)
    levels = {}
    for (g, s), block in zip(blocks, turned):
        for u in range(step):
            home, c = (s + u) // slots, (s + u) % slots
            rows = block[u * group : (u + 1) * group]
            mixed = jnp.dot(
                rows[:, :seg].astype(jnp.bfloat16),
                values[pl.ds(base(home) + c * seg, seg), g * HD : (g + 1) * HD],
                preferred_element_type=jnp.float32,
            )
            mixed = mixed + rows[:, seg : seg + 1] * values_own[g][s + u : s + u + 1]
            to = c * q_heads + g * group
            outs[home][to : to + group, :] = (mixed * rows[:, seg + 1 : seg + 2]).astype(jnp.bfloat16)
            levels[home, g] = levels.get((home, g), 0.0) + jnp.where(kept, rows, 0.0)
    for (home, g), level in levels.items():
        to = slots * q_heads + g * group
        outs[home][to : to + group, :] = level.astype(jnp.bfloat16)


def merge_kernel(pool, slots, rows_local, q_heads, rows_ref, *rest):
    found, (out, o_buf, f_buf) = rest[:pool], rest[pool:]
    per = pool * slots
    block = slots * q_heads
    lane = lax.broadcasted_iota(jnp.int32, (q_heads, HD), 1)
    level = jnp.zeros((q_heads, HD), jnp.float32)
    for p in range(pool):
        o_buf[p * block : (p + 1) * block, :] = found[p][:block, :].astype(jnp.float32)
        got = found[p][block : block + q_heads, :].astype(jnp.float32)
        got = sum(
            pltpu.roll(got, (p * slots - MARKS - piece * slots) % HD, axis=1) for piece in range(3)
        )
        level = jnp.where((lane >= p * slots) & (lane < (p + 1) * slots), got, level)
    rows = rows_ref[...]
    for r in range(rows_local):
        match = rows == r
        top = jnp.max(jnp.where(match, level, LOW), axis=1, keepdims=True)
        factor = jnp.where(match, jnp.exp(level - top), 0.0)
        factor = factor / jnp.sum(factor, axis=1, keepdims=True)
        high = factor.astype(jnp.bfloat16).astype(jnp.float32)
        low = pltpu.roll(factor - high, per, axis=1)
        f_buf[pl.ds(r, q_heads, stride=rows_local), :] = high + low
    for i in range(q_heads):
        o = o_buf[pl.ds(i, per, stride=q_heads), :].astype(jnp.bfloat16)
        f = f_buf[i * rows_local : (i + 1) * rows_local, : 2 * per].astype(jnp.bfloat16)
        out[:, i * HD : (i + 1) * HD] = jnp.dot(
            f, jnp.concatenate([o, o], axis=0), preferred_element_type=jnp.float32
        ).astype(jnp.bfloat16)


def exchange(parts):
    pool = len(parts)
    return [parts[0]] + [
        lax.ppermute(parts[k], "pool", [(i, (i + k) % pool) for i in range(pool)])
        for k in range(1, pool)
    ]


def onwards(x, start):
    return lax.dynamic_slice_in_dim(jnp.concatenate([x, x], 0), start, x.shape[0], 0)


def in_hbm(x):
    return pltpu.with_memory_space_constraint(x, pltpu.HBM)


SMEM = pl.BlockSpec(memory_space=pltpu.SMEM)
VMEM = pl.BlockSpec(memory_space=pltpu.VMEM)
HBM = pl.BlockSpec(memory_space=pltpu.HBM)


def body(
    hidden_in,
    norm_gain,
    w_query,
    w_key,
    w_value,
    cache_keys,
    cache_values,
    send_row,
    piece_len,
    row_len,
):
    pool = lax.axis_size("pool")
    me = lax.axis_index("pool").astype(jnp.int32)
    n_rows, depth = hidden_in.shape
    width_d = depth * pool
    rows_local = n_rows // pool
    slots = send_row.shape[2]
    per = pool * slots
    seg = cache_keys.shape[0] // per
    q_cols, kv_cols = w_query.shape[1], w_key.shape[1]
    q_heads, kv_heads = q_cols // HD, kv_cols // HD
    group = q_heads // kv_heads
    cols = q_cols + 2 * kv_cols + HD

    sends = send_row if pool <= 8 else send_row.reshape(-1)
    deep = divides(depth, DEEP)
    batches = 2 if q_heads % 16 == 0 and kv_heads > 1 else 1
    width = q_cols // batches

    def parts(width):
        return [jax.ShapeDtypeStruct((per, width), jnp.bfloat16)] * pool

    operands = [in_hbm(x) for x in (sends, row_len, hidden_in, norm_gain, w_key, w_value, w_query)]
    *first_terms, lhs, positions = pl.pallas_call(
        functools.partial(project_kernel, pool, slots, rows_local, width),
        out_shape=[
            *parts(2 * kv_cols + width + HD),
            jax.ShapeDtypeStruct((depth // deep, pool * per, deep), jnp.bfloat16),
            jax.ShapeDtypeStruct((per, HD), jnp.float32),
        ],
        in_specs=[SMEM] + [HBM] * 7,
        out_specs=[VMEM] * (pool + 2),
        scratch_shapes=[
            pltpu.SMEM(sends.shape, jnp.int32),
            pltpu.SMEM(row_len.shape, jnp.int32),
            pltpu.VMEM((n_rows, depth), jnp.bfloat16),
            pltpu.VMEM((depth,), jnp.bfloat16),
            pltpu.VMEM((pool * per, n_rows), jnp.float32),
            pltpu.VMEM((1, depth, kv_cols), jnp.bfloat16),
            pltpu.VMEM((1, depth, kv_cols), jnp.bfloat16),
            pltpu.VMEM((depth // deep, deep, width), jnp.bfloat16),
            pltpu.VMEM((pool * per, 2 * kv_cols + width), jnp.float32),
            pltpu.SemaphoreType.DMA((4,)),
            pltpu.SemaphoreType.DMA((depth // deep + 2,)),
        ],
        compiler_params=pltpu.CompilerParams(vmem_limit_bytes=40 * 2**20),
        name="project",
    )(me[None], *operands)
    terms = exchange(first_terms)
    for batch in range(1, batches):
        terms += exchange(
            pl.pallas_call(
                functools.partial(project_rest_kernel, pool, batch * width),
                out_shape=parts(width),
                in_specs=[VMEM, HBM],
                out_specs=[VMEM] * pool,
                scratch_shapes=[
                    pltpu.VMEM((depth // deep, deep, width), jnp.bfloat16),
                    pltpu.VMEM((pool * per, width), jnp.float32),
                    pltpu.SemaphoreType.DMA((depth // deep,)),
                ],
                compiler_params=pltpu.CompilerParams(vmem_limit_bytes=40 * 2**20),
                name="project_rest",
            )(lhs, operands[-1])
        )

    named = send_row.reshape(pool, per)
    mine = lax.dynamic_slice_in_dim(send_row, me, 1, 1)[:, 0, :]
    order = me * slots + jnp.arange(slots, dtype=jnp.int32)
    earlier = (named[:, None, :] == mine[:, :, None]) & (
        jnp.arange(per, dtype=jnp.int32)[None, None, :] < order[None, :, None]
    )
    first = ((mine >= 0) & ~jnp.any(earlier, axis=2)).astype(jnp.int32).reshape(-1)
    marks = onwards(jnp.stack([piece_len.reshape(-1), first], 1), me * slots).T
    marks = jnp.broadcast_to(marks[:, :, None], (2, per, group)).reshape(2, per * group)
    owners = lax.dynamic_slice_in_dim(send_row, me, 1, 0)[0, ::-1]
    slot_rows = onwards(owners, pool - 1 - me).reshape(1, per)
    slot_rows = jnp.concatenate([slot_rows, jnp.full((1, HD - per), -1, jnp.int32)], 1)

    half = HD // 2
    freq = THETA ** (-(np.arange(half) * 2.0) / HD)
    angles = positions * np.concatenate([freq, freq]).astype(np.float32)[None, :]
    sign = np.concatenate([-np.ones(half), np.ones(half)]).astype(np.float32)[None, :]
    cosines, sines = jnp.cos(angles), jnp.sin(angles) * sign

    found = pl.pallas_call(
        functools.partial(attend_kernel, pool, slots, seg, width_d, q_heads, kv_heads, batches),
        out_shape=[jax.ShapeDtypeStruct(((slots + 1) * q_heads, HD), jnp.bfloat16)] * pool,
        in_specs=[SMEM] + [VMEM] * (pool * batches + 5),
        out_specs=[VMEM] * pool,
        scratch_shapes=[pltpu.VMEM((q_heads * per, HD), jnp.float32)],
        compiler_params=pltpu.CompilerParams(vmem_limit_bytes=24 * 2**20),
        name="attend",
    )(me[None], *terms, cosines, sines, marks, cache_keys, cache_values)

    found = exchange(found)

    return pl.pallas_call(
        functools.partial(merge_kernel, pool, slots, rows_local, q_heads),
        out_shape=jax.ShapeDtypeStruct((rows_local, q_cols), jnp.bfloat16),
        in_specs=[VMEM] * (1 + pool),
        out_specs=VMEM,
        scratch_shapes=[
            pltpu.VMEM((per * q_heads, HD), jnp.float32),
            pltpu.VMEM((rows_local * q_heads, HD), jnp.float32),
        ],
        compiler_params=pltpu.CompilerParams(vmem_limit_bytes=24 * 2**20),
        name="merge",
    )(slot_rows, *found)


def solution(mesh):
    return jax.shard_map(
        body,
        mesh=mesh,
        in_specs=(
            P("groups", "pool"),
            P("pool"),
            P("pool", "tensor"),
            P("pool", "tensor"),
            P("pool", "tensor"),
            P(("groups", "pool"), "tensor"),
            P(("groups", "pool"), "tensor"),
            P("groups", None, None),
            P(("groups", "pool"), None, None),
            P("groups"),
        ),
        out_specs=P(("groups", "pool"), "tensor"),
        check_vma=False,
    )
```

time: 51.7 us -> 43.8 us (0.85)
  waiting for transfers between devices: 21.5 us -> 11.3 us
  starting transfers between devices: 9.69 us -> 12 us
    all_to_all x2 -> x0, waiting for transfers between devices: 21.5 us -> none  [exchange(): return lax.all_to_all(x, 'pool', split_axis=0, concat_axis=0, tiled=True)]
    ppermute x0 -> x9, starting transfers between devices: none -> 12 us  [exchange(): lax.ppermute(parts[k], 'pool', [(i, (i + k) % pool) for i in range(pool)])]
    ppermute x0 -> x9, waiting for transfers between devices: none -> 11.3 us  [exchange(): lax.ppermute(parts[k], 'pool', [(i, (i + k) % pool) for i in range(pool)])]
    all_to_all x2 -> x0, starting transfers between devices: 9.69 us -> none  [exchange(): return lax.all_to_all(x, 'pool', split_axis=0, concat_axis=0, tiled=True)]
    pallas_call x1, Pallas kernels: 1.64 us -> 0.99 us  [body(): pl.pallas_call(functools.partial(attend_kernel, pool, slots, seg, width_d...]
    pallas_call x1 -> x2, Pallas kernels: 16.1 us -> 16.7 us  [the longest x1 9.89 us: body(): pl.pallas_call(functools.partial(project_kernel, pool, slots, rows_local,...]
  transfers between devices with their start and end apart: 2 -> 9, of which waited for: 2 -> 4; matrix products, arithmetic and copies ran while one was open for 2% -> 3% of each run, Pallas kernels for 0% -> 15%
where the time goes in v3:
time: 43.8 us; the launch traced here: 43.7 us
  Pallas kernels  19.1 us (44%)
  starting transfers between devices  12 us (27%)
  waiting for transfers between devices  11.3 us (26%)
  local copies, waits for them, and re-layouts  0.73 us (2%)
  other arithmetic  0.48 us (1%)
    ppermute x9, starting transfers between devices, exchange(): lax.ppermute(parts[k], 'pool', [(i, (i + k) % pool) for i in range(pool)])  12 us
    ppermute x9, waiting for transfers between devices, exchange(): lax.ppermute(parts[k], 'pool', [(i, (i + k) % pool) for i in range(pool)])  11.3 us
    pallas_call x1, Pallas kernels, body(): pl.pallas_call(functools.partial(project_kernel, pool, slots, rows_local,...  9.89 us
    pallas_call x1, Pallas kernels, body(): pl.pallas_call(functools.partial(project_rest_kernel, pool, batch * width...  6.76 us
    pallas_call x1, Pallas kernels, body(): pl.pallas_call(functools.partial(merge_kernel, pool, slots, rows_local, q...  1.41 us
    pallas_call x1, Pallas kernels, body(): pl.pallas_call(functools.partial(attend_kernel, pool, slots, seg, width_d...  0.99 us
  transfers between devices with their start and end apart: 9, of which 4 were waited for; matrix products, arithmetic and copies ran while one was open for 3% of the time, Pallas kernels for 15%

profile of v3, /device:TPU:0, one launch (start us, length us, event | category | flops | bytes accessed | tf_op | source)
XLA Modules:
  0.0 43.7 jit_solution(12060476383531663248)
XLA Ops:
  0.0 9.9 %project.1 = (bf16[16,2688]{1,0:T(8,128)(2,1)S(1)}, bf16[16,2688]{1,0:T(8,128)(2,1)S(1)}, bf16[16,2688]{1,0:T(8,128)(2,1)S(1)}, bf16[16,2688]{1,0:T(8,128)(2,1)S...) custom-call(s32[1]{0:T(128)} %bitcast.1.me_ref, s32[4,4,4]{2,1,0:T(4,128)} %send.1, s32[64]{0:T(128)} %row_len.1, ...), custom_call_target="tpu_custom_call" | custom-call | tf_op jit(solution)/shard_map/project/pallas_call | solution.py:391
  9.9 3.1 %collective-permute-start = (bf16[16,2688]{1,0:T(8,128)(2,1)S(1)}, bf16[16,2688]{1,0:T(8,128)(2,1)S(1)}, u32[]{:S(2)}, u32[]{:S(2)}) collective-permute-start(bf16[16,2688]{1,0:T(8,128)(2,1)S(1)} %get-tuple-element.20), channel_id=1, source_target_pairs={{0,4},{4,8},{8,12},{12,0},{1,5},{5,9},{9,13},{13,1},{2,6},{6,10},{... | collective-permute-start | bytes 258056 | tf_op jit(solution)/shard_map/ppermute | solution.py:339
  13.0 2.6 %collective-permute-start.1 = (bf16[16,2688]{1,0:T(8,128)(2,1)S(1)}, bf16[16,2688]{1,0:T(8,128)(2,1)S(1)}, u32[]{:S(2)}, u32[]{:S(2)}) collective-permute-start(bf16[16,2688]{1,0:T(8,128)(2,1)S(1)} %get-tuple-element.21), channel_id=1, source_target_pairs={{0,8},{4,12},{8,0},{12,4},{1,9},{5,13},{9,1},{13,5},{2,10},{6,14},... | collective-permute-start | bytes 258056 | tf_op jit(solution)/shard_map/ppermute | solution.py:339
  15.6 1.3 %collective-permute-start.2 = (bf16[16,2688]{1,0:T(8,128)(2,1)S(1)}, bf16[16,2688]{1,0:T(8,128)(2,1)S(1)}, u32[]{:S(2)}, u32[]{:S(2)}) collective-permute-start(bf16[16,2688]{1,0:T(8,128)(2,1)S(1)} %get-tuple-element.22), channel_id=1, source_target_pairs={{0,12},{4,0},{8,4},{12,8},{1,13},{5,1},{9,5},{13,9},{2,14},{6,2},{... | collective-permute-start | bytes 258056 | tf_op jit(solution)/shard_map/ppermute | solution.py:339
  16.9 0.0 copy-start.2
  16.9 0.0 copy-start.3
  16.9 0.0 copy-start.4
  16.9 0.0 copy-start.5
  16.9 0.0 copy-start
  16.9 0.0 copy-start.1
  17.0 6.8 %project_rest.1 = (bf16[16,2048]{1,0:T(8,128)(2,1)S(1)}, bf16[16,2048]{1,0:T(8,128)(2,1)S(1)}, bf16[16,2048]{1,0:T(8,128)(2,1)S(1)}, bf16[16,2048]{1,0:T(8,128)(2,1)S(1)}) custom-call(bf16[8,64,512]{2,1,0:T(8,128)(2,1)S(1)} %get-tuple-element.23.lhs, bf16[4096,4096]{1,0:T(8,128)(2,1)} %w_query.1), custom_call_target="tpu_custom_call" | custom-call | tf_op jit(solution)/shard_map/project_rest/pallas_call | solution.py:419
  23.7 0.7 %collective-permute-start.3 = (bf16[16,2048]{1,0:T(8,128)(2,1)S(1)}, bf16[16,2048]{1,0:T(8,128)(2,1)S(1)}, u32[]{:S(2)}, u32[]{:S(2)}) collective-permute-start(bf16[16,2048]{1,0:T(8,128)(2,1)S(1)} %get-tuple-element.25), channel_id=1, source_target_pairs={{0,4},{4,8},{8,12},{12,0},{1,5},{5,9},{9,13},{13,1},{2,6},{6,10},{... | collective-permute-start | bytes 196616 | tf_op jit(solution)/shard_map/ppermute | solution.py:339
  24.5 0.3 collective-permute-start.4
  24.8 0.0 copy-done.2
  24.8 0.1 eq.17
  24.9 0.1 ge.14
  25.0 0.1 iota_compare_fusion
  25.1 0.2 and_reduce_fusion
  25.3 0.1 not.14
  25.4 0.0 copy-done.3
  25.4 0.1 stack_reshape.4
  25.5 0.1 add_add_fusion
  25.6 0.0 copy-done.4
  25.6 0.0 copy-done.5
  25.6 0.1 sine_multiply_fusion
  25.7 0.1 dynamic-slice_bitcast_fusion
  25.7 0.1 broadcast_in_dim.5
  25.8 0.1 reshape.66.rest_10_
  25.9 4.6 %collective-permute-done.3.rest_5_ = bf16[16,2048]{1,0:T(8,128)(2,1)S(1)} collective-permute-done((bf16[16,2048]{1,0:T(8,128)(2,1)S(1)}, bf16[16,2048]{1,0:T(8,128)(2,1)S(1)}, u32[]{:S(2)}, u32[]{:S(2)}) %collective-permute-start.3) | collective-permute-done | bytes 65568 | tf_op jit(solution)/shard_map/ppermute | solution.py:339
  30.5 0.0 collective-permute-start.5
  30.5 0.0 collective-permute-done.4.rest_6_
  30.5 4.2 %collective-permute-done.5.rest_7_ = bf16[16,2048]{1,0:T(8,128)(2,1)S(1)} collective-permute-done((bf16[16,2048]{1,0:T(8,128)(2,1)S(1)}, bf16[16,2048]{1,0:T(8,128)(2,1)S(1)}, u32[]{:S(2)}, u32[]{:S(2)}) %collective-permute-start.5) | collective-permute-done | bytes 65568 | tf_op jit(solution)/shard_map/ppermute | solution.py:339
  34.8 0.0 collective-permute-done.rest_1_
  34.8 0.0 collective-permute-done.1.rest_2_
  34.8 0.0 collective-permute-done.2.rest_3_
  34.8 0.0 copy-done
  34.8 0.0 copy-done.1
  34.8 1.0 %attend.1 = (bf16[160,128]{1,0:T(8,128)(2,1)S(1)}, bf16[160,128]{1,0:T(8,128)(2,1)S(1)}, bf16[160,128]{1,0:T(8,128)(2,1)S(1)}, bf16[160,128]{1,0:T(8,128)(2,1)S(1)}) custom-call(s32[1]{0:T(128)} %bitcast.1.me_ref, bf16[16,2688]{1,0:T(8,128)(2,1)S(1)} %get-tuple-element.19.rest_0_, bf16[16,2688]{1,0:T(8,128)(2,1)S(1)} %collective-permute-done.rest_1_, ...), custom_call_target="tpu_custom_call" | custom-call | tf_op jit(solution)/shard_map/attend/pallas_call | solution.py:453
  35.8 0.1 collective-permute-start.6
  35.9 2.4 %collective-permute-start.7 = (bf16[160,128]{1,0:T(8,128)(2,1)S(1)}, bf16[160,128]{1,0:T(8,128)(2,1)S(1)}, u32[]{:S(2)}, u32[]{:S(2)}) collective-permute-start(bf16[160,128]{1,0:T(8,128)(2,1)S(1)} %get-tuple-element.31), channel_id=1, source_target_pairs={{0,8},{4,12},{8,0},{12,4},{1,9},{5,13},{9,1},{13,5},{2,10},{6,14},... | collective-permute-start | bytes 122888 | tf_op jit(solution)/shard_map/ppermute | solution.py:339
  38.2 1.4 %collective-permute-start.8 = (bf16[160,128]{1,0:T(8,128)(2,1)S(1)}, bf16[160,128]{1,0:T(8,128)(2,1)S(1)}, u32[]{:S(2)}, u32[]{:S(2)}) collective-permute-start(bf16[160,128]{1,0:T(8,128)(2,1)S(1)} %get-tuple-element.32), channel_id=1, source_target_pairs={{0,12},{4,0},{8,4},{12,8},{1,13},{5,1},{9,5},{13,9},{2,14},{6,2},{... | collective-permute-start | bytes 122888 | tf_op jit(solution)/shard_map/ppermute | solution.py:339
  39.7 0.1 reshape.65
  39.8 1.9 %collective-permute-done.6.rest_1_ = bf16[160,128]{1,0:T(8,128)(2,1)S(1)} collective-permute-done((bf16[160,128]{1,0:T(8,128)(2,1)S(1)}, bf16[160,128]{1,0:T(8,128)(2,1)S(1)}, u32[]{:S(2)}, u32[]{:S(2)}) %collective-permute-start.6) | collective-permute-done | bytes 40992 | tf_op jit(solution)/shard_map/ppermute | solution.py:339
  41.7 0.0 collective-permute-done.7.rest_2_
  41.7 0.6 %collective-permute-done.8.rest_3_ = bf16[160,128]{1,0:T(8,128)(2,1)S(1)} collective-permute-done((bf16[160,128]{1,0:T(8,128)(2,1)S(1)}, bf16[160,128]{1,0:T(8,128)(2,1)S(1)}, u32[]{:S(2)}, u32[]{:S(2)}) %collective-permute-start.8) | collective-permute-done | bytes 40992 | tf_op jit(solution)/shard_map/ppermute | solution.py:339
  42.2 1.4 %merge.1 = bf16[16,4096]{1,0:T(8,128)(2,1)} custom-call(s32[1,128]{1,0:T(1,128)S(1)} %concatenate.10.rows_ref, bf16[160,128]{1,0:T(8,128)(2,1)S(1)} %get-tuple-element.29.rest_0_, bf16[160,128]{1,0:T(8,128)(2,1)S(1)} %collective-permute-done.6.rest_1_, bf16[160,128]{1,0:T(8,128)(2,1)S(1)} %collective-permute-done.7.rest_2_, ...), custom_call_target="tpu_custom_call" | custom-call | tf_op jit(solution)/shard_map/merge/pallas_call | solution.py:465
  (9 shorter events, 0.1 us)
Async XLA Ops:
  9.9 24.9 %collective-permute-start = (bf16[16,2688]{1,0:T(8,128)(2,1)S(1)}, bf16[16,2688]{1,0:T(8,128)(2,1)S(1)}, u32[]{:S(2)}, u32[]{:S(2)}) collective-permute-start(bf16[16,2688]{1,0:T(8,128)(2,1)S(1)} %get-tuple-element.20), channel_id=1, source_target_pairs={{0,4},{4,8},{8,12},{12,0},{1,5},{5,9},{9,13},{13,1},{2,6},{6,10},{... | collective-permute-start | bytes 258056 | tf_op jit(solution)/shard_map/ppermute | solution.py:339
  13.0 21.8 %collective-permute-start.1 = (bf16[16,2688]{1,0:T(8,128)(2,1)S(1)}, bf16[16,2688]{1,0:T(8,128)(2,1)S(1)}, u32[]{:S(2)}, u32[]{:S(2)}) collective-permute-start(bf16[16,2688]{1,0:T(8,128)(2,1)S(1)} %get-tuple-element.21), channel_id=1, source_target_pairs={{0,8},{4,12},{8,0},{12,4},{1,9},{5,13},{9,1},{13,5},{2,10},{6,14},... | collective-permute-start | bytes 258056 | tf_op jit(solution)/shard_map/ppermute | solution.py:339
  15.6 19.2 %collective-permute-start.2 = (bf16[16,2688]{1,0:T(8,128)(2,1)S(1)}, bf16[16,2688]{1,0:T(8,128)(2,1)S(1)}, u32[]{:S(2)}, u32[]{:S(2)}) collective-permute-start(bf16[16,2688]{1,0:T(8,128)(2,1)S(1)} %get-tuple-element.22), channel_id=1, source_target_pairs={{0,12},{4,0},{8,4},{12,8},{1,13},{5,1},{9,5},{13,9},{2,14},{6,2},{... | collective-permute-start | bytes 258056 | tf_op jit(solution)/shard_map/ppermute | solution.py:339
  16.9 7.9 %copy-start.2 = (s32[4,4,4]{2,1,0:T(4,128)S(1)}, s32[4,4,4]{2,1,0:T(4,128)}, u32[]{:S(2)}) copy-start(s32[4,4,4]{2,1,0:T(4,128)} %send.1) | copy-start | bytes 772
  16.9 8.5 %copy-start.3 = (s32[1,4,4]{2,1,0:T(4,128)S(1)}, s32[1,4,4]{2,1,0:T(4,128)}, u32[]{:S(2)}) copy-start(s32[1,4,4]{2,1,0:T(4,128)} %param.20) | copy-start | bytes 196
  16.9 8.7 %copy-start.4 = (f32[128]{0:T(128)S(1)}, f32[128]{0:T(128)}, u32[]{:S(2)}) copy-start(f32[128]{0:T(128)} %constant.31) | copy-start | bytes 1540
  16.9 8.7 %copy-start.5 = (f32[128]{0:T(128)S(1)}, f32[128]{0:T(128)}, u32[]{:S(2)}) copy-start(f32[128]{0:T(128)} %constant.30) | copy-start | bytes 1540
  16.9 17.9 %copy-start = (bf16[1024,256]{1,0:T(8,128)(2,1)S(1)}, bf16[1024,256]{1,0:T(8,128)(2,1)}, u32[]{:S(2)}) copy-start(bf16[1024,256]{1,0:T(8,128)(2,1)} %rest_11_.1) | copy-start | bytes 1572868
  16.9 17.9 %copy-start.1 = (bf16[1024,256]{1,0:T(8,128)(2,1)S(1)}, bf16[1024,256]{1,0:T(8,128)(2,1)}, u32[]{:S(2)}) copy-start(bf16[1024,256]{1,0:T(8,128)(2,1)} %rest_12_.1) | copy-start | bytes 1572868
  23.7 6.8 %collective-permute-start.3 = (bf16[16,2048]{1,0:T(8,128)(2,1)S(1)}, bf16[16,2048]{1,0:T(8,128)(2,1)S(1)}, u32[]{:S(2)}, u32[]{:S(2)}) collective-permute-start(bf16[16,2048]{1,0:T(8,128)(2,1)S(1)} %get-tuple-element.25), channel_id=1, source_target_pairs={{0,4},{4,8},{8,12},{12,0},{1,5},{5,9},{9,13},{13,1},{2,6},{6,10},{... | collective-permute-start | bytes 196616 | tf_op jit(solution)/shard_map/ppermute | solution.py:339
  24.5 6.1 %collective-permute-start.4 = (bf16[16,2048]{1,0:T(8,128)(2,1)S(1)}, bf16[16,2048]{1,0:T(8,128)(2,1)S(1)}, u32[]{:S(2)}, u32[]{:S(2)}) collective-permute-start(bf16[16,2048]{1,0:T(8,128)(2,1)S(1)} %get-tuple-element.26), channel_id=1, source_target_pairs={{0,8},{4,12},{8,0},{12,4},{1,9},{5,13},{9,1},{13,5},{2,10},{6,14},... | collective-permute-start | bytes 196616 | tf_op jit(solution)/shard_map/ppermute | solution.py:339
  30.5 4.3 %collective-permute-start.5 = (bf16[16,2048]{1,0:T(8,128)(2,1)S(1)}, bf16[16,2048]{1,0:T(8,128)(2,1)S(1)}, u32[]{:S(2)}, u32[]{:S(2)}) collective-permute-start(bf16[16,2048]{1,0:T(8,128)(2,1)S(1)} %get-tuple-element.27), channel_id=1, source_target_pairs={{0,12},{4,0},{8,4},{12,8},{1,13},{5,1},{9,5},{13,9},{2,14},{6,2},{... | collective-permute-start | bytes 196616 | tf_op jit(solution)/shard_map/ppermute | solution.py:339
  35.8 5.9 %collective-permute-start.6 = (bf16[160,128]{1,0:T(8,128)(2,1)S(1)}, bf16[160,128]{1,0:T(8,128)(2,1)S(1)}, u32[]{:S(2)}, u32[]{:S(2)}) collective-permute-start(bf16[160,128]{1,0:T(8,128)(2,1)S(1)} %get-tuple-element.30), channel_id=1, source_target_pairs={{0,4},{4,8},{8,12},{12,0},{1,5},{5,9},{9,13},{13,1},{2,6},{6,10},{... | collective-permute-start | bytes 122888 | tf_op jit(solution)/shard_map/ppermute | solution.py:339
  35.9 5.8 %collective-permute-start.7 = (bf16[160,128]{1,0:T(8,128)(2,1)S(1)}, bf16[160,128]{1,0:T(8,128)(2,1)S(1)}, u32[]{:S(2)}, u32[]{:S(2)}) collective-permute-start(bf16[160,128]{1,0:T(8,128)(2,1)S(1)} %get-tuple-element.31), channel_id=1, source_target_pairs={{0,8},{4,12},{8,0},{12,4},{1,9},{5,13},{9,1},{13,5},{2,10},{6,14},... | collective-permute-start | bytes 122888 | tf_op jit(solution)/shard_map/ppermute | solution.py:339
  38.2 4.0 %collective-permute-start.8 = (bf16[160,128]{1,0:T(8,128)(2,1)S(1)}, bf16[160,128]{1,0:T(8,128)(2,1)S(1)}, u32[]{:S(2)}, u32[]{:S(2)}) collective-permute-start(bf16[160,128]{1,0:T(8,128)(2,1)S(1)} %get-tuple-element.32), channel_id=1, source_target_pairs={{0,12},{4,0},{8,4},{12,8},{1,13},{5,1},{9,5},{13,9},{2,14},{6,2},{... | collective-permute-start | bytes 122888 | tf_op jit(solution)/shard_map/ppermute | solution.py:339

commit v4 on v3

v4 whole, which is shorter than its diff:
```python
import functools

import jax
import jax.numpy as jnp
import numpy as np
from jax import lax
from jax.experimental import pallas as pl
from jax.experimental.pallas import tpu as pltpu
from jax.sharding import PartitionSpec as P

HD = 128
EPS = 1e-05
THETA = 500000.0
LOW = -1e30
WINDOW = 8
DEEP = 512
LEVELS = 16


def divides(width, limit):
    while width % limit:
        limit //= 2
    return limit


def split3(x):
    a = x.astype(jnp.bfloat16).astype(jnp.float32)
    r = x - a
    b = r.astype(jnp.bfloat16).astype(jnp.float32)
    return a, b, (r - b).astype(jnp.bfloat16).astype(jnp.float32)


def partner(me, k):
    return lax.bitwise_xor(me, k)


def project_blocks(plan, sems):
    blocks = [(n, t) for n, entry in enumerate(plan) for t in range(entry[2].shape[0])]

    def copy(n, t, i):
        w, column, buf, _ = plan[n]
        _, deep, width = buf.shape
        at = t * deep if isinstance(t, int) else pl.multiple_of(t * deep, deep)
        return pltpu.make_async_copy(
            w.at[pl.ds(at, deep), column : column + width], buf.at[t], sems.at[i]
        )

    def begin():
        for i in range(min(WINDOW, len(blocks))):
            copy(*blocks[i], i).start()

    def finish(between=None):
        first = 0
        for n, (_, _, buf, use) in enumerate(plan):
            count = buf.shape[0]
            if n == len(plan) - 1 and between is not None:
                between()

            def work(t, carry, n=n, first=first, use=use):
                copy(n, t, first + t).wait()
                use(t)
                return carry

            t = 0
            while t < count:
                ahead = first + t + WINDOW
                if ahead < len(blocks):
                    m, u = blocks[ahead]
                    run = 1
                    while (
                        t + run < count
                        and ahead + run < len(blocks)
                        and blocks[ahead + run][0] == m
                    ):
                        run += 1

                    def step(q, carry, m=m, u=u, t=t, ahead=ahead, work=work):
                        copy(m, u + q, ahead + q).start()
                        return work(t + q, carry)

                    lax.fori_loop(0, run, step, 0)
                else:
                    run = count - t
                    lax.fori_loop(t, count, work, 0)
                t += run
            first += count

    return begin, finish


def add_products(left, buf, t, sums):
    width = buf.shape[2]
    tile = divides(width, 512)
    for at in range(0, width, tile):
        sums[:, at : at + tile] += jnp.dot(
            left, buf[t, :, at : at + tile], preferred_element_type=jnp.float32
        )


def spread(chosen, sums, outs, at):
    width = sums.shape[1]
    tile = divides(width, 512)
    per = chosen.shape[0] // len(outs)
    for column in range(0, width, tile):
        rows = jnp.dot(
            chosen,
            sums[:, column : column + tile].astype(jnp.bfloat16),
            preferred_element_type=jnp.float32,
        ).astype(jnp.bfloat16)
        for k, out in enumerate(outs):
            out[:, at + column : at + column + tile] = rows[k * per : (k + 1) * per]


def project_kernel(pool, slots, rows_local, me_ref, send, lens, row_len, hidden, gain, *rest):
    w_key, w_value, w_query, *rest = rest
    outs, rest = rest[:pool], rest[pool:]
    lhs, pick, positions, marks, home_rows, home_slots, *rest = rest
    send_buf, lens_buf, row_len_buf, x_buf, g_buf, *rest = rest
    query_buf, key_buf, value_buf, late_buf, sums, squares, in_sem, sems = rest
    per = pool * slots
    n_rows, depth = x_buf.shape
    count, deep, _ = query_buf.shape
    me = me_ref[0]

    def named(home, owner, c):
        if len(send_buf.shape) == 3:
            return send_buf[home, owner, c]
        return send_buf[home * per + owner * slots + c]

    lane = lax.broadcasted_iota(jnp.int32, (1, n_rows), 1)
    place = lax.broadcasted_iota(jnp.int32, (1, HD), 1)
    group = marks.shape[1] // per
    slot_of = lax.broadcasted_iota(jnp.int32, (1, marks.shape[1]), 1) // group

    def choose(i):
        owner = partner(me, i // per)
        s = lax.rem(i, per)
        home = partner(owner, s // slots)
        r = named(home, owner, lax.rem(s, slots))
        row = jnp.where(r >= 0, home * rows_local + r, -1)
        pick[pl.ds(i, 1), :] = (lane == row).astype(jnp.float32)

    def describe(s):
        k, c = s // slots, lax.rem(s, slots)
        home = partner(me, k)
        r = named(home, me, c)
        at = row_len_buf[home * rows_local + jnp.maximum(r, 0)].astype(jnp.float32)
        positions[pl.ds(s, 1), :] = jnp.full((1, HD), at, jnp.float32)
        length = lens_buf[0, home, c] if len(lens_buf.shape) == 3 else lens_buf[home * slots + c]
        earlier = jnp.int32(0)
        for e in range(per):
            same = (named(home, e // slots, e % slots) == r) & (e < me * slots + c)
            earlier = earlier | same.astype(jnp.int32)
        first = jnp.where((earlier == 0) & (r >= 0), 1, 0)
        marks[0:1, :] = jnp.where(slot_of == s, length, marks[0:1, :])
        marks[1:2, :] = jnp.where(slot_of == s, first, marks[1:2, :])
        mine = named(me, home, c)
        home_slots[...] = jnp.where(lax.rem(place, per) == s, mine, home_slots[...])
        home_rows[pl.ds(k, 1), :] = jnp.where(
            lax.rem(place // group, slots) == c, mine, home_rows[pl.ds(k, 1), :]
        )

    def each(do, total, t):
        share = -(-total // count)
        if share <= 16 and total % count == 0:
            for q in range(share):
                do(t * share + q)
        else:

            @pl.when(t == 0)
            def _():
                def one(i, carry):
                    do(i)
                    return carry

                lax.fori_loop(0, total, one, 0)

    def use_query(t):
        at = pl.multiple_of(t * deep, deep)
        x = x_buf[:, pl.ds(at, deep)].astype(jnp.float32)
        gains = g_buf[pl.ds(at, deep)].astype(jnp.float32).reshape(1, deep)
        left = (x * gains).astype(jnp.bfloat16)
        lhs[t] = left
        squared = x * x
        for column in range(0, deep, HD):
            squares[...] += squared[:, column : column + HD]
        add_products(left, query_buf, t, sums.at[:, 2 * kv_cols : late])
        each(choose, pool * per, t)
        each(describe, per, t)

    def use_late(t):
        add_products(lhs[t], late_buf, t, sums.at[:, late:])

    kv_cols = w_key.shape[1]
    late = 2 * kv_cols + query_buf.shape[2]

    def use_narrow(buf, at):
        halves, tall, _ = buf.shape

        def use(t):
            part = 0.0
            for k in range(tall // deep):
                part = part + jnp.dot(
                    lhs[t * (tall // deep) + k],
                    buf[t, k * deep : (k + 1) * deep, :],
                    preferred_element_type=jnp.float32,
                )
            sums[:, at : at + kv_cols] += part

        return use

    begin, finish = project_blocks(
        [
            (w_query, 0, query_buf, use_query),
            (w_key, 0, key_buf, use_narrow(key_buf, 0)),
            (w_value, 0, value_buf, use_narrow(value_buf, kv_cols)),
            (w_query, query_buf.shape[2], late_buf, use_late),
        ],
        sems,
    )
    inputs = [
        pltpu.make_async_copy(source, target, in_sem.at[i])
        for i, (source, target) in enumerate(
            (
                (gain, g_buf),
                (hidden, x_buf),
                (send, send_buf),
                (lens, lens_buf),
                (row_len, row_len_buf),
            )
        )
    ]
    for one in inputs:
        one.start()
    begin()
    sums[...] = jnp.zeros(sums.shape, jnp.float32)
    squares[...] = jnp.zeros((n_rows, HD), jnp.float32)
    marks[...] = jnp.zeros(marks.shape, jnp.int32)
    home_rows[...] = jnp.full(home_rows.shape, -1, jnp.int32)
    home_slots[...] = jnp.full(home_slots.shape, -1, jnp.int32)
    for one in inputs:
        one.wait()

    def between():
        power = jnp.sum(squares[...], axis=1, keepdims=True)
        at = lax.broadcasted_iota(jnp.int32, (n_rows, HD), 1)
        a, b, c = split3(power)
        squares[...] = jnp.where(at == 0, a, jnp.where(at == 1, b, jnp.where(at == 2, c, 0.0)))
        chosen = pick[...].astype(jnp.bfloat16)
        spread(chosen, squares, outs, sums.shape[1])
        spread(chosen, sums.at[:, :late], outs, 0)

    finish(between)
    spread(pick[...].astype(jnp.bfloat16), sums.at[:, late:], outs, late)


def project_rest_kernel(pool, column, lhs, pick, w_query, near, *rest):
    outs, (query_buf, sums, sems) = rest[:pool], rest[pool:]
    done = near.shape[1]

    def use(t):
        add_products(lhs[t], query_buf, t, sums)

    begin, finish = project_blocks([(w_query, column, query_buf, use)], sems)
    begin()
    sums[...] = jnp.zeros(sums.shape, jnp.float32)
    outs[1][:, :done] = near[...]
    finish()
    outs = [out.at[:, done:] if k == 1 else out for k, out in enumerate(outs)]
    spread(pick[...].astype(jnp.bfloat16), sums, outs, 0)


def attend_kernel(pool, slots, seg, width_d, q_heads, kv_heads, me_ref, *rest):
    terms, rest = rest[: 2 * pool - 1], rest[2 * pool - 1 :]
    cos, sin, marks, keys, values = rest[:5]
    outs, (q_buf,) = rest[5 : 5 + pool], rest[5 + pool :]
    per = pool * slots
    group = q_heads // kv_heads
    step = HD // group
    scale = HD ** (-0.5)

    own, own_rest, near = terms[:3]
    far, far_rest = terms[3 : 1 + pool], terms[1 + pool :]
    first_cols, cols = own.shape[1], near.shape[1]

    def total(at):
        if at < first_cols:
            got, others = own[:, at : at + HD], far
        else:
            got, others = own_rest[:, at - first_cols : at - first_cols + HD], far_rest
        got = got.astype(jnp.float32) + near[:, at : at + HD].astype(jnp.float32)
        at = at if at < first_cols else at - first_cols
        for part in others:
            got = got + part[:, at : at + HD].astype(jnp.float32)
        return got

    heads = [at for at in range(2 * kv_heads * HD, cols, HD) if at != first_cols - HD]
    power = jnp.sum(total(first_cols - HD), axis=1, keepdims=True)
    factor = lax.rsqrt(power * (1.0 / width_d) + EPS)
    cosines, sines = cos[...], sin[...]

    def rounded(x):
        return x.astype(jnp.bfloat16).astype(jnp.float32)

    def rotated(x):
        return rounded(x * cosines + pltpu.roll(x, HD // 2, axis=1) * sines)

    for i in range(q_heads):
        q_buf[i * per : (i + 1) * per, :] = rotated(total(heads[i]) * factor)
    keys_own = [rotated(total(g * HD) * factor) for g in range(kv_heads)]
    values_own = [
        rounded(total((kv_heads + g) * HD) * factor) for g in range(kv_heads)
    ]

    me = me_ref[0]

    def base(j):
        return pl.multiple_of(partner(me, j) * (slots * seg), slots * seg)

    lane = lax.broadcasted_iota(jnp.int32, (1, HD), 1)
    slot_of = lane // group
    at = lax.broadcasted_iota(jnp.int32, (seg, HD), 0)
    at_own = lax.broadcasted_iota(jnp.int32, (step, HD), 0)
    blocks = [(g, s) for s in range(0, per, step) for g in range(kv_heads)]
    columns = []
    for g, s in blocks:
        query = jnp.concatenate(
            [q_buf[pl.ds(g * group * per + s + u, group, stride=per), :] for u in range(step)], 0
        )
        columns.append(query.T.astype(jnp.bfloat16))
    scores = []
    for (g, s), query in zip(blocks, columns):
        score = None
        for u in range(0, step, slots):
            wide = jnp.dot(
                keys[pl.ds(base((s + u) // slots), slots * seg), g * HD : (g + 1) * HD],
                query,
                preferred_element_type=jnp.float32,
            )
            for c in range(slots):
                each = wide[c * seg : (c + 1) * seg]
                score = each if score is None else jnp.where(slot_of == u + c, each, score)
        own = jnp.dot(
            keys_own[g][s : s + step].astype(jnp.bfloat16),
            query,
            preferred_element_type=jnp.float32,
        )
        own = jnp.sum(jnp.where(at_own == slot_of, own, 0.0), axis=0, keepdims=True)
        scores.append((score * scale, own * scale))
    turned, levels = [], {}
    for (g, s), (score, own) in zip(blocks, scores):
        length = marks[0:1, s * group : s * group + HD]
        with_own = marks[1:2, s * group : s * group + HD] > 0
        usable = at < length
        own = jnp.where(with_own, own, LOW)
        top = jnp.maximum(jnp.max(jnp.where(usable, score, LOW), axis=0, keepdims=True), own)
        weight = jnp.where(usable, jnp.exp(score - top), 0.0)
        weight_own = jnp.where(with_own, jnp.exp(own - top), 0.0)
        sums = jnp.sum(weight, axis=0, keepdims=True) + weight_own
        sums = jnp.where(length > 0, sums, 1.0)
        level = top + jnp.log(sums)
        for u in range(0, step, slots):
            at_lane = g * slots * group
            moved = level if at_lane == u * group else pltpu.roll(level, (at_lane - u * group) % HD, axis=1)
            there = (lane >= at_lane) & (lane < at_lane + slots * group)
            home = (s + u) // slots
            levels[home] = jnp.where(there, moved, levels.get(home, 0.0))
        rows = [weight_own, 1.0 / sums, jnp.zeros((HD - seg - 2, HD), jnp.float32)]
        turned.append(jnp.concatenate([weight] + rows, 0).T)
    for (g, s), block in zip(blocks, turned):
        for u in range(step):
            home, c = (s + u) // slots, (s + u) % slots
            rows = block[u * group : (u + 1) * group]
            mixed = jnp.dot(
                rows[:, :seg].astype(jnp.bfloat16),
                values[pl.ds(base(home) + c * seg, seg), g * HD : (g + 1) * HD],
                preferred_element_type=jnp.float32,
            )
            mixed = mixed + rows[:, seg : seg + 1] * values_own[g][s + u : s + u + 1]
            to = c * q_heads + g * group
            outs[home][to : to + group, :] = (mixed * rows[:, seg + 1 : seg + 2]).astype(jnp.bfloat16)
    for home, level in levels.items():
        block = jnp.concatenate([*split3(level), jnp.zeros((LEVELS - 3, HD), jnp.float32)], 0)
        outs[home][slots * q_heads :, :] = block.astype(jnp.bfloat16)


def merge_kernel(pool, slots, rows_local, q_heads, kv_heads, slots_ref, rows_ref, *rest):
    found, (out, scaled) = rest[:pool], rest[pool:]
    per = pool * slots
    group = q_heads // kv_heads
    block = slots * q_heads
    span = slots * group
    level = jnp.concatenate(
        [jnp.sum(part[block : block + LEVELS, :].astype(jnp.float32), 0, keepdims=True) for part in found], 0
    )
    named = rows_ref[...]
    lane = lax.broadcasted_iota(jnp.int32, (pool, HD), 1)

    def turns(x):
        for c in range(slots):
            y = x
            if c:
                y = jnp.where(
                    lax.rem(lane, span) < span - c * group,
                    pltpu.roll(x, HD - c * group, axis=1),
                    pltpu.roll(x, span - c * group, axis=1),
                )
            for k in range(pool):
                yield jnp.concatenate([y[k:], y[:k]], 0) if k else y

    same = [other == named for other in turns(named)]
    top = level
    for match, other in zip(same, turns(level)):
        top = jnp.maximum(top, jnp.where(match, other, LOW))
    weight = jnp.exp(level - top)
    total = jnp.zeros_like(weight)
    for match, other in zip(same, turns(weight)):
        total = total + jnp.where(match, other, 0.0)
    share = jnp.where(named >= 0, weight / total, 0.0)
    share = jnp.concatenate([share, jnp.zeros((HD - pool, HD), jnp.float32)], 0).T
    for k in range(pool):
        for c in range(slots):
            for g in range(kv_heads):
                at = c * q_heads + g * group
                each = g * span + c * group
                scaled[k * block + at : k * block + at + group, :] = (
                    found[k][at : at + group, :].astype(jnp.float32)
                    * share[each : each + group, k : k + 1]
                )
    row = lax.broadcasted_iota(jnp.int32, (rows_local, 2 * per), 0)
    match = (slots_ref[:, : 2 * per] == row).astype(jnp.float32).astype(jnp.bfloat16)
    for i in range(q_heads):
        part = scaled[pl.ds(i, per, stride=q_heads), :]
        high = part.astype(jnp.bfloat16)
        low = (part - high.astype(jnp.float32)).astype(jnp.bfloat16)
        out[:, i * HD : (i + 1) * HD] = jnp.dot(
            match, jnp.concatenate([high, low], 0), preferred_element_type=jnp.float32
        ).astype(jnp.bfloat16)


def exchange(parts, order):
    got = list(parts)
    for k in order:
        got[k] = lax.ppermute(parts[k], "pool", [(i, i ^ k) for i in range(len(parts))])
    return got


def in_hbm(x):
    return pltpu.with_memory_space_constraint(x, pltpu.HBM)


SMEM = pl.BlockSpec(memory_space=pltpu.SMEM)
VMEM = pl.BlockSpec(memory_space=pltpu.VMEM)
HBM = pl.BlockSpec(memory_space=pltpu.HBM)


def body(
    hidden_in,
    norm_gain,
    w_query,
    w_key,
    w_value,
    cache_keys,
    cache_values,
    send_row,
    piece_len,
    row_len,
):
    pool = lax.axis_size("pool")
    me = lax.axis_index("pool").astype(jnp.int32)
    n_rows, depth = hidden_in.shape
    width_d = depth * pool
    rows_local = n_rows // pool
    slots = send_row.shape[2]
    per = pool * slots
    seg = cache_keys.shape[0] // per
    q_cols, kv_cols = w_query.shape[1], w_key.shape[1]
    q_heads, kv_heads = q_cols // HD, kv_cols // HD
    group = q_heads // kv_heads
    cols = q_cols + 2 * kv_cols + HD

    if pool <= 8:
        indices = [send_row, piece_len, row_len]
    else:
        indices = [send_row.reshape(-1), piece_len.reshape(-1), row_len]
    deep = divides(depth, DEEP)
    count = depth // deep
    halves = 2 if count % 2 == 0 else 1
    widths = [3 * q_cols // 4, q_cols // 4]

    def parts(width):
        return [jax.ShapeDtypeStruct((per, width), jnp.bfloat16)] * pool

    operands = [in_hbm(x) for x in (*indices, hidden_in, norm_gain, w_key, w_value, w_query)]
    *first_terms, lhs, pick, positions, marks, home_rows, home_slots = pl.pallas_call(
        functools.partial(project_kernel, pool, slots, rows_local),
        out_shape=[
            *parts(2 * kv_cols + widths[0] + HD),
            jax.ShapeDtypeStruct((count, n_rows, deep), jnp.bfloat16),
            jax.ShapeDtypeStruct((pool * per, n_rows), jnp.float32),
            jax.ShapeDtypeStruct((per, HD), jnp.float32),
            jax.ShapeDtypeStruct((2, per * group), jnp.int32),
            jax.ShapeDtypeStruct((pool, HD), jnp.int32),
            jax.ShapeDtypeStruct((1, HD), jnp.int32),
        ],
        in_specs=[SMEM] + [HBM] * 8,
        out_specs=[VMEM] * (pool + 6),
        scratch_shapes=[
            *(pltpu.SMEM(x.shape, jnp.int32) for x in indices),
            pltpu.VMEM((n_rows, depth), jnp.bfloat16),
            pltpu.VMEM((depth,), jnp.bfloat16),
            pltpu.VMEM((count, deep, widths[0] // 2), jnp.bfloat16),
            pltpu.VMEM((halves, depth // halves, kv_cols), jnp.bfloat16),
            pltpu.VMEM((halves, depth // halves, kv_cols), jnp.bfloat16),
            pltpu.VMEM((count, deep, widths[0] // 2), jnp.bfloat16),
            pltpu.VMEM((n_rows, 2 * kv_cols + widths[0]), jnp.float32),
            pltpu.VMEM((n_rows, HD), jnp.float32),
            pltpu.SemaphoreType.DMA((5,)),
            pltpu.SemaphoreType.DMA((2 * count + 2 * halves,)),
        ],
        compiler_params=pltpu.CompilerParams(vmem_limit_bytes=46 * 2**20),
        name="project",
    )(me[None], *operands)
    first_cols = 2 * kv_cols + widths[0] + HD
    rest_shapes = parts(widths[1])
    rest_shapes[1] = jax.ShapeDtypeStruct((per, first_cols + widths[1]), jnp.bfloat16)
    rest_terms = pl.pallas_call(
        functools.partial(project_rest_kernel, pool, widths[0]),
        out_shape=rest_shapes,
        in_specs=[VMEM, VMEM, HBM, VMEM],
        out_specs=[VMEM] * pool,
        scratch_shapes=[
            pltpu.VMEM((count, deep, widths[1]), jnp.bfloat16),
            pltpu.VMEM((n_rows, widths[1]), jnp.float32),
            pltpu.SemaphoreType.DMA((count,)),
        ],
        compiler_params=pltpu.CompilerParams(vmem_limit_bytes=40 * 2**20),
        cost_estimate=pl.CostEstimate(
            flops=2 * n_rows * depth * widths[1],
            bytes_accessed=2 * depth * (widths[1] + n_rows),
            transcendentals=0,
        ),
        name="project_rest",
    )(lhs, pick, operands[-1], first_terms[1])
    first_terms = exchange(first_terms, range(2, pool))
    first_terms[2], rest_terms = lax.optimization_barrier((first_terms[2], list(rest_terms)))
    rest_terms = exchange(rest_terms, range(1, pool))
    terms = [first_terms[0], *rest_terms[:2], *first_terms[2:], *rest_terms[2:]]

    half = HD // 2
    freq = THETA ** (-(np.arange(half) * 2.0) / HD)
    angles = positions * np.concatenate([freq, freq]).astype(np.float32)[None, :]
    sign = np.concatenate([-np.ones(half), np.ones(half)]).astype(np.float32)[None, :]
    cosines, sines = jnp.cos(angles), jnp.sin(angles) * sign

    found = pl.pallas_call(
        functools.partial(attend_kernel, pool, slots, seg, width_d, q_heads, kv_heads),
        out_shape=[jax.ShapeDtypeStruct((slots * q_heads + LEVELS, HD), jnp.bfloat16)] * pool,
        in_specs=[SMEM] + [VMEM] * (2 * pool + 4),
        out_specs=[VMEM] * pool,
        scratch_shapes=[pltpu.VMEM((q_heads * per, HD), jnp.float32)],
        compiler_params=pltpu.CompilerParams(vmem_limit_bytes=24 * 2**20),
        name="attend",
    )(me[None], *terms, cosines, sines, marks, cache_keys, cache_values)

    found = exchange(found, [*range(2, pool), 1])

    return pl.pallas_call(
        functools.partial(merge_kernel, pool, slots, rows_local, q_heads, kv_heads),
        out_shape=jax.ShapeDtypeStruct((rows_local, q_cols), jnp.bfloat16),
        in_specs=[VMEM] * (2 + pool),
        out_specs=VMEM,
        scratch_shapes=[
            pltpu.VMEM((per * q_heads, HD), jnp.float32),
        ],
        compiler_params=pltpu.CompilerParams(vmem_limit_bytes=24 * 2**20),
        name="merge",
    )(home_slots, home_rows, *found)


def solution(mesh):
    return jax.shard_map(
        body,
        mesh=mesh,
        in_specs=(
            P("groups", "pool"),
            P("pool"),
            P("pool", "tensor"),
            P("pool", "tensor"),
            P("pool", "tensor"),
            P(("groups", "pool"), "tensor"),
            P(("groups", "pool"), "tensor"),
            P("groups", None, None),
            P(("groups", "pool"), None, None),
            P("groups"),
        ),
        out_specs=P(("groups", "pool"), "tensor"),
        check_vma=False,
    )
```

time: 43.8 us -> 44.5 us (1.016)
  starting transfers between devices: 12 us -> 14.3 us
  local copies, waits for them, and re-layouts: 0.73 us -> 0.01 us
    ppermute x9 -> x8, starting transfers between devices: 12 us -> 14.3 us  [exchange(): lax.ppermute(parts[k], 'pool', [(i, i ^ k) for i in range(len(parts))])]
    ppermute x9 -> x8, waiting for transfers between devices: 11.3 us -> 11.3 us  [exchange(): lax.ppermute(parts[k], 'pool', [(i, i ^ k) for i in range(len(parts))])]
  transfers between devices with their start and end apart: 9 -> 8, of which waited for: 4 -> 5; matrix products, arithmetic and copies ran while one was open for 3% -> 0% of each run, Pallas kernels for 15% -> 9%
where the time goes in v4:
time: 44.5 us; the launch traced here: 44.4 us
  Pallas kernels  18.7 us (42%)
  starting transfers between devices  14.3 us (32%)
  waiting for transfers between devices  11.3 us (25%)
    ppermute x8, starting transfers between devices, exchange(): lax.ppermute(parts[k], 'pool', [(i, i ^ k) for i in range(len(parts))])  14.3 us
    pallas_call x1, Pallas kernels, body(): pl.pallas_call(functools.partial(project_kernel, pool, slots, rows_local)...  12.2 us
    ppermute x8, waiting for transfers between devices, exchange(): lax.ppermute(parts[k], 'pool', [(i, i ^ k) for i in range(len(parts))])  11.3 us
    pallas_call x1, Pallas kernels, body(): pl.pallas_call(functools.partial(project_rest_kernel, pool, widths[0]), o...  4.06 us
    pallas_call x1, Pallas kernels, body(): pl.pallas_call(functools.partial(merge_kernel, pool, slots, rows_local, q...  1.33 us
    pallas_call x1, Pallas kernels, body(): pl.pallas_call(functools.partial(attend_kernel, pool, slots, seg, width_d...  1.06 us
  transfers between devices with their start and end apart: 8, of which 5 were waited for; matrix products, arithmetic and copies ran while one was open for 0% of the time, Pallas kernels for 9%

profile of v4, /device:TPU:0, one launch (start us, length us, event | category | flops | bytes accessed | tf_op | source)
XLA Modules:
  0.0 44.4 jit_solution(4970667557457407332)
XLA Ops:
  0.0 12.2 %project.1 = (bf16[16,3712]{1,0:T(8,128)(2,1)S(1)}, bf16[16,3712]{1,0:T(8,128)(2,1)S(1)}, bf16[16,3712]{1,0:T(8,128)(2,1)S(1)}, bf16[16,3712]{1,0:T(8,128)(2,1)S...) custom-call(s32[1]{0:T(128)} %bitcast.me_ref, ...), custom_call_target="tpu_custom_call" | custom-call | tf_op jit(solution)/shard_map/project/pallas_call | solution.py:495
  12.2 4.1 %collective-permute-start = (bf16[16,3712]{1,0:T(8,128)(2,1)S(1)}, bf16[16,3712]{1,0:T(8,128)(2,1)S(1)}, u32[]{:S(2)}, u32[]{:S(2)}) collective-permute-start(bf16[16,3712]{1,0:T(8,128)(2,1)S(1)} %get-tuple-element.31), channel_id=1, source_target_pairs={{0,8},{4,12},{8,0},{12,4},{1,9},{5,13},{9,1},{13,5},{2,10},{6,14},... | collective-permute-start | bytes 356360 | tf_op jit(solution)/shard_map/ppermute | solution.py:444
  16.3 1.3 %collective-permute-start.2 = (bf16[16,3712]{1,0:T(8,128)(2,1)S(1)}, bf16[16,3712]{1,0:T(8,128)(2,1)S(1)}, u32[]{:S(2)}, u32[]{:S(2)}) collective-permute-start(bf16[16,3712]{1,0:T(8,128)(2,1)S(1)} %get-tuple-element.42), channel_id=1, source_target_pairs={{0,12},{4,8},{8,4},{12,0},{1,13},{5,9},{9,5},{13,1},{2,14},{6,10},... | collective-permute-start | bytes 356360 | tf_op jit(solution)/shard_map/ppermute | solution.py:444
  17.7 0.0 copy-start.2
  17.7 0.0 copy-start.3
  17.7 0.0 copy-start
  17.7 0.0 copy-start.1
  17.7 4.1 %project_rest.1 = (bf16[16,1024]{1,0:T(8,128)(2,1)S(1)}, bf16[16,4736]{1,0:T(8,128)(2,1)S(1)}, bf16[16,1024]{1,0:T(8,128)(2,1)S(1)}, bf16[16,1024]{1,0:T(8,128)(2,1)S(1)}) custom-call(bf16[8,64,512]{2,1,0:T(8,128)(2,1)S(1)} %get-tuple-element.32.lhs, f32[64,64]{1,0:T(8,128)S(1)} %get-tuple-element.33.pick, bf16[4096,4096]{1,0:T(8,128)(2,1)} %w_query.1, ...), custom_call_target="tpu_custom_call" | custom-call | flops 536870912 | bytes 8912896 | tf_op jit(solution)/shard_map/project_rest/pallas_call | solution.py:527
  21.8 3.7 %collective-permute-done.rest_3_ = bf16[16,3712]{1,0:T(8,128)(2,1)S(1)} collective-permute-done((bf16[16,3712]{1,0:T(8,128)(2,1)S(1)}, bf16[16,3712]{1,0:T(8,128)(2,1)S(1)}, u32[]{:S(2)}, u32[]{:S(2)}) %collective-permute-start) | collective-permute-done | bytes 118816 | tf_op jit(solution)/shard_map/ppermute | solution.py:444
  25.5 0.0 collective-permute-start.1
  25.5 3.4 %collective-permute-start.3 = (bf16[16,1024]{1,0:T(8,128)(2,1)S(1)}, bf16[16,1024]{1,0:T(8,128)(2,1)S(1)}, u32[]{:S(2)}, u32[]{:S(2)}) collective-permute-start(bf16[16,1024]{1,0:T(8,128)(2,1)S(1)} %get-tuple-element.43), channel_id=1, source_target_pairs={{0,8},{4,12},{8,0},{12,4},{1,9},{5,13},{9,1},{13,5},{2,10},{6,14},... | collective-permute-start | bytes 98312 | tf_op jit(solution)/shard_map/ppermute | solution.py:444
  28.9 1.0 %collective-permute-start.4 = (bf16[16,1024]{1,0:T(8,128)(2,1)S(1)}, bf16[16,1024]{1,0:T(8,128)(2,1)S(1)}, u32[]{:S(2)}, u32[]{:S(2)}) collective-permute-start(bf16[16,1024]{1,0:T(8,128)(2,1)S(1)} %get-tuple-element.44), channel_id=1, source_target_pairs={{0,12},{4,8},{8,4},{12,0},{1,13},{5,9},{9,5},{13,1},{2,14},{6,10},... | collective-permute-start | bytes 98312 | tf_op jit(solution)/shard_map/ppermute | solution.py:444
  29.9 0.0 copy-done.2
  29.9 0.0 copy-done.3
  29.9 0.1 sine_multiply_fusion
  29.9 0.0 collective-permute-done.2.rest_4_
  30.0 1.0 %collective-permute-done.3.rest_5_ = bf16[16,1024]{1,0:T(8,128)(2,1)S(1)} collective-permute-done((bf16[16,1024]{1,0:T(8,128)(2,1)S(1)}, bf16[16,1024]{1,0:T(8,128)(2,1)S(1)}, u32[]{:S(2)}, u32[]{:S(2)}) %collective-permute-start.3) | collective-permute-done | bytes 32800 | tf_op jit(solution)/shard_map/ppermute | solution.py:444
  31.0 3.6 %collective-permute-done.4.rest_6_ = bf16[16,1024]{1,0:T(8,128)(2,1)S(1)} collective-permute-done((bf16[16,1024]{1,0:T(8,128)(2,1)S(1)}, bf16[16,1024]{1,0:T(8,128)(2,1)S(1)}, u32[]{:S(2)}, u32[]{:S(2)}) %collective-permute-start.4) | collective-permute-done | bytes 32800 | tf_op jit(solution)/shard_map/ppermute | solution.py:444
  34.6 0.0 collective-permute-done.1.rest_2_
  34.6 0.0 copy-done
  34.6 0.0 copy-done.1
  34.6 1.1 %attend.1 = (bf16[144,128]{1,0:T(8,128)(2,1)S(1)}, bf16[144,128]{1,0:T(8,128)(2,1)S(1)}, bf16[144,128]{1,0:T(8,128)(2,1)S(1)}, bf16[144,128]{1,0:T(8,128)(2,1)S(1)}) custom-call(s32[1]{0:T(128)} %bitcast.me_ref, bf16[16,3712]{1,0:T(8,128)(2,1)S(1)} %get-tuple-element.30.rest_0_, bf16[16,1024]{1,0:T(8,128)(2,1)S(1)} %get-tuple-element.39.rest_1_, ...), custom_call_target="tpu_custom_call" | custom-call | tf_op jit(solution)/shard_map/attend/pallas_call | solution.py:556
  35.7 0.1 collective-permute-start.5
  35.7 1.6 %collective-permute-start.6 = (bf16[144,128]{1,0:T(8,128)(2,1)S(1)}, bf16[144,128]{1,0:T(8,128)(2,1)S(1)}, u32[]{:S(2)}, u32[]{:S(2)}) collective-permute-start(bf16[144,128]{1,0:T(8,128)(2,1)S(1)} %get-tuple-element.49), channel_id=1, source_target_pairs={{0,8},{4,12},{8,0},{12,4},{1,9},{5,13},{9,1},{13,5},{2,10},{6,14},... | collective-permute-start | bytes 110600 | tf_op jit(solution)/shard_map/ppermute | solution.py:444
  37.3 2.8 %collective-permute-start.7 = (bf16[144,128]{1,0:T(8,128)(2,1)S(1)}, bf16[144,128]{1,0:T(8,128)(2,1)S(1)}, u32[]{:S(2)}, u32[]{:S(2)}) collective-permute-start(bf16[144,128]{1,0:T(8,128)(2,1)S(1)} %get-tuple-element.50), channel_id=1, source_target_pairs={{0,12},{4,8},{8,4},{12,0},{1,13},{5,9},{9,5},{13,1},{2,14},{6,10},... | collective-permute-start | bytes 110600 | tf_op jit(solution)/shard_map/ppermute | solution.py:444
  40.1 0.0 collective-permute-done.5.rest_1_
  40.1 0.5 %collective-permute-done.6.rest_2_ = bf16[144,128]{1,0:T(8,128)(2,1)S(1)} collective-permute-done((bf16[144,128]{1,0:T(8,128)(2,1)S(1)}, bf16[144,128]{1,0:T(8,128)(2,1)S(1)}, u32[]{:S(2)}, u32[]{:S(2)}) %collective-permute-start.6) | collective-permute-done | bytes 36896 | tf_op jit(solution)/shard_map/ppermute | solution.py:444
  40.7 2.4 %collective-permute-done.7.rest_3_ = bf16[144,128]{1,0:T(8,128)(2,1)S(1)} collective-permute-done((bf16[144,128]{1,0:T(8,128)(2,1)S(1)}, bf16[144,128]{1,0:T(8,128)(2,1)S(1)}, u32[]{:S(2)}, u32[]{:S(2)}) %collective-permute-start.7) | collective-permute-done | bytes 36896 | tf_op jit(solution)/shard_map/ppermute | solution.py:444
  43.1 1.3 %merge.1 = bf16[16,4096]{1,0:T(8,128)(2,1)} custom-call(s32[1,128]{1,0:T(1,128)S(1)} %get-tuple-element.28.slots_ref, s32[4,128]{1,0:T(4,128)S(1)} %get-tuple-element.29.rows_ref, bf16[144,128]{1,0:T(8,128)(2,1)S(1)} %get-tuple-element.47.rest_0_, bf16[144,128]{1,0:T(8,128)(2,1)S(1)} %collective-permute-done.5.rest_1_, ...), custom_call_target="tpu_custom_call" | custom-call | tf_op jit(solution)/shard_map/merge/pallas_call | solution.py:568
Async XLA Ops:
  12.2 13.3 %collective-permute-start = (bf16[16,3712]{1,0:T(8,128)(2,1)S(1)}, bf16[16,3712]{1,0:T(8,128)(2,1)S(1)}, u32[]{:S(2)}, u32[]{:S(2)}) collective-permute-start(bf16[16,3712]{1,0:T(8,128)(2,1)S(1)} %get-tuple-element.31), channel_id=1, source_target_pairs={{0,8},{4,12},{8,0},{12,4},{1,9},{5,13},{9,1},{13,5},{2,10},{6,14},... | collective-permute-start | bytes 356360 | tf_op jit(solution)/shard_map/ppermute | solution.py:444
  16.3 13.6 %collective-permute-start.2 = (bf16[16,3712]{1,0:T(8,128)(2,1)S(1)}, bf16[16,3712]{1,0:T(8,128)(2,1)S(1)}, u32[]{:S(2)}, u32[]{:S(2)}) collective-permute-start(bf16[16,3712]{1,0:T(8,128)(2,1)S(1)} %get-tuple-element.42), channel_id=1, source_target_pairs={{0,12},{4,8},{8,4},{12,0},{1,13},{5,9},{9,5},{13,1},{2,14},{6,10},... | collective-permute-start | bytes 356360 | tf_op jit(solution)/shard_map/ppermute | solution.py:444
  17.7 12.2 %copy-start.2 = (f32[128]{0:T(128)S(1)}, f32[128]{0:T(128)}, u32[]{:S(2)}) copy-start(f32[128]{0:T(128)} %constant.12) | copy-start | bytes 1540
  17.7 12.2 %copy-start.3 = (f32[128]{0:T(128)S(1)}, f32[128]{0:T(128)}, u32[]{:S(2)}) copy-start(f32[128]{0:T(128)} %constant.13) | copy-start | bytes 1540
  17.7 16.9 %copy-start = (bf16[1024,256]{1,0:T(8,128)(2,1)S(1)}, bf16[1024,256]{1,0:T(8,128)(2,1)}, u32[]{:S(2)}) copy-start(bf16[1024,256]{1,0:T(8,128)(2,1)} %rest_10_.1) | copy-start | bytes 1572868
  17.7 16.9 %copy-start.1 = (bf16[1024,256]{1,0:T(8,128)(2,1)S(1)}, bf16[1024,256]{1,0:T(8,128)(2,1)}, u32[]{:S(2)}) copy-start(bf16[1024,256]{1,0:T(8,128)(2,1)} %rest_11_.1) | copy-start | bytes 1572868
  25.5 9.1 %collective-permute-start.1 = (bf16[16,4736]{1,0:T(8,128)(2,1)S(1)}, bf16[16,4736]{1,0:T(8,128)(2,1)S(1)}, u32[]{:S(2)}, u32[]{:S(2)}) collective-permute-start(bf16[16,4736]{1,0:T(8,128)(2,1)S(1)} %get-tuple-element.40), channel_id=1, source_target_pairs={{0,4},{4,0},{8,12},{12,8},{1,5},{5,1},{9,13},{13,9},{2,6},{6,2},{1... | collective-permute-start | bytes 454664 | tf_op jit(solution)/shard_map/ppermute | solution.py:444
  25.5 5.5 %collective-permute-start.3 = (bf16[16,1024]{1,0:T(8,128)(2,1)S(1)}, bf16[16,1024]{1,0:T(8,128)(2,1)S(1)}, u32[]{:S(2)}, u32[]{:S(2)}) collective-permute-start(bf16[16,1024]{1,0:T(8,128)(2,1)S(1)} %get-tuple-element.43), channel_id=1, source_target_pairs={{0,8},{4,12},{8,0},{12,4},{1,9},{5,13},{9,1},{13,5},{2,10},{6,14},... | collective-permute-start | bytes 98312 | tf_op jit(solution)/shard_map/ppermute | solution.py:444
  28.9 5.7 %collective-permute-start.4 = (bf16[16,1024]{1,0:T(8,128)(2,1)S(1)}, bf16[16,1024]{1,0:T(8,128)(2,1)S(1)}, u32[]{:S(2)}, u32[]{:S(2)}) collective-permute-start(bf16[16,1024]{1,0:T(8,128)(2,1)S(1)} %get-tuple-element.44), channel_id=1, source_target_pairs={{0,12},{4,8},{8,4},{12,0},{1,13},{5,9},{9,5},{13,1},{2,14},{6,10},... | collective-permute-start | bytes 98312 | tf_op jit(solution)/shard_map/ppermute | solution.py:444
  35.7 4.5 %collective-permute-start.5 = (bf16[144,128]{1,0:T(8,128)(2,1)S(1)}, bf16[144,128]{1,0:T(8,128)(2,1)S(1)}, u32[]{:S(2)}, u32[]{:S(2)}) collective-permute-start(bf16[144,128]{1,0:T(8,128)(2,1)S(1)} %get-tuple-element.48), channel_id=1, source_target_pairs={{0,4},{4,0},{8,12},{12,8},{1,5},{5,1},{9,13},{13,9},{2,6},{6,2},{1... | collective-permute-start | bytes 110600 | tf_op jit(solution)/shard_map/ppermute | solution.py:444
  35.7 4.9 %collective-permute-start.6 = (bf16[144,128]{1,0:T(8,128)(2,1)S(1)}, bf16[144,128]{1,0:T(8,128)(2,1)S(1)}, u32[]{:S(2)}, u32[]{:S(2)}) collective-permute-start(bf16[144,128]{1,0:T(8,128)(2,1)S(1)} %get-tuple-element.49), channel_id=1, source_target_pairs={{0,8},{4,12},{8,0},{12,4},{1,9},{5,13},{9,1},{13,5},{2,10},{6,14},... | collective-permute-start | bytes 110600 | tf_op jit(solution)/shard_map/ppermute | solution.py:444
  37.3 5.8 %collective-permute-start.7 = (bf16[144,128]{1,0:T(8,128)(2,1)S(1)}, bf16[144,128]{1,0:T(8,128)(2,1)S(1)}, u32[]{:S(2)}, u32[]{:S(2)}) collective-permute-start(bf16[144,128]{1,0:T(8,128)(2,1)S(1)} %get-tuple-element.50), channel_id=1, source_target_pairs={{0,12},{4,8},{8,4},{12,0},{1,13},{5,9},{9,5},{13,1},{2,14},{6,10},... | collective-permute-start | bytes 110600 | tf_op jit(solution)/shard_map/ppermute | solution.py:444

commit v5 on v4

--- a/solution.py
+++ b/solution.py
@@ -13,7 +13,7 @@
 THETA = 500000.0
 LOW = -1e30
 WINDOW = 8
-DEEP = 512
+DEEP = 1024
 LEVELS = 16
 
 
@@ -176,15 +176,18 @@
                 lax.fori_loop(0, total, one, 0)
 
     def use_query(t):
-        at = pl.multiple_of(t * deep, deep)
-        x = x_buf[:, pl.ds(at, deep)].astype(jnp.float32)
-        gains = g_buf[pl.ds(at, deep)].astype(jnp.float32).reshape(1, deep)
-        left = (x * gains).astype(jnp.bfloat16)
-        lhs[t] = left
-        squared = x * x
-        for column in range(0, deep, HD):
-            squares[...] += squared[:, column : column + HD]
-        add_products(left, query_buf, t, sums.at[:, 2 * kv_cols : late])
+        short = divides(deep, 512)
+        for part in range(0, deep, short):
+            at = pl.multiple_of(t * deep + part, short)
+            x = x_buf[:, pl.ds(at, short)].astype(jnp.float32)
+            gains = g_buf[pl.ds(at, short)].astype(jnp.float32).reshape(1, short)
+            lhs[t, :, part : part + short] = (x * gains).astype(jnp.bfloat16)
+            squared = x * x
+            total = squared[:, :HD]
+            for column in range(HD, short, HD):
+                total = total + squared[:, column : column + HD]
+            squares[...] += total
+        add_products(lhs[t], query_buf, t, sums.at[:, 2 * kv_cols : late])
         each(choose, pool * per, t)
         each(describe, per, t)
 
@@ -485,7 +488,7 @@
         indices = [send_row.reshape(-1), piece_len.reshape(-1), row_len]
     deep = divides(depth, DEEP)
     count = depth // deep
-    halves = 2 if count % 2 == 0 else 1
+    halves = 1
     widths = [3 * q_cols // 4, q_cols // 4]
 
     def parts(width):
@@ -543,7 +546,15 @@
         name="project_rest",
     )(lhs, pick, operands[-1], first_terms[1])
     first_terms = exchange(first_terms, range(2, pool))
-    first_terms[2], rest_terms = lax.optimization_barrier((first_terms[2], list(rest_terms)))
+    rest_terms = list(rest_terms)
+    early, late = range(2, pool), range(3, pool)
+    got, tied = lax.optimization_barrier(
+        ([first_terms[k] for k in early], [rest_terms[k] for k in late])
+    )
+    for k, part in zip(early, got):
+        first_terms[k] = part
+    for k, part in zip(late, tied):
+        rest_terms[k] = part
     rest_terms = exchange(rest_terms, range(1, pool))
     terms = [first_terms[0], *rest_terms[:2], *first_terms[2:], *rest_terms[2:]]
 

time: 44.5 us -> 44.1 us (level)
  waiting for transfers between devices: 11.3 us -> 7.62 us
  starting transfers between devices: 14.3 us -> 16.3 us
  Pallas kernels: 18.7 us -> 19.9 us
    ppermute x8, waiting for transfers between devices: 11.3 us -> 7.62 us  [exchange(): lax.ppermute(parts[k], 'pool', [(i, i ^ k) for i in range(len(parts))])]
    ppermute x8, starting transfers between devices: 14.3 us -> 16.3 us  [exchange(): lax.ppermute(parts[k], 'pool', [(i, i ^ k) for i in range(len(parts))])]
    pallas_call x1, Pallas kernels: 12.2 us -> 13.2 us  [body(): pl.pallas_call(functools.partial(project_kernel, pool, slots, rows_local)...]
  transfers between devices with their start and end apart: 8 -> 8, of which waited for: 5 -> 4; matrix products, arithmetic and copies ran while one was open for 0% -> 0% of each run, Pallas kernels for 9% -> 10%
where the time goes in v5:
time: 44.1 us; the launch traced here: 43.9 us
  Pallas kernels  19.9 us (45%)
  starting transfers between devices  16.3 us (37%)
  waiting for transfers between devices  7.62 us (17%)
    ppermute x8, starting transfers between devices, exchange(): lax.ppermute(parts[k], 'pool', [(i, i ^ k) for i in range(len(parts))])  16.3 us
    pallas_call x1, Pallas kernels, body(): pl.pallas_call(functools.partial(project_kernel, pool, slots, rows_local)...  13.2 us
    ppermute x8, waiting for transfers between devices, exchange(): lax.ppermute(parts[k], 'pool', [(i, i ^ k) for i in range(len(parts))])  7.62 us
    pallas_call x1, Pallas kernels, body(): pl.pallas_call(functools.partial(project_rest_kernel, pool, widths[0]), o...  4.26 us
    pallas_call x1, Pallas kernels, body(): pl.pallas_call(functools.partial(merge_kernel, pool, slots, rows_local, q...  1.33 us
    pallas_call x1, Pallas kernels, body(): pl.pallas_call(functools.partial(attend_kernel, pool, slots, seg, width_d...  1.07 us
  transfers between devices with their start and end apart: 8, of which 4 were waited for; matrix products, arithmetic and copies ran while one was open for 0% of the time, Pallas kernels for 10%

profile of v5, /device:TPU:0, one launch (start us, length us, event | category | flops | bytes accessed | tf_op | source)
XLA Modules:
  0.0 43.9 jit_solution(17362691940741967009)
XLA Ops:
  0.0 13.2 %project.1 = (bf16[16,3712]{1,0:T(8,128)(2,1)S(1)}, bf16[16,3712]{1,0:T(8,128)(2,1)S(1)}, bf16[16,3712]{1,0:T(8,128)(2,1)S(1)}, bf16[16,3712]{1,0:T(8,128)(2,1)S...) custom-call(s32[1]{0:T(128)} %bitcast.me_ref, ...), custom_call_target="tpu_custom_call" | custom-call | tf_op jit(solution)/shard_map/project/pallas_call | solution.py:498
  13.3 4.1 %collective-permute-start.1 = (bf16[16,3712]{1,0:T(8,128)(2,1)S(1)}, bf16[16,3712]{1,0:T(8,128)(2,1)S(1)}, u32[]{:S(2)}, u32[]{:S(2)}) collective-permute-start(bf16[16,3712]{1,0:T(8,128)(2,1)S(1)} %get-tuple-element.34), channel_id=1, source_target_pairs={{0,8},{4,12},{8,0},{12,4},{1,9},{5,13},{9,1},{13,5},{2,10},{6,14},... | collective-permute-start | bytes 356360 | tf_op jit(solution)/shard_map/ppermute | solution.py:447
  17.4 1.3 %collective-permute-start.2 = (bf16[16,3712]{1,0:T(8,128)(2,1)S(1)}, bf16[16,3712]{1,0:T(8,128)(2,1)S(1)}, u32[]{:S(2)}, u32[]{:S(2)}) collective-permute-start(bf16[16,3712]{1,0:T(8,128)(2,1)S(1)} %get-tuple-element.35), channel_id=1, source_target_pairs={{0,12},{4,8},{8,4},{12,0},{1,13},{5,9},{9,5},{13,1},{2,14},{6,10},... | collective-permute-start | bytes 356360 | tf_op jit(solution)/shard_map/ppermute | solution.py:447
  18.7 0.0 copy-start.2
  18.7 0.0 copy-start.3
  18.7 0.0 copy-start
  18.7 0.0 copy-start.1
  18.7 4.3 %project_rest.1 = (bf16[16,1024]{1,0:T(8,128)(2,1)S(1)}, bf16[16,4736]{1,0:T(8,128)(2,1)S(1)}, bf16[16,1024]{1,0:T(8,128)(2,1)S(1)}, bf16[16,1024]{1,0:T(8,128)(2,1)S(1)}) custom-call(bf16[4,64,1024]{2,1,0:T(8,128)(2,1)S(1)} %get-tuple-element.29.lhs, f32[64,64]{1,0:T(8,128)S(1)} %get-tuple-element.30.pick, bf16[4096,4096]{1,0:T(8,128)(2,1)} %w_query.1, ...), custom_call_target="tpu_custom_call" | custom-call | flops 536870912 | bytes 8912896 | tf_op jit(solution)/shard_map/project_rest/pallas_call | solution.py:530
  23.0 0.3 collective-permute-start
  23.3 2.8 %collective-permute-start.3 = (bf16[16,1024]{1,0:T(8,128)(2,1)S(1)}, bf16[16,1024]{1,0:T(8,128)(2,1)S(1)}, u32[]{:S(2)}, u32[]{:S(2)}) collective-permute-start(bf16[16,1024]{1,0:T(8,128)(2,1)S(1)} %get-tuple-element.39), channel_id=1, source_target_pairs={{0,8},{4,12},{8,0},{12,4},{1,9},{5,13},{9,1},{13,5},{2,10},{6,14},... | collective-permute-start | bytes 98312 | tf_op jit(solution)/shard_map/ppermute | solution.py:447
  26.1 0.4 collective-permute-done.1.rest_3_
  26.5 0.0 collective-permute-done.2.rest_4_
  26.5 2.8 %collective-permute-start.4 = (bf16[16,1024]{1,0:T(8,128)(2,1)S(1)}, bf16[16,1024]{1,0:T(8,128)(2,1)S(1)}, u32[]{:S(2)}, u32[]{:S(2)}) collective-permute-start(bf16[16,1024]{1,0:T(8,128)(2,1)S(1)} %get-tuple-element.40), channel_id=1, source_target_pairs={{0,12},{4,8},{8,4},{12,0},{1,13},{5,9},{9,5},{13,1},{2,14},{6,10},... | collective-permute-start | bytes 98312 | tf_op jit(solution)/shard_map/ppermute | solution.py:447
  29.3 0.0 copy-done.2
  29.3 0.0 copy-done.3
  29.4 0.1 sine_multiply_fusion
  29.4 0.0 collective-permute-done.3.rest_5_
  29.4 2.8 %collective-permute-done.4.rest_6_ = bf16[16,1024]{1,0:T(8,128)(2,1)S(1)} collective-permute-done((bf16[16,1024]{1,0:T(8,128)(2,1)S(1)}, bf16[16,1024]{1,0:T(8,128)(2,1)S(1)}, u32[]{:S(2)}, u32[]{:S(2)}) %collective-permute-start.4) | collective-permute-done | bytes 32800 | tf_op jit(solution)/shard_map/ppermute | solution.py:447
  32.2 0.0 collective-permute-done.rest_2_
  32.2 0.0 copy-done
  32.2 0.0 copy-done.1
  32.2 1.1 %attend.1 = (bf16[144,128]{1,0:T(8,128)(2,1)S(1)}, bf16[144,128]{1,0:T(8,128)(2,1)S(1)}, bf16[144,128]{1,0:T(8,128)(2,1)S(1)}, bf16[144,128]{1,0:T(8,128)(2,1)S(1)}) custom-call(s32[1]{0:T(128)} %bitcast.me_ref, bf16[16,3712]{1,0:T(8,128)(2,1)S(1)} %get-tuple-element.28.rest_0_, bf16[16,1024]{1,0:T(8,128)(2,1)S(1)} %get-tuple-element.32.rest_1_, ...), custom_call_target="tpu_custom_call" | custom-call | tf_op jit(solution)/shard_map/attend/pallas_call | solution.py:567
  33.3 2.0 %collective-permute-start.5 = (bf16[144,128]{1,0:T(8,128)(2,1)S(1)}, bf16[144,128]{1,0:T(8,128)(2,1)S(1)}, u32[]{:S(2)}, u32[]{:S(2)}) collective-permute-start(bf16[144,128]{1,0:T(8,128)(2,1)S(1)} %get-tuple-element.44), channel_id=1, source_target_pairs={{0,4},{4,0},{8,12},{12,8},{1,5},{5,1},{9,13},{13,9},{2,6},{6,2},{1... | collective-permute-start | bytes 110600 | tf_op jit(solution)/shard_map/ppermute | solution.py:447
  35.3 1.5 %collective-permute-start.6 = (bf16[144,128]{1,0:T(8,128)(2,1)S(1)}, bf16[144,128]{1,0:T(8,128)(2,1)S(1)}, u32[]{:S(2)}, u32[]{:S(2)}) collective-permute-start(bf16[144,128]{1,0:T(8,128)(2,1)S(1)} %get-tuple-element.45), channel_id=1, source_target_pairs={{0,8},{4,12},{8,0},{12,4},{1,9},{5,13},{9,1},{13,5},{2,10},{6,14},... | collective-permute-start | bytes 110600 | tf_op jit(solution)/shard_map/ppermute | solution.py:447
  36.8 1.4 %collective-permute-start.7 = (bf16[144,128]{1,0:T(8,128)(2,1)S(1)}, bf16[144,128]{1,0:T(8,128)(2,1)S(1)}, u32[]{:S(2)}, u32[]{:S(2)}) collective-permute-start(bf16[144,128]{1,0:T(8,128)(2,1)S(1)} %get-tuple-element.46), channel_id=1, source_target_pairs={{0,12},{4,8},{8,4},{12,0},{1,13},{5,9},{9,5},{13,1},{2,14},{6,10},... | collective-permute-start | bytes 110600 | tf_op jit(solution)/shard_map/ppermute | solution.py:447
  38.2 0.0 collective-permute-done.5.rest_1_
  38.2 2.3 %collective-permute-done.6.rest_2_ = bf16[144,128]{1,0:T(8,128)(2,1)S(1)} collective-permute-done((bf16[144,128]{1,0:T(8,128)(2,1)S(1)}, bf16[144,128]{1,0:T(8,128)(2,1)S(1)}, u32[]{:S(2)}, u32[]{:S(2)}) %collective-permute-start.6) | collective-permute-done | bytes 36896 | tf_op jit(solution)/shard_map/ppermute | solution.py:447
  40.5 2.1 %collective-permute-done.7.rest_3_ = bf16[144,128]{1,0:T(8,128)(2,1)S(1)} collective-permute-done((bf16[144,128]{1,0:T(8,128)(2,1)S(1)}, bf16[144,128]{1,0:T(8,128)(2,1)S(1)}, u32[]{:S(2)}, u32[]{:S(2)}) %collective-permute-start.7) | collective-permute-done | bytes 36896 | tf_op jit(solution)/shard_map/ppermute | solution.py:447
  42.6 1.3 %merge.1 = bf16[16,4096]{1,0:T(8,128)(2,1)} custom-call(s32[1,128]{1,0:T(1,128)S(1)} %get-tuple-element.26.slots_ref, s32[4,128]{1,0:T(4,128)S(1)} %get-tuple-element.27.rows_ref, bf16[144,128]{1,0:T(8,128)(2,1)S(1)} %get-tuple-element.43.rest_0_, bf16[144,128]{1,0:T(8,128)(2,1)S(1)} %collective-permute-done.5.rest_1_, ...), custom_call_target="tpu_custom_call" | custom-call | tf_op jit(solution)/shard_map/merge/pallas_call | solution.py:579
Async XLA Ops:
  13.3 13.3 %collective-permute-start.1 = (bf16[16,3712]{1,0:T(8,128)(2,1)S(1)}, bf16[16,3712]{1,0:T(8,128)(2,1)S(1)}, u32[]{:S(2)}, u32[]{:S(2)}) collective-permute-start(bf16[16,3712]{1,0:T(8,128)(2,1)S(1)} %get-tuple-element.34), channel_id=1, source_target_pairs={{0,8},{4,12},{8,0},{12,4},{1,9},{5,13},{9,1},{13,5},{2,10},{6,14},... | collective-permute-start | bytes 356360 | tf_op jit(solution)/shard_map/ppermute | solution.py:447
  17.4 9.2 %collective-permute-start.2 = (bf16[16,3712]{1,0:T(8,128)(2,1)S(1)}, bf16[16,3712]{1,0:T(8,128)(2,1)S(1)}, u32[]{:S(2)}, u32[]{:S(2)}) collective-permute-start(bf16[16,3712]{1,0:T(8,128)(2,1)S(1)} %get-tuple-element.35), channel_id=1, source_target_pairs={{0,12},{4,8},{8,4},{12,0},{1,13},{5,9},{9,5},{13,1},{2,14},{6,10},... | collective-permute-start | bytes 356360 | tf_op jit(solution)/shard_map/ppermute | solution.py:447
  18.7 10.6 %copy-start.2 = (f32[128]{0:T(128)S(1)}, f32[128]{0:T(128)}, u32[]{:S(2)}) copy-start(f32[128]{0:T(128)} %constant.12) | copy-start | bytes 1540
  18.7 10.6 %copy-start.3 = (f32[128]{0:T(128)S(1)}, f32[128]{0:T(128)}, u32[]{:S(2)}) copy-start(f32[128]{0:T(128)} %constant.13) | copy-start | bytes 1540
  18.7 13.5 %copy-start = (bf16[1024,256]{1,0:T(8,128)(2,1)S(1)}, bf16[1024,256]{1,0:T(8,128)(2,1)}, u32[]{:S(2)}) copy-start(bf16[1024,256]{1,0:T(8,128)(2,1)} %rest_10_.1) | copy-start | bytes 1572868
  18.7 13.5 %copy-start.1 = (bf16[1024,256]{1,0:T(8,128)(2,1)S(1)}, bf16[1024,256]{1,0:T(8,128)(2,1)}, u32[]{:S(2)}) copy-start(bf16[1024,256]{1,0:T(8,128)(2,1)} %rest_11_.1) | copy-start | bytes 1572868
  23.0 9.3 %collective-permute-start = (bf16[16,4736]{1,0:T(8,128)(2,1)S(1)}, bf16[16,4736]{1,0:T(8,128)(2,1)S(1)}, u32[]{:S(2)}, u32[]{:S(2)}) collective-permute-start(bf16[16,4736]{1,0:T(8,128)(2,1)S(1)} %get-tuple-element.33), channel_id=1, source_target_pairs={{0,4},{4,0},{8,12},{12,8},{1,5},{5,1},{9,13},{13,9},{2,6},{6,2},{1... | collective-permute-start | bytes 454664 | tf_op jit(solution)/shard_map/ppermute | solution.py:447
  23.3 6.1 %collective-permute-start.3 = (bf16[16,1024]{1,0:T(8,128)(2,1)S(1)}, bf16[16,1024]{1,0:T(8,128)(2,1)S(1)}, u32[]{:S(2)}, u32[]{:S(2)}) collective-permute-start(bf16[16,1024]{1,0:T(8,128)(2,1)S(1)} %get-tuple-element.39), channel_id=1, source_target_pairs={{0,8},{4,12},{8,0},{12,4},{1,9},{5,13},{9,1},{13,5},{2,10},{6,14},... | collective-permute-start | bytes 98312 | tf_op jit(solution)/shard_map/ppermute | solution.py:447
  26.5 5.7 %collective-permute-start.4 = (bf16[16,1024]{1,0:T(8,128)(2,1)S(1)}, bf16[16,1024]{1,0:T(8,128)(2,1)S(1)}, u32[]{:S(2)}, u32[]{:S(2)}) collective-permute-start(bf16[16,1024]{1,0:T(8,128)(2,1)S(1)} %get-tuple-element.40), channel_id=1, source_target_pairs={{0,12},{4,8},{8,4},{12,0},{1,13},{5,9},{9,5},{13,1},{2,14},{6,10},... | collective-permute-start | bytes 98312 | tf_op jit(solution)/shard_map/ppermute | solution.py:447
  33.3 4.9 %collective-permute-start.5 = (bf16[144,128]{1,0:T(8,128)(2,1)S(1)}, bf16[144,128]{1,0:T(8,128)(2,1)S(1)}, u32[]{:S(2)}, u32[]{:S(2)}) collective-permute-start(bf16[144,128]{1,0:T(8,128)(2,1)S(1)} %get-tuple-element.44), channel_id=1, source_target_pairs={{0,4},{4,0},{8,12},{12,8},{1,5},{5,1},{9,13},{13,9},{2,6},{6,2},{1... | collective-permute-start | bytes 110600 | tf_op jit(solution)/shard_map/ppermute | solution.py:447
  35.3 5.2 %collective-permute-start.6 = (bf16[144,128]{1,0:T(8,128)(2,1)S(1)}, bf16[144,128]{1,0:T(8,128)(2,1)S(1)}, u32[]{:S(2)}, u32[]{:S(2)}) collective-permute-start(bf16[144,128]{1,0:T(8,128)(2,1)S(1)} %get-tuple-element.45), channel_id=1, source_target_pairs={{0,8},{4,12},{8,0},{12,4},{1,9},{5,13},{9,1},{13,5},{2,10},{6,14},... | collective-permute-start | bytes 110600 | tf_op jit(solution)/shard_map/ppermute | solution.py:447
  36.8 5.8 %collective-permute-start.7 = (bf16[144,128]{1,0:T(8,128)(2,1)S(1)}, bf16[144,128]{1,0:T(8,128)(2,1)S(1)}, u32[]{:S(2)}, u32[]{:S(2)}) collective-permute-start(bf16[144,128]{1,0:T(8,128)(2,1)S(1)} %get-tuple-element.46), channel_id=1, source_target_pairs={{0,12},{4,8},{8,4},{12,0},{1,13},{5,9},{9,5},{13,1},{2,14},{6,10},... | collective-permute-start | bytes 110600 | tf_op jit(solution)/shard_map/ppermute | solution.py:447

commit v6 on v5

--- a/solution.py
+++ b/solution.py
@@ -12,8 +12,8 @@
 EPS = 1e-05
 THETA = 500000.0
 LOW = -1e30
-WINDOW = 8
-DEEP = 1024
+WINDOW = 3
+DEEP = 512
 LEVELS = 16
 
 
@@ -34,7 +34,7 @@
     return lax.bitwise_xor(me, k)
 
 
-def project_blocks(plan, sems):
+def project_blocks(plan, sems, window):
     blocks = [(n, t) for n, entry in enumerate(plan) for t in range(entry[2].shape[0])]
 
     def copy(n, t, i):
@@ -46,15 +46,13 @@
         )
 
     def begin():
-        for i in range(min(WINDOW, len(blocks))):
+        for i in range(min(window, len(blocks))):
             copy(*blocks[i], i).start()
 
-    def finish(between=None):
+    def finish():
         first = 0
         for n, (_, _, buf, use) in enumerate(plan):
             count = buf.shape[0]
-            if n == len(plan) - 1 and between is not None:
-                between()
 
             def work(t, carry, n=n, first=first, use=use):
                 copy(n, t, first + t).wait()
@@ -63,7 +61,7 @@
 
             t = 0
             while t < count:
-                ahead = first + t + WINDOW
+                ahead = first + t + window
                 if ahead < len(blocks):
                     m, u = blocks[ahead]
                     run = 1
@@ -112,11 +110,11 @@
 
 
 def project_kernel(pool, slots, rows_local, me_ref, send, lens, row_len, hidden, gain, *rest):
-    w_key, w_value, w_query, *rest = rest
+    w_query, *rest = rest
     outs, rest = rest[:pool], rest[pool:]
     lhs, pick, positions, marks, home_rows, home_slots, *rest = rest
     send_buf, lens_buf, row_len_buf, x_buf, g_buf, *rest = rest
-    query_buf, key_buf, value_buf, late_buf, sums, squares, in_sem, sems = rest
+    query_buf, sums, squares, in_sem, sems = rest
     per = pool * slots
     n_rows, depth = x_buf.shape
     count, deep, _ = query_buf.shape
@@ -187,40 +185,11 @@
             for column in range(HD, short, HD):
                 total = total + squared[:, column : column + HD]
             squares[...] += total
-        add_products(lhs[t], query_buf, t, sums.at[:, 2 * kv_cols : late])
+        add_products(lhs[t], query_buf, t, sums)
         each(choose, pool * per, t)
         each(describe, per, t)
 
-    def use_late(t):
-        add_products(lhs[t], late_buf, t, sums.at[:, late:])
-
-    kv_cols = w_key.shape[1]
-    late = 2 * kv_cols + query_buf.shape[2]
-
-    def use_narrow(buf, at):
-        halves, tall, _ = buf.shape
-
-        def use(t):
-            part = 0.0
-            for k in range(tall // deep):
-                part = part + jnp.dot(
-                    lhs[t * (tall // deep) + k],
-                    buf[t, k * deep : (k + 1) * deep, :],
-                    preferred_element_type=jnp.float32,
-                )
-            sums[:, at : at + kv_cols] += part
-
-        return use
-
-    begin, finish = project_blocks(
-        [
-            (w_query, 0, query_buf, use_query),
-            (w_key, 0, key_buf, use_narrow(key_buf, 0)),
-            (w_value, 0, value_buf, use_narrow(value_buf, kv_cols)),
-            (w_query, query_buf.shape[2], late_buf, use_late),
-        ],
-        sems,
-    )
+    begin, finish = project_blocks([(w_query, 0, query_buf, use_query)], sems, WINDOW)
     inputs = [
         pltpu.make_async_copy(source, target, in_sem.at[i])
         for i, (source, target) in enumerate(
@@ -243,30 +212,35 @@
     home_slots[...] = jnp.full(home_slots.shape, -1, jnp.int32)
     for one in inputs:
         one.wait()
-
-    def between():
-        power = jnp.sum(squares[...], axis=1, keepdims=True)
-        at = lax.broadcasted_iota(jnp.int32, (n_rows, HD), 1)
-        a, b, c = split3(power)
-        squares[...] = jnp.where(at == 0, a, jnp.where(at == 1, b, jnp.where(at == 2, c, 0.0)))
-        chosen = pick[...].astype(jnp.bfloat16)
-        spread(chosen, squares, outs, sums.shape[1])
-        spread(chosen, sums.at[:, :late], outs, 0)
-
-    finish(between)
-    spread(pick[...].astype(jnp.bfloat16), sums.at[:, late:], outs, late)
-
-
-def project_rest_kernel(pool, column, lhs, pick, w_query, near, *rest):
+    finish()
+    power = jnp.sum(squares[...], axis=1, keepdims=True)
+    at = lax.broadcasted_iota(jnp.int32, (n_rows, HD), 1)
+    a, b, c = split3(power)
+    squares[...] = jnp.where(at == 0, a, jnp.where(at == 1, b, jnp.where(at == 2, c, 0.0)))
+    chosen = pick[...].astype(jnp.bfloat16)
+    spread(chosen, squares, outs, sums.shape[1])
+    spread(chosen, sums, outs, 0)
+
+
+def project_rest_kernel(pool, column, lhs, pick, w_key, w_value, w_query, near, *rest):
     outs, (query_buf, sums, sems) = rest[:pool], rest[pool:]
     done = near.shape[1]
+    count, _, deep = lhs.shape
+    kv_cols = w_key.shape[1]
 
     def use(t):
-        add_products(lhs[t], query_buf, t, sums)
-
-    begin, finish = project_blocks([(w_query, column, query_buf, use)], sems)
+        add_products(lhs[t], query_buf, t, sums.at[:, 2 * kv_cols :])
+
+    begin, finish = project_blocks([(w_query, column, query_buf, use)], sems, count)
     begin()
-    sums[...] = jnp.zeros(sums.shape, jnp.float32)
+    for n, w in enumerate((w_key, w_value)):
+        part = 0.0
+        for k in range(count):
+            part = part + jnp.dot(
+                lhs[k], w[k * deep : (k + 1) * deep, :], preferred_element_type=jnp.float32
+            )
+        sums[:, n * kv_cols : (n + 1) * kv_cols] = part
+    sums[:, 2 * kv_cols :] = jnp.zeros((sums.shape[0], sums.shape[1] - 2 * kv_cols), jnp.float32)
     outs[1][:, :done] = near[...]
     finish()
     outs = [out.at[:, done:] if k == 1 else out for k, out in enumerate(outs)]
@@ -297,7 +271,8 @@
             got = got + part[:, at : at + HD].astype(jnp.float32)
         return got
 
-    heads = [at for at in range(2 * kv_heads * HD, cols, HD) if at != first_cols - HD]
+    late = first_cols + 2 * kv_heads * HD
+    heads = [*range(0, first_cols - HD, HD), *range(late, cols, HD)]
     power = jnp.sum(total(first_cols - HD), axis=1, keepdims=True)
     factor = lax.rsqrt(power * (1.0 / width_d) + EPS)
     cosines, sines = cos[...], sin[...]
@@ -310,9 +285,9 @@
 
     for i in range(q_heads):
         q_buf[i * per : (i + 1) * per, :] = rotated(total(heads[i]) * factor)
-    keys_own = [rotated(total(g * HD) * factor) for g in range(kv_heads)]
+    keys_own = [rotated(total(first_cols + g * HD) * factor) for g in range(kv_heads)]
     values_own = [
-        rounded(total((kv_heads + g) * HD) * factor) for g in range(kv_heads)
+        rounded(total(first_cols + (kv_heads + g) * HD) * factor) for g in range(kv_heads)
     ]
 
     me = me_ref[0]
@@ -387,8 +362,8 @@
         outs[home][slots * q_heads :, :] = block.astype(jnp.bfloat16)
 
 
-def merge_kernel(pool, slots, rows_local, q_heads, kv_heads, slots_ref, rows_ref, *rest):
-    found, (out, scaled) = rest[:pool], rest[pool:]
+def merge_kernel(pool, slots, rows_local, q_heads, kv_heads, slots_ref, rows_ref, own, *rest):
+    found, (out, scaled) = [own, rest[pool - 2], *rest[: pool - 2]], rest[pool - 1 :]
     per = pool * slots
     group = q_heads // kv_heads
     block = slots * q_heads
@@ -488,17 +463,16 @@
         indices = [send_row.reshape(-1), piece_len.reshape(-1), row_len]
     deep = divides(depth, DEEP)
     count = depth // deep
-    halves = 1
     widths = [3 * q_cols // 4, q_cols // 4]
 
     def parts(width):
         return [jax.ShapeDtypeStruct((per, width), jnp.bfloat16)] * pool
 
-    operands = [in_hbm(x) for x in (*indices, hidden_in, norm_gain, w_key, w_value, w_query)]
+    operands = [in_hbm(x) for x in (*indices, hidden_in, norm_gain, w_query)]
     *first_terms, lhs, pick, positions, marks, home_rows, home_slots = pl.pallas_call(
         functools.partial(project_kernel, pool, slots, rows_local),
         out_shape=[
-            *parts(2 * kv_cols + widths[0] + HD),
+            *parts(widths[0] + HD),
             jax.ShapeDtypeStruct((count, n_rows, deep), jnp.bfloat16),
             jax.ShapeDtypeStruct((pool * per, n_rows), jnp.float32),
             jax.ShapeDtypeStruct((per, HD), jnp.float32),
@@ -506,45 +480,43 @@
             jax.ShapeDtypeStruct((pool, HD), jnp.int32),
             jax.ShapeDtypeStruct((1, HD), jnp.int32),
         ],
-        in_specs=[SMEM] + [HBM] * 8,
+        in_specs=[SMEM] + [HBM] * 6,
         out_specs=[VMEM] * (pool + 6),
         scratch_shapes=[
             *(pltpu.SMEM(x.shape, jnp.int32) for x in indices),
             pltpu.VMEM((n_rows, depth), jnp.bfloat16),
             pltpu.VMEM((depth,), jnp.bfloat16),
-            pltpu.VMEM((count, deep, widths[0] // 2), jnp.bfloat16),
-            pltpu.VMEM((halves, depth // halves, kv_cols), jnp.bfloat16),
-            pltpu.VMEM((halves, depth // halves, kv_cols), jnp.bfloat16),
-            pltpu.VMEM((count, deep, widths[0] // 2), jnp.bfloat16),
-            pltpu.VMEM((n_rows, 2 * kv_cols + widths[0]), jnp.float32),
+            pltpu.VMEM((count, deep, widths[0]), jnp.bfloat16),
+            pltpu.VMEM((n_rows, widths[0]), jnp.float32),
             pltpu.VMEM((n_rows, HD), jnp.float32),
             pltpu.SemaphoreType.DMA((5,)),
-            pltpu.SemaphoreType.DMA((2 * count + 2 * halves,)),
+            pltpu.SemaphoreType.DMA((count,)),
         ],
         compiler_params=pltpu.CompilerParams(vmem_limit_bytes=46 * 2**20),
         name="project",
     )(me[None], *operands)
-    first_cols = 2 * kv_cols + widths[0] + HD
-    rest_shapes = parts(widths[1])
-    rest_shapes[1] = jax.ShapeDtypeStruct((per, first_cols + widths[1]), jnp.bfloat16)
+    first_terms, kv_weights = lax.optimization_barrier((list(first_terms), (w_key, w_value)))
+    rest_cols = 2 * kv_cols + widths[1]
+    rest_shapes = parts(rest_cols)
+    rest_shapes[1] = jax.ShapeDtypeStruct((per, widths[0] + HD + rest_cols), jnp.bfloat16)
     rest_terms = pl.pallas_call(
         functools.partial(project_rest_kernel, pool, widths[0]),
         out_shape=rest_shapes,
-        in_specs=[VMEM, VMEM, HBM, VMEM],
+        in_specs=[VMEM, VMEM, VMEM, VMEM, HBM, VMEM],
         out_specs=[VMEM] * pool,
         scratch_shapes=[
             pltpu.VMEM((count, deep, widths[1]), jnp.bfloat16),
-            pltpu.VMEM((n_rows, widths[1]), jnp.float32),
+            pltpu.VMEM((n_rows, rest_cols), jnp.float32),
             pltpu.SemaphoreType.DMA((count,)),
         ],
         compiler_params=pltpu.CompilerParams(vmem_limit_bytes=40 * 2**20),
         cost_estimate=pl.CostEstimate(
-            flops=2 * n_rows * depth * widths[1],
-            bytes_accessed=2 * depth * (widths[1] + n_rows),
+            flops=2 * n_rows * depth * rest_cols,
+            bytes_accessed=2 * depth * (rest_cols + n_rows),
             transcendentals=0,
         ),
         name="project_rest",
-    )(lhs, pick, operands[-1], first_terms[1])
+    )(lhs, pick, *kv_weights, operands[-1], first_terms[1])
     first_terms = exchange(first_terms, range(2, pool))
     rest_terms = list(rest_terms)
     early, late = range(2, pool), range(3, pool)
@@ -586,7 +558,7 @@
         ],
         compiler_params=pltpu.CompilerParams(vmem_limit_bytes=24 * 2**20),
         name="merge",
-    )(home_slots, home_rows, *found)
+    )(home_slots, home_rows, found[0], *found[2:], found[1])
 
 
 def solution(mesh):

time: 44.1 us -> 40 us (0.907)
  Pallas kernels: 19.9 us -> 17 us
  starting transfers between devices: 16.3 us -> 14.2 us
  waiting for transfers between devices: 7.62 us -> 8.55 us
    pallas_call x1, Pallas kernels: 13.2 us -> 10.2 us  [body(): pl.pallas_call(functools.partial(project_kernel, pool, slots, rows_local)...]
    ppermute x8, starting transfers between devices: 16.3 us -> 14.2 us  [exchange(): lax.ppermute(parts[k], 'pool', [(i, i ^ k) for i in range(len(parts))])]
    ppermute x8, waiting for transfers between devices: 7.62 us -> 8.55 us  [exchange(): lax.ppermute(parts[k], 'pool', [(i, i ^ k) for i in range(len(parts))])]
  transfers between devices with their start and end apart: 8 -> 8, of which waited for: 4 -> 4; matrix products, arithmetic and copies ran while one was open for 0% -> 0% of each run, Pallas kernels for 10% -> 11%
where the time goes in v6:
time: 40 us; the launch traced here: 39.9 us
  Pallas kernels  17 us (42%)
  starting transfers between devices  14.2 us (36%)
  waiting for transfers between devices  8.55 us (21%)
    ppermute x8, starting transfers between devices, exchange(): lax.ppermute(parts[k], 'pool', [(i, i ^ k) for i in range(len(parts))])  14.2 us
    pallas_call x1, Pallas kernels, body(): pl.pallas_call(functools.partial(project_kernel, pool, slots, rows_local)...  10.2 us
    ppermute x8, waiting for transfers between devices, exchange(): lax.ppermute(parts[k], 'pool', [(i, i ^ k) for i in range(len(parts))])  8.55 us
    pallas_call x1, Pallas kernels, body(): pl.pallas_call(functools.partial(project_rest_kernel, pool, widths[0]), o...  4.44 us
    pallas_call x1, Pallas kernels, body(): pl.pallas_call(functools.partial(merge_kernel, pool, slots, rows_local, q...  1.33 us
    pallas_call x1, Pallas kernels, body(): pl.pallas_call(functools.partial(attend_kernel, pool, slots, seg, width_d...  1.06 us
  transfers between devices with their start and end apart: 8, of which 4 were waited for; matrix products, arithmetic and copies ran while one was open for 0% of the time, Pallas kernels for 11%

profile of v6, /device:TPU:0, one launch (start us, length us, event | category | flops | bytes accessed | tf_op | source)
XLA Modules:
  0.0 39.9 jit_solution(1226286623320275994)
XLA Ops:
  0.0 0.0 copy-start
  0.0 0.0 copy-start.1
  0.0 10.2 %project.1 = (bf16[16,3200]{1,0:T(8,128)(2,1)S(1)}, bf16[16,3200]{1,0:T(8,128)(2,1)S(1)}, bf16[16,3200]{1,0:T(8,128)(2,1)S(1)}, bf16[16,3200]{1,0:T(8,128)(2,1)S...) custom-call(s32[1]{0:T(128)} %bitcast.me_ref, ...), custom_call_target="tpu_custom_call" | custom-call | tf_op jit(solution)/shard_map/project/pallas_call | solution.py:472
  10.2 4.1 %collective-permute-start.1 = (bf16[16,3200]{1,0:T(8,128)(2,1)S(1)}, bf16[16,3200]{1,0:T(8,128)(2,1)S(1)}, u32[]{:S(2)}, u32[]{:S(2)}) collective-permute-start(bf16[16,3200]{1,0:T(8,128)(2,1)S(1)} %get-tuple-element.46), channel_id=1, source_target_pairs={{0,8},{4,12},{8,0},{12,4},{1,9},{5,13},{9,1},{13,5},{2,10},{6,14},... | collective-permute-start | bytes 307208 | tf_op jit(solution)/shard_map/ppermute | solution.py:422
  14.3 1.4 %collective-permute-start.2 = (bf16[16,3200]{1,0:T(8,128)(2,1)S(1)}, bf16[16,3200]{1,0:T(8,128)(2,1)S(1)}, u32[]{:S(2)}, u32[]{:S(2)}) collective-permute-start(bf16[16,3200]{1,0:T(8,128)(2,1)S(1)} %get-tuple-element.47), channel_id=1, source_target_pairs={{0,12},{4,8},{8,4},{12,0},{1,13},{5,9},{9,5},{13,1},{2,14},{6,10},... | collective-permute-start | bytes 307208 | tf_op jit(solution)/shard_map/ppermute | solution.py:422
  15.6 0.0 copy-done
  15.6 0.0 copy-done.1
  15.6 0.0 copy-start.4
  15.6 0.0 copy-start.5
  15.7 0.0 copy-start.2
  15.7 0.0 copy-start.3
  15.7 4.4 %project_rest.1 = (bf16[16,1536]{1,0:T(8,128)(2,1)S(1)}, bf16[16,4736]{1,0:T(8,128)(2,1)S(1)}, bf16[16,1536]{1,0:T(8,128)(2,1)S(1)}, bf16[16,1536]{1,0:T(8,128)(2,1)S(1)}) custom-call(bf16[8,64,512]{2,1,0:T(8,128)(2,1)S(1)} %get-tuple-element.39.lhs, f32[64,64]{1,0:T(8,128)S(1)} %get-tuple-element.40.pick, bf16[4096,256]{1,0:T(8,128)(2,1)S(1)} %copy-done, ...), custom_call_target="tpu_custom_call" | custom-call | flops 805306368 | bytes 13107200 | tf_op jit(solution)/shard_map/project_rest/pallas_call | solution.py:502
  20.1 1.8 %collective-permute-start.3 = (bf16[16,1536]{1,0:T(8,128)(2,1)S(1)}, bf16[16,1536]{1,0:T(8,128)(2,1)S(1)}, u32[]{:S(2)}, u32[]{:S(2)}) collective-permute-start(bf16[16,1536]{1,0:T(8,128)(2,1)S(1)} %get-tuple-element.51), channel_id=1, source_target_pairs={{0,8},{4,12},{8,0},{12,4},{1,9},{5,13},{9,1},{13,5},{2,10},{6,14},... | collective-permute-start | bytes 147464 | tf_op jit(solution)/shard_map/ppermute | solution.py:422
  21.9 1.3 %collective-permute-start = (bf16[16,4736]{1,0:T(8,128)(2,1)S(1)}, bf16[16,4736]{1,0:T(8,128)(2,1)S(1)}, u32[]{:S(2)}, u32[]{:S(2)}) collective-permute-start(bf16[16,4736]{1,0:T(8,128)(2,1)S(1)} %get-tuple-element.45), channel_id=1, source_target_pairs={{0,4},{4,0},{8,12},{12,8},{1,5},{5,1},{9,13},{13,9},{2,6},{6,2},{1... | collective-permute-start | bytes 454664 | tf_op jit(solution)/shard_map/ppermute | solution.py:422
  23.2 0.0 collective-permute-done.1.rest_3_
  23.2 0.0 collective-permute-done.2.rest_4_
  23.2 2.0 %collective-permute-start.4 = (bf16[16,1536]{1,0:T(8,128)(2,1)S(1)}, bf16[16,1536]{1,0:T(8,128)(2,1)S(1)}, u32[]{:S(2)}, u32[]{:S(2)}) collective-permute-start(bf16[16,1536]{1,0:T(8,128)(2,1)S(1)} %get-tuple-element.52), channel_id=1, source_target_pairs={{0,12},{4,8},{8,4},{12,0},{1,13},{5,9},{9,5},{13,1},{2,14},{6,10},... | collective-permute-start | bytes 147464 | tf_op jit(solution)/shard_map/ppermute | solution.py:422
  25.2 0.0 copy-done.4
  25.2 0.0 copy-done.5
  25.2 0.1 sine_multiply_fusion
  25.2 0.7 %collective-permute-done.3.rest_5_ = bf16[16,1536]{1,0:T(8,128)(2,1)S(1)} collective-permute-done((bf16[16,1536]{1,0:T(8,128)(2,1)S(1)}, bf16[16,1536]{1,0:T(8,128)(2,1)S(1)}, u32[]{:S(2)}, u32[]{:S(2)}) %collective-permute-start.3) | collective-permute-done | bytes 49184 | tf_op jit(solution)/shard_map/ppermute | solution.py:422
  26.0 3.3 %collective-permute-done.4.rest_6_ = bf16[16,1536]{1,0:T(8,128)(2,1)S(1)} collective-permute-done((bf16[16,1536]{1,0:T(8,128)(2,1)S(1)}, bf16[16,1536]{1,0:T(8,128)(2,1)S(1)}, u32[]{:S(2)}, u32[]{:S(2)}) %collective-permute-start.4) | collective-permute-done | bytes 49184 | tf_op jit(solution)/shard_map/ppermute | solution.py:422
  29.2 0.0 collective-permute-done.rest_2_
  29.2 0.0 copy-done.2
  29.2 0.0 copy-done.3
  29.2 1.1 %attend.1 = (bf16[144,128]{1,0:T(8,128)(2,1)S(1)}, bf16[144,128]{1,0:T(8,128)(2,1)S(1)}, bf16[144,128]{1,0:T(8,128)(2,1)S(1)}, bf16[144,128]{1,0:T(8,128)(2,1)S(1)}) custom-call(s32[1]{0:T(128)} %bitcast.me_ref, bf16[16,3200]{1,0:T(8,128)(2,1)S(1)} %get-tuple-element.38.rest_0_, bf16[16,1536]{1,0:T(8,128)(2,1)S(1)} %get-tuple-element.44.rest_1_, ...), custom_call_target="tpu_custom_call" | custom-call | tf_op jit(solution)/shard_map/attend/pallas_call | solution.py:539
  30.3 2.5 %collective-permute-start.5 = (bf16[144,128]{1,0:T(8,128)(2,1)S(1)}, bf16[144,128]{1,0:T(8,128)(2,1)S(1)}, u32[]{:S(2)}, u32[]{:S(2)}) collective-permute-start(bf16[144,128]{1,0:T(8,128)(2,1)S(1)} %get-tuple-element.56), channel_id=1, source_target_pairs={{0,8},{4,12},{8,0},{12,4},{1,9},{5,13},{9,1},{13,5},{2,10},{6,14},... | collective-permute-start | bytes 110600 | tf_op jit(solution)/shard_map/ppermute | solution.py:422
  32.8 1.2 %collective-permute-start.6 = (bf16[144,128]{1,0:T(8,128)(2,1)S(1)}, bf16[144,128]{1,0:T(8,128)(2,1)S(1)}, u32[]{:S(2)}, u32[]{:S(2)}) collective-permute-start(bf16[144,128]{1,0:T(8,128)(2,1)S(1)} %get-tuple-element.57), channel_id=1, source_target_pairs={{0,12},{4,8},{8,4},{12,0},{1,13},{5,9},{9,5},{13,1},{2,14},{6,10},... | collective-permute-start | bytes 110600 | tf_op jit(solution)/shard_map/ppermute | solution.py:422
  34.0 0.0 collective-permute-start.7
  34.0 1.3 %collective-permute-done.5.rest_0_ = bf16[144,128]{1,0:T(8,128)(2,1)S(1)} collective-permute-done((bf16[144,128]{1,0:T(8,128)(2,1)S(1)}, bf16[144,128]{1,0:T(8,128)(2,1)S(1)}, u32[]{:S(2)}, u32[]{:S(2)}) %collective-permute-start.5) | collective-permute-done | bytes 36896 | tf_op jit(solution)/shard_map/ppermute | solution.py:422
  35.2 3.3 %collective-permute-done.6.rest_1_ = bf16[144,128]{1,0:T(8,128)(2,1)S(1)} collective-permute-done((bf16[144,128]{1,0:T(8,128)(2,1)S(1)}, bf16[144,128]{1,0:T(8,128)(2,1)S(1)}, u32[]{:S(2)}, u32[]{:S(2)}) %collective-permute-start.6) | collective-permute-done | bytes 36896 | tf_op jit(solution)/shard_map/ppermute | solution.py:422
  38.5 0.0 collective-permute-done.7.rest_2_
  38.5 1.3 %merge.1 = bf16[16,4096]{1,0:T(8,128)(2,1)} custom-call(s32[1,128]{1,0:T(1,128)S(1)} %get-tuple-element.32.slots_ref, s32[4,128]{1,0:T(4,128)S(1)} %get-tuple-element.33.rows_ref, bf16[144,128]{1,0:T(8,128)(2,1)S(1)} %get-tuple-element.55.own, bf16[144,128]{1,0:T(8,128)(2,1)S(1)} %collective-permute-done.5.rest_0_, ...), custom_call_target="tpu_custom_call" | custom-call | tf_op jit(solution)/shard_map/merge/pallas_call | solution.py:551
Async XLA Ops:
  0.0 15.6 %copy-start = (bf16[4096,256]{1,0:T(8,128)(2,1)S(1)}, bf16[4096,256]{1,0:T(8,128)(2,1)}, u32[]{:S(2)}) copy-start(bf16[4096,256]{1,0:T(8,128)(2,1)} %w_key) | copy-start | bytes 6291460
  0.0 15.6 %copy-start.1 = (bf16[4096,256]{1,0:T(8,128)(2,1)S(1)}, bf16[4096,256]{1,0:T(8,128)(2,1)}, u32[]{:S(2)}) copy-start(bf16[4096,256]{1,0:T(8,128)(2,1)} %w_value) | copy-start | bytes 6291460
  10.2 13.0 %collective-permute-start.1 = (bf16[16,3200]{1,0:T(8,128)(2,1)S(1)}, bf16[16,3200]{1,0:T(8,128)(2,1)S(1)}, u32[]{:S(2)}, u32[]{:S(2)}) collective-permute-start(bf16[16,3200]{1,0:T(8,128)(2,1)S(1)} %get-tuple-element.46), channel_id=1, source_target_pairs={{0,8},{4,12},{8,0},{12,4},{1,9},{5,13},{9,1},{13,5},{2,10},{6,14},... | collective-permute-start | bytes 307208 | tf_op jit(solution)/shard_map/ppermute | solution.py:422
  14.3 8.9 %collective-permute-start.2 = (bf16[16,3200]{1,0:T(8,128)(2,1)S(1)}, bf16[16,3200]{1,0:T(8,128)(2,1)S(1)}, u32[]{:S(2)}, u32[]{:S(2)}) collective-permute-start(bf16[16,3200]{1,0:T(8,128)(2,1)S(1)} %get-tuple-element.47), channel_id=1, source_target_pairs={{0,12},{4,8},{8,4},{12,0},{1,13},{5,9},{9,5},{13,1},{2,14},{6,10},... | collective-permute-start | bytes 307208 | tf_op jit(solution)/shard_map/ppermute | solution.py:422
  15.6 9.6 %copy-start.4 = (f32[128]{0:T(128)S(1)}, f32[128]{0:T(128)}, u32[]{:S(2)}) copy-start(f32[128]{0:T(128)} %constant.13) | copy-start | bytes 1540
  15.6 9.6 %copy-start.5 = (f32[128]{0:T(128)S(1)}, f32[128]{0:T(128)}, u32[]{:S(2)}) copy-start(f32[128]{0:T(128)} %constant.12) | copy-start | bytes 1540
  15.7 13.6 %copy-start.2 = (bf16[1024,256]{1,0:T(8,128)(2,1)S(1)}, bf16[1024,256]{1,0:T(8,128)(2,1)}, u32[]{:S(2)}) copy-start(bf16[1024,256]{1,0:T(8,128)(2,1)} %rest_10_.1) | copy-start | bytes 1572868
  15.7 13.6 %copy-start.3 = (bf16[1024,256]{1,0:T(8,128)(2,1)S(1)}, bf16[1024,256]{1,0:T(8,128)(2,1)}, u32[]{:S(2)}) copy-start(bf16[1024,256]{1,0:T(8,128)(2,1)} %rest_11_.1) | copy-start | bytes 1572868
  20.1 5.8 %collective-permute-start.3 = (bf16[16,1536]{1,0:T(8,128)(2,1)S(1)}, bf16[16,1536]{1,0:T(8,128)(2,1)S(1)}, u32[]{:S(2)}, u32[]{:S(2)}) collective-permute-start(bf16[16,1536]{1,0:T(8,128)(2,1)S(1)} %get-tuple-element.51), channel_id=1, source_target_pairs={{0,8},{4,12},{8,0},{12,4},{1,9},{5,13},{9,1},{13,5},{2,10},{6,14},... | collective-permute-start | bytes 147464 | tf_op jit(solution)/shard_map/ppermute | solution.py:422
  21.9 7.3 %collective-permute-start = (bf16[16,4736]{1,0:T(8,128)(2,1)S(1)}, bf16[16,4736]{1,0:T(8,128)(2,1)S(1)}, u32[]{:S(2)}, u32[]{:S(2)}) collective-permute-start(bf16[16,4736]{1,0:T(8,128)(2,1)S(1)} %get-tuple-element.45), channel_id=1, source_target_pairs={{0,4},{4,0},{8,12},{12,8},{1,5},{5,1},{9,13},{13,9},{2,6},{6,2},{1... | collective-permute-start | bytes 454664 | tf_op jit(solution)/shard_map/ppermute | solution.py:422
  23.2 6.0 %collective-permute-start.4 = (bf16[16,1536]{1,0:T(8,128)(2,1)S(1)}, bf16[16,1536]{1,0:T(8,128)(2,1)S(1)}, u32[]{:S(2)}, u32[]{:S(2)}) collective-permute-start(bf16[16,1536]{1,0:T(8,128)(2,1)S(1)} %get-tuple-element.52), channel_id=1, source_target_pairs={{0,12},{4,8},{8,4},{12,0},{1,13},{5,9},{9,5},{13,1},{2,14},{6,10},... | collective-permute-start | bytes 147464 | tf_op jit(solution)/shard_map/ppermute | solution.py:422
  30.3 4.9 %collective-permute-start.5 = (bf16[144,128]{1,0:T(8,128)(2,1)S(1)}, bf16[144,128]{1,0:T(8,128)(2,1)S(1)}, u32[]{:S(2)}, u32[]{:S(2)}) collective-permute-start(bf16[144,128]{1,0:T(8,128)(2,1)S(1)} %get-tuple-element.56), channel_id=1, source_target_pairs={{0,8},{4,12},{8,0},{12,4},{1,9},{5,13},{9,1},{13,5},{2,10},{6,14},... | collective-permute-start | bytes 110600 | tf_op jit(solution)/shard_map/ppermute | solution.py:422
  32.8 5.8 %collective-permute-start.6 = (bf16[144,128]{1,0:T(8,128)(2,1)S(1)}, bf16[144,128]{1,0:T(8,128)(2,1)S(1)}, u32[]{:S(2)}, u32[]{:S(2)}) collective-permute-start(bf16[144,128]{1,0:T(8,128)(2,1)S(1)} %get-tuple-element.57), channel_id=1, source_target_pairs={{0,12},{4,8},{8,4},{12,0},{1,13},{5,9},{9,5},{13,1},{2,14},{6,10},... | collective-permute-start | bytes 110600 | tf_op jit(solution)/shard_map/ppermute | solution.py:422
  34.0 4.6 %collective-permute-start.7 = (bf16[144,128]{1,0:T(8,128)(2,1)S(1)}, bf16[144,128]{1,0:T(8,128)(2,1)S(1)}, u32[]{:S(2)}, u32[]{:S(2)}) collective-permute-start(bf16[144,128]{1,0:T(8,128)(2,1)S(1)} %get-tuple-element.58), channel_id=1, source_target_pairs={{0,4},{4,0},{8,12},{12,8},{1,5},{5,1},{9,13},{13,9},{2,6},{6,2},{1... | collective-permute-start | bytes 110600 | tf_op jit(solution)/shard_map/ppermute | solution.py:422

commit v7 on v6

--- a/solution.py
+++ b/solution.py
@@ -222,24 +222,36 @@
     spread(chosen, sums, outs, 0)
 
 
-def project_rest_kernel(pool, column, lhs, pick, w_key, w_value, w_query, near, *rest):
-    outs, (query_buf, sums, sems) = rest[:pool], rest[pool:]
+def project_rest_kernel(pool, column, lhs, pick, near, w_key, w_value, w_query, *rest):
+    outs, (key_buf, value_buf, query_buf, sums, sems) = rest[:pool], rest[pool:]
     done = near.shape[1]
     count, _, deep = lhs.shape
     kv_cols = w_key.shape[1]
 
-    def use(t):
+    def use_narrow(buf, at):
+        def use(t):
+            part = 0.0
+            for k in range(count):
+                part = part + jnp.dot(
+                    lhs[k], buf[t, k * deep : (k + 1) * deep, :], preferred_element_type=jnp.float32
+                )
+            sums[:, at : at + kv_cols] = part
+
+        return use
+
+    def use_query(t):
         add_products(lhs[t], query_buf, t, sums.at[:, 2 * kv_cols :])
 
-    begin, finish = project_blocks([(w_query, column, query_buf, use)], sems, count)
+    begin, finish = project_blocks(
+        [
+            (w_key, 0, key_buf, use_narrow(key_buf, 0)),
+            (w_value, 0, value_buf, use_narrow(value_buf, kv_cols)),
+            (w_query, column, query_buf, use_query),
+        ],
+        sems,
+        2 * WINDOW,
+    )
     begin()
-    for n, w in enumerate((w_key, w_value)):
-        part = 0.0
-        for k in range(count):
-            part = part + jnp.dot(
-                lhs[k], w[k * deep : (k + 1) * deep, :], preferred_element_type=jnp.float32
-            )
-        sums[:, n * kv_cols : (n + 1) * kv_cols] = part
     sums[:, 2 * kv_cols :] = jnp.zeros((sums.shape[0], sums.shape[1] - 2 * kv_cols), jnp.float32)
     outs[1][:, :done] = near[...]
     finish()
@@ -256,8 +268,8 @@
     step = HD // group
     scale = HD ** (-0.5)
 
-    own, own_rest, near = terms[:3]
-    far, far_rest = terms[3 : 1 + pool], terms[1 + pool :]
+    own, own_rest, near = terms[0], terms[1], terms[-1]
+    far_rest, far = terms[2:pool], terms[pool:-1]
     first_cols, cols = own.shape[1], near.shape[1]
 
     def total(at):
@@ -463,12 +475,12 @@
         indices = [send_row.reshape(-1), piece_len.reshape(-1), row_len]
     deep = divides(depth, DEEP)
     count = depth // deep
-    widths = [3 * q_cols // 4, q_cols // 4]
+    widths = [11 * q_cols // 16, 5 * q_cols // 16]
 
     def parts(width):
         return [jax.ShapeDtypeStruct((per, width), jnp.bfloat16)] * pool
 
-    operands = [in_hbm(x) for x in (*indices, hidden_in, norm_gain, w_query)]
+    operands = [in_hbm(x) for x in (*indices, hidden_in, norm_gain, w_query, w_key, w_value)]
     *first_terms, lhs, pick, positions, marks, home_rows, home_slots = pl.pallas_call(
         functools.partial(project_kernel, pool, slots, rows_local),
         out_shape=[
@@ -494,20 +506,21 @@
         ],
         compiler_params=pltpu.CompilerParams(vmem_limit_bytes=46 * 2**20),
         name="project",
-    )(me[None], *operands)
-    first_terms, kv_weights = lax.optimization_barrier((list(first_terms), (w_key, w_value)))
+    )(me[None], *operands[:6])
     rest_cols = 2 * kv_cols + widths[1]
     rest_shapes = parts(rest_cols)
     rest_shapes[1] = jax.ShapeDtypeStruct((per, widths[0] + HD + rest_cols), jnp.bfloat16)
     rest_terms = pl.pallas_call(
         functools.partial(project_rest_kernel, pool, widths[0]),
         out_shape=rest_shapes,
-        in_specs=[VMEM, VMEM, VMEM, VMEM, HBM, VMEM],
+        in_specs=[VMEM] * 3 + [HBM] * 3,
         out_specs=[VMEM] * pool,
         scratch_shapes=[
+            pltpu.VMEM((1, depth, kv_cols), jnp.bfloat16),
+            pltpu.VMEM((1, depth, kv_cols), jnp.bfloat16),
             pltpu.VMEM((count, deep, widths[1]), jnp.bfloat16),
             pltpu.VMEM((n_rows, rest_cols), jnp.float32),
-            pltpu.SemaphoreType.DMA((count,)),
+            pltpu.SemaphoreType.DMA((count + 2,)),
         ],
         compiler_params=pltpu.CompilerParams(vmem_limit_bytes=40 * 2**20),
         cost_estimate=pl.CostEstimate(
@@ -516,7 +529,7 @@
             transcendentals=0,
         ),
         name="project_rest",
-    )(lhs, pick, *kv_weights, operands[-1], first_terms[1])
+    )(lhs, pick, first_terms[1], operands[6], operands[7], operands[5])
     first_terms = exchange(first_terms, range(2, pool))
     rest_terms = list(rest_terms)
     early, late = range(2, pool), range(3, pool)
@@ -528,7 +541,7 @@
     for k, part in zip(late, tied):
         rest_terms[k] = part
     rest_terms = exchange(rest_terms, range(1, pool))
-    terms = [first_terms[0], *rest_terms[:2], *first_terms[2:], *rest_terms[2:]]
+    terms = [first_terms[0], rest_terms[0], *rest_terms[2:], *first_terms[2:], rest_terms[1]]
 
     half = HD // 2
     freq = THETA ** (-(np.arange(half) * 2.0) / HD)

time: 40 us -> 39.8 us (level)
  Pallas kernels: 17 us -> 18.1 us
  starting transfers between devices: 14.2 us -> 13.5 us
  waiting for transfers between devices: 8.55 us -> 7.95 us
    pallas_call x1, Pallas kernels: 4.44 us -> 6.41 us  [body(): pl.pallas_call(functools.partial(project_rest_kernel, pool, widths[0]), o...]
    pallas_call x1, Pallas kernels: 10.2 us -> 9.25 us  [body(): pl.pallas_call(functools.partial(project_kernel, pool, slots, rows_local)...]
    ppermute x8, starting transfers between devices: 14.2 us -> 13.5 us  [exchange(): lax.ppermute(parts[k], 'pool', [(i, i ^ k) for i in range(len(parts))])]
    ppermute x8, waiting for transfers between devices: 8.55 us -> 7.95 us  [exchange(): lax.ppermute(parts[k], 'pool', [(i, i ^ k) for i in range(len(parts))])]
  transfers between devices with their start and end apart: 8 -> 8, of which waited for: 4 -> 4; matrix products, arithmetic and copies ran while one was open for 0% -> 0% of each run, Pallas kernels for 11% -> 16%
where the time goes in v7:
time: 39.8 us; the launch traced here: 39.6 us
  Pallas kernels  18.1 us (45%)
  starting transfers between devices  13.5 us (34%)
  waiting for transfers between devices  7.95 us (20%)
    ppermute x8, starting transfers between devices, exchange(): lax.ppermute(parts[k], 'pool', [(i, i ^ k) for i in range(len(parts))])  13.5 us
    pallas_call x1, Pallas kernels, body(): pl.pallas_call(functools.partial(project_kernel, pool, slots, rows_local)...  9.25 us
    ppermute x8, waiting for transfers between devices, exchange(): lax.ppermute(parts[k], 'pool', [(i, i ^ k) for i in range(len(parts))])  7.95 us
    pallas_call x1, Pallas kernels, body(): pl.pallas_call(functools.partial(project_rest_kernel, pool, widths[0]), o...  6.41 us
    pallas_call x1, Pallas kernels, body(): pl.pallas_call(functools.partial(merge_kernel, pool, slots, rows_local, q...  1.33 us
    pallas_call x1, Pallas kernels, body(): pl.pallas_call(functools.partial(attend_kernel, pool, slots, seg, width_d...  1.06 us
  transfers between devices with their start and end apart: 8, of which 4 were waited for; matrix products, arithmetic and copies ran while one was open for 0% of the time, Pallas kernels for 16%

profile of v7, /device:TPU:0, one launch (start us, length us, event | category | flops | bytes accessed | tf_op | source)
XLA Modules:
  0.0 39.6 jit_solution(895309417063213343)
XLA Ops:
  0.0 9.3 %project.1 = (bf16[16,2944]{1,0:T(8,128)(2,1)S(1)}, bf16[16,2944]{1,0:T(8,128)(2,1)S(1)}, bf16[16,2944]{1,0:T(8,128)(2,1)S(1)}, bf16[16,2944]{1,0:T(8,128)(2,1)S...) custom-call(s32[1]{0:T(128)} %bitcast.me_ref, ...), custom_call_target="tpu_custom_call" | custom-call | tf_op jit(solution)/shard_map/project/pallas_call | solution.py:484
  9.3 4.1 %collective-permute-start.1 = (bf16[16,2944]{1,0:T(8,128)(2,1)S(1)}, bf16[16,2944]{1,0:T(8,128)(2,1)S(1)}, u32[]{:S(2)}, u32[]{:S(2)}) collective-permute-start(bf16[16,2944]{1,0:T(8,128)(2,1)S(1)} %get-tuple-element.34), channel_id=1, source_target_pairs={{0,8},{4,12},{8,0},{12,4},{1,9},{5,13},{9,1},{13,5},{2,10},{6,14},... | collective-permute-start | bytes 282632 | tf_op jit(solution)/shard_map/ppermute | solution.py:434
  13.4 1.3 %collective-permute-start.2 = (bf16[16,2944]{1,0:T(8,128)(2,1)S(1)}, bf16[16,2944]{1,0:T(8,128)(2,1)S(1)}, u32[]{:S(2)}, u32[]{:S(2)}) collective-permute-start(bf16[16,2944]{1,0:T(8,128)(2,1)S(1)} %get-tuple-element.35), channel_id=1, source_target_pairs={{0,12},{4,8},{8,4},{12,0},{1,13},{5,9},{9,5},{13,1},{2,14},{6,10},... | collective-permute-start | bytes 282632 | tf_op jit(solution)/shard_map/ppermute | solution.py:434
  14.7 0.0 copy-start.2
  14.7 0.0 copy-start.3
  14.7 0.0 copy-start
  14.7 0.0 copy-start.1
  14.7 6.4 %project_rest.1 = (bf16[16,1792]{1,0:T(8,128)(2,1)S(1)}, bf16[16,4736]{1,0:T(8,128)(2,1)S(1)}, bf16[16,1792]{1,0:T(8,128)(2,1)S(1)}, bf16[16,1792]{1,0:T(8,128)(2,1)S(1)}) custom-call(bf16[8,64,512]{2,1,0:T(8,128)(2,1)S(1)} %get-tuple-element.29.lhs, f32[64,64]{1,0:T(8,128)S(1)} %get-tuple-element.30.pick, bf16[16,2944]{1,0:T(8,128)(2,1)S(1)} %get-tuple-element.31.near, ...), custom_call_target="tpu_custom_call" | custom-call | flops 939524096 | bytes 15204352 | tf_op jit(solution)/shard_map/project_rest/pallas_call | solution.py:513
  21.1 0.3 collective-permute-start.4
  21.4 2.8 %collective-permute-start = (bf16[16,1792]{1,0:T(8,128)(2,1)S(1)}, bf16[16,1792]{1,0:T(8,128)(2,1)S(1)}, u32[]{:S(2)}, u32[]{:S(2)}) collective-permute-start(bf16[16,1792]{1,0:T(8,128)(2,1)S(1)} %get-tuple-element.33), channel_id=1, source_target_pairs={{0,8},{4,12},{8,0},{12,4},{1,9},{5,13},{9,1},{13,5},{2,10},{6,14},... | collective-permute-start | bytes 172040 | tf_op jit(solution)/shard_map/ppermute | solution.py:434
  24.3 0.0 collective-permute-done.1.rest_4_
  24.3 0.0 collective-permute-done.2.rest_5_
  24.3 1.3 %collective-permute-start.3 = (bf16[16,1792]{1,0:T(8,128)(2,1)S(1)}, bf16[16,1792]{1,0:T(8,128)(2,1)S(1)}, u32[]{:S(2)}, u32[]{:S(2)}) collective-permute-start(bf16[16,1792]{1,0:T(8,128)(2,1)S(1)} %get-tuple-element.37), channel_id=1, source_target_pairs={{0,12},{4,8},{8,4},{12,0},{1,13},{5,9},{9,5},{13,1},{2,14},{6,10},... | collective-permute-start | bytes 172040 | tf_op jit(solution)/shard_map/ppermute | solution.py:434
  25.6 0.0 copy-done.2
  25.6 0.0 copy-done.3
  25.6 0.1 sine_multiply_fusion
  25.7 2.0 %collective-permute-done.rest_2_ = bf16[16,1792]{1,0:T(8,128)(2,1)S(1)} collective-permute-done((bf16[16,1792]{1,0:T(8,128)(2,1)S(1)}, bf16[16,1792]{1,0:T(8,128)(2,1)S(1)}, u32[]{:S(2)}, u32[]{:S(2)}) %collective-permute-start) | collective-permute-done | bytes 57376 | tf_op jit(solution)/shard_map/ppermute | solution.py:434
  27.7 2.6 %collective-permute-done.3.rest_3_ = bf16[16,1792]{1,0:T(8,128)(2,1)S(1)} collective-permute-done((bf16[16,1792]{1,0:T(8,128)(2,1)S(1)}, bf16[16,1792]{1,0:T(8,128)(2,1)S(1)}, u32[]{:S(2)}, u32[]{:S(2)}) %collective-permute-start.3) | collective-permute-done | bytes 57376 | tf_op jit(solution)/shard_map/ppermute | solution.py:434
  30.2 0.0 collective-permute-done.4.rest_6_
  30.2 0.0 copy-done
  30.2 0.0 copy-done.1
  30.2 1.1 %attend.1 = (bf16[144,128]{1,0:T(8,128)(2,1)S(1)}, bf16[144,128]{1,0:T(8,128)(2,1)S(1)}, bf16[144,128]{1,0:T(8,128)(2,1)S(1)}, bf16[144,128]{1,0:T(8,128)(2,1)S(1)}) custom-call(s32[1]{0:T(128)} %bitcast.me_ref, bf16[16,2944]{1,0:T(8,128)(2,1)S(1)} %get-tuple-element.28.rest_0_, bf16[16,1792]{1,0:T(8,128)(2,1)S(1)} %get-tuple-element.32.rest_1_, ...), custom_call_target="tpu_custom_call" | custom-call | tf_op jit(solution)/shard_map/attend/pallas_call | solution.py:552
  31.3 1.2 %collective-permute-start.5 = (bf16[144,128]{1,0:T(8,128)(2,1)S(1)}, bf16[144,128]{1,0:T(8,128)(2,1)S(1)}, u32[]{:S(2)}, u32[]{:S(2)}) collective-permute-start(bf16[144,128]{1,0:T(8,128)(2,1)S(1)} %get-tuple-element.44), channel_id=1, source_target_pairs={{0,8},{4,12},{8,0},{12,4},{1,9},{5,13},{9,1},{13,5},{2,10},{6,14},... | collective-permute-start | bytes 110600 | tf_op jit(solution)/shard_map/ppermute | solution.py:434
  32.5 1.1 %collective-permute-start.6 = (bf16[144,128]{1,0:T(8,128)(2,1)S(1)}, bf16[144,128]{1,0:T(8,128)(2,1)S(1)}, u32[]{:S(2)}, u32[]{:S(2)}) collective-permute-start(bf16[144,128]{1,0:T(8,128)(2,1)S(1)} %get-tuple-element.45), channel_id=1, source_target_pairs={{0,12},{4,8},{8,4},{12,0},{1,13},{5,9},{9,5},{13,1},{2,14},{6,10},... | collective-permute-start | bytes 110600 | tf_op jit(solution)/shard_map/ppermute | solution.py:434
  33.6 1.3 %collective-permute-start.7 = (bf16[144,128]{1,0:T(8,128)(2,1)S(1)}, bf16[144,128]{1,0:T(8,128)(2,1)S(1)}, u32[]{:S(2)}, u32[]{:S(2)}) collective-permute-start(bf16[144,128]{1,0:T(8,128)(2,1)S(1)} %get-tuple-element.46), channel_id=1, source_target_pairs={{0,4},{4,0},{8,12},{12,8},{1,5},{5,1},{9,13},{13,9},{2,6},{6,2},{1... | collective-permute-start | bytes 110600 | tf_op jit(solution)/shard_map/ppermute | solution.py:434
  34.9 1.4 %collective-permute-done.5.rest_0_ = bf16[144,128]{1,0:T(8,128)(2,1)S(1)} collective-permute-done((bf16[144,128]{1,0:T(8,128)(2,1)S(1)}, bf16[144,128]{1,0:T(8,128)(2,1)S(1)}, u32[]{:S(2)}, u32[]{:S(2)}) %collective-permute-start.5) | collective-permute-done | bytes 36896 | tf_op jit(solution)/shard_map/ppermute | solution.py:434
  36.3 2.0 %collective-permute-done.6.rest_1_ = bf16[144,128]{1,0:T(8,128)(2,1)S(1)} collective-permute-done((bf16[144,128]{1,0:T(8,128)(2,1)S(1)}, bf16[144,128]{1,0:T(8,128)(2,1)S(1)}, u32[]{:S(2)}, u32[]{:S(2)}) %collective-permute-start.6) | collective-permute-done | bytes 36896 | tf_op jit(solution)/shard_map/ppermute | solution.py:434
  38.2 0.0 collective-permute-done.7.rest_2_
  38.2 1.3 %merge.1 = bf16[16,4096]{1,0:T(8,128)(2,1)} custom-call(s32[1,128]{1,0:T(1,128)S(1)} %get-tuple-element.26.slots_ref, s32[4,128]{1,0:T(4,128)S(1)} %get-tuple-element.27.rows_ref, bf16[144,128]{1,0:T(8,128)(2,1)S(1)} %get-tuple-element.43.own, bf16[144,128]{1,0:T(8,128)(2,1)S(1)} %collective-permute-done.5.rest_0_, ...), custom_call_target="tpu_custom_call" | custom-call | tf_op jit(solution)/shard_map/merge/pallas_call | solution.py:564
Async XLA Ops:
  9.3 15.0 %collective-permute-start.1 = (bf16[16,2944]{1,0:T(8,128)(2,1)S(1)}, bf16[16,2944]{1,0:T(8,128)(2,1)S(1)}, u32[]{:S(2)}, u32[]{:S(2)}) collective-permute-start(bf16[16,2944]{1,0:T(8,128)(2,1)S(1)} %get-tuple-element.34), channel_id=1, source_target_pairs={{0,8},{4,12},{8,0},{12,4},{1,9},{5,13},{9,1},{13,5},{2,10},{6,14},... | collective-permute-start | bytes 282632 | tf_op jit(solution)/shard_map/ppermute | solution.py:434
  13.4 10.9 %collective-permute-start.2 = (bf16[16,2944]{1,0:T(8,128)(2,1)S(1)}, bf16[16,2944]{1,0:T(8,128)(2,1)S(1)}, u32[]{:S(2)}, u32[]{:S(2)}) collective-permute-start(bf16[16,2944]{1,0:T(8,128)(2,1)S(1)} %get-tuple-element.35), channel_id=1, source_target_pairs={{0,12},{4,8},{8,4},{12,0},{1,13},{5,9},{9,5},{13,1},{2,14},{6,10},... | collective-permute-start | bytes 282632 | tf_op jit(solution)/shard_map/ppermute | solution.py:434
  14.7 10.9 %copy-start.2 = (f32[128]{0:T(128)S(1)}, f32[128]{0:T(128)}, u32[]{:S(2)}) copy-start(f32[128]{0:T(128)} %constant.12) | copy-start | bytes 1540
  14.7 10.9 %copy-start.3 = (f32[128]{0:T(128)S(1)}, f32[128]{0:T(128)}, u32[]{:S(2)}) copy-start(f32[128]{0:T(128)} %constant.13) | copy-start | bytes 1540
  14.7 15.5 %copy-start = (bf16[1024,256]{1,0:T(8,128)(2,1)S(1)}, bf16[1024,256]{1,0:T(8,128)(2,1)}, u32[]{:S(2)}) copy-start(bf16[1024,256]{1,0:T(8,128)(2,1)} %rest_10_.1) | copy-start | bytes 1572868
  14.7 15.5 %copy-start.1 = (bf16[1024,256]{1,0:T(8,128)(2,1)S(1)}, bf16[1024,256]{1,0:T(8,128)(2,1)}, u32[]{:S(2)}) copy-start(bf16[1024,256]{1,0:T(8,128)(2,1)} %rest_11_.1) | copy-start | bytes 1572868
  21.1 9.1 %collective-permute-start.4 = (bf16[16,4736]{1,0:T(8,128)(2,1)S(1)}, bf16[16,4736]{1,0:T(8,128)(2,1)S(1)}, u32[]{:S(2)}, u32[]{:S(2)}) collective-permute-start(bf16[16,4736]{1,0:T(8,128)(2,1)S(1)} %get-tuple-element.40), channel_id=1, source_target_pairs={{0,4},{4,0},{8,12},{12,8},{1,5},{5,1},{9,13},{13,9},{2,6},{6,2},{1... | collective-permute-start | bytes 454664 | tf_op jit(solution)/shard_map/ppermute | solution.py:434
  21.4 6.2 %collective-permute-start = (bf16[16,1792]{1,0:T(8,128)(2,1)S(1)}, bf16[16,1792]{1,0:T(8,128)(2,1)S(1)}, u32[]{:S(2)}, u32[]{:S(2)}) collective-permute-start(bf16[16,1792]{1,0:T(8,128)(2,1)S(1)} %get-tuple-element.33), channel_id=1, source_target_pairs={{0,8},{4,12},{8,0},{12,4},{1,9},{5,13},{9,1},{13,5},{2,10},{6,14},... | collective-permute-start | bytes 172040 | tf_op jit(solution)/shard_map/ppermute | solution.py:434
  24.3 6.0 %collective-permute-start.3 = (bf16[16,1792]{1,0:T(8,128)(2,1)S(1)}, bf16[16,1792]{1,0:T(8,128)(2,1)S(1)}, u32[]{:S(2)}, u32[]{:S(2)}) collective-permute-start(bf16[16,1792]{1,0:T(8,128)(2,1)S(1)} %get-tuple-element.37), channel_id=1, source_target_pairs={{0,12},{4,8},{8,4},{12,0},{1,13},{5,9},{9,5},{13,1},{2,14},{6,10},... | collective-permute-start | bytes 172040 | tf_op jit(solution)/shard_map/ppermute | solution.py:434
  31.3 5.0 %collective-permute-start.5 = (bf16[144,128]{1,0:T(8,128)(2,1)S(1)}, bf16[144,128]{1,0:T(8,128)(2,1)S(1)}, u32[]{:S(2)}, u32[]{:S(2)}) collective-permute-start(bf16[144,128]{1,0:T(8,128)(2,1)S(1)} %get-tuple-element.44), channel_id=1, source_target_pairs={{0,8},{4,12},{8,0},{12,4},{1,9},{5,13},{9,1},{13,5},{2,10},{6,14},... | collective-permute-start | bytes 110600 | tf_op jit(solution)/shard_map/ppermute | solution.py:434
  32.5 5.8 %collective-permute-start.6 = (bf16[144,128]{1,0:T(8,128)(2,1)S(1)}, bf16[144,128]{1,0:T(8,128)(2,1)S(1)}, u32[]{:S(2)}, u32[]{:S(2)}) collective-permute-start(bf16[144,128]{1,0:T(8,128)(2,1)S(1)} %get-tuple-element.45), channel_id=1, source_target_pairs={{0,12},{4,8},{8,4},{12,0},{1,13},{5,9},{9,5},{13,1},{2,14},{6,10},... | collective-permute-start | bytes 110600 | tf_op jit(solution)/shard_map/ppermute | solution.py:434
  33.6 4.7 %collective-permute-start.7 = (bf16[144,128]{1,0:T(8,128)(2,1)S(1)}, bf16[144,128]{1,0:T(8,128)(2,1)S(1)}, u32[]{:S(2)}, u32[]{:S(2)}) collective-permute-start(bf16[144,128]{1,0:T(8,128)(2,1)S(1)} %get-tuple-element.46), channel_id=1, source_target_pairs={{0,4},{4,0},{8,12},{12,8},{1,5},{5,1},{9,13},{13,9},{2,6},{6,2},{1... | collective-permute-start | bytes 110600 | tf_op jit(solution)/shard_map/ppermute | solution.py:434

commit v8 on v7

--- a/solution.py
+++ b/solution.py
@@ -12,7 +12,6 @@
 EPS = 1e-05
 THETA = 500000.0
 LOW = -1e30
-WINDOW = 3
 DEEP = 512
 LEVELS = 16
 
@@ -34,79 +33,53 @@
     return lax.bitwise_xor(me, k)
 
 
-def project_blocks(plan, sems, window):
-    blocks = [(n, t) for n, entry in enumerate(plan) for t in range(entry[2].shape[0])]
-
-    def copy(n, t, i):
-        w, column, buf, _ = plan[n]
-        _, deep, width = buf.shape
-        at = t * deep if isinstance(t, int) else pl.multiple_of(t * deep, deep)
-        return pltpu.make_async_copy(
-            w.at[pl.ds(at, deep), column : column + width], buf.at[t], sems.at[i]
-        )
-
+def stream(count, pieces, following, ahead):
     def begin():
-        for i in range(min(window, len(blocks))):
-            copy(*blocks[i], i).start()
-
-    def finish():
-        first = 0
-        for n, (_, _, buf, use) in enumerate(plan):
-            count = buf.shape[0]
-
-            def work(t, carry, n=n, first=first, use=use):
-                copy(n, t, first + t).wait()
-                use(t)
-                return carry
-
-            t = 0
-            while t < count:
-                ahead = first + t + window
-                if ahead < len(blocks):
-                    m, u = blocks[ahead]
-                    run = 1
-                    while (
-                        t + run < count
-                        and ahead + run < len(blocks)
-                        and blocks[ahead + run][0] == m
-                    ):
-                        run += 1
-
-                    def step(q, carry, m=m, u=u, t=t, ahead=ahead, work=work):
-                        copy(m, u + q, ahead + q).start()
-                        return work(t + q, carry)
-
-                    lax.fori_loop(0, run, step, 0)
-                else:
-                    run = count - t
-                    lax.fori_loop(t, count, work, 0)
-                t += run
-            first += count
-
-    return begin, finish
-
-
-def add_products(left, buf, t, sums):
-    width = buf.shape[2]
+        for t in range(min(ahead, count)):
+            for copy in pieces(t):
+                copy.start()
+        for copy in following[: max(ahead - count, 0)]:
+            copy.start()
+
+    def advance(t):
+        @pl.when(t + ahead < count)
+        def _():
+            for copy in pieces(t + ahead):
+                copy.start()
+
+        for j, copy in enumerate(following):
+            pl.when(t + ahead == count + j)(copy.start)
+
+    return begin, advance
+
+
+def add_products(left, block, sums):
+    width = block.shape[1]
     tile = divides(width, 512)
     for at in range(0, width, tile):
         sums[:, at : at + tile] += jnp.dot(
-            left, buf[t, :, at : at + tile], preferred_element_type=jnp.float32
+            left, block[:, at : at + tile], preferred_element_type=jnp.float32
         )
 
 
 def spread(chosen, sums, outs, at):
     width = sums.shape[1]
+    per = chosen.shape[0] // len(outs)
+    rows = jnp.dot(
+        chosen, sums.astype(jnp.bfloat16), preferred_element_type=jnp.float32
+    ).astype(jnp.bfloat16)
+    for k, out in enumerate(outs):
+        out[:, at : at + width] = rows[k * per : (k + 1) * per]
+
+
+def spread_products(chosen, left, block, sums, outs, to):
+    width = block.shape[1]
     tile = divides(width, 512)
-    per = chosen.shape[0] // len(outs)
-    for column in range(0, width, tile):
-        rows = jnp.dot(
-            chosen,
-            sums[:, column : column + tile].astype(jnp.bfloat16),
-            preferred_element_type=jnp.float32,
-        ).astype(jnp.bfloat16)
-        for k, out in enumerate(outs):
-            out[:, at + column : at + column + tile] = rows[k * per : (k + 1) * per]
+    for at in range(0, width, tile):
+        done = sums[:, at : at + tile] + jnp.dot(
+            left, block[:, at : at + tile], preferred_element_type=jnp.float32
+        )
+        spread(chosen, done, outs, to + at)
 
 
 def project_kernel(pool, slots, rows_local, me_ref, send, lens, row_len, hidden, gain, *rest):
@@ -114,10 +87,10 @@
     outs, rest = rest[:pool], rest[pool:]
     lhs, pick, positions, marks, home_rows, home_slots, *rest = rest
     send_buf, lens_buf, row_len_buf, x_buf, g_buf, *rest = rest
-    query_buf, sums, squares, in_sem, sems = rest
+    *bufs, sums, squares, in_sem, sems = rest
     per = pool * slots
     n_rows, depth = x_buf.shape
-    count, deep, _ = query_buf.shape
+    count, deep, _ = bufs[0].shape
     me = me_ref[0]
 
     def named(home, owner, c):
@@ -158,9 +131,11 @@
             lax.rem(place // group, slots) == c, mine, home_rows[pl.ds(k, 1), :]
         )
 
+    chore_steps = max(count // 2, 1)
+
     def each(do, total, t):
-        share = -(-total // count)
-        if share <= 16 and total % count == 0:
+        share = -(-total // chore_steps)
+        if share <= 16 and total % chore_steps == 0:
             for q in range(share):
                 do(t * share + q)
         else:
@@ -173,23 +148,60 @@
 
                 lax.fori_loop(0, total, one, 0)
 
-    def use_query(t):
-        short = divides(deep, 512)
-        for part in range(0, deep, short):
-            at = pl.multiple_of(t * deep + part, short)
-            x = x_buf[:, pl.ds(at, short)].astype(jnp.float32)
-            gains = g_buf[pl.ds(at, short)].astype(jnp.float32).reshape(1, short)
-            lhs[t, :, part : part + short] = (x * gains).astype(jnp.bfloat16)
-            squared = x * x
-            total = squared[:, :HD]
-            for column in range(HD, short, HD):
-                total = total + squared[:, column : column + HD]
-            squares[...] += total
-        add_products(lhs[t], query_buf, t, sums)
+    def scale(t):
+        at = pl.multiple_of(t * deep, deep)
+        x = x_buf[:, pl.ds(at, deep)].astype(jnp.float32)
+        gains = g_buf[pl.ds(at, deep)].astype(jnp.float32).reshape(1, deep)
+        left = (x * gains).astype(jnp.bfloat16)
+        lhs[t] = left
+        squared = x * x
+        total = squares[...]
+        for column in range(0, deep, HD):
+            total = total + squared[:, column : column + HD]
+        squares[...] = total
+        return left
+
+    starts = [sum(buf.shape[2] for buf in bufs[:n]) for n in range(len(bufs))]
+
+    def pieces(t):
+        rows = pl.ds(pl.multiple_of(t * deep, deep), deep)
+        return [
+            pltpu.make_async_copy(
+                w_query.at[rows, start : start + buf.shape[2]], buf.at[t], sems.at[n, t]
+            )
+            for n, (buf, start) in enumerate(zip(bufs, starts))
+        ]
+
+    begin, advance = stream(count, pieces, [], 2)
+
+    def use(t):
+        advance(t)
+        left = scale(t)
+        for copy, buf, start in zip(pieces(t), bufs, starts):
+            copy.wait()
+            add_products(left, buf.at[t], sums.at[:, start : start + buf.shape[2]])
+
+    def use_early(t):
+        use(t)
         each(choose, pool * per, t)
         each(describe, per, t)
 
-    begin, finish = project_blocks([(w_query, 0, query_buf, use_query)], sems, WINDOW)
+    def use_last(t):
+        left = scale(t)
+        if count == 1:
+            each(choose, pool * per, t)
+            each(describe, per, t)
+        chosen = pick[...].astype(jnp.bfloat16)
+        for copy, buf, start in zip(pieces(t), bufs, starts):
+            copy.wait()
+            part = sums.at[:, start : start + buf.shape[2]]
+            spread_products(chosen, left, buf.at[t], part, outs, start)
+        power = jnp.sum(squares[...], axis=1, keepdims=True)
+        at = lax.broadcasted_iota(jnp.int32, (n_rows, HD), 1)
+        a, b, c = split3(power)
+        parts = jnp.where(at == 0, a, jnp.where(at == 1, b, jnp.where(at == 2, c, 0.0)))
+        spread(chosen, parts, outs, sums.shape[1])
+
     inputs = [
         pltpu.make_async_copy(source, target, in_sem.at[i])
         for i, (source, target) in enumerate(
@@ -212,51 +224,60 @@
     home_slots[...] = jnp.full(home_slots.shape, -1, jnp.int32)
     for one in inputs:
         one.wait()
-    finish()
-    power = jnp.sum(squares[...], axis=1, keepdims=True)
-    at = lax.broadcasted_iota(jnp.int32, (n_rows, HD), 1)
-    a, b, c = split3(power)
-    squares[...] = jnp.where(at == 0, a, jnp.where(at == 1, b, jnp.where(at == 2, c, 0.0)))
-    chosen = pick[...].astype(jnp.bfloat16)
-    spread(chosen, squares, outs, sums.shape[1])
-    spread(chosen, sums, outs, 0)
+    early = min(chore_steps, count - 1)
+    pl.loop(0, early)(use_early)
+    pl.loop(early, count - 1)(use)
+    use_last(count - 1)
 
 
 def project_rest_kernel(pool, column, lhs, pick, near, w_key, w_value, w_query, *rest):
-    outs, (key_buf, value_buf, query_buf, sums, sems) = rest[:pool], rest[pool:]
+    outs, (query_buf, key_buf, value_buf, sums, sems) = rest[:pool], rest[pool:]
     done = near.shape[1]
     count, _, deep = lhs.shape
-    kv_cols = w_key.shape[1]
-
-    def use_narrow(buf, at):
-        def use(t):
+    halves, tall, kv_cols = key_buf.shape
+    chosen = pick[...].astype(jnp.bfloat16)
+    targets = [out.at[:, done:] if k == 1 else out for k, out in enumerate(outs)]
+
+    def pieces(t):
+        rows = pl.ds(pl.multiple_of(t * deep, deep), deep)
+        block = w_query.at[rows, column : column + query_buf.shape[2]]
+        return [pltpu.make_async_copy(block, query_buf.at[t], sems.at[t])]
+
+    narrow = [(n, half) for n in range(2) for half in range(halves)]
+    following = [
+        pltpu.make_async_copy(
+            (w_key, w_value)[n].at[half * tall : (half + 1) * tall, :],
+            (key_buf, value_buf)[n].at[half],
+            sems.at[count + n * halves + half],
+        )
+        for n, half in narrow
+    ]
+    begin, advance = stream(count, pieces, following, 4)
+    begin()
+    sums[...] = jnp.zeros(sums.shape, jnp.float32)
+    outs[1][:, :done] = near[...]
+
+    @pl.loop(0, count - 1)
+    def _(t):
+        advance(t)
+        pieces(t)[0].wait()
+        add_products(lhs[t], query_buf.at[t], sums)
+
+    advance(count - 1)
+    pieces(count - 1)[0].wait()
+    spread_products(chosen, lhs[count - 1], query_buf.at[count - 1], sums, targets, 2 * kv_cols)
+    part = 0.0
+    for (n, half), copy in zip(narrow, following):
+        copy.wait()
+        for k in range(tall // deep):
+            part = part + jnp.dot(
+                lhs[half * (tall // deep) + k],
+                (key_buf, value_buf)[n][half, k * deep : (k + 1) * deep, :],
+                preferred_element_type=jnp.float32,
+            )
+        if half == halves - 1:
+            spread(chosen, part, targets, n * kv_cols)
             part = 0.0
-            for k in range(count):
-                part = part + jnp.dot(
-                    lhs[k], buf[t, k * deep : (k + 1) * deep, :], preferred_element_type=jnp.float32
-                )
-            sums[:, at : at + kv_cols] = part
-
-        return use
-
-    def use_query(t):
-        add_products(lhs[t], query_buf, t, sums.at[:, 2 * kv_cols :])
-
-    begin, finish = project_blocks(
-        [
-            (w_key, 0, key_buf, use_narrow(key_buf, 0)),
-            (w_value, 0, value_buf, use_narrow(value_buf, kv_cols)),
-            (w_query, column, query_buf, use_query),
-        ],
-        sems,
-        2 * WINDOW,
-    )
-    begin()
-    sums[:, 2 * kv_cols :] = jnp.zeros((sums.shape[0], sums.shape[1] - 2 * kv_cols), jnp.float32)
-    outs[1][:, :done] = near[...]
-    finish()
-    outs = [out.at[:, done:] if k == 1 else out for k, out in enumerate(outs)]
-    spread(pick[...].astype(jnp.bfloat16), sums, outs, 0)
 
 
 def attend_kernel(pool, slots, seg, width_d, q_heads, kv_heads, me_ref, *rest):
@@ -477,6 +498,9 @@
     count = depth // deep
     widths = [11 * q_cols // 16, 5 * q_cols // 16]
 
+    left_cols = -(-widths[0] // 512) * 256
+    halves = 2 if count % 2 == 0 else 1
+
     def parts(width):
         return [jax.ShapeDtypeStruct((per, width), jnp.bfloat16)] * pool
 
@@ -498,11 +522,12 @@
             *(pltpu.SMEM(x.shape, jnp.int32) for x in indices),
             pltpu.VMEM((n_rows, depth), jnp.bfloat16),
             pltpu.VMEM((depth,), jnp.bfloat16),
-            pltpu.VMEM((count, deep, widths[0]), jnp.bfloat16),
+            pltpu.VMEM((count, deep, left_cols), jnp.bfloat16),
+            pltpu.VMEM((count, deep, widths[0] - left_cols), jnp.bfloat16),
             pltpu.VMEM((n_rows, widths[0]), jnp.float32),
             pltpu.VMEM((n_rows, HD), jnp.float32),
             pltpu.SemaphoreType.DMA((5,)),
-            pltpu.SemaphoreType.DMA((count,)),
+            pltpu.SemaphoreType.DMA((2, count)),
         ],
         compiler_params=pltpu.CompilerParams(vmem_limit_bytes=46 * 2**20),
         name="project",
@@ -516,11 +541,11 @@
         in_specs=[VMEM] * 3 + [HBM] * 3,
         out_specs=[VMEM] * pool,
         scratch_shapes=[
-            pltpu.VMEM((1, depth, kv_cols), jnp.bfloat16),
-            pltpu.VMEM((1, depth, kv_cols), jnp.bfloat16),
             pltpu.VMEM((count, deep, widths[1]), jnp.bfloat16),
-            pltpu.VMEM((n_rows, rest_cols), jnp.float32),
-            pltpu.SemaphoreType.DMA((count + 2,)),
+            pltpu.VMEM((halves, depth // halves, kv_cols), jnp.bfloat16),
+            pltpu.VMEM((halves, depth // halves, kv_cols), jnp.bfloat16),
+            pltpu.VMEM((n_rows, widths[1]), jnp.float32),
+            pltpu.SemaphoreType.DMA((count + 2 * halves,)),
         ],
         compiler_params=pltpu.CompilerParams(vmem_limit_bytes=40 * 2**20),
         cost_estimate=pl.CostEstimate(

time: 39.8 us -> 40.9 us (1.028)
  Pallas kernels: 18.1 us -> 19.5 us
    pallas_call x1, Pallas kernels: 6.41 us -> 7.24 us  [body(): pl.pallas_call(functools.partial(project_rest_kernel, pool, widths[0]), o...]
    pallas_call x1, Pallas kernels: 9.25 us -> 9.88 us  [body(): pl.pallas_call(functools.partial(project_kernel, pool, slots, rows_local)...]
  transfers between devices with their start and end apart: 8 -> 8, of which waited for: 4 -> 4; matrix products, arithmetic and copies ran while one was open for 0% -> 0% of each run, Pallas kernels for 16% -> 18%
where the time goes in v8:
time: 40.9 us; the launch traced here: 40.7 us
  Pallas kernels  19.5 us (48%)
  starting transfers between devices  13.5 us (33%)
  waiting for transfers between devices  7.65 us (19%)
    ppermute x8, starting transfers between devices, exchange(): lax.ppermute(parts[k], 'pool', [(i, i ^ k) for i in range(len(parts))])  13.5 us
    pallas_call x1, Pallas kernels, body(): pl.pallas_call(functools.partial(project_kernel, pool, slots, rows_local)...  9.88 us
    ppermute x8, waiting for transfers between devices, exchange(): lax.ppermute(parts[k], 'pool', [(i, i ^ k) for i in range(len(parts))])  7.65 us
    pallas_call x1, Pallas kernels, body(): pl.pallas_call(functools.partial(project_rest_kernel, pool, widths[0]), o...  7.24 us
    pallas_call x1, Pallas kernels, body(): pl.pallas_call(functools.partial(merge_kernel, pool, slots, rows_local, q...  1.33 us
    pallas_call x1, Pallas kernels, body(): pl.pallas_call(functools.partial(attend_kernel, pool, slots, seg, width_d...  1.07 us
  transfers between devices with their start and end apart: 8, of which 4 were waited for; matrix products, arithmetic and copies ran while one was open for 0% of the time, Pallas kernels for 18%

profile of v8, /device:TPU:0, one launch (start us, length us, event | category | flops | bytes accessed | tf_op | source)
XLA Modules:
  0.0 40.7 jit_solution(13734710069768977553)
XLA Ops:
  0.0 9.9 %project.1 = (bf16[16,2944]{1,0:T(8,128)(2,1)S(1)}, bf16[16,2944]{1,0:T(8,128)(2,1)S(1)}, bf16[16,2944]{1,0:T(8,128)(2,1)S(1)}, bf16[16,2944]{1,0:T(8,128)(2,1)S...) custom-call(s32[1]{0:T(128)} %bitcast.me_ref, ...), custom_call_target="tpu_custom_call" | custom-call | tf_op jit(solution)/shard_map/project/pallas_call | solution.py:508
  9.9 4.1 %collective-permute-start.1 = (bf16[16,2944]{1,0:T(8,128)(2,1)S(1)}, bf16[16,2944]{1,0:T(8,128)(2,1)S(1)}, u32[]{:S(2)}, u32[]{:S(2)}) collective-permute-start(bf16[16,2944]{1,0:T(8,128)(2,1)S(1)} %get-tuple-element.34), channel_id=1, source_target_pairs={{0,8},{4,12},{8,0},{12,4},{1,9},{5,13},{9,1},{13,5},{2,10},{6,14},... | collective-permute-start | bytes 282632 | tf_op jit(solution)/shard_map/ppermute | solution.py:455
  14.0 1.3 %collective-permute-start.2 = (bf16[16,2944]{1,0:T(8,128)(2,1)S(1)}, bf16[16,2944]{1,0:T(8,128)(2,1)S(1)}, u32[]{:S(2)}, u32[]{:S(2)}) collective-permute-start(bf16[16,2944]{1,0:T(8,128)(2,1)S(1)} %get-tuple-element.35), channel_id=1, source_target_pairs={{0,12},{4,8},{8,4},{12,0},{1,13},{5,9},{9,5},{13,1},{2,14},{6,10},... | collective-permute-start | bytes 282632 | tf_op jit(solution)/shard_map/ppermute | solution.py:455
  15.3 0.0 copy-start.2
  15.3 0.0 copy-start.3
  15.3 0.0 copy-start
  15.3 0.0 copy-start.1
  15.4 7.2 %project_rest.1 = (bf16[16,1792]{1,0:T(8,128)(2,1)S(1)}, bf16[16,4736]{1,0:T(8,128)(2,1)S(1)}, bf16[16,1792]{1,0:T(8,128)(2,1)S(1)}, bf16[16,1792]{1,0:T(8,128)(2,1)S(1)}) custom-call(bf16[8,64,512]{2,1,0:T(8,128)(2,1)S(1)} %get-tuple-element.29.lhs, f32[64,64]{1,0:T(8,128)S(1)} %get-tuple-element.30.pick, bf16[16,2944]{1,0:T(8,128)(2,1)S(1)} %get-tuple-element.31.near, ...), custom_call_target="tpu_custom_call" | custom-call | flops 939524096 | bytes 15204352 | tf_op jit(solution)/shard_map/project_rest/pallas_call | solution.py:538
  22.6 0.3 collective-permute-start.4
  22.9 2.8 %collective-permute-start = (bf16[16,1792]{1,0:T(8,128)(2,1)S(1)}, bf16[16,1792]{1,0:T(8,128)(2,1)S(1)}, u32[]{:S(2)}, u32[]{:S(2)}) collective-permute-start(bf16[16,1792]{1,0:T(8,128)(2,1)S(1)} %get-tuple-element.33), channel_id=1, source_target_pairs={{0,8},{4,12},{8,0},{12,4},{1,9},{5,13},{9,1},{13,5},{2,10},{6,14},... | collective-permute-start | bytes 172040 | tf_op jit(solution)/shard_map/ppermute | solution.py:455
  25.7 0.0 collective-permute-done.1.rest_4_
  25.7 0.0 collective-permute-done.2.rest_5_
  25.7 1.3 %collective-permute-start.3 = (bf16[16,1792]{1,0:T(8,128)(2,1)S(1)}, bf16[16,1792]{1,0:T(8,128)(2,1)S(1)}, u32[]{:S(2)}, u32[]{:S(2)}) collective-permute-start(bf16[16,1792]{1,0:T(8,128)(2,1)S(1)} %get-tuple-element.37), channel_id=1, source_target_pairs={{0,12},{4,8},{8,4},{12,0},{1,13},{5,9},{9,5},{13,1},{2,14},{6,10},... | collective-permute-start | bytes 172040 | tf_op jit(solution)/shard_map/ppermute | solution.py:455
  27.1 0.0 copy-done.2
  27.1 0.0 copy-done.3
  27.1 0.1 sine_multiply_fusion
  27.1 2.0 %collective-permute-done.rest_2_ = bf16[16,1792]{1,0:T(8,128)(2,1)S(1)} collective-permute-done((bf16[16,1792]{1,0:T(8,128)(2,1)S(1)}, bf16[16,1792]{1,0:T(8,128)(2,1)S(1)}, u32[]{:S(2)}, u32[]{:S(2)}) %collective-permute-start) | collective-permute-done | bytes 57376 | tf_op jit(solution)/shard_map/ppermute | solution.py:455
  29.1 2.6 %collective-permute-done.3.rest_3_ = bf16[16,1792]{1,0:T(8,128)(2,1)S(1)} collective-permute-done((bf16[16,1792]{1,0:T(8,128)(2,1)S(1)}, bf16[16,1792]{1,0:T(8,128)(2,1)S(1)}, u32[]{:S(2)}, u32[]{:S(2)}) %collective-permute-start.3) | collective-permute-done | bytes 57376 | tf_op jit(solution)/shard_map/ppermute | solution.py:455
  31.7 0.0 collective-permute-done.4.rest_6_
  31.7 0.0 copy-done
  31.7 0.0 copy-done.1
  31.7 1.1 %attend.1 = (bf16[144,128]{1,0:T(8,128)(2,1)S(1)}, bf16[144,128]{1,0:T(8,128)(2,1)S(1)}, bf16[144,128]{1,0:T(8,128)(2,1)S(1)}, bf16[144,128]{1,0:T(8,128)(2,1)S(1)}) custom-call(s32[1]{0:T(128)} %bitcast.me_ref, bf16[16,2944]{1,0:T(8,128)(2,1)S(1)} %get-tuple-element.28.rest_0_, bf16[16,1792]{1,0:T(8,128)(2,1)S(1)} %get-tuple-element.32.rest_1_, ...), custom_call_target="tpu_custom_call" | custom-call | tf_op jit(solution)/shard_map/attend/pallas_call | solution.py:577
  32.8 0.8 %collective-permute-start.5 = (bf16[144,128]{1,0:T(8,128)(2,1)S(1)}, bf16[144,128]{1,0:T(8,128)(2,1)S(1)}, u32[]{:S(2)}, u32[]{:S(2)}) collective-permute-start(bf16[144,128]{1,0:T(8,128)(2,1)S(1)} %get-tuple-element.44), channel_id=1, source_target_pairs={{0,8},{4,12},{8,0},{12,4},{1,9},{5,13},{9,1},{13,5},{2,10},{6,14},... | collective-permute-start | bytes 110600 | tf_op jit(solution)/shard_map/ppermute | solution.py:455
  33.6 1.5 %collective-permute-start.6 = (bf16[144,128]{1,0:T(8,128)(2,1)S(1)}, bf16[144,128]{1,0:T(8,128)(2,1)S(1)}, u32[]{:S(2)}, u32[]{:S(2)}) collective-permute-start(bf16[144,128]{1,0:T(8,128)(2,1)S(1)} %get-tuple-element.45), channel_id=1, source_target_pairs={{0,12},{4,8},{8,4},{12,0},{1,13},{5,9},{9,5},{13,1},{2,14},{6,10},... | collective-permute-start | bytes 110600 | tf_op jit(solution)/shard_map/ppermute | solution.py:455
  35.0 1.3 %collective-permute-start.7 = (bf16[144,128]{1,0:T(8,128)(2,1)S(1)}, bf16[144,128]{1,0:T(8,128)(2,1)S(1)}, u32[]{:S(2)}, u32[]{:S(2)}) collective-permute-start(bf16[144,128]{1,0:T(8,128)(2,1)S(1)} %get-tuple-element.46), channel_id=1, source_target_pairs={{0,4},{4,0},{8,12},{12,8},{1,5},{5,1},{9,13},{13,9},{2,6},{6,2},{1... | collective-permute-start | bytes 110600 | tf_op jit(solution)/shard_map/ppermute | solution.py:455
  36.3 1.4 %collective-permute-done.5.rest_0_ = bf16[144,128]{1,0:T(8,128)(2,1)S(1)} collective-permute-done((bf16[144,128]{1,0:T(8,128)(2,1)S(1)}, bf16[144,128]{1,0:T(8,128)(2,1)S(1)}, u32[]{:S(2)}, u32[]{:S(2)}) %collective-permute-start.5) | collective-permute-done | bytes 36896 | tf_op jit(solution)/shard_map/ppermute | solution.py:455
  37.7 1.7 %collective-permute-done.6.rest_1_ = bf16[144,128]{1,0:T(8,128)(2,1)S(1)} collective-permute-done((bf16[144,128]{1,0:T(8,128)(2,1)S(1)}, bf16[144,128]{1,0:T(8,128)(2,1)S(1)}, u32[]{:S(2)}, u32[]{:S(2)}) %collective-permute-start.6) | collective-permute-done | bytes 36896 | tf_op jit(solution)/shard_map/ppermute | solution.py:455
  39.4 0.0 collective-permute-done.7.rest_2_
  39.4 1.3 %merge.1 = bf16[16,4096]{1,0:T(8,128)(2,1)} custom-call(s32[1,128]{1,0:T(1,128)S(1)} %get-tuple-element.26.slots_ref, s32[4,128]{1,0:T(4,128)S(1)} %get-tuple-element.27.rows_ref, bf16[144,128]{1,0:T(8,128)(2,1)S(1)} %get-tuple-element.43.own, bf16[144,128]{1,0:T(8,128)(2,1)S(1)} %collective-permute-done.5.rest_0_, ...), custom_call_target="tpu_custom_call" | custom-call | tf_op jit(solution)/shard_map/merge/pallas_call | solution.py:589
Async XLA Ops:
  9.9 15.8 %collective-permute-start.1 = (bf16[16,2944]{1,0:T(8,128)(2,1)S(1)}, bf16[16,2944]{1,0:T(8,128)(2,1)S(1)}, u32[]{:S(2)}, u32[]{:S(2)}) collective-permute-start(bf16[16,2944]{1,0:T(8,128)(2,1)S(1)} %get-tuple-element.34), channel_id=1, source_target_pairs={{0,8},{4,12},{8,0},{12,4},{1,9},{5,13},{9,1},{13,5},{2,10},{6,14},... | collective-permute-start | bytes 282632 | tf_op jit(solution)/shard_map/ppermute | solution.py:455
  14.0 11.7 %collective-permute-start.2 = (bf16[16,2944]{1,0:T(8,128)(2,1)S(1)}, bf16[16,2944]{1,0:T(8,128)(2,1)S(1)}, u32[]{:S(2)}, u32[]{:S(2)}) collective-permute-start(bf16[16,2944]{1,0:T(8,128)(2,1)S(1)} %get-tuple-element.35), channel_id=1, source_target_pairs={{0,12},{4,8},{8,4},{12,0},{1,13},{5,9},{9,5},{13,1},{2,14},{6,10},... | collective-permute-start | bytes 282632 | tf_op jit(solution)/shard_map/ppermute | solution.py:455
  15.3 11.7 %copy-start.2 = (f32[128]{0:T(128)S(1)}, f32[128]{0:T(128)}, u32[]{:S(2)}) copy-start(f32[128]{0:T(128)} %constant.12) | copy-start | bytes 1540
  15.3 11.7 %copy-start.3 = (f32[128]{0:T(128)S(1)}, f32[128]{0:T(128)}, u32[]{:S(2)}) copy-start(f32[128]{0:T(128)} %constant.13) | copy-start | bytes 1540
  15.3 16.3 %copy-start = (bf16[1024,256]{1,0:T(8,128)(2,1)S(1)}, bf16[1024,256]{1,0:T(8,128)(2,1)}, u32[]{:S(2)}) copy-start(bf16[1024,256]{1,0:T(8,128)(2,1)} %rest_10_.1) | copy-start | bytes 1572868
  15.3 16.3 %copy-start.1 = (bf16[1024,256]{1,0:T(8,128)(2,1)S(1)}, bf16[1024,256]{1,0:T(8,128)(2,1)}, u32[]{:S(2)}) copy-start(bf16[1024,256]{1,0:T(8,128)(2,1)} %rest_11_.1) | copy-start | bytes 1572868
  22.6 9.1 %collective-permute-start.4 = (bf16[16,4736]{1,0:T(8,128)(2,1)S(1)}, bf16[16,4736]{1,0:T(8,128)(2,1)S(1)}, u32[]{:S(2)}, u32[]{:S(2)}) collective-permute-start(bf16[16,4736]{1,0:T(8,128)(2,1)S(1)} %get-tuple-element.40), channel_id=1, source_target_pairs={{0,4},{4,0},{8,12},{12,8},{1,5},{5,1},{9,13},{13,9},{2,6},{6,2},{1... | collective-permute-start | bytes 454664 | tf_op jit(solution)/shard_map/ppermute | solution.py:455
  22.9 6.2 %collective-permute-start = (bf16[16,1792]{1,0:T(8,128)(2,1)S(1)}, bf16[16,1792]{1,0:T(8,128)(2,1)S(1)}, u32[]{:S(2)}, u32[]{:S(2)}) collective-permute-start(bf16[16,1792]{1,0:T(8,128)(2,1)S(1)} %get-tuple-element.33), channel_id=1, source_target_pairs={{0,8},{4,12},{8,0},{12,4},{1,9},{5,13},{9,1},{13,5},{2,10},{6,14},... | collective-permute-start | bytes 172040 | tf_op jit(solution)/shard_map/ppermute | solution.py:455
  25.7 6.0 %collective-permute-start.3 = (bf16[16,1792]{1,0:T(8,128)(2,1)S(1)}, bf16[16,1792]{1,0:T(8,128)(2,1)S(1)}, u32[]{:S(2)}, u32[]{:S(2)}) collective-permute-start(bf16[16,1792]{1,0:T(8,128)(2,1)S(1)} %get-tuple-element.37), channel_id=1, source_target_pairs={{0,12},{4,8},{8,4},{12,0},{1,13},{5,9},{9,5},{13,1},{2,14},{6,10},... | collective-permute-start | bytes 172040 | tf_op jit(solution)/shard_map/ppermute | solution.py:455
  32.8 4.9 %collective-permute-start.5 = (bf16[144,128]{1,0:T(8,128)(2,1)S(1)}, bf16[144,128]{1,0:T(8,128)(2,1)S(1)}, u32[]{:S(2)}, u32[]{:S(2)}) collective-permute-start(bf16[144,128]{1,0:T(8,128)(2,1)S(1)} %get-tuple-element.44), channel_id=1, source_target_pairs={{0,8},{4,12},{8,0},{12,4},{1,9},{5,13},{9,1},{13,5},{2,10},{6,14},... | collective-permute-start | bytes 110600 | tf_op jit(solution)/shard_map/ppermute | solution.py:455
  33.6 5.8 %collective-permute-start.6 = (bf16[144,128]{1,0:T(8,128)(2,1)S(1)}, bf16[144,128]{1,0:T(8,128)(2,1)S(1)}, u32[]{:S(2)}, u32[]{:S(2)}) collective-permute-start(bf16[144,128]{1,0:T(8,128)(2,1)S(1)} %get-tuple-element.45), channel_id=1, source_target_pairs={{0,12},{4,8},{8,4},{12,0},{1,13},{5,9},{9,5},{13,1},{2,14},{6,10},... | collective-permute-start | bytes 110600 | tf_op jit(solution)/shard_map/ppermute | solution.py:455
  35.0 4.4 %collective-permute-start.7 = (bf16[144,128]{1,0:T(8,128)(2,1)S(1)}, bf16[144,128]{1,0:T(8,128)(2,1)S(1)}, u32[]{:S(2)}, u32[]{:S(2)}) collective-permute-start(bf16[144,128]{1,0:T(8,128)(2,1)S(1)} %get-tuple-element.46), channel_id=1, source_target_pairs={{0,4},{4,0},{8,12},{12,8},{1,5},{5,1},{9,13},{13,9},{2,6},{6,2},{1... | collective-permute-start | bytes 110600 | tf_op jit(solution)/shard_map/ppermute | solution.py:455

commit v9 on v8

--- a/solution.py
+++ b/solution.py
@@ -83,14 +83,14 @@
 
 
 def project_kernel(pool, slots, rows_local, me_ref, send, lens, row_len, hidden, gain, *rest):
-    w_query, *rest = rest
+    w_query, w_key, w_value, *rest = rest
     outs, rest = rest[:pool], rest[pool:]
-    lhs, pick, positions, marks, home_rows, home_slots, *rest = rest
+    lhs, pick, positions, marks, home_rows, home_slots, key_out, value_out, *rest = rest
     send_buf, lens_buf, row_len_buf, x_buf, g_buf, *rest = rest
-    *bufs, sums, squares, in_sem, sems = rest
+    query_buf, sums, squares, in_sem, sems = rest
     per = pool * slots
     n_rows, depth = x_buf.shape
-    count, deep, _ = bufs[0].shape
+    count, deep, width = query_buf.shape
     me = me_ref[0]
 
     def named(home, owner, c):
@@ -131,22 +131,17 @@
             lax.rem(place // group, slots) == c, mine, home_rows[pl.ds(k, 1), :]
         )
 
-    chore_steps = max(count // 2, 1)
+    chore_steps = 4
+    spread_chores = count > chore_steps + 1 and pool * per <= 64 and per % chore_steps == 0
 
     def each(do, total, t):
         share = -(-total // chore_steps)
-        if share <= 16 and total % chore_steps == 0:
+        if spread_chores:
             for q in range(share):
                 do(t * share + q)
         else:
-
-            @pl.when(t == 0)
-            def _():
-                def one(i, carry):
-                    do(i)
-                    return carry
-
-                lax.fori_loop(0, total, one, 0)
+            assert isinstance(t, int)
+            pl.loop(0, total)(do)
 
     def scale(t):
         at = pl.multiple_of(t * deep, deep)
@@ -161,41 +156,50 @@
         squares[...] = total
         return left
 
-    starts = [sum(buf.shape[2] for buf in bufs[:n]) for n in range(len(bufs))]
+    cuts = [0, deep // 4, deep // 2, deep] if count > 1 else [0, deep]
 
     def pieces(t):
+        if isinstance(t, int) and t == 0:
+            return [
+                pltpu.make_async_copy(
+                    w_query.at[a:b, :width], query_buf.at[0, a:b], sems.at[0 if n == 0 else count + n]
+                )
+                for n, (a, b) in enumerate(zip(cuts[:-1], cuts[1:]))
+            ]
         rows = pl.ds(pl.multiple_of(t * deep, deep), deep)
-        return [
-            pltpu.make_async_copy(
-                w_query.at[rows, start : start + buf.shape[2]], buf.at[t], sems.at[n, t]
-            )
-            for n, (buf, start) in enumerate(zip(bufs, starts))
-        ]
-
-    begin, advance = stream(count, pieces, [], 2)
+        return [pltpu.make_async_copy(w_query.at[rows, :width], query_buf.at[t], sems.at[t])]
+
+    following = [
+        pltpu.make_async_copy(w, target, in_sem.at[5 + n])
+        for n, (w, target) in enumerate(((w_key, key_out), (w_value, value_out)))
+    ]
+    begin, advance = stream(count, pieces, following, 3)
 
     def use(t):
         advance(t)
         left = scale(t)
-        for copy, buf, start in zip(pieces(t), bufs, starts):
+        for copy in pieces(t):
             copy.wait()
-            add_products(left, buf.at[t], sums.at[:, start : start + buf.shape[2]])
+        add_products(left, query_buf.at[t], sums)
 
     def use_early(t):
         use(t)
-        each(choose, pool * per, t)
-        each(describe, per, t)
+        each(choose, pool * per, t - 1)
+        each(describe, per, t - 1)
+
+    def use_first():
+        advance(0)
+        left = scale(0)
+        for copy, a, b in zip(pieces(0), cuts[:-1], cuts[1:]):
+            copy.wait()
+            add_products(left[:, a:b], query_buf.at[0, a:b], sums)
 
     def use_last(t):
         left = scale(t)
-        if count == 1:
-            each(choose, pool * per, t)
-            each(describe, per, t)
+        for copy in pieces(t):
+            copy.wait()
         chosen = pick[...].astype(jnp.bfloat16)
-        for copy, buf, start in zip(pieces(t), bufs, starts):
-            copy.wait()
-            part = sums.at[:, start : start + buf.shape[2]]
-            spread_products(chosen, left, buf.at[t], part, outs, start)
+        spread_products(chosen, left, query_buf.at[t], sums, outs, 0)
         power = jnp.sum(squares[...], axis=1, keepdims=True)
         at = lax.broadcasted_iota(jnp.int32, (n_rows, HD), 1)
         a, b, c = split3(power)
@@ -224,17 +228,26 @@
     home_slots[...] = jnp.full(home_slots.shape, -1, jnp.int32)
     for one in inputs:
         one.wait()
-    early = min(chore_steps, count - 1)
-    pl.loop(0, early)(use_early)
-    pl.loop(early, count - 1)(use)
+    if not spread_chores:
+        each(choose, pool * per, 0)
+        each(describe, per, 0)
+    if count > 1:
+        use_first()
+    early = 1 + chore_steps if spread_chores else 1
+    if spread_chores:
+        pl.loop(1, early)(use_early)
+    if count > early + 1:
+        pl.loop(early, count - 1)(use)
     use_last(count - 1)
+    for copy in following:
+        copy.wait()
 
 
 def project_rest_kernel(pool, column, lhs, pick, near, w_key, w_value, w_query, *rest):
-    outs, (query_buf, key_buf, value_buf, sums, sems) = rest[:pool], rest[pool:]
+    outs, (query_buf, sums, sems) = rest[:pool], rest[pool:]
     done = near.shape[1]
     count, _, deep = lhs.shape
-    halves, tall, kv_cols = key_buf.shape
+    kv_cols = w_key.shape[1]
     chosen = pick[...].astype(jnp.bfloat16)
     targets = [out.at[:, done:] if k == 1 else out for k, out in enumerate(outs)]
 
@@ -243,41 +256,25 @@
         block = w_query.at[rows, column : column + query_buf.shape[2]]
         return [pltpu.make_async_copy(block, query_buf.at[t], sems.at[t])]
 
-    narrow = [(n, half) for n in range(2) for half in range(halves)]
-    following = [
-        pltpu.make_async_copy(
-            (w_key, w_value)[n].at[half * tall : (half + 1) * tall, :],
-            (key_buf, value_buf)[n].at[half],
-            sems.at[count + n * halves + half],
-        )
-        for n, half in narrow
-    ]
-    begin, advance = stream(count, pieces, following, 4)
+    begin, _ = stream(count, pieces, [], count)
     begin()
     sums[...] = jnp.zeros(sums.shape, jnp.float32)
     outs[1][:, :done] = near[...]
+    for n, w in enumerate((w_key, w_value)):
+        part = 0.0
+        for k in range(count):
+            part = part + jnp.dot(
+                lhs[k], w[k * deep : (k + 1) * deep, :], preferred_element_type=jnp.float32
+            )
+        spread(chosen, part, targets, n * kv_cols)
 
     @pl.loop(0, count - 1)
     def _(t):
-        advance(t)
         pieces(t)[0].wait()
         add_products(lhs[t], query_buf.at[t], sums)
 
-    advance(count - 1)
     pieces(count - 1)[0].wait()
     spread_products(chosen, lhs[count - 1], query_buf.at[count - 1], sums, targets, 2 * kv_cols)
-    part = 0.0
-    for (n, half), copy in zip(narrow, following):
-        copy.wait()
-        for k in range(tall // deep):
-            part = part + jnp.dot(
-                lhs[half * (tall // deep) + k],
-                (key_buf, value_buf)[n][half, k * deep : (k + 1) * deep, :],
-                preferred_element_type=jnp.float32,
-            )
-        if half == halves - 1:
-            spread(chosen, part, targets, n * kv_cols)
-            part = 0.0
 
 
 def attend_kernel(pool, slots, seg, width_d, q_heads, kv_heads, me_ref, *rest):
@@ -498,14 +495,12 @@
     count = depth // deep
     widths = [11 * q_cols // 16, 5 * q_cols // 16]
 
-    left_cols = -(-widths[0] // 512) * 256
-    halves = 2 if count % 2 == 0 else 1
 
     def parts(width):
         return [jax.ShapeDtypeStruct((per, width), jnp.bfloat16)] * pool
 
     operands = [in_hbm(x) for x in (*indices, hidden_in, norm_gain, w_query, w_key, w_value)]
-    *first_terms, lhs, pick, positions, marks, home_rows, home_slots = pl.pallas_call(
+    *first_terms, lhs, pick, positions, marks, home_rows, home_slots, key_in, value_in = pl.pallas_call(
         functools.partial(project_kernel, pool, slots, rows_local),
         out_shape=[
             *parts(widths[0] + HD),
@@ -515,37 +510,36 @@
             jax.ShapeDtypeStruct((2, per * group), jnp.int32),
             jax.ShapeDtypeStruct((pool, HD), jnp.int32),
             jax.ShapeDtypeStruct((1, HD), jnp.int32),
+            jax.ShapeDtypeStruct(w_key.shape, jnp.bfloat16),
+            jax.ShapeDtypeStruct(w_value.shape, jnp.bfloat16),
         ],
-        in_specs=[SMEM] + [HBM] * 6,
-        out_specs=[VMEM] * (pool + 6),
+        in_specs=[SMEM] + [HBM] * 8,
+        out_specs=[VMEM] * (pool + 8),
         scratch_shapes=[
             *(pltpu.SMEM(x.shape, jnp.int32) for x in indices),
             pltpu.VMEM((n_rows, depth), jnp.bfloat16),
             pltpu.VMEM((depth,), jnp.bfloat16),
-            pltpu.VMEM((count, deep, left_cols), jnp.bfloat16),
-            pltpu.VMEM((count, deep, widths[0] - left_cols), jnp.bfloat16),
+            pltpu.VMEM((count, deep, widths[0]), jnp.bfloat16),
             pltpu.VMEM((n_rows, widths[0]), jnp.float32),
             pltpu.VMEM((n_rows, HD), jnp.float32),
-            pltpu.SemaphoreType.DMA((5,)),
-            pltpu.SemaphoreType.DMA((2, count)),
+            pltpu.SemaphoreType.DMA((7,)),
+            pltpu.SemaphoreType.DMA((count + 3,)),
         ],
         compiler_params=pltpu.CompilerParams(vmem_limit_bytes=46 * 2**20),
         name="project",
-    )(me[None], *operands[:6])
+    )(me[None], *operands)
     rest_cols = 2 * kv_cols + widths[1]
     rest_shapes = parts(rest_cols)
     rest_shapes[1] = jax.ShapeDtypeStruct((per, widths[0] + HD + rest_cols), jnp.bfloat16)
     rest_terms = pl.pallas_call(
         functools.partial(project_rest_kernel, pool, widths[0]),
         out_shape=rest_shapes,
-        in_specs=[VMEM] * 3 + [HBM] * 3,
+        in_specs=[VMEM] * 5 + [HBM],
         out_specs=[VMEM] * pool,
         scratch_shapes=[
             pltpu.VMEM((count, deep, widths[1]), jnp.bfloat16),
-            pltpu.VMEM((halves, depth // halves, kv_cols), jnp.bfloat16),
-            pltpu.VMEM((halves, depth // halves, kv_cols), jnp.bfloat16),
             pltpu.VMEM((n_rows, widths[1]), jnp.float32),
-            pltpu.SemaphoreType.DMA((count + 2 * halves,)),
+            pltpu.SemaphoreType.DMA((count,)),
         ],
         compiler_params=pltpu.CompilerParams(vmem_limit_bytes=40 * 2**20),
         cost_estimate=pl.CostEstimate(
@@ -554,7 +548,7 @@
             transcendentals=0,
         ),
         name="project_rest",
-    )(lhs, pick, first_terms[1], operands[6], operands[7], operands[5])
+    )(lhs, pick, first_terms[1], key_in, value_in, operands[5])
     first_terms = exchange(first_terms, range(2, pool))
     rest_terms = list(rest_terms)
     early, late = range(2, pool), range(3, pool)

time: 40.9 us -> 40.4 us (0.988)
  Pallas kernels: 19.5 us -> 18.4 us
  waiting for transfers between devices: 7.65 us -> 8.23 us
    pallas_call x1, Pallas kernels: 7.24 us -> 5.69 us  [body(): pl.pallas_call(functools.partial(project_rest_kernel, pool, widths[0]), o...]
    ppermute x8, waiting for transfers between devices: 7.65 us -> 8.23 us  [exchange(): lax.ppermute(parts[k], 'pool', [(i, i ^ k) for i in range(len(parts))])]
    pallas_call x1, Pallas kernels: 9.88 us -> 10.3 us  [body(): pl.pallas_call(functools.partial(project_kernel, pool, slots, rows_local)...]
  transfers between devices with their start and end apart: 8 -> 8, of which waited for: 4 -> 4; matrix products, arithmetic and copies ran while one was open for 0% -> 0% of each run, Pallas kernels for 18% -> 14%
where the time goes in v9:
time: 40.4 us; the launch traced here: 40.2 us
  Pallas kernels  18.4 us (46%)
  starting transfers between devices  13.5 us (33%)
  waiting for transfers between devices  8.23 us (20%)
    ppermute x8, starting transfers between devices, exchange(): lax.ppermute(parts[k], 'pool', [(i, i ^ k) for i in range(len(parts))])  13.5 us
    pallas_call x1, Pallas kernels, body(): pl.pallas_call(functools.partial(project_kernel, pool, slots, rows_local)...  10.3 us
    ppermute x8, waiting for transfers between devices, exchange(): lax.ppermute(parts[k], 'pool', [(i, i ^ k) for i in range(len(parts))])  8.23 us
    pallas_call x1, Pallas kernels, body(): pl.pallas_call(functools.partial(project_rest_kernel, pool, widths[0]), o...  5.69 us
    pallas_call x1, Pallas kernels, body(): pl.pallas_call(functools.partial(merge_kernel, pool, slots, rows_local, q...  1.33 us
    pallas_call x1, Pallas kernels, body(): pl.pallas_call(functools.partial(attend_kernel, pool, slots, seg, width_d...  1.06 us
  transfers between devices with their start and end apart: 8, of which 4 were waited for; matrix products, arithmetic and copies ran while one was open for 0% of the time, Pallas kernels for 14%

profile of v9, /device:TPU:0, one launch (start us, length us, event | category | flops | bytes accessed | tf_op | source)
XLA Modules:
  0.0 40.2 jit_solution(17049500200975067009)
XLA Ops:
  0.0 10.3 %project.1 = (bf16[16,2944]{1,0:T(8,128)(2,1)S(1)}, bf16[16,2944]{1,0:T(8,128)(2,1)S(1)}, bf16[16,2944]{1,0:T(8,128)(2,1)S(1)}, bf16[16,2944]{1,0:T(8,128)(2,1)S...) custom-call(s32[1]{0:T(128)} %bitcast.me_ref, ...), custom_call_target="tpu_custom_call" | custom-call | tf_op jit(solution)/shard_map/project/pallas_call | solution.py:503
  10.3 4.1 %collective-permute-start.1 = (bf16[16,2944]{1,0:T(8,128)(2,1)S(1)}, bf16[16,2944]{1,0:T(8,128)(2,1)S(1)}, u32[]{:S(2)}, u32[]{:S(2)}) collective-permute-start(bf16[16,2944]{1,0:T(8,128)(2,1)S(1)} %get-tuple-element.38), channel_id=1, source_target_pairs={{0,8},{4,12},{8,0},{12,4},{1,9},{5,13},{9,1},{13,5},{2,10},{6,14},... | collective-permute-start | bytes 282632 | tf_op jit(solution)/shard_map/ppermute | solution.py:452
  14.4 1.4 %collective-permute-start.2 = (bf16[16,2944]{1,0:T(8,128)(2,1)S(1)}, bf16[16,2944]{1,0:T(8,128)(2,1)S(1)}, u32[]{:S(2)}, u32[]{:S(2)}) collective-permute-start(bf16[16,2944]{1,0:T(8,128)(2,1)S(1)} %get-tuple-element.39), channel_id=1, source_target_pairs={{0,12},{4,8},{8,4},{12,0},{1,13},{5,9},{9,5},{13,1},{2,14},{6,10},... | collective-permute-start | bytes 282632 | tf_op jit(solution)/shard_map/ppermute | solution.py:452
  15.8 0.0 copy-start.2
  15.8 0.0 copy-start.3
  15.8 0.0 copy-start
  15.8 0.0 copy-start.1
  15.8 5.7 %project_rest.1 = (bf16[16,1792]{1,0:T(8,128)(2,1)S(1)}, bf16[16,4736]{1,0:T(8,128)(2,1)S(1)}, bf16[16,1792]{1,0:T(8,128)(2,1)S(1)}, bf16[16,1792]{1,0:T(8,128)(2,1)S(1)}) custom-call(bf16[8,64,512]{2,1,0:T(8,128)(2,1)S(1)} %get-tuple-element.31.lhs, f32[64,64]{1,0:T(8,128)S(1)} %get-tuple-element.32.pick, bf16[16,2944]{1,0:T(8,128)(2,1)S(1)} %get-tuple-element.33.near, ...), custom_call_target="tpu_custom_call" | custom-call | flops 939524096 | bytes 15204352 | tf_op jit(solution)/shard_map/project_rest/pallas_call | solution.py:534
  21.5 0.3 collective-permute-start.4
  21.8 2.8 %collective-permute-start = (bf16[16,1792]{1,0:T(8,128)(2,1)S(1)}, bf16[16,1792]{1,0:T(8,128)(2,1)S(1)}, u32[]{:S(2)}, u32[]{:S(2)}) collective-permute-start(bf16[16,1792]{1,0:T(8,128)(2,1)S(1)} %get-tuple-element.37), channel_id=1, source_target_pairs={{0,8},{4,12},{8,0},{12,4},{1,9},{5,13},{9,1},{13,5},{2,10},{6,14},... | collective-permute-start | bytes 172040 | tf_op jit(solution)/shard_map/ppermute | solution.py:452
  24.6 0.0 collective-permute-done.1.rest_4_
  24.6 0.0 collective-permute-done.2.rest_5_
  24.6 1.3 %collective-permute-start.3 = (bf16[16,1792]{1,0:T(8,128)(2,1)S(1)}, bf16[16,1792]{1,0:T(8,128)(2,1)S(1)}, u32[]{:S(2)}, u32[]{:S(2)}) collective-permute-start(bf16[16,1792]{1,0:T(8,128)(2,1)S(1)} %get-tuple-element.41), channel_id=1, source_target_pairs={{0,12},{4,8},{8,4},{12,0},{1,13},{5,9},{9,5},{13,1},{2,14},{6,10},... | collective-permute-start | bytes 172040 | tf_op jit(solution)/shard_map/ppermute | solution.py:452
  25.9 0.0 copy-done.2
  25.9 0.0 copy-done.3
  25.9 0.1 sine_multiply_fusion
  26.0 1.9 %collective-permute-done.rest_2_ = bf16[16,1792]{1,0:T(8,128)(2,1)S(1)} collective-permute-done((bf16[16,1792]{1,0:T(8,128)(2,1)S(1)}, bf16[16,1792]{1,0:T(8,128)(2,1)S(1)}, u32[]{:S(2)}, u32[]{:S(2)}) %collective-permute-start) | collective-permute-done | bytes 57376 | tf_op jit(solution)/shard_map/ppermute | solution.py:452
  27.9 2.6 %collective-permute-done.3.rest_3_ = bf16[16,1792]{1,0:T(8,128)(2,1)S(1)} collective-permute-done((bf16[16,1792]{1,0:T(8,128)(2,1)S(1)}, bf16[16,1792]{1,0:T(8,128)(2,1)S(1)}, u32[]{:S(2)}, u32[]{:S(2)}) %collective-permute-start.3) | collective-permute-done | bytes 57376 | tf_op jit(solution)/shard_map/ppermute | solution.py:452
  30.6 0.0 collective-permute-done.4.rest_6_
  30.6 0.0 copy-done
  30.6 0.0 copy-done.1
  30.6 1.1 %attend.1 = (bf16[144,128]{1,0:T(8,128)(2,1)S(1)}, bf16[144,128]{1,0:T(8,128)(2,1)S(1)}, bf16[144,128]{1,0:T(8,128)(2,1)S(1)}, bf16[144,128]{1,0:T(8,128)(2,1)S(1)}) custom-call(s32[1]{0:T(128)} %bitcast.me_ref, bf16[16,2944]{1,0:T(8,128)(2,1)S(1)} %get-tuple-element.30.rest_0_, bf16[16,1792]{1,0:T(8,128)(2,1)S(1)} %get-tuple-element.36.rest_1_, ...), custom_call_target="tpu_custom_call" | custom-call | tf_op jit(solution)/shard_map/attend/pallas_call | solution.py:571
  31.6 1.4 %collective-permute-start.5 = (bf16[144,128]{1,0:T(8,128)(2,1)S(1)}, bf16[144,128]{1,0:T(8,128)(2,1)S(1)}, u32[]{:S(2)}, u32[]{:S(2)}) collective-permute-start(bf16[144,128]{1,0:T(8,128)(2,1)S(1)} %get-tuple-element.48), channel_id=1, source_target_pairs={{0,8},{4,12},{8,0},{12,4},{1,9},{5,13},{9,1},{13,5},{2,10},{6,14},... | collective-permute-start | bytes 110600 | tf_op jit(solution)/shard_map/ppermute | solution.py:452
  33.1 0.8 %collective-permute-start.6 = (bf16[144,128]{1,0:T(8,128)(2,1)S(1)}, bf16[144,128]{1,0:T(8,128)(2,1)S(1)}, u32[]{:S(2)}, u32[]{:S(2)}) collective-permute-start(bf16[144,128]{1,0:T(8,128)(2,1)S(1)} %get-tuple-element.49), channel_id=1, source_target_pairs={{0,12},{4,8},{8,4},{12,0},{1,13},{5,9},{9,5},{13,1},{2,14},{6,10},... | collective-permute-start | bytes 110600 | tf_op jit(solution)/shard_map/ppermute | solution.py:452
  33.9 1.3 %collective-permute-start.7 = (bf16[144,128]{1,0:T(8,128)(2,1)S(1)}, bf16[144,128]{1,0:T(8,128)(2,1)S(1)}, u32[]{:S(2)}, u32[]{:S(2)}) collective-permute-start(bf16[144,128]{1,0:T(8,128)(2,1)S(1)} %get-tuple-element.50), channel_id=1, source_target_pairs={{0,4},{4,0},{8,12},{12,8},{1,5},{5,1},{9,13},{13,9},{2,6},{6,2},{1... | collective-permute-start | bytes 110600 | tf_op jit(solution)/shard_map/ppermute | solution.py:452
  35.2 1.4 %collective-permute-done.5.rest_0_ = bf16[144,128]{1,0:T(8,128)(2,1)S(1)} collective-permute-done((bf16[144,128]{1,0:T(8,128)(2,1)S(1)}, bf16[144,128]{1,0:T(8,128)(2,1)S(1)}, u32[]{:S(2)}, u32[]{:S(2)}) %collective-permute-start.5) | collective-permute-done | bytes 36896 | tf_op jit(solution)/shard_map/ppermute | solution.py:452
  36.5 2.3 %collective-permute-done.6.rest_1_ = bf16[144,128]{1,0:T(8,128)(2,1)S(1)} collective-permute-done((bf16[144,128]{1,0:T(8,128)(2,1)S(1)}, bf16[144,128]{1,0:T(8,128)(2,1)S(1)}, u32[]{:S(2)}, u32[]{:S(2)}) %collective-permute-start.6) | collective-permute-done | bytes 36896 | tf_op jit(solution)/shard_map/ppermute | solution.py:452
  38.8 0.0 collective-permute-done.7.rest_2_
  38.8 1.3 %merge.1 = bf16[16,4096]{1,0:T(8,128)(2,1)} custom-call(s32[1,128]{1,0:T(1,128)S(1)} %get-tuple-element.28.slots_ref, s32[4,128]{1,0:T(4,128)S(1)} %get-tuple-element.29.rows_ref, bf16[144,128]{1,0:T(8,128)(2,1)S(1)} %get-tuple-element.47.own, bf16[144,128]{1,0:T(8,128)(2,1)S(1)} %collective-permute-done.5.rest_0_, ...), custom_call_target="tpu_custom_call" | custom-call | tf_op jit(solution)/shard_map/merge/pallas_call | solution.py:583
Async XLA Ops:
  10.3 14.3 %collective-permute-start.1 = (bf16[16,2944]{1,0:T(8,128)(2,1)S(1)}, bf16[16,2944]{1,0:T(8,128)(2,1)S(1)}, u32[]{:S(2)}, u32[]{:S(2)}) collective-permute-start(bf16[16,2944]{1,0:T(8,128)(2,1)S(1)} %get-tuple-element.38), channel_id=1, source_target_pairs={{0,8},{4,12},{8,0},{12,4},{1,9},{5,13},{9,1},{13,5},{2,10},{6,14},... | collective-permute-start | bytes 282632 | tf_op jit(solution)/shard_map/ppermute | solution.py:452
  14.4 10.2 %collective-permute-start.2 = (bf16[16,2944]{1,0:T(8,128)(2,1)S(1)}, bf16[16,2944]{1,0:T(8,128)(2,1)S(1)}, u32[]{:S(2)}, u32[]{:S(2)}) collective-permute-start(bf16[16,2944]{1,0:T(8,128)(2,1)S(1)} %get-tuple-element.39), channel_id=1, source_target_pairs={{0,12},{4,8},{8,4},{12,0},{1,13},{5,9},{9,5},{13,1},{2,14},{6,10},... | collective-permute-start | bytes 282632 | tf_op jit(solution)/shard_map/ppermute | solution.py:452
  15.8 10.2 %copy-start.2 = (f32[128]{0:T(128)S(1)}, f32[128]{0:T(128)}, u32[]{:S(2)}) copy-start(f32[128]{0:T(128)} %constant.12) | copy-start | bytes 1540
  15.8 10.2 %copy-start.3 = (f32[128]{0:T(128)S(1)}, f32[128]{0:T(128)}, u32[]{:S(2)}) copy-start(f32[128]{0:T(128)} %constant.13) | copy-start | bytes 1540
  15.8 14.8 %copy-start = (bf16[1024,256]{1,0:T(8,128)(2,1)S(1)}, bf16[1024,256]{1,0:T(8,128)(2,1)}, u32[]{:S(2)}) copy-start(bf16[1024,256]{1,0:T(8,128)(2,1)} %rest_10_.1) | copy-start | bytes 1572868
  15.8 14.8 %copy-start.1 = (bf16[1024,256]{1,0:T(8,128)(2,1)S(1)}, bf16[1024,256]{1,0:T(8,128)(2,1)}, u32[]{:S(2)}) copy-start(bf16[1024,256]{1,0:T(8,128)(2,1)} %rest_11_.1) | copy-start | bytes 1572868
  21.5 9.1 %collective-permute-start.4 = (bf16[16,4736]{1,0:T(8,128)(2,1)S(1)}, bf16[16,4736]{1,0:T(8,128)(2,1)S(1)}, u32[]{:S(2)}, u32[]{:S(2)}) collective-permute-start(bf16[16,4736]{1,0:T(8,128)(2,1)S(1)} %get-tuple-element.44), channel_id=1, source_target_pairs={{0,4},{4,0},{8,12},{12,8},{1,5},{5,1},{9,13},{13,9},{2,6},{6,2},{1... | collective-permute-start | bytes 454664 | tf_op jit(solution)/shard_map/ppermute | solution.py:452
  21.8 6.1 %collective-permute-start = (bf16[16,1792]{1,0:T(8,128)(2,1)S(1)}, bf16[16,1792]{1,0:T(8,128)(2,1)S(1)}, u32[]{:S(2)}, u32[]{:S(2)}) collective-permute-start(bf16[16,1792]{1,0:T(8,128)(2,1)S(1)} %get-tuple-element.37), channel_id=1, source_target_pairs={{0,8},{4,12},{8,0},{12,4},{1,9},{5,13},{9,1},{13,5},{2,10},{6,14},... | collective-permute-start | bytes 172040 | tf_op jit(solution)/shard_map/ppermute | solution.py:452
  24.6 6.0 %collective-permute-start.3 = (bf16[16,1792]{1,0:T(8,128)(2,1)S(1)}, bf16[16,1792]{1,0:T(8,128)(2,1)S(1)}, u32[]{:S(2)}, u32[]{:S(2)}) collective-permute-start(bf16[16,1792]{1,0:T(8,128)(2,1)S(1)} %get-tuple-element.41), channel_id=1, source_target_pairs={{0,12},{4,8},{8,4},{12,0},{1,13},{5,9},{9,5},{13,1},{2,14},{6,10},... | collective-permute-start | bytes 172040 | tf_op jit(solution)/shard_map/ppermute | solution.py:452
  31.6 4.9 %collective-permute-start.5 = (bf16[144,128]{1,0:T(8,128)(2,1)S(1)}, bf16[144,128]{1,0:T(8,128)(2,1)S(1)}, u32[]{:S(2)}, u32[]{:S(2)}) collective-permute-start(bf16[144,128]{1,0:T(8,128)(2,1)S(1)} %get-tuple-element.48), channel_id=1, source_target_pairs={{0,8},{4,12},{8,0},{12,4},{1,9},{5,13},{9,1},{13,5},{2,10},{6,14},... | collective-permute-start | bytes 110600 | tf_op jit(solution)/shard_map/ppermute | solution.py:452
  33.1 5.8 %collective-permute-start.6 = (bf16[144,128]{1,0:T(8,128)(2,1)S(1)}, bf16[144,128]{1,0:T(8,128)(2,1)S(1)}, u32[]{:S(2)}, u32[]{:S(2)}) collective-permute-start(bf16[144,128]{1,0:T(8,128)(2,1)S(1)} %get-tuple-element.49), channel_id=1, source_target_pairs={{0,12},{4,8},{8,4},{12,0},{1,13},{5,9},{9,5},{13,1},{2,14},{6,10},... | collective-permute-start | bytes 110600 | tf_op jit(solution)/shard_map/ppermute | solution.py:452
  33.9 4.9 %collective-permute-start.7 = (bf16[144,128]{1,0:T(8,128)(2,1)S(1)}, bf16[144,128]{1,0:T(8,128)(2,1)S(1)}, u32[]{:S(2)}, u32[]{:S(2)}) collective-permute-start(bf16[144,128]{1,0:T(8,128)(2,1)S(1)} %get-tuple-element.50), channel_id=1, source_target_pairs={{0,4},{4,0},{8,12},{12,8},{1,5},{5,1},{9,13},{13,9},{2,6},{6,2},{1... | collective-permute-start | bytes 110600 | tf_op jit(solution)/shard_map/ppermute | solution.py:452

commit v10 on v9

--- a/solution.py
+++ b/solution.py
@@ -14,12 +14,17 @@
 LOW = -1e30
 DEEP = 512
 LEVELS = 16
+TILE = 1536
 
 
 def divides(width, limit):
     while width % limit:
         limit //= 2
     return limit
+
+
+def widest(width, limit):
+    return max(tile for tile in range(128, limit + 1, 128) if width % tile == 0)
 
 
 def split3(x):
@@ -55,7 +60,7 @@
 
 def add_products(left, block, sums):
     width = block.shape[1]
-    tile = divides(width, 512)
+    tile = widest(width, TILE)
     for at in range(0, width, tile):
         sums[:, at : at + tile] += jnp.dot(
             left, block[:, at : at + tile], preferred_element_type=jnp.float32
@@ -74,7 +79,7 @@
 
 def spread_products(chosen, left, block, sums, outs, to):
     width = block.shape[1]
-    tile = divides(width, 512)
+    tile = widest(width, TILE)
     for at in range(0, width, tile):
         done = sums[:, at : at + tile] + jnp.dot(
             left, block[:, at : at + tile], preferred_element_type=jnp.float32
@@ -85,7 +90,7 @@
 def project_kernel(pool, slots, rows_local, me_ref, send, lens, row_len, hidden, gain, *rest):
     w_query, w_key, w_value, *rest = rest
     outs, rest = rest[:pool], rest[pool:]
-    lhs, pick, positions, marks, home_rows, home_slots, key_out, value_out, *rest = rest
+    lhs, pick, positions, marks, home_rows, home_slots, narrow, *rest = rest
     send_buf, lens_buf, row_len_buf, x_buf, g_buf, *rest = rest
     query_buf, sums, squares, in_sem, sems = rest
     per = pool * slots
@@ -148,7 +153,7 @@
         x = x_buf[:, pl.ds(at, deep)].astype(jnp.float32)
         gains = g_buf[pl.ds(at, deep)].astype(jnp.float32).reshape(1, deep)
         left = (x * gains).astype(jnp.bfloat16)
-        lhs[t] = left
+        lhs[:, pl.ds(at, deep)] = left
         squared = x * x
         total = squares[...]
         for column in range(0, deep, HD):
@@ -156,6 +161,7 @@
         squares[...] = total
         return left
 
+    kv_cols = w_key.shape[1]
     cuts = [0, deep // 4, deep // 2, deep] if count > 1 else [0, deep]
 
     def pieces(t):
@@ -171,7 +177,9 @@
 
     following = [
         pltpu.make_async_copy(w, target, in_sem.at[5 + n])
-        for n, (w, target) in enumerate(((w_key, key_out), (w_value, value_out)))
+        for n, (w, target) in enumerate(
+            ((w_key, narrow.at[:, :kv_cols]), (w_value, narrow.at[:, kv_cols:]))
+        )
     ]
     begin, advance = stream(count, pieces, following, 3)
 
@@ -243,11 +251,10 @@
         copy.wait()
 
 
-def project_rest_kernel(pool, column, lhs, pick, near, w_key, w_value, w_query, *rest):
+def project_rest_kernel(pool, column, lhs, pick, near, narrow, w_query, *rest):
     outs, (query_buf, sums, sems) = rest[:pool], rest[pool:]
     done = near.shape[1]
-    count, _, deep = lhs.shape
-    kv_cols = w_key.shape[1]
+    count, deep, _ = query_buf.shape
     chosen = pick[...].astype(jnp.bfloat16)
     targets = [out.at[:, done:] if k == 1 else out for k, out in enumerate(outs)]
 
@@ -260,21 +267,17 @@
     begin()
     sums[...] = jnp.zeros(sums.shape, jnp.float32)
     outs[1][:, :done] = near[...]
-    for n, w in enumerate((w_key, w_value)):
-        part = 0.0
-        for k in range(count):
-            part = part + jnp.dot(
-                lhs[k], w[k * deep : (k + 1) * deep, :], preferred_element_type=jnp.float32
-            )
-        spread(chosen, part, targets, n * kv_cols)
+    part = jnp.dot(lhs[...], narrow[...], preferred_element_type=jnp.float32)
+    spread(chosen, part, targets, 0)
 
     @pl.loop(0, count - 1)
     def _(t):
         pieces(t)[0].wait()
-        add_products(lhs[t], query_buf.at[t], sums)
+        add_products(lhs[:, pl.ds(pl.multiple_of(t * deep, deep), deep)], query_buf.at[t], sums)
 
     pieces(count - 1)[0].wait()
-    spread_products(chosen, lhs[count - 1], query_buf.at[count - 1], sums, targets, 2 * kv_cols)
+    left = lhs[:, (count - 1) * deep :]
+    spread_products(chosen, left, query_buf.at[count - 1], sums, targets, narrow.shape[1])
 
 
 def attend_kernel(pool, slots, seg, width_d, q_heads, kv_heads, me_ref, *rest):
@@ -493,28 +496,27 @@
         indices = [send_row.reshape(-1), piece_len.reshape(-1), row_len]
     deep = divides(depth, DEEP)
     count = depth // deep
-    widths = [11 * q_cols // 16, 5 * q_cols // 16]
+    widths = [5 * q_cols // 8, 3 * q_cols // 8]
 
 
     def parts(width):
         return [jax.ShapeDtypeStruct((per, width), jnp.bfloat16)] * pool
 
     operands = [in_hbm(x) for x in (*indices, hidden_in, norm_gain, w_query, w_key, w_value)]
-    *first_terms, lhs, pick, positions, marks, home_rows, home_slots, key_in, value_in = pl.pallas_call(
+    *first_terms, lhs, pick, positions, marks, home_rows, home_slots, narrow = pl.pallas_call(
         functools.partial(project_kernel, pool, slots, rows_local),
         out_shape=[
             *parts(widths[0] + HD),
-            jax.ShapeDtypeStruct((count, n_rows, deep), jnp.bfloat16),
+            jax.ShapeDtypeStruct((n_rows, depth), jnp.bfloat16),
             jax.ShapeDtypeStruct((pool * per, n_rows), jnp.float32),
             jax.ShapeDtypeStruct((per, HD), jnp.float32),
             jax.ShapeDtypeStruct((2, per * group), jnp.int32),
             jax.ShapeDtypeStruct((pool, HD), jnp.int32),
             jax.ShapeDtypeStruct((1, HD), jnp.int32),
-            jax.ShapeDtypeStruct(w_key.shape, jnp.bfloat16),
-            jax.ShapeDtypeStruct(w_value.shape, jnp.bfloat16),
+            jax.ShapeDtypeStruct((depth, 2 * kv_cols), jnp.bfloat16),
         ],
         in_specs=[SMEM] + [HBM] * 8,
-        out_specs=[VMEM] * (pool + 8),
+        out_specs=[VMEM] * (pool + 7),
         scratch_shapes=[
             *(pltpu.SMEM(x.shape, jnp.int32) for x in indices),
             pltpu.VMEM((n_rows, depth), jnp.bfloat16),
@@ -534,7 +536,7 @@
     rest_terms = pl.pallas_call(
         functools.partial(project_rest_kernel, pool, widths[0]),
         out_shape=rest_shapes,
-        in_specs=[VMEM] * 5 + [HBM],
+        in_specs=[VMEM] * 4 + [HBM],
         out_specs=[VMEM] * pool,
         scratch_shapes=[
             pltpu.VMEM((count, deep, widths[1]), jnp.bfloat16),
@@ -548,7 +550,7 @@
             transcendentals=0,
         ),
         name="project_rest",
-    )(lhs, pick, first_terms[1], key_in, value_in, operands[5])
+    )(lhs, pick, first_terms[1], narrow, operands[5])
     first_terms = exchange(first_terms, range(2, pool))
     rest_terms = list(rest_terms)
     early, late = range(2, pool), range(3, pool)

time: 40.4 us -> 39.6 us (0.980)
  Pallas kernels: 18.4 us -> 17.2 us
  waiting for transfers between devices: 8.23 us -> 8.72 us
    pallas_call x1, Pallas kernels: 10.3 us -> 8.8 us  [body(): pl.pallas_call(functools.partial(project_kernel, pool, slots, rows_local)...]
    ppermute x8, waiting for transfers between devices: 8.23 us -> 8.72 us  [exchange(): lax.ppermute(parts[k], 'pool', [(i, i ^ k) for i in range(len(parts))])]
  transfers between devices with their start and end apart: 8 -> 8, of which waited for: 4 -> 5; matrix products, arithmetic and copies ran while one was open for 0% -> 0% of each run, Pallas kernels for 14% -> 15%
where the time goes in v10:
time: 39.6 us; the launch traced here: 39.5 us
  Pallas kernels  17.2 us (43%)
  starting transfers between devices  13.5 us (34%)
  waiting for transfers between devices  8.72 us (22%)
    ppermute x8, starting transfers between devices, exchange(): lax.ppermute(parts[k], 'pool', [(i, i ^ k) for i in range(len(parts))])  13.5 us
    pallas_call x1, Pallas kernels, body(): pl.pallas_call(functools.partial(project_kernel, pool, slots, rows_local)...  8.8 us
    ppermute x8, waiting for transfers between devices, exchange(): lax.ppermute(parts[k], 'pool', [(i, i ^ k) for i in range(len(parts))])  8.72 us
    pallas_call x1, Pallas kernels, body(): pl.pallas_call(functools.partial(project_rest_kernel, pool, widths[0]), o...  5.97 us
    pallas_call x1, Pallas kernels, body(): pl.pallas_call(functools.partial(merge_kernel, pool, slots, rows_local, q...  1.33 us
    pallas_call x1, Pallas kernels, body(): pl.pallas_call(functools.partial(attend_kernel, pool, slots, seg, width_d...  1.06 us
  transfers between devices with their start and end apart: 8, of which 5 were waited for; matrix products, arithmetic and copies ran while one was open for 0% of the time, Pallas kernels for 15%

profile of v10, /device:TPU:0, one launch (start us, length us, event | category | flops | bytes accessed | tf_op | source)
XLA Modules:
  0.0 39.5 jit_solution(9372300048361129296)
XLA Ops:
  0.0 8.8 %project.1 = (bf16[16,2688]{1,0:T(8,128)(2,1)S(1)}, bf16[16,2688]{1,0:T(8,128)(2,1)S(1)}, bf16[16,2688]{1,0:T(8,128)(2,1)S(1)}, bf16[16,2688]{1,0:T(8,128)(2,1)S...) custom-call(s32[1]{0:T(128)} %bitcast.me_ref, ...), custom_call_target="tpu_custom_call" | custom-call | tf_op jit(solution)/shard_map/project/pallas_call | solution.py:506
  8.8 4.1 %collective-permute-start.1 = (bf16[16,2688]{1,0:T(8,128)(2,1)S(1)}, bf16[16,2688]{1,0:T(8,128)(2,1)S(1)}, u32[]{:S(2)}, u32[]{:S(2)}) collective-permute-start(bf16[16,2688]{1,0:T(8,128)(2,1)S(1)} %get-tuple-element.36), channel_id=1, source_target_pairs={{0,8},{4,12},{8,0},{12,4},{1,9},{5,13},{9,1},{13,5},{2,10},{6,14},... | collective-permute-start | bytes 258056 | tf_op jit(solution)/shard_map/ppermute | solution.py:455
  12.9 1.3 %collective-permute-start.2 = (bf16[16,2688]{1,0:T(8,128)(2,1)S(1)}, bf16[16,2688]{1,0:T(8,128)(2,1)S(1)}, u32[]{:S(2)}, u32[]{:S(2)}) collective-permute-start(bf16[16,2688]{1,0:T(8,128)(2,1)S(1)} %get-tuple-element.37), channel_id=1, source_target_pairs={{0,12},{4,8},{8,4},{12,0},{1,13},{5,9},{9,5},{13,1},{2,14},{6,10},... | collective-permute-start | bytes 258056 | tf_op jit(solution)/shard_map/ppermute | solution.py:455
  14.3 0.0 copy-start.2
  14.3 0.0 copy-start.3
  14.3 0.0 copy-start
  14.3 0.0 copy-start.1
  14.3 6.0 %project_rest.1 = (bf16[16,2048]{1,0:T(8,128)(2,1)S(1)}, bf16[16,4736]{1,0:T(8,128)(2,1)S(1)}, bf16[16,2048]{1,0:T(8,128)(2,1)S(1)}, bf16[16,2048]{1,0:T(8,128)(2,1)S(1)}) custom-call(bf16[64,4096]{1,0:T(8,128)(2,1)S(1)} %get-tuple-element.30.lhs, f32[64,64]{1,0:T(8,128)S(1)} %get-tuple-element.31.pick, bf16[16,2688]{1,0:T(8,128)(2,1)S(1)} %get-tuple-element.32.near, ...), custom_call_target="tpu_custom_call" | custom-call | flops 1073741824 | bytes 17301504 | tf_op jit(solution)/shard_map/project_rest/pallas_call | solution.py:536
  20.3 0.3 collective-permute-start.4
  20.6 2.8 %collective-permute-start = (bf16[16,2048]{1,0:T(8,128)(2,1)S(1)}, bf16[16,2048]{1,0:T(8,128)(2,1)S(1)}, u32[]{:S(2)}, u32[]{:S(2)}) collective-permute-start(bf16[16,2048]{1,0:T(8,128)(2,1)S(1)} %get-tuple-element.35), channel_id=1, source_target_pairs={{0,8},{4,12},{8,0},{12,4},{1,9},{5,13},{9,1},{13,5},{2,10},{6,14},... | collective-permute-start | bytes 196616 | tf_op jit(solution)/shard_map/ppermute | solution.py:455
  23.4 0.0 collective-permute-done.1.rest_4_
  23.4 0.0 collective-permute-done.2.rest_5_
  23.4 1.4 %collective-permute-start.3 = (bf16[16,2048]{1,0:T(8,128)(2,1)S(1)}, bf16[16,2048]{1,0:T(8,128)(2,1)S(1)}, u32[]{:S(2)}, u32[]{:S(2)}) collective-permute-start(bf16[16,2048]{1,0:T(8,128)(2,1)S(1)} %get-tuple-element.39), channel_id=1, source_target_pairs={{0,12},{4,8},{8,4},{12,0},{1,13},{5,9},{9,5},{13,1},{2,14},{6,10},... | collective-permute-start | bytes 196616 | tf_op jit(solution)/shard_map/ppermute | solution.py:455
  24.7 0.0 copy-done.2
  24.7 0.0 copy-done.3
  24.7 0.1 sine_multiply_fusion
  24.8 2.5 %collective-permute-done.rest_2_ = bf16[16,2048]{1,0:T(8,128)(2,1)S(1)} collective-permute-done((bf16[16,2048]{1,0:T(8,128)(2,1)S(1)}, bf16[16,2048]{1,0:T(8,128)(2,1)S(1)}, u32[]{:S(2)}, u32[]{:S(2)}) %collective-permute-start) | collective-permute-done | bytes 65568 | tf_op jit(solution)/shard_map/ppermute | solution.py:455
  27.2 2.2 %collective-permute-done.3.rest_3_ = bf16[16,2048]{1,0:T(8,128)(2,1)S(1)} collective-permute-done((bf16[16,2048]{1,0:T(8,128)(2,1)S(1)}, bf16[16,2048]{1,0:T(8,128)(2,1)S(1)}, u32[]{:S(2)}, u32[]{:S(2)}) %collective-permute-start.3) | collective-permute-done | bytes 65568 | tf_op jit(solution)/shard_map/ppermute | solution.py:455
  29.5 0.0 collective-permute-done.4.rest_6_
  29.5 0.0 copy-done
  29.5 0.0 copy-done.1
  29.5 1.1 %attend.1 = (bf16[144,128]{1,0:T(8,128)(2,1)S(1)}, bf16[144,128]{1,0:T(8,128)(2,1)S(1)}, bf16[144,128]{1,0:T(8,128)(2,1)S(1)}, bf16[144,128]{1,0:T(8,128)(2,1)S(1)}) custom-call(s32[1]{0:T(128)} %bitcast.me_ref, bf16[16,2688]{1,0:T(8,128)(2,1)S(1)} %get-tuple-element.29.rest_0_, bf16[16,2048]{1,0:T(8,128)(2,1)S(1)} %get-tuple-element.34.rest_1_, ...), custom_call_target="tpu_custom_call" | custom-call | tf_op jit(solution)/shard_map/attend/pallas_call | solution.py:573
  30.6 1.5 %collective-permute-start.5 = (bf16[144,128]{1,0:T(8,128)(2,1)S(1)}, bf16[144,128]{1,0:T(8,128)(2,1)S(1)}, u32[]{:S(2)}, u32[]{:S(2)}) collective-permute-start(bf16[144,128]{1,0:T(8,128)(2,1)S(1)} %get-tuple-element.46), channel_id=1, source_target_pairs={{0,8},{4,12},{8,0},{12,4},{1,9},{5,13},{9,1},{13,5},{2,10},{6,14},... | collective-permute-start | bytes 110600 | tf_op jit(solution)/shard_map/ppermute | solution.py:455
  32.0 1.7 %collective-permute-start.6 = (bf16[144,128]{1,0:T(8,128)(2,1)S(1)}, bf16[144,128]{1,0:T(8,128)(2,1)S(1)}, u32[]{:S(2)}, u32[]{:S(2)}) collective-permute-start(bf16[144,128]{1,0:T(8,128)(2,1)S(1)} %get-tuple-element.47), channel_id=1, source_target_pairs={{0,12},{4,8},{8,4},{12,0},{1,13},{5,9},{9,5},{13,1},{2,14},{6,10},... | collective-permute-start | bytes 110600 | tf_op jit(solution)/shard_map/ppermute | solution.py:455
  33.8 0.3 collective-permute-start.7
  34.1 1.8 %collective-permute-done.5.rest_0_ = bf16[144,128]{1,0:T(8,128)(2,1)S(1)} collective-permute-done((bf16[144,128]{1,0:T(8,128)(2,1)S(1)}, bf16[144,128]{1,0:T(8,128)(2,1)S(1)}, u32[]{:S(2)}, u32[]{:S(2)}) %collective-permute-start.5) | collective-permute-done | bytes 36896 | tf_op jit(solution)/shard_map/ppermute | solution.py:455
  35.9 2.0 %collective-permute-done.6.rest_1_ = bf16[144,128]{1,0:T(8,128)(2,1)S(1)} collective-permute-done((bf16[144,128]{1,0:T(8,128)(2,1)S(1)}, bf16[144,128]{1,0:T(8,128)(2,1)S(1)}, u32[]{:S(2)}, u32[]{:S(2)}) %collective-permute-start.6) | collective-permute-done | bytes 36896 | tf_op jit(solution)/shard_map/ppermute | solution.py:455
  37.9 0.2 collective-permute-done.7.rest_2_
  38.1 1.3 %merge.1 = bf16[16,4096]{1,0:T(8,128)(2,1)} custom-call(s32[1,128]{1,0:T(1,128)S(1)} %get-tuple-element.27.slots_ref, s32[4,128]{1,0:T(4,128)S(1)} %get-tuple-element.28.rows_ref, bf16[144,128]{1,0:T(8,128)(2,1)S(1)} %get-tuple-element.45.own, bf16[144,128]{1,0:T(8,128)(2,1)S(1)} %collective-permute-done.5.rest_0_, ...), custom_call_target="tpu_custom_call" | custom-call | tf_op jit(solution)/shard_map/merge/pallas_call | solution.py:585
Async XLA Ops:
  8.8 14.5 %collective-permute-start.1 = (bf16[16,2688]{1,0:T(8,128)(2,1)S(1)}, bf16[16,2688]{1,0:T(8,128)(2,1)S(1)}, u32[]{:S(2)}, u32[]{:S(2)}) collective-permute-start(bf16[16,2688]{1,0:T(8,128)(2,1)S(1)} %get-tuple-element.36), channel_id=1, source_target_pairs={{0,8},{4,12},{8,0},{12,4},{1,9},{5,13},{9,1},{13,5},{2,10},{6,14},... | collective-permute-start | bytes 258056 | tf_op jit(solution)/shard_map/ppermute | solution.py:455
  12.9 10.4 %collective-permute-start.2 = (bf16[16,2688]{1,0:T(8,128)(2,1)S(1)}, bf16[16,2688]{1,0:T(8,128)(2,1)S(1)}, u32[]{:S(2)}, u32[]{:S(2)}) collective-permute-start(bf16[16,2688]{1,0:T(8,128)(2,1)S(1)} %get-tuple-element.37), channel_id=1, source_target_pairs={{0,12},{4,8},{8,4},{12,0},{1,13},{5,9},{9,5},{13,1},{2,14},{6,10},... | collective-permute-start | bytes 258056 | tf_op jit(solution)/shard_map/ppermute | solution.py:455
  14.3 10.5 %copy-start.2 = (f32[128]{0:T(128)S(1)}, f32[128]{0:T(128)}, u32[]{:S(2)}) copy-start(f32[128]{0:T(128)} %constant.12) | copy-start | bytes 1540
  14.3 10.5 %copy-start.3 = (f32[128]{0:T(128)S(1)}, f32[128]{0:T(128)}, u32[]{:S(2)}) copy-start(f32[128]{0:T(128)} %constant.13) | copy-start | bytes 1540
  14.3 15.2 %copy-start = (bf16[1024,256]{1,0:T(8,128)(2,1)S(1)}, bf16[1024,256]{1,0:T(8,128)(2,1)}, u32[]{:S(2)}) copy-start(bf16[1024,256]{1,0:T(8,128)(2,1)} %rest_10_.1) | copy-start | bytes 1572868
  14.3 15.2 %copy-start.1 = (bf16[1024,256]{1,0:T(8,128)(2,1)S(1)}, bf16[1024,256]{1,0:T(8,128)(2,1)}, u32[]{:S(2)}) copy-start(bf16[1024,256]{1,0:T(8,128)(2,1)} %rest_11_.1) | copy-start | bytes 1572868
  20.3 9.2 %collective-permute-start.4 = (bf16[16,4736]{1,0:T(8,128)(2,1)S(1)}, bf16[16,4736]{1,0:T(8,128)(2,1)S(1)}, u32[]{:S(2)}, u32[]{:S(2)}) collective-permute-start(bf16[16,4736]{1,0:T(8,128)(2,1)S(1)} %get-tuple-element.42), channel_id=1, source_target_pairs={{0,4},{4,0},{8,12},{12,8},{1,5},{5,1},{9,13},{13,9},{2,6},{6,2},{1... | collective-permute-start | bytes 454664 | tf_op jit(solution)/shard_map/ppermute | solution.py:455
  20.6 6.7 %collective-permute-start = (bf16[16,2048]{1,0:T(8,128)(2,1)S(1)}, bf16[16,2048]{1,0:T(8,128)(2,1)S(1)}, u32[]{:S(2)}, u32[]{:S(2)}) collective-permute-start(bf16[16,2048]{1,0:T(8,128)(2,1)S(1)} %get-tuple-element.35), channel_id=1, source_target_pairs={{0,8},{4,12},{8,0},{12,4},{1,9},{5,13},{9,1},{13,5},{2,10},{6,14},... | collective-permute-start | bytes 196616 | tf_op jit(solution)/shard_map/ppermute | solution.py:455
  23.4 6.1 %collective-permute-start.3 = (bf16[16,2048]{1,0:T(8,128)(2,1)S(1)}, bf16[16,2048]{1,0:T(8,128)(2,1)S(1)}, u32[]{:S(2)}, u32[]{:S(2)}) collective-permute-start(bf16[16,2048]{1,0:T(8,128)(2,1)S(1)} %get-tuple-element.39), channel_id=1, source_target_pairs={{0,12},{4,8},{8,4},{12,0},{1,13},{5,9},{9,5},{13,1},{2,14},{6,10},... | collective-permute-start | bytes 196616 | tf_op jit(solution)/shard_map/ppermute | solution.py:455
  30.6 5.3 %collective-permute-start.5 = (bf16[144,128]{1,0:T(8,128)(2,1)S(1)}, bf16[144,128]{1,0:T(8,128)(2,1)S(1)}, u32[]{:S(2)}, u32[]{:S(2)}) collective-permute-start(bf16[144,128]{1,0:T(8,128)(2,1)S(1)} %get-tuple-element.46), channel_id=1, source_target_pairs={{0,8},{4,12},{8,0},{12,4},{1,9},{5,13},{9,1},{13,5},{2,10},{6,14},... | collective-permute-start | bytes 110600 | tf_op jit(solution)/shard_map/ppermute | solution.py:455
  32.0 5.9 %collective-permute-start.6 = (bf16[144,128]{1,0:T(8,128)(2,1)S(1)}, bf16[144,128]{1,0:T(8,128)(2,1)S(1)}, u32[]{:S(2)}, u32[]{:S(2)}) collective-permute-start(bf16[144,128]{1,0:T(8,128)(2,1)S(1)} %get-tuple-element.47), channel_id=1, source_target_pairs={{0,12},{4,8},{8,4},{12,0},{1,13},{5,9},{9,5},{13,1},{2,14},{6,10},... | collective-permute-start | bytes 110600 | tf_op jit(solution)/shard_map/ppermute | solution.py:455
  33.8 4.4 %collective-permute-start.7 = (bf16[144,128]{1,0:T(8,128)(2,1)S(1)}, bf16[144,128]{1,0:T(8,128)(2,1)S(1)}, u32[]{:S(2)}, u32[]{:S(2)}) collective-permute-start(bf16[144,128]{1,0:T(8,128)(2,1)S(1)} %get-tuple-element.48), channel_id=1, source_target_pairs={{0,4},{4,0},{8,12},{12,8},{1,5},{5,1},{9,13},{13,9},{2,6},{6,2},{1... | collective-permute-start | bytes 110600 | tf_op jit(solution)/shard_map/ppermute | solution.py:455

commit v11 on v10

--- a/solution.py
+++ b/solution.py
@@ -396,7 +396,7 @@
 
 
 def merge_kernel(pool, slots, rows_local, q_heads, kv_heads, slots_ref, rows_ref, own, *rest):
-    found, (out, scaled) = [own, rest[pool - 2], *rest[: pool - 2]], rest[pool - 1 :]
+    found, (out, buf, scaled, sems) = [own, rest[pool - 2], *rest[: pool - 2]], rest[pool - 1 :]
     per = pool * slots
     group = q_heads // kv_heads
     block = slots * q_heads
@@ -440,13 +440,22 @@
                 )
     row = lax.broadcasted_iota(jnp.int32, (rows_local, 2 * per), 0)
     match = (slots_ref[:, : 2 * per] == row).astype(jnp.float32).astype(jnp.bfloat16)
+    quarter = q_heads // 4
+    copies = [
+        pltpu.make_async_copy(buf.at[:, columns], out.at[:, columns], sems.at[n])
+        for n, columns in enumerate(pl.ds(n * quarter * HD, quarter * HD) for n in range(4))
+    ]
     for i in range(q_heads):
         part = scaled[pl.ds(i, per, stride=q_heads), :]
         high = part.astype(jnp.bfloat16)
         low = (part - high.astype(jnp.float32)).astype(jnp.bfloat16)
-        out[:, i * HD : (i + 1) * HD] = jnp.dot(
+        buf[:, i * HD : (i + 1) * HD] = jnp.dot(
             match, jnp.concatenate([high, low], 0), preferred_element_type=jnp.float32
         ).astype(jnp.bfloat16)
+        if (i + 1) % quarter == 0:
+            copies[i // quarter].start()
+    for copy in copies:
+        copy.wait()
 
 
 def exchange(parts, order):
@@ -496,7 +505,7 @@
         indices = [send_row.reshape(-1), piece_len.reshape(-1), row_len]
     deep = divides(depth, DEEP)
     count = depth // deep
-    widths = [5 * q_cols // 8, 3 * q_cols // 8]
+    widths = [11 * q_cols // 16, 5 * q_cols // 16]
 
 
     def parts(width):
@@ -586,9 +595,11 @@
         functools.partial(merge_kernel, pool, slots, rows_local, q_heads, kv_heads),
         out_shape=jax.ShapeDtypeStruct((rows_local, q_cols), jnp.bfloat16),
         in_specs=[VMEM] * (2 + pool),
-        out_specs=VMEM,
+        out_specs=HBM,
         scratch_shapes=[
+            pltpu.VMEM((rows_local, q_cols), jnp.bfloat16),
             pltpu.VMEM((per * q_heads, HD), jnp.float32),
+            pltpu.SemaphoreType.DMA((4,)),
         ],
         compiler_params=pltpu.CompilerParams(vmem_limit_bytes=24 * 2**20),
         name="merge",

time: 39.6 us -> 39.1 us (0.987)
  waiting for transfers between devices: 8.72 us -> 8.23 us
    pallas_call x1, Pallas kernels: 5.97 us -> 5.33 us  [body(): pl.pallas_call(functools.partial(project_rest_kernel, pool, widths[0]), o...]
    pallas_call x1, Pallas kernels: 8.8 us -> 9.39 us  [body(): pl.pallas_call(functools.partial(project_kernel, pool, slots, rows_local)...]
    ppermute x8, waiting for transfers between devices: 8.72 us -> 8.23 us  [exchange(): lax.ppermute(parts[k], 'pool', [(i, i ^ k) for i in range(len(parts))])]
  transfers between devices with their start and end apart: 8 -> 8, of which waited for: 5 -> 4; matrix products, arithmetic and copies ran while one was open for 0% -> 0% of each run, Pallas kernels for 15% -> 14%
where the time goes in v11:
time: 39.1 us; the launch traced here: 38.9 us
  Pallas kernels  17.1 us (44%)
  starting transfers between devices  13.5 us (35%)
  waiting for transfers between devices  8.23 us (21%)
    ppermute x8, starting transfers between devices, exchange(): lax.ppermute(parts[k], 'pool', [(i, i ^ k) for i in range(len(parts))])  13.5 us
    pallas_call x1, Pallas kernels, body(): pl.pallas_call(functools.partial(project_kernel, pool, slots, rows_local)...  9.39 us
    ppermute x8, waiting for transfers between devices, exchange(): lax.ppermute(parts[k], 'pool', [(i, i ^ k) for i in range(len(parts))])  8.23 us
    pallas_call x1, Pallas kernels, body(): pl.pallas_call(functools.partial(project_rest_kernel, pool, widths[0]), o...  5.33 us
    pallas_call x1, Pallas kernels, body(): pl.pallas_call(functools.partial(merge_kernel, pool, slots, rows_local, q...  1.33 us
    pallas_call x1, Pallas kernels, body(): pl.pallas_call(functools.partial(attend_kernel, pool, slots, seg, width_d...  1.06 us
  transfers between devices with their start and end apart: 8, of which 4 were waited for; matrix products, arithmetic and copies ran while one was open for 0% of the time, Pallas kernels for 14%

profile of v11, /device:TPU:0, one launch (start us, length us, event | category | flops | bytes accessed | tf_op | source)
XLA Modules:
  0.0 38.9 jit_solution(18135107377792661130)
XLA Ops:
  0.0 9.4 %project.1 = (bf16[16,2944]{1,0:T(8,128)(2,1)S(1)}, bf16[16,2944]{1,0:T(8,128)(2,1)S(1)}, bf16[16,2944]{1,0:T(8,128)(2,1)S(1)}, bf16[16,2944]{1,0:T(8,128)(2,1)S...) custom-call(s32[1]{0:T(128)} %bitcast.me_ref, ...), custom_call_target="tpu_custom_call" | custom-call | tf_op jit(solution)/shard_map/project/pallas_call | solution.py:515
  9.4 4.1 %collective-permute-start.1 = (bf16[16,2944]{1,0:T(8,128)(2,1)S(1)}, bf16[16,2944]{1,0:T(8,128)(2,1)S(1)}, u32[]{:S(2)}, u32[]{:S(2)}) collective-permute-start(bf16[16,2944]{1,0:T(8,128)(2,1)S(1)} %get-tuple-element.36), channel_id=1, source_target_pairs={{0,8},{4,12},{8,0},{12,4},{1,9},{5,13},{9,1},{13,5},{2,10},{6,14},... | collective-permute-start | bytes 282632 | tf_op jit(solution)/shard_map/ppermute | solution.py:464
  13.5 1.3 %collective-permute-start.2 = (bf16[16,2944]{1,0:T(8,128)(2,1)S(1)}, bf16[16,2944]{1,0:T(8,128)(2,1)S(1)}, u32[]{:S(2)}, u32[]{:S(2)}) collective-permute-start(bf16[16,2944]{1,0:T(8,128)(2,1)S(1)} %get-tuple-element.37), channel_id=1, source_target_pairs={{0,12},{4,8},{8,4},{12,0},{1,13},{5,9},{9,5},{13,1},{2,14},{6,10},... | collective-permute-start | bytes 282632 | tf_op jit(solution)/shard_map/ppermute | solution.py:464
  14.8 0.0 copy-start.2
  14.8 0.0 copy-start.3
  14.9 0.0 copy-start
  14.9 0.0 copy-start.1
  14.9 5.3 %project_rest.1 = (bf16[16,1792]{1,0:T(8,128)(2,1)S(1)}, bf16[16,4736]{1,0:T(8,128)(2,1)S(1)}, bf16[16,1792]{1,0:T(8,128)(2,1)S(1)}, bf16[16,1792]{1,0:T(8,128)(2,1)S(1)}) custom-call(bf16[64,4096]{1,0:T(8,128)(2,1)S(1)} %get-tuple-element.30.lhs, f32[64,64]{1,0:T(8,128)S(1)} %get-tuple-element.31.pick, bf16[16,2944]{1,0:T(8,128)(2,1)S(1)} %get-tuple-element.32.near, ...), custom_call_target="tpu_custom_call" | custom-call | flops 939524096 | bytes 15204352 | tf_op jit(solution)/shard_map/project_rest/pallas_call | solution.py:545
  20.2 0.3 collective-permute-start.4
  20.5 2.8 %collective-permute-start = (bf16[16,1792]{1,0:T(8,128)(2,1)S(1)}, bf16[16,1792]{1,0:T(8,128)(2,1)S(1)}, u32[]{:S(2)}, u32[]{:S(2)}) collective-permute-start(bf16[16,1792]{1,0:T(8,128)(2,1)S(1)} %get-tuple-element.35), channel_id=1, source_target_pairs={{0,8},{4,12},{8,0},{12,4},{1,9},{5,13},{9,1},{13,5},{2,10},{6,14},... | collective-permute-start | bytes 172040 | tf_op jit(solution)/shard_map/ppermute | solution.py:464
  23.3 0.0 collective-permute-done.1.rest_4_
  23.3 0.0 collective-permute-done.2.rest_5_
  23.3 1.3 %collective-permute-start.3 = (bf16[16,1792]{1,0:T(8,128)(2,1)S(1)}, bf16[16,1792]{1,0:T(8,128)(2,1)S(1)}, u32[]{:S(2)}, u32[]{:S(2)}) collective-permute-start(bf16[16,1792]{1,0:T(8,128)(2,1)S(1)} %get-tuple-element.39), channel_id=1, source_target_pairs={{0,12},{4,8},{8,4},{12,0},{1,13},{5,9},{9,5},{13,1},{2,14},{6,10},... | collective-permute-start | bytes 172040 | tf_op jit(solution)/shard_map/ppermute | solution.py:464
  24.7 0.0 copy-done.2
  24.7 0.0 copy-done.3
  24.7 0.1 sine_multiply_fusion
  24.7 1.7 %collective-permute-done.rest_2_ = bf16[16,1792]{1,0:T(8,128)(2,1)S(1)} collective-permute-done((bf16[16,1792]{1,0:T(8,128)(2,1)S(1)}, bf16[16,1792]{1,0:T(8,128)(2,1)S(1)}, u32[]{:S(2)}, u32[]{:S(2)}) %collective-permute-start) | collective-permute-done | bytes 57376 | tf_op jit(solution)/shard_map/ppermute | solution.py:464
  26.4 2.9 %collective-permute-done.3.rest_3_ = bf16[16,1792]{1,0:T(8,128)(2,1)S(1)} collective-permute-done((bf16[16,1792]{1,0:T(8,128)(2,1)S(1)}, bf16[16,1792]{1,0:T(8,128)(2,1)S(1)}, u32[]{:S(2)}, u32[]{:S(2)}) %collective-permute-start.3) | collective-permute-done | bytes 57376 | tf_op jit(solution)/shard_map/ppermute | solution.py:464
  29.3 0.0 collective-permute-done.4.rest_6_
  29.3 0.0 copy-done
  29.3 0.0 copy-done.1
  29.3 1.1 %attend.1 = (bf16[144,128]{1,0:T(8,128)(2,1)S(1)}, bf16[144,128]{1,0:T(8,128)(2,1)S(1)}, bf16[144,128]{1,0:T(8,128)(2,1)S(1)}, bf16[144,128]{1,0:T(8,128)(2,1)S(1)}) custom-call(s32[1]{0:T(128)} %bitcast.me_ref, bf16[16,2944]{1,0:T(8,128)(2,1)S(1)} %get-tuple-element.29.rest_0_, bf16[16,1792]{1,0:T(8,128)(2,1)S(1)} %get-tuple-element.34.rest_1_, ...), custom_call_target="tpu_custom_call" | custom-call | tf_op jit(solution)/shard_map/attend/pallas_call | solution.py:582
  30.4 1.4 %collective-permute-start.5 = (bf16[144,128]{1,0:T(8,128)(2,1)S(1)}, bf16[144,128]{1,0:T(8,128)(2,1)S(1)}, u32[]{:S(2)}, u32[]{:S(2)}) collective-permute-start(bf16[144,128]{1,0:T(8,128)(2,1)S(1)} %get-tuple-element.46), channel_id=1, source_target_pairs={{0,8},{4,12},{8,0},{12,4},{1,9},{5,13},{9,1},{13,5},{2,10},{6,14},... | collective-permute-start | bytes 110600 | tf_op jit(solution)/shard_map/ppermute | solution.py:464
  31.8 0.8 %collective-permute-start.6 = (bf16[144,128]{1,0:T(8,128)(2,1)S(1)}, bf16[144,128]{1,0:T(8,128)(2,1)S(1)}, u32[]{:S(2)}, u32[]{:S(2)}) collective-permute-start(bf16[144,128]{1,0:T(8,128)(2,1)S(1)} %get-tuple-element.47), channel_id=1, source_target_pairs={{0,12},{4,8},{8,4},{12,0},{1,13},{5,9},{9,5},{13,1},{2,14},{6,10},... | collective-permute-start | bytes 110600 | tf_op jit(solution)/shard_map/ppermute | solution.py:464
  32.6 1.3 %collective-permute-start.7 = (bf16[144,128]{1,0:T(8,128)(2,1)S(1)}, bf16[144,128]{1,0:T(8,128)(2,1)S(1)}, u32[]{:S(2)}, u32[]{:S(2)}) collective-permute-start(bf16[144,128]{1,0:T(8,128)(2,1)S(1)} %get-tuple-element.48), channel_id=1, source_target_pairs={{0,4},{4,0},{8,12},{12,8},{1,5},{5,1},{9,13},{13,9},{2,6},{6,2},{1... | collective-permute-start | bytes 110600 | tf_op jit(solution)/shard_map/ppermute | solution.py:464
  33.9 1.4 %collective-permute-done.5.rest_0_ = bf16[144,128]{1,0:T(8,128)(2,1)S(1)} collective-permute-done((bf16[144,128]{1,0:T(8,128)(2,1)S(1)}, bf16[144,128]{1,0:T(8,128)(2,1)S(1)}, u32[]{:S(2)}, u32[]{:S(2)}) %collective-permute-start.5) | collective-permute-done | bytes 36896 | tf_op jit(solution)/shard_map/ppermute | solution.py:464
  35.3 2.3 %collective-permute-done.6.rest_1_ = bf16[144,128]{1,0:T(8,128)(2,1)S(1)} collective-permute-done((bf16[144,128]{1,0:T(8,128)(2,1)S(1)}, bf16[144,128]{1,0:T(8,128)(2,1)S(1)}, u32[]{:S(2)}, u32[]{:S(2)}) %collective-permute-start.6) | collective-permute-done | bytes 36896 | tf_op jit(solution)/shard_map/ppermute | solution.py:464
  37.6 0.0 collective-permute-done.7.rest_2_
  37.6 1.3 %merge.1 = bf16[16,4096]{1,0:T(8,128)(2,1)} custom-call(s32[1,128]{1,0:T(1,128)S(1)} %get-tuple-element.27.slots_ref, s32[4,128]{1,0:T(4,128)S(1)} %get-tuple-element.28.rows_ref, bf16[144,128]{1,0:T(8,128)(2,1)S(1)} %get-tuple-element.45.own, bf16[144,128]{1,0:T(8,128)(2,1)S(1)} %collective-permute-done.5.rest_0_, ...), custom_call_target="tpu_custom_call" | custom-call | tf_op jit(solution)/shard_map/merge/pallas_call | solution.py:594
Async XLA Ops:
  9.4 13.9 %collective-permute-start.1 = (bf16[16,2944]{1,0:T(8,128)(2,1)S(1)}, bf16[16,2944]{1,0:T(8,128)(2,1)S(1)}, u32[]{:S(2)}, u32[]{:S(2)}) collective-permute-start(bf16[16,2944]{1,0:T(8,128)(2,1)S(1)} %get-tuple-element.36), channel_id=1, source_target_pairs={{0,8},{4,12},{8,0},{12,4},{1,9},{5,13},{9,1},{13,5},{2,10},{6,14},... | collective-permute-start | bytes 282632 | tf_op jit(solution)/shard_map/ppermute | solution.py:464
  13.5 9.8 %collective-permute-start.2 = (bf16[16,2944]{1,0:T(8,128)(2,1)S(1)}, bf16[16,2944]{1,0:T(8,128)(2,1)S(1)}, u32[]{:S(2)}, u32[]{:S(2)}) collective-permute-start(bf16[16,2944]{1,0:T(8,128)(2,1)S(1)} %get-tuple-element.37), channel_id=1, source_target_pairs={{0,12},{4,8},{8,4},{12,0},{1,13},{5,9},{9,5},{13,1},{2,14},{6,10},... | collective-permute-start | bytes 282632 | tf_op jit(solution)/shard_map/ppermute | solution.py:464
  14.8 9.8 %copy-start.2 = (f32[128]{0:T(128)S(1)}, f32[128]{0:T(128)}, u32[]{:S(2)}) copy-start(f32[128]{0:T(128)} %constant.12) | copy-start | bytes 1540
  14.8 9.8 %copy-start.3 = (f32[128]{0:T(128)S(1)}, f32[128]{0:T(128)}, u32[]{:S(2)}) copy-start(f32[128]{0:T(128)} %constant.13) | copy-start | bytes 1540
  14.9 14.4 %copy-start = (bf16[1024,256]{1,0:T(8,128)(2,1)S(1)}, bf16[1024,256]{1,0:T(8,128)(2,1)}, u32[]{:S(2)}) copy-start(bf16[1024,256]{1,0:T(8,128)(2,1)} %rest_10_.1) | copy-start | bytes 1572868
  14.9 14.4 %copy-start.1 = (bf16[1024,256]{1,0:T(8,128)(2,1)S(1)}, bf16[1024,256]{1,0:T(8,128)(2,1)}, u32[]{:S(2)}) copy-start(bf16[1024,256]{1,0:T(8,128)(2,1)} %rest_11_.1) | copy-start | bytes 1572868
  20.2 9.1 %collective-permute-start.4 = (bf16[16,4736]{1,0:T(8,128)(2,1)S(1)}, bf16[16,4736]{1,0:T(8,128)(2,1)S(1)}, u32[]{:S(2)}, u32[]{:S(2)}) collective-permute-start(bf16[16,4736]{1,0:T(8,128)(2,1)S(1)} %get-tuple-element.42), channel_id=1, source_target_pairs={{0,4},{4,0},{8,12},{12,8},{1,5},{5,1},{9,13},{13,9},{2,6},{6,2},{1... | collective-permute-start | bytes 454664 | tf_op jit(solution)/shard_map/ppermute | solution.py:464
  20.5 5.9 %collective-permute-start = (bf16[16,1792]{1,0:T(8,128)(2,1)S(1)}, bf16[16,1792]{1,0:T(8,128)(2,1)S(1)}, u32[]{:S(2)}, u32[]{:S(2)}) collective-permute-start(bf16[16,1792]{1,0:T(8,128)(2,1)S(1)} %get-tuple-element.35), channel_id=1, source_target_pairs={{0,8},{4,12},{8,0},{12,4},{1,9},{5,13},{9,1},{13,5},{2,10},{6,14},... | collective-permute-start | bytes 172040 | tf_op jit(solution)/shard_map/ppermute | solution.py:464
  23.3 6.0 %collective-permute-start.3 = (bf16[16,1792]{1,0:T(8,128)(2,1)S(1)}, bf16[16,1792]{1,0:T(8,128)(2,1)S(1)}, u32[]{:S(2)}, u32[]{:S(2)}) collective-permute-start(bf16[16,1792]{1,0:T(8,128)(2,1)S(1)} %get-tuple-element.39), channel_id=1, source_target_pairs={{0,12},{4,8},{8,4},{12,0},{1,13},{5,9},{9,5},{13,1},{2,14},{6,10},... | collective-permute-start | bytes 172040 | tf_op jit(solution)/shard_map/ppermute | solution.py:464
  30.4 4.9 %collective-permute-start.5 = (bf16[144,128]{1,0:T(8,128)(2,1)S(1)}, bf16[144,128]{1,0:T(8,128)(2,1)S(1)}, u32[]{:S(2)}, u32[]{:S(2)}) collective-permute-start(bf16[144,128]{1,0:T(8,128)(2,1)S(1)} %get-tuple-element.46), channel_id=1, source_target_pairs={{0,8},{4,12},{8,0},{12,4},{1,9},{5,13},{9,1},{13,5},{2,10},{6,14},... | collective-permute-start | bytes 110600 | tf_op jit(solution)/shard_map/ppermute | solution.py:464
  31.8 5.8 %collective-permute-start.6 = (bf16[144,128]{1,0:T(8,128)(2,1)S(1)}, bf16[144,128]{1,0:T(8,128)(2,1)S(1)}, u32[]{:S(2)}, u32[]{:S(2)}) collective-permute-start(bf16[144,128]{1,0:T(8,128)(2,1)S(1)} %get-tuple-element.47), channel_id=1, source_target_pairs={{0,12},{4,8},{8,4},{12,0},{1,13},{5,9},{9,5},{13,1},{2,14},{6,10},... | collective-permute-start | bytes 110600 | tf_op jit(solution)/shard_map/ppermute | solution.py:464
  32.6 4.9 %collective-permute-start.7 = (bf16[144,128]{1,0:T(8,128)(2,1)S(1)}, bf16[144,128]{1,0:T(8,128)(2,1)S(1)}, u32[]{:S(2)}, u32[]{:S(2)}) collective-permute-start(bf16[144,128]{1,0:T(8,128)(2,1)S(1)} %get-tuple-element.48), channel_id=1, source_target_pairs={{0,4},{4,0},{8,12},{12,8},{1,5},{5,1},{9,13},{13,9},{2,6},{6,2},{1... | collective-permute-start | bytes 110600 | tf_op jit(solution)/shard_map/ppermute | solution.py:464

commit v12 on v11

--- a/solution.py
+++ b/solution.py
@@ -38,22 +38,17 @@
     return lax.bitwise_xor(me, k)
 
 
-def stream(count, pieces, following, ahead):
+def stream(count, pieces, ahead):
     def begin():
         for t in range(min(ahead, count)):
             for copy in pieces(t):
                 copy.start()
-        for copy in following[: max(ahead - count, 0)]:
-            copy.start()
 
     def advance(t):
         @pl.when(t + ahead < count)
         def _():
             for copy in pieces(t + ahead):
                 copy.start()
-
-        for j, copy in enumerate(following):
-            pl.when(t + ahead == count + j)(copy.start)
 
     return begin, advance
 
@@ -88,9 +83,9 @@
 
 
 def project_kernel(pool, slots, rows_local, me_ref, send, lens, row_len, hidden, gain, *rest):
-    w_query, w_key, w_value, *rest = rest
+    w_query, *rest = rest
     outs, rest = rest[:pool], rest[pool:]
-    lhs, pick, positions, marks, home_rows, home_slots, narrow, *rest = rest
+    lhs, pick, positions, marks, home_rows, home_slots, *rest = rest
     send_buf, lens_buf, row_len_buf, x_buf, g_buf, *rest = rest
     query_buf, sums, squares, in_sem, sems = rest
     per = pool * slots
@@ -161,7 +156,6 @@
         squares[...] = total
         return left
 
-    kv_cols = w_key.shape[1]
     cuts = [0, deep // 4, deep // 2, deep] if count > 1 else [0, deep]
 
     def pieces(t):
@@ -175,13 +169,7 @@
         rows = pl.ds(pl.multiple_of(t * deep, deep), deep)
         return [pltpu.make_async_copy(w_query.at[rows, :width], query_buf.at[t], sems.at[t])]
 
-    following = [
-        pltpu.make_async_copy(w, target, in_sem.at[5 + n])
-        for n, (w, target) in enumerate(
-            ((w_key, narrow.at[:, :kv_cols]), (w_value, narrow.at[:, kv_cols:]))
-        )
-    ]
-    begin, advance = stream(count, pieces, following, 3)
+    begin, advance = stream(count, pieces, 3)
 
     def use(t):
         advance(t)
@@ -247,37 +235,43 @@
     if count > early + 1:
         pl.loop(early, count - 1)(use)
     use_last(count - 1)
-    for copy in following:
-        copy.wait()
-
-
-def project_rest_kernel(pool, column, lhs, pick, near, narrow, w_query, *rest):
-    outs, (query_buf, sums, sems) = rest[:pool], rest[pool:]
+
+
+def project_rest_kernel(pool, column, lhs, pick, near, w_key, w_value, w_query, *rest):
+    outs, (block_buf, sums, sems) = rest[:pool], rest[pool:]
     done = near.shape[1]
-    count, deep, _ = query_buf.shape
-    chosen = pick[...].astype(jnp.bfloat16)
-    targets = [out.at[:, done:] if k == 1 else out for k, out in enumerate(outs)]
+    count, deep, width = block_buf.shape
+    kv_cols = w_key.shape[1]
+    spans = [(w_key, 0, 0, kv_cols), (w_value, 0, kv_cols, kv_cols)]
+    spans.append((w_query, column, 2 * kv_cols, width - 2 * kv_cols))
 
     def pieces(t):
         rows = pl.ds(pl.multiple_of(t * deep, deep), deep)
-        block = w_query.at[rows, column : column + query_buf.shape[2]]
-        return [pltpu.make_async_copy(block, query_buf.at[t], sems.at[t])]
-
-    begin, _ = stream(count, pieces, [], count)
+        return [
+            pltpu.make_async_copy(
+                w.at[rows, start : start + size], block_buf.at[t, :, to : to + size], sems.at[n, t]
+            )
+            for n, (w, start, to, size) in enumerate(spans)
+        ]
+
+    begin, _ = stream(count, pieces, count)
     begin()
     sums[...] = jnp.zeros(sums.shape, jnp.float32)
     outs[1][:, :done] = near[...]
-    part = jnp.dot(lhs[...], narrow[...], preferred_element_type=jnp.float32)
-    spread(chosen, part, targets, 0)
+    chosen = pick[...].astype(jnp.bfloat16)
+    targets = [out.at[:, done:] if k == 1 else out for k, out in enumerate(outs)]
 
     @pl.loop(0, count - 1)
     def _(t):
-        pieces(t)[0].wait()
-        add_products(lhs[:, pl.ds(pl.multiple_of(t * deep, deep), deep)], query_buf.at[t], sums)
-
-    pieces(count - 1)[0].wait()
+        for copy in pieces(t):
+            copy.wait()
+        left = lhs[:, pl.ds(pl.multiple_of(t * deep, deep), deep)]
+        add_products(left, block_buf.at[t], sums)
+
+    for copy in pieces(count - 1):
+        copy.wait()
     left = lhs[:, (count - 1) * deep :]
-    spread_products(chosen, left, query_buf.at[count - 1], sums, targets, narrow.shape[1])
+    spread_products(chosen, left, block_buf.at[count - 1], sums, targets, 0)
 
 
 def attend_kernel(pool, slots, seg, width_d, q_heads, kv_heads, me_ref, *rest):
@@ -512,7 +506,7 @@
         return [jax.ShapeDtypeStruct((per, width), jnp.bfloat16)] * pool
 
     operands = [in_hbm(x) for x in (*indices, hidden_in, norm_gain, w_query, w_key, w_value)]
-    *first_terms, lhs, pick, positions, marks, home_rows, home_slots, narrow = pl.pallas_call(
+    *first_terms, lhs, pick, positions, marks, home_rows, home_slots = pl.pallas_call(
         functools.partial(project_kernel, pool, slots, rows_local),
         out_shape=[
             *parts(widths[0] + HD),
@@ -522,10 +516,9 @@
             jax.ShapeDtypeStruct((2, per * group), jnp.int32),
             jax.ShapeDtypeStruct((pool, HD), jnp.int32),
             jax.ShapeDtypeStruct((1, HD), jnp.int32),
-            jax.ShapeDtypeStruct((depth, 2 * kv_cols), jnp.bfloat16),
         ],
-        in_specs=[SMEM] + [HBM] * 8,
-        out_specs=[VMEM] * (pool + 7),
+        in_specs=[SMEM] + [HBM] * 6,
+        out_specs=[VMEM] * (pool + 6),
         scratch_shapes=[
             *(pltpu.SMEM(x.shape, jnp.int32) for x in indices),
             pltpu.VMEM((n_rows, depth), jnp.bfloat16),
@@ -533,24 +526,24 @@
             pltpu.VMEM((count, deep, widths[0]), jnp.bfloat16),
             pltpu.VMEM((n_rows, widths[0]), jnp.float32),
             pltpu.VMEM((n_rows, HD), jnp.float32),
-            pltpu.SemaphoreType.DMA((7,)),
+            pltpu.SemaphoreType.DMA((5,)),
             pltpu.SemaphoreType.DMA((count + 3,)),
         ],
         compiler_params=pltpu.CompilerParams(vmem_limit_bytes=46 * 2**20),
         name="project",
-    )(me[None], *operands)
+    )(me[None], *operands[:6])
     rest_cols = 2 * kv_cols + widths[1]
     rest_shapes = parts(rest_cols)
     rest_shapes[1] = jax.ShapeDtypeStruct((per, widths[0] + HD + rest_cols), jnp.bfloat16)
     rest_terms = pl.pallas_call(
         functools.partial(project_rest_kernel, pool, widths[0]),
         out_shape=rest_shapes,
-        in_specs=[VMEM] * 4 + [HBM],
+        in_specs=[VMEM] * 3 + [HBM] * 3,
         out_specs=[VMEM] * pool,
         scratch_shapes=[
-            pltpu.VMEM((count, deep, widths[1]), jnp.bfloat16),
-            pltpu.VMEM((n_rows, widths[1]), jnp.float32),
-            pltpu.SemaphoreType.DMA((count,)),
+            pltpu.VMEM((count, deep, rest_cols), jnp.bfloat16),
+            pltpu.VMEM((n_rows, rest_cols), jnp.float32),
+            pltpu.SemaphoreType.DMA((3, count)),
         ],
         compiler_params=pltpu.CompilerParams(vmem_limit_bytes=40 * 2**20),
         cost_estimate=pl.CostEstimate(
@@ -559,7 +552,7 @@
             transcendentals=0,
         ),
         name="project_rest",
-    )(lhs, pick, first_terms[1], narrow, operands[5])
+    )(lhs, pick, first_terms[1], operands[6], operands[7], operands[5])
     first_terms = exchange(first_terms, range(2, pool))
     rest_terms = list(rest_terms)
     early, late = range(2, pool), range(3, pool)

time: 39.1 us -> 39.5 us (1.010)
  Pallas kernels: 17.1 us -> 17.8 us
    pallas_call x1, Pallas kernels: 5.33 us -> 6.26 us  [body(): pl.pallas_call(functools.partial(project_rest_kernel, pool, widths[0]), o...]
  transfers between devices with their start and end apart: 8 -> 8, of which waited for: 4 -> 4; matrix products, arithmetic and copies ran while one was open for 0% -> 0% of each run, Pallas kernels for 14% -> 16%
where the time goes in v12:
time: 39.5 us; the launch traced here: 39.4 us
  Pallas kernels  17.8 us (45%)
  starting transfers between devices  13.5 us (34%)
  waiting for transfers between devices  8.03 us (20%)
    ppermute x8, starting transfers between devices, exchange(): lax.ppermute(parts[k], 'pool', [(i, i ^ k) for i in range(len(parts))])  13.5 us
    pallas_call x1, Pallas kernels, body(): pl.pallas_call(functools.partial(project_kernel, pool, slots, rows_local)...  9.1 us
    ppermute x8, waiting for transfers between devices, exchange(): lax.ppermute(parts[k], 'pool', [(i, i ^ k) for i in range(len(parts))])  8.03 us
    pallas_call x1, Pallas kernels, body(): pl.pallas_call(functools.partial(project_rest_kernel, pool, widths[0]), o...  6.26 us
    pallas_call x1, Pallas kernels, body(): pl.pallas_call(functools.partial(merge_kernel, pool, slots, rows_local, q...  1.33 us
    pallas_call x1, Pallas kernels, body(): pl.pallas_call(functools.partial(attend_kernel, pool, slots, seg, width_d...  1.07 us
  transfers between devices with their start and end apart: 8, of which 4 were waited for; matrix products, arithmetic and copies ran while one was open for 0% of the time, Pallas kernels for 16%

profile of v12, /device:TPU:0, one launch (start us, length us, event | category | flops | bytes accessed | tf_op | source)
XLA Modules:
  0.0 39.4 jit_solution(10989361293514028687)
XLA Ops:
  0.0 9.1 %project.1 = (bf16[16,2944]{1,0:T(8,128)(2,1)S(1)}, bf16[16,2944]{1,0:T(8,128)(2,1)S(1)}, bf16[16,2944]{1,0:T(8,128)(2,1)S(1)}, bf16[16,2944]{1,0:T(8,128)(2,1)S...) custom-call(s32[1]{0:T(128)} %bitcast.me_ref, ...), custom_call_target="tpu_custom_call" | custom-call | tf_op jit(solution)/shard_map/project/pallas_call | solution.py:509
  9.1 4.1 %collective-permute-start.1 = (bf16[16,2944]{1,0:T(8,128)(2,1)S(1)}, bf16[16,2944]{1,0:T(8,128)(2,1)S(1)}, u32[]{:S(2)}, u32[]{:S(2)}) collective-permute-start(bf16[16,2944]{1,0:T(8,128)(2,1)S(1)} %get-tuple-element.34), channel_id=1, source_target_pairs={{0,8},{4,12},{8,0},{12,4},{1,9},{5,13},{9,1},{13,5},{2,10},{6,14},... | collective-permute-start | bytes 282632 | tf_op jit(solution)/shard_map/ppermute | solution.py:458
  13.2 1.3 %collective-permute-start.2 = (bf16[16,2944]{1,0:T(8,128)(2,1)S(1)}, bf16[16,2944]{1,0:T(8,128)(2,1)S(1)}, u32[]{:S(2)}, u32[]{:S(2)}) collective-permute-start(bf16[16,2944]{1,0:T(8,128)(2,1)S(1)} %get-tuple-element.35), channel_id=1, source_target_pairs={{0,12},{4,8},{8,4},{12,0},{1,13},{5,9},{9,5},{13,1},{2,14},{6,10},... | collective-permute-start | bytes 282632 | tf_op jit(solution)/shard_map/ppermute | solution.py:458
  14.6 0.0 copy-start.2
  14.6 0.0 copy-start.3
  14.6 0.0 copy-start
  14.6 0.0 copy-start.1
  14.6 6.3 %project_rest.1 = (bf16[16,1792]{1,0:T(8,128)(2,1)S(1)}, bf16[16,4736]{1,0:T(8,128)(2,1)S(1)}, bf16[16,1792]{1,0:T(8,128)(2,1)S(1)}, bf16[16,1792]{1,0:T(8,128)(2,1)S(1)}) custom-call(bf16[64,4096]{1,0:T(8,128)(2,1)S(1)} %get-tuple-element.29.lhs, f32[64,64]{1,0:T(8,128)S(1)} %get-tuple-element.30.pick, bf16[16,2944]{1,0:T(8,128)(2,1)S(1)} %get-tuple-element.31.near, ...), custom_call_target="tpu_custom_call" | custom-call | flops 939524096 | bytes 15204352 | tf_op jit(solution)/shard_map/project_rest/pallas_call | solution.py:538
  20.8 0.3 collective-permute-start.4
  21.1 2.8 %collective-permute-start = (bf16[16,1792]{1,0:T(8,128)(2,1)S(1)}, bf16[16,1792]{1,0:T(8,128)(2,1)S(1)}, u32[]{:S(2)}, u32[]{:S(2)}) collective-permute-start(bf16[16,1792]{1,0:T(8,128)(2,1)S(1)} %get-tuple-element.33), channel_id=1, source_target_pairs={{0,8},{4,12},{8,0},{12,4},{1,9},{5,13},{9,1},{13,5},{2,10},{6,14},... | collective-permute-start | bytes 172040 | tf_op jit(solution)/shard_map/ppermute | solution.py:458
  23.9 0.0 collective-permute-done.1.rest_4_
  23.9 0.0 collective-permute-done.2.rest_5_
  23.9 1.4 %collective-permute-start.3 = (bf16[16,1792]{1,0:T(8,128)(2,1)S(1)}, bf16[16,1792]{1,0:T(8,128)(2,1)S(1)}, u32[]{:S(2)}, u32[]{:S(2)}) collective-permute-start(bf16[16,1792]{1,0:T(8,128)(2,1)S(1)} %get-tuple-element.37), channel_id=1, source_target_pairs={{0,12},{4,8},{8,4},{12,0},{1,13},{5,9},{9,5},{13,1},{2,14},{6,10},... | collective-permute-start | bytes 172040 | tf_op jit(solution)/shard_map/ppermute | solution.py:458
  25.3 0.0 copy-done.2
  25.3 0.0 copy-done.3
  25.3 0.1 sine_multiply_fusion
  25.4 2.2 %collective-permute-done.rest_2_ = bf16[16,1792]{1,0:T(8,128)(2,1)S(1)} collective-permute-done((bf16[16,1792]{1,0:T(8,128)(2,1)S(1)}, bf16[16,1792]{1,0:T(8,128)(2,1)S(1)}, u32[]{:S(2)}, u32[]{:S(2)}) %collective-permute-start) | collective-permute-done | bytes 57376 | tf_op jit(solution)/shard_map/ppermute | solution.py:458
  27.5 2.4 %collective-permute-done.3.rest_3_ = bf16[16,1792]{1,0:T(8,128)(2,1)S(1)} collective-permute-done((bf16[16,1792]{1,0:T(8,128)(2,1)S(1)}, bf16[16,1792]{1,0:T(8,128)(2,1)S(1)}, u32[]{:S(2)}, u32[]{:S(2)}) %collective-permute-start.3) | collective-permute-done | bytes 57376 | tf_op jit(solution)/shard_map/ppermute | solution.py:458
  29.9 0.0 collective-permute-done.4.rest_6_
  29.9 0.0 copy-done
  29.9 0.0 copy-done.1
  29.9 1.1 %attend.1 = (bf16[144,128]{1,0:T(8,128)(2,1)S(1)}, bf16[144,128]{1,0:T(8,128)(2,1)S(1)}, bf16[144,128]{1,0:T(8,128)(2,1)S(1)}, bf16[144,128]{1,0:T(8,128)(2,1)S(1)}) custom-call(s32[1]{0:T(128)} %bitcast.me_ref, bf16[16,2944]{1,0:T(8,128)(2,1)S(1)} %get-tuple-element.28.rest_0_, bf16[16,1792]{1,0:T(8,128)(2,1)S(1)} %get-tuple-element.32.rest_1_, ...), custom_call_target="tpu_custom_call" | custom-call | tf_op jit(solution)/shard_map/attend/pallas_call | solution.py:575
  31.0 1.3 %collective-permute-start.5 = (bf16[144,128]{1,0:T(8,128)(2,1)S(1)}, bf16[144,128]{1,0:T(8,128)(2,1)S(1)}, u32[]{:S(2)}, u32[]{:S(2)}) collective-permute-start(bf16[144,128]{1,0:T(8,128)(2,1)S(1)} %get-tuple-element.44), channel_id=1, source_target_pairs={{0,8},{4,12},{8,0},{12,4},{1,9},{5,13},{9,1},{13,5},{2,10},{6,14},... | collective-permute-start | bytes 110600 | tf_op jit(solution)/shard_map/ppermute | solution.py:458
  32.3 1.0 %collective-permute-start.6 = (bf16[144,128]{1,0:T(8,128)(2,1)S(1)}, bf16[144,128]{1,0:T(8,128)(2,1)S(1)}, u32[]{:S(2)}, u32[]{:S(2)}) collective-permute-start(bf16[144,128]{1,0:T(8,128)(2,1)S(1)} %get-tuple-element.45), channel_id=1, source_target_pairs={{0,12},{4,8},{8,4},{12,0},{1,13},{5,9},{9,5},{13,1},{2,14},{6,10},... | collective-permute-start | bytes 110600 | tf_op jit(solution)/shard_map/ppermute | solution.py:458
  33.3 1.3 %collective-permute-start.7 = (bf16[144,128]{1,0:T(8,128)(2,1)S(1)}, bf16[144,128]{1,0:T(8,128)(2,1)S(1)}, u32[]{:S(2)}, u32[]{:S(2)}) collective-permute-start(bf16[144,128]{1,0:T(8,128)(2,1)S(1)} %get-tuple-element.46), channel_id=1, source_target_pairs={{0,4},{4,0},{8,12},{12,8},{1,5},{5,1},{9,13},{13,9},{2,6},{6,2},{1... | collective-permute-start | bytes 110600 | tf_op jit(solution)/shard_map/ppermute | solution.py:458
  34.6 1.4 %collective-permute-done.5.rest_0_ = bf16[144,128]{1,0:T(8,128)(2,1)S(1)} collective-permute-done((bf16[144,128]{1,0:T(8,128)(2,1)S(1)}, bf16[144,128]{1,0:T(8,128)(2,1)S(1)}, u32[]{:S(2)}, u32[]{:S(2)}) %collective-permute-start.5) | collective-permute-done | bytes 36896 | tf_op jit(solution)/shard_map/ppermute | solution.py:458
  36.0 2.0 %collective-permute-done.6.rest_1_ = bf16[144,128]{1,0:T(8,128)(2,1)S(1)} collective-permute-done((bf16[144,128]{1,0:T(8,128)(2,1)S(1)}, bf16[144,128]{1,0:T(8,128)(2,1)S(1)}, u32[]{:S(2)}, u32[]{:S(2)}) %collective-permute-start.6) | collective-permute-done | bytes 36896 | tf_op jit(solution)/shard_map/ppermute | solution.py:458
  38.0 0.0 collective-permute-done.7.rest_2_
  38.0 1.3 %merge.1 = bf16[16,4096]{1,0:T(8,128)(2,1)} custom-call(s32[1,128]{1,0:T(1,128)S(1)} %get-tuple-element.26.slots_ref, s32[4,128]{1,0:T(4,128)S(1)} %get-tuple-element.27.rows_ref, bf16[144,128]{1,0:T(8,128)(2,1)S(1)} %get-tuple-element.43.own, bf16[144,128]{1,0:T(8,128)(2,1)S(1)} %collective-permute-done.5.rest_0_, ...), custom_call_target="tpu_custom_call" | custom-call | tf_op jit(solution)/shard_map/merge/pallas_call | solution.py:587
Async XLA Ops:
  9.1 14.8 %collective-permute-start.1 = (bf16[16,2944]{1,0:T(8,128)(2,1)S(1)}, bf16[16,2944]{1,0:T(8,128)(2,1)S(1)}, u32[]{:S(2)}, u32[]{:S(2)}) collective-permute-start(bf16[16,2944]{1,0:T(8,128)(2,1)S(1)} %get-tuple-element.34), channel_id=1, source_target_pairs={{0,8},{4,12},{8,0},{12,4},{1,9},{5,13},{9,1},{13,5},{2,10},{6,14},... | collective-permute-start | bytes 282632 | tf_op jit(solution)/shard_map/ppermute | solution.py:458
  13.2 10.7 %collective-permute-start.2 = (bf16[16,2944]{1,0:T(8,128)(2,1)S(1)}, bf16[16,2944]{1,0:T(8,128)(2,1)S(1)}, u32[]{:S(2)}, u32[]{:S(2)}) collective-permute-start(bf16[16,2944]{1,0:T(8,128)(2,1)S(1)} %get-tuple-element.35), channel_id=1, source_target_pairs={{0,12},{4,8},{8,4},{12,0},{1,13},{5,9},{9,5},{13,1},{2,14},{6,10},... | collective-permute-start | bytes 282632 | tf_op jit(solution)/shard_map/ppermute | solution.py:458
  14.6 10.7 %copy-start.2 = (f32[128]{0:T(128)S(1)}, f32[128]{0:T(128)}, u32[]{:S(2)}) copy-start(f32[128]{0:T(128)} %constant.12) | copy-start | bytes 1540
  14.6 10.7 %copy-start.3 = (f32[128]{0:T(128)S(1)}, f32[128]{0:T(128)}, u32[]{:S(2)}) copy-start(f32[128]{0:T(128)} %constant.13) | copy-start | bytes 1540
  14.6 15.4 %copy-start = (bf16[1024,256]{1,0:T(8,128)(2,1)S(1)}, bf16[1024,256]{1,0:T(8,128)(2,1)}, u32[]{:S(2)}) copy-start(bf16[1024,256]{1,0:T(8,128)(2,1)} %rest_10_.1) | copy-start | bytes 1572868
  14.6 15.4 %copy-start.1 = (bf16[1024,256]{1,0:T(8,128)(2,1)S(1)}, bf16[1024,256]{1,0:T(8,128)(2,1)}, u32[]{:S(2)}) copy-start(bf16[1024,256]{1,0:T(8,128)(2,1)} %rest_11_.1) | copy-start | bytes 1572868
  20.8 9.1 %collective-permute-start.4 = (bf16[16,4736]{1,0:T(8,128)(2,1)S(1)}, bf16[16,4736]{1,0:T(8,128)(2,1)S(1)}, u32[]{:S(2)}, u32[]{:S(2)}) collective-permute-start(bf16[16,4736]{1,0:T(8,128)(2,1)S(1)} %get-tuple-element.40), channel_id=1, source_target_pairs={{0,4},{4,0},{8,12},{12,8},{1,5},{5,1},{9,13},{13,9},{2,6},{6,2},{1... | collective-permute-start | bytes 454664 | tf_op jit(solution)/shard_map/ppermute | solution.py:458
  21.1 6.4 %collective-permute-start = (bf16[16,1792]{1,0:T(8,128)(2,1)S(1)}, bf16[16,1792]{1,0:T(8,128)(2,1)S(1)}, u32[]{:S(2)}, u32[]{:S(2)}) collective-permute-start(bf16[16,1792]{1,0:T(8,128)(2,1)S(1)} %get-tuple-element.33), channel_id=1, source_target_pairs={{0,8},{4,12},{8,0},{12,4},{1,9},{5,13},{9,1},{13,5},{2,10},{6,14},... | collective-permute-start | bytes 172040 | tf_op jit(solution)/shard_map/ppermute | solution.py:458
  23.9 6.0 %collective-permute-start.3 = (bf16[16,1792]{1,0:T(8,128)(2,1)S(1)}, bf16[16,1792]{1,0:T(8,128)(2,1)S(1)}, u32[]{:S(2)}, u32[]{:S(2)}) collective-permute-start(bf16[16,1792]{1,0:T(8,128)(2,1)S(1)} %get-tuple-element.37), channel_id=1, source_target_pairs={{0,12},{4,8},{8,4},{12,0},{1,13},{5,9},{9,5},{13,1},{2,14},{6,10},... | collective-permute-start | bytes 172040 | tf_op jit(solution)/shard_map/ppermute | solution.py:458
  31.0 5.0 %collective-permute-start.5 = (bf16[144,128]{1,0:T(8,128)(2,1)S(1)}, bf16[144,128]{1,0:T(8,128)(2,1)S(1)}, u32[]{:S(2)}, u32[]{:S(2)}) collective-permute-start(bf16[144,128]{1,0:T(8,128)(2,1)S(1)} %get-tuple-element.44), channel_id=1, source_target_pairs={{0,8},{4,12},{8,0},{12,4},{1,9},{5,13},{9,1},{13,5},{2,10},{6,14},... | collective-permute-start | bytes 110600 | tf_op jit(solution)/shard_map/ppermute | solution.py:458
  32.3 5.8 %collective-permute-start.6 = (bf16[144,128]{1,0:T(8,128)(2,1)S(1)}, bf16[144,128]{1,0:T(8,128)(2,1)S(1)}, u32[]{:S(2)}, u32[]{:S(2)}) collective-permute-start(bf16[144,128]{1,0:T(8,128)(2,1)S(1)} %get-tuple-element.45), channel_id=1, source_target_pairs={{0,12},{4,8},{8,4},{12,0},{1,13},{5,9},{9,5},{13,1},{2,14},{6,10},... | collective-permute-start | bytes 110600 | tf_op jit(solution)/shard_map/ppermute | solution.py:458
  33.3 4.7 %collective-permute-start.7 = (bf16[144,128]{1,0:T(8,128)(2,1)S(1)}, bf16[144,128]{1,0:T(8,128)(2,1)S(1)}, u32[]{:S(2)}, u32[]{:S(2)}) collective-permute-start(bf16[144,128]{1,0:T(8,128)(2,1)S(1)} %get-tuple-element.46), channel_id=1, source_target_pairs={{0,4},{4,0},{8,12},{12,8},{1,5},{5,1},{9,13},{13,9},{2,6},{6,2},{1... | collective-permute-start | bytes 110600 | tf_op jit(solution)/shard_map/ppermute | solution.py:458

commit v13 on v11

--- a/solution.py
+++ b/solution.py
@@ -23,8 +23,10 @@
     return limit
 
 
-def widest(width, limit):
-    return max(tile for tile in range(128, limit + 1, 128) if width % tile == 0)
+def tiles(width):
+    count = -(-width // TILE)
+    each = -(-width // (256 * count)) * 256
+    return [(at, min(each, width - at)) for at in range(0, width, each)]
 
 
 def split3(x):
@@ -59,9 +61,7 @@
 
 
 def add_products(left, block, sums):
-    width = block.shape[1]
-    tile = widest(width, TILE)
-    for at in range(0, width, tile):
+    for at, tile in tiles(block.shape[1]):
         sums[:, at : at + tile] += jnp.dot(
             left, block[:, at : at + tile], preferred_element_type=jnp.float32
         )
@@ -78,9 +78,7 @@
 
 
 def spread_products(chosen, left, block, sums, outs, to):
-    width = block.shape[1]
-    tile = widest(width, TILE)
-    for at in range(0, width, tile):
+    for at, tile in tiles(block.shape[1]):
         done = sums[:, at : at + tile] + jnp.dot(
             left, block[:, at : at + tile], preferred_element_type=jnp.float32
         )

time: 39.1 us -> 39.1 us (level)
  no operation moved by 1% of the time
where the time goes in v13:
time: 39.1 us; the launch traced here: 38.9 us
  Pallas kernels  17.1 us (44%)
  starting transfers between devices  13.5 us (35%)
  waiting for transfers between devices  8.23 us (21%)
    ppermute x8, starting transfers between devices, exchange(): lax.ppermute(parts[k], 'pool', [(i, i ^ k) for i in range(len(parts))])  13.5 us
    pallas_call x1, Pallas kernels, body(): pl.pallas_call(functools.partial(project_kernel, pool, slots, rows_local)...  9.39 us
    ppermute x8, waiting for transfers between devices, exchange(): lax.ppermute(parts[k], 'pool', [(i, i ^ k) for i in range(len(parts))])  8.23 us
    pallas_call x1, Pallas kernels, body(): pl.pallas_call(functools.partial(project_rest_kernel, pool, widths[0]), o...  5.33 us
    pallas_call x1, Pallas kernels, body(): pl.pallas_call(functools.partial(merge_kernel, pool, slots, rows_local, q...  1.33 us
    pallas_call x1, Pallas kernels, body(): pl.pallas_call(functools.partial(attend_kernel, pool, slots, seg, width_d...  1.06 us
  transfers between devices with their start and end apart: 8, of which 4 were waited for; matrix products, arithmetic and copies ran while one was open for 0% of the time, Pallas kernels for 14%

profile of v13, /device:TPU:0, one launch (start us, length us, event | category | flops | bytes accessed | tf_op | source)
XLA Modules:
  0.0 38.9 jit_solution(690546535694444557)
XLA Ops:
  0.0 9.4 %project.1 = (bf16[16,2944]{1,0:T(8,128)(2,1)S(1)}, bf16[16,2944]{1,0:T(8,128)(2,1)S(1)}, bf16[16,2944]{1,0:T(8,128)(2,1)S(1)}, bf16[16,2944]{1,0:T(8,128)(2,1)S...) custom-call(s32[1]{0:T(128)} %bitcast.me_ref, ...), custom_call_target="tpu_custom_call" | custom-call | tf_op jit(solution)/shard_map/project/pallas_call | solution.py:513
  9.4 4.1 %collective-permute-start.1 = (bf16[16,2944]{1,0:T(8,128)(2,1)S(1)}, bf16[16,2944]{1,0:T(8,128)(2,1)S(1)}, u32[]{:S(2)}, u32[]{:S(2)}) collective-permute-start(bf16[16,2944]{1,0:T(8,128)(2,1)S(1)} %get-tuple-element.36), channel_id=1, source_target_pairs={{0,8},{4,12},{8,0},{12,4},{1,9},{5,13},{9,1},{13,5},{2,10},{6,14},... | collective-permute-start | bytes 282632 | tf_op jit(solution)/shard_map/ppermute | solution.py:462
  13.5 1.3 %collective-permute-start.2 = (bf16[16,2944]{1,0:T(8,128)(2,1)S(1)}, bf16[16,2944]{1,0:T(8,128)(2,1)S(1)}, u32[]{:S(2)}, u32[]{:S(2)}) collective-permute-start(bf16[16,2944]{1,0:T(8,128)(2,1)S(1)} %get-tuple-element.37), channel_id=1, source_target_pairs={{0,12},{4,8},{8,4},{12,0},{1,13},{5,9},{9,5},{13,1},{2,14},{6,10},... | collective-permute-start | bytes 282632 | tf_op jit(solution)/shard_map/ppermute | solution.py:462
  14.8 0.0 copy-start.2
  14.9 0.0 copy-start.3
  14.9 0.0 copy-start
  14.9 0.0 copy-start.1
  14.9 5.3 %project_rest.1 = (bf16[16,1792]{1,0:T(8,128)(2,1)S(1)}, bf16[16,4736]{1,0:T(8,128)(2,1)S(1)}, bf16[16,1792]{1,0:T(8,128)(2,1)S(1)}, bf16[16,1792]{1,0:T(8,128)(2,1)S(1)}) custom-call(bf16[64,4096]{1,0:T(8,128)(2,1)S(1)} %get-tuple-element.30.lhs, f32[64,64]{1,0:T(8,128)S(1)} %get-tuple-element.31.pick, bf16[16,2944]{1,0:T(8,128)(2,1)S(1)} %get-tuple-element.32.near, ...), custom_call_target="tpu_custom_call" | custom-call | flops 939524096 | bytes 15204352 | tf_op jit(solution)/shard_map/project_rest/pallas_call | solution.py:543
  20.2 0.3 collective-permute-start.4
  20.5 2.8 %collective-permute-start = (bf16[16,1792]{1,0:T(8,128)(2,1)S(1)}, bf16[16,1792]{1,0:T(8,128)(2,1)S(1)}, u32[]{:S(2)}, u32[]{:S(2)}) collective-permute-start(bf16[16,1792]{1,0:T(8,128)(2,1)S(1)} %get-tuple-element.35), channel_id=1, source_target_pairs={{0,8},{4,12},{8,0},{12,4},{1,9},{5,13},{9,1},{13,5},{2,10},{6,14},... | collective-permute-start | bytes 172040 | tf_op jit(solution)/shard_map/ppermute | solution.py:462
  23.3 0.0 collective-permute-done.1.rest_4_
  23.3 0.0 collective-permute-done.2.rest_5_
  23.3 1.3 %collective-permute-start.3 = (bf16[16,1792]{1,0:T(8,128)(2,1)S(1)}, bf16[16,1792]{1,0:T(8,128)(2,1)S(1)}, u32[]{:S(2)}, u32[]{:S(2)}) collective-permute-start(bf16[16,1792]{1,0:T(8,128)(2,1)S(1)} %get-tuple-element.39), channel_id=1, source_target_pairs={{0,12},{4,8},{8,4},{12,0},{1,13},{5,9},{9,5},{13,1},{2,14},{6,10},... | collective-permute-start | bytes 172040 | tf_op jit(solution)/shard_map/ppermute | solution.py:462
  24.7 0.0 copy-done.2
  24.7 0.0 copy-done.3
  24.7 0.1 sine_multiply_fusion
  24.7 1.7 %collective-permute-done.rest_2_ = bf16[16,1792]{1,0:T(8,128)(2,1)S(1)} collective-permute-done((bf16[16,1792]{1,0:T(8,128)(2,1)S(1)}, bf16[16,1792]{1,0:T(8,128)(2,1)S(1)}, u32[]{:S(2)}, u32[]{:S(2)}) %collective-permute-start) | collective-permute-done | bytes 57376 | tf_op jit(solution)/shard_map/ppermute | solution.py:462
  26.4 2.9 %collective-permute-done.3.rest_3_ = bf16[16,1792]{1,0:T(8,128)(2,1)S(1)} collective-permute-done((bf16[16,1792]{1,0:T(8,128)(2,1)S(1)}, bf16[16,1792]{1,0:T(8,128)(2,1)S(1)}, u32[]{:S(2)}, u32[]{:S(2)}) %collective-permute-start.3) | collective-permute-done | bytes 57376 | tf_op jit(solution)/shard_map/ppermute | solution.py:462
  29.3 0.0 collective-permute-done.4.rest_6_
  29.3 0.0 copy-done
  29.3 0.0 copy-done.1
  29.3 1.1 %attend.1 = (bf16[144,128]{1,0:T(8,128)(2,1)S(1)}, bf16[144,128]{1,0:T(8,128)(2,1)S(1)}, bf16[144,128]{1,0:T(8,128)(2,1)S(1)}, bf16[144,128]{1,0:T(8,128)(2,1)S(1)}) custom-call(s32[1]{0:T(128)} %bitcast.me_ref, bf16[16,2944]{1,0:T(8,128)(2,1)S(1)} %get-tuple-element.29.rest_0_, bf16[16,1792]{1,0:T(8,128)(2,1)S(1)} %get-tuple-element.34.rest_1_, ...), custom_call_target="tpu_custom_call" | custom-call | tf_op jit(solution)/shard_map/attend/pallas_call | solution.py:580
  30.4 1.4 %collective-permute-start.5 = (bf16[144,128]{1,0:T(8,128)(2,1)S(1)}, bf16[144,128]{1,0:T(8,128)(2,1)S(1)}, u32[]{:S(2)}, u32[]{:S(2)}) collective-permute-start(bf16[144,128]{1,0:T(8,128)(2,1)S(1)} %get-tuple-element.46), channel_id=1, source_target_pairs={{0,8},{4,12},{8,0},{12,4},{1,9},{5,13},{9,1},{13,5},{2,10},{6,14},... | collective-permute-start | bytes 110600 | tf_op jit(solution)/shard_map/ppermute | solution.py:462
  31.8 0.8 %collective-permute-start.6 = (bf16[144,128]{1,0:T(8,128)(2,1)S(1)}, bf16[144,128]{1,0:T(8,128)(2,1)S(1)}, u32[]{:S(2)}, u32[]{:S(2)}) collective-permute-start(bf16[144,128]{1,0:T(8,128)(2,1)S(1)} %get-tuple-element.47), channel_id=1, source_target_pairs={{0,12},{4,8},{8,4},{12,0},{1,13},{5,9},{9,5},{13,1},{2,14},{6,10},... | collective-permute-start | bytes 110600 | tf_op jit(solution)/shard_map/ppermute | solution.py:462
  32.6 1.3 %collective-permute-start.7 = (bf16[144,128]{1,0:T(8,128)(2,1)S(1)}, bf16[144,128]{1,0:T(8,128)(2,1)S(1)}, u32[]{:S(2)}, u32[]{:S(2)}) collective-permute-start(bf16[144,128]{1,0:T(8,128)(2,1)S(1)} %get-tuple-element.48), channel_id=1, source_target_pairs={{0,4},{4,0},{8,12},{12,8},{1,5},{5,1},{9,13},{13,9},{2,6},{6,2},{1... | collective-permute-start | bytes 110600 | tf_op jit(solution)/shard_map/ppermute | solution.py:462
  33.9 1.4 %collective-permute-done.5.rest_0_ = bf16[144,128]{1,0:T(8,128)(2,1)S(1)} collective-permute-done((bf16[144,128]{1,0:T(8,128)(2,1)S(1)}, bf16[144,128]{1,0:T(8,128)(2,1)S(1)}, u32[]{:S(2)}, u32[]{:S(2)}) %collective-permute-start.5) | collective-permute-done | bytes 36896 | tf_op jit(solution)/shard_map/ppermute | solution.py:462
  35.3 2.3 %collective-permute-done.6.rest_1_ = bf16[144,128]{1,0:T(8,128)(2,1)S(1)} collective-permute-done((bf16[144,128]{1,0:T(8,128)(2,1)S(1)}, bf16[144,128]{1,0:T(8,128)(2,1)S(1)}, u32[]{:S(2)}, u32[]{:S(2)}) %collective-permute-start.6) | collective-permute-done | bytes 36896 | tf_op jit(solution)/shard_map/ppermute | solution.py:462
  37.6 0.0 collective-permute-done.7.rest_2_
  37.6 1.3 %merge.1 = bf16[16,4096]{1,0:T(8,128)(2,1)} custom-call(s32[1,128]{1,0:T(1,128)S(1)} %get-tuple-element.27.slots_ref, s32[4,128]{1,0:T(4,128)S(1)} %get-tuple-element.28.rows_ref, bf16[144,128]{1,0:T(8,128)(2,1)S(1)} %get-tuple-element.45.own, bf16[144,128]{1,0:T(8,128)(2,1)S(1)} %collective-permute-done.5.rest_0_, ...), custom_call_target="tpu_custom_call" | custom-call | tf_op jit(solution)/shard_map/merge/pallas_call | solution.py:592
Async XLA Ops:
  9.4 13.9 %collective-permute-start.1 = (bf16[16,2944]{1,0:T(8,128)(2,1)S(1)}, bf16[16,2944]{1,0:T(8,128)(2,1)S(1)}, u32[]{:S(2)}, u32[]{:S(2)}) collective-permute-start(bf16[16,2944]{1,0:T(8,128)(2,1)S(1)} %get-tuple-element.36), channel_id=1, source_target_pairs={{0,8},{4,12},{8,0},{12,4},{1,9},{5,13},{9,1},{13,5},{2,10},{6,14},... | collective-permute-start | bytes 282632 | tf_op jit(solution)/shard_map/ppermute | solution.py:462
  13.5 9.8 %collective-permute-start.2 = (bf16[16,2944]{1,0:T(8,128)(2,1)S(1)}, bf16[16,2944]{1,0:T(8,128)(2,1)S(1)}, u32[]{:S(2)}, u32[]{:S(2)}) collective-permute-start(bf16[16,2944]{1,0:T(8,128)(2,1)S(1)} %get-tuple-element.37), channel_id=1, source_target_pairs={{0,12},{4,8},{8,4},{12,0},{1,13},{5,9},{9,5},{13,1},{2,14},{6,10},... | collective-permute-start | bytes 282632 | tf_op jit(solution)/shard_map/ppermute | solution.py:462
  14.8 9.8 %copy-start.2 = (f32[128]{0:T(128)S(1)}, f32[128]{0:T(128)}, u32[]{:S(2)}) copy-start(f32[128]{0:T(128)} %constant.12) | copy-start | bytes 1540
  14.9 9.8 %copy-start.3 = (f32[128]{0:T(128)S(1)}, f32[128]{0:T(128)}, u32[]{:S(2)}) copy-start(f32[128]{0:T(128)} %constant.13) | copy-start | bytes 1540
  14.9 14.4 %copy-start = (bf16[1024,256]{1,0:T(8,128)(2,1)S(1)}, bf16[1024,256]{1,0:T(8,128)(2,1)}, u32[]{:S(2)}) copy-start(bf16[1024,256]{1,0:T(8,128)(2,1)} %rest_10_.1) | copy-start | bytes 1572868
  14.9 14.4 %copy-start.1 = (bf16[1024,256]{1,0:T(8,128)(2,1)S(1)}, bf16[1024,256]{1,0:T(8,128)(2,1)}, u32[]{:S(2)}) copy-start(bf16[1024,256]{1,0:T(8,128)(2,1)} %rest_11_.1) | copy-start | bytes 1572868
  20.2 9.1 %collective-permute-start.4 = (bf16[16,4736]{1,0:T(8,128)(2,1)S(1)}, bf16[16,4736]{1,0:T(8,128)(2,1)S(1)}, u32[]{:S(2)}, u32[]{:S(2)}) collective-permute-start(bf16[16,4736]{1,0:T(8,128)(2,1)S(1)} %get-tuple-element.42), channel_id=1, source_target_pairs={{0,4},{4,0},{8,12},{12,8},{1,5},{5,1},{9,13},{13,9},{2,6},{6,2},{1... | collective-permute-start | bytes 454664 | tf_op jit(solution)/shard_map/ppermute | solution.py:462
  20.5 5.9 %collective-permute-start = (bf16[16,1792]{1,0:T(8,128)(2,1)S(1)}, bf16[16,1792]{1,0:T(8,128)(2,1)S(1)}, u32[]{:S(2)}, u32[]{:S(2)}) collective-permute-start(bf16[16,1792]{1,0:T(8,128)(2,1)S(1)} %get-tuple-element.35), channel_id=1, source_target_pairs={{0,8},{4,12},{8,0},{12,4},{1,9},{5,13},{9,1},{13,5},{2,10},{6,14},... | collective-permute-start | bytes 172040 | tf_op jit(solution)/shard_map/ppermute | solution.py:462
  23.3 6.0 %collective-permute-start.3 = (bf16[16,1792]{1,0:T(8,128)(2,1)S(1)}, bf16[16,1792]{1,0:T(8,128)(2,1)S(1)}, u32[]{:S(2)}, u32[]{:S(2)}) collective-permute-start(bf16[16,1792]{1,0:T(8,128)(2,1)S(1)} %get-tuple-element.39), channel_id=1, source_target_pairs={{0,12},{4,8},{8,4},{12,0},{1,13},{5,9},{9,5},{13,1},{2,14},{6,10},... | collective-permute-start | bytes 172040 | tf_op jit(solution)/shard_map/ppermute | solution.py:462
  30.4 4.9 %collective-permute-start.5 = (bf16[144,128]{1,0:T(8,128)(2,1)S(1)}, bf16[144,128]{1,0:T(8,128)(2,1)S(1)}, u32[]{:S(2)}, u32[]{:S(2)}) collective-permute-start(bf16[144,128]{1,0:T(8,128)(2,1)S(1)} %get-tuple-element.46), channel_id=1, source_target_pairs={{0,8},{4,12},{8,0},{12,4},{1,9},{5,13},{9,1},{13,5},{2,10},{6,14},... | collective-permute-start | bytes 110600 | tf_op jit(solution)/shard_map/ppermute | solution.py:462
  31.8 5.8 %collective-permute-start.6 = (bf16[144,128]{1,0:T(8,128)(2,1)S(1)}, bf16[144,128]{1,0:T(8,128)(2,1)S(1)}, u32[]{:S(2)}, u32[]{:S(2)}) collective-permute-start(bf16[144,128]{1,0:T(8,128)(2,1)S(1)} %get-tuple-element.47), channel_id=1, source_target_pairs={{0,12},{4,8},{8,4},{12,0},{1,13},{5,9},{9,5},{13,1},{2,14},{6,10},... | collective-permute-start | bytes 110600 | tf_op jit(solution)/shard_map/ppermute | solution.py:462
  32.6 4.9 %collective-permute-start.7 = (bf16[144,128]{1,0:T(8,128)(2,1)S(1)}, bf16[144,128]{1,0:T(8,128)(2,1)S(1)}, u32[]{:S(2)}, u32[]{:S(2)}) collective-permute-start(bf16[144,128]{1,0:T(8,128)(2,1)S(1)} %get-tuple-element.48), channel_id=1, source_target_pairs={{0,4},{4,0},{8,12},{12,8},{1,5},{5,1},{9,13},{13,9},{2,6},{6,2},{1... | collective-permute-start | bytes 110600 | tf_op jit(solution)/shard_map/ppermute | solution.py:462

commit v14 on v13

--- a/solution.py
+++ b/solution.py
@@ -12,7 +12,7 @@
 EPS = 1e-05
 THETA = 500000.0
 LOW = -1e30
-DEEP = 512
+DEEP = 1024
 LEVELS = 16
 TILE = 1536
 
@@ -134,7 +134,7 @@
             lax.rem(place // group, slots) == c, mine, home_rows[pl.ds(k, 1), :]
         )
 
-    chore_steps = 4
+    chore_steps = 2
     spread_chores = count > chore_steps + 1 and pool * per <= 64 and per % chore_steps == 0
 
     def each(do, total, t):
@@ -160,7 +160,7 @@
         return left
 
     kv_cols = w_key.shape[1]
-    cuts = [0, deep // 4, deep // 2, deep] if count > 1 else [0, deep]
+    cuts = [0, deep // 8, deep // 4, deep // 2, deep] if count > 1 else [0, deep]
 
     def pieces(t):
         if isinstance(t, int) and t == 0:
@@ -179,7 +179,7 @@
             ((w_key, narrow.at[:, :kv_cols]), (w_value, narrow.at[:, kv_cols:]))
         )
     ]
-    begin, advance = stream(count, pieces, following, 3)
+    begin, advance = stream(count, pieces, following, 2)
 
     def use(t):
         advance(t)
@@ -201,6 +201,7 @@
             add_products(left[:, a:b], query_buf.at[0, a:b], sums)
 
     def use_last(t):
+        advance(t)
         left = scale(t)
         for copy in pieces(t):
             copy.wait()
@@ -532,7 +533,7 @@
             pltpu.VMEM((n_rows, widths[0]), jnp.float32),
             pltpu.VMEM((n_rows, HD), jnp.float32),
             pltpu.SemaphoreType.DMA((7,)),
-            pltpu.SemaphoreType.DMA((count + 3,)),
+            pltpu.SemaphoreType.DMA((count + 4,)),
         ],
         compiler_params=pltpu.CompilerParams(vmem_limit_bytes=46 * 2**20),
         name="project",

time: 39.1 us -> 39.6 us (1.013)
  Pallas kernels: 17.1 us -> 17.6 us
where the time goes in v14:
time: 39.6 us; the launch traced here: 39.4 us
  Pallas kernels  17.6 us (44%)
  starting transfers between devices  13.5 us (34%)
  waiting for transfers between devices  8.22 us (21%)
    ppermute x8, starting transfers between devices, exchange(): lax.ppermute(parts[k], 'pool', [(i, i ^ k) for i in range(len(parts))])  13.5 us
    pallas_call x1, Pallas kernels, body(): pl.pallas_call(functools.partial(project_kernel, pool, slots, rows_local)...  9.64 us
    ppermute x8, waiting for transfers between devices, exchange(): lax.ppermute(parts[k], 'pool', [(i, i ^ k) for i in range(len(parts))])  8.22 us
    pallas_call x1, Pallas kernels, body(): pl.pallas_call(functools.partial(project_rest_kernel, pool, widths[0]), o...  5.57 us
    pallas_call x1, Pallas kernels, body(): pl.pallas_call(functools.partial(merge_kernel, pool, slots, rows_local, q...  1.33 us
    pallas_call x1, Pallas kernels, body(): pl.pallas_call(functools.partial(attend_kernel, pool, slots, seg, width_d...  1.07 us
  transfers between devices with their start and end apart: 8, of which 4 were waited for; matrix products, arithmetic and copies ran while one was open for 0% of the time, Pallas kernels for 14%

profile of v14, /device:TPU:0, one launch (start us, length us, event | category | flops | bytes accessed | tf_op | source)
XLA Modules:
  0.0 39.4 jit_solution(14252350857246009565)
XLA Ops:
  0.0 9.6 %project.1 = (bf16[16,2944]{1,0:T(8,128)(2,1)S(1)}, bf16[16,2944]{1,0:T(8,128)(2,1)S(1)}, bf16[16,2944]{1,0:T(8,128)(2,1)S(1)}, bf16[16,2944]{1,0:T(8,128)(2,1)S...) custom-call(s32[1]{0:T(128)} %bitcast.me_ref, ...), custom_call_target="tpu_custom_call" | custom-call | tf_op jit(solution)/shard_map/project/pallas_call | solution.py:514
  9.7 4.1 %collective-permute-start.1 = (bf16[16,2944]{1,0:T(8,128)(2,1)S(1)}, bf16[16,2944]{1,0:T(8,128)(2,1)S(1)}, u32[]{:S(2)}, u32[]{:S(2)}) collective-permute-start(bf16[16,2944]{1,0:T(8,128)(2,1)S(1)} %get-tuple-element.36), channel_id=1, source_target_pairs={{0,8},{4,12},{8,0},{12,4},{1,9},{5,13},{9,1},{13,5},{2,10},{6,14},... | collective-permute-start | bytes 282632 | tf_op jit(solution)/shard_map/ppermute | solution.py:463
  13.8 1.3 %collective-permute-start.2 = (bf16[16,2944]{1,0:T(8,128)(2,1)S(1)}, bf16[16,2944]{1,0:T(8,128)(2,1)S(1)}, u32[]{:S(2)}, u32[]{:S(2)}) collective-permute-start(bf16[16,2944]{1,0:T(8,128)(2,1)S(1)} %get-tuple-element.37), channel_id=1, source_target_pairs={{0,12},{4,8},{8,4},{12,0},{1,13},{5,9},{9,5},{13,1},{2,14},{6,10},... | collective-permute-start | bytes 282632 | tf_op jit(solution)/shard_map/ppermute | solution.py:463
  15.1 0.0 copy-start.2
  15.1 0.0 copy-start.3
  15.1 0.0 copy-start
  15.1 0.0 copy-start.1
  15.1 5.6 %project_rest.1 = (bf16[16,1792]{1,0:T(8,128)(2,1)S(1)}, bf16[16,4736]{1,0:T(8,128)(2,1)S(1)}, bf16[16,1792]{1,0:T(8,128)(2,1)S(1)}, bf16[16,1792]{1,0:T(8,128)(2,1)S(1)}) custom-call(bf16[64,4096]{1,0:T(8,128)(2,1)S(1)} %get-tuple-element.30.lhs, f32[64,64]{1,0:T(8,128)S(1)} %get-tuple-element.31.pick, bf16[16,2944]{1,0:T(8,128)(2,1)S(1)} %get-tuple-element.32.near, ...), custom_call_target="tpu_custom_call" | custom-call | flops 939524096 | bytes 15204352 | tf_op jit(solution)/shard_map/project_rest/pallas_call | solution.py:544
  20.7 0.3 collective-permute-start.4
  21.0 2.8 %collective-permute-start = (bf16[16,1792]{1,0:T(8,128)(2,1)S(1)}, bf16[16,1792]{1,0:T(8,128)(2,1)S(1)}, u32[]{:S(2)}, u32[]{:S(2)}) collective-permute-start(bf16[16,1792]{1,0:T(8,128)(2,1)S(1)} %get-tuple-element.35), channel_id=1, source_target_pairs={{0,8},{4,12},{8,0},{12,4},{1,9},{5,13},{9,1},{13,5},{2,10},{6,14},... | collective-permute-start | bytes 172040 | tf_op jit(solution)/shard_map/ppermute | solution.py:463
  23.8 0.0 collective-permute-done.1.rest_4_
  23.8 0.0 collective-permute-done.2.rest_5_
  23.8 1.3 %collective-permute-start.3 = (bf16[16,1792]{1,0:T(8,128)(2,1)S(1)}, bf16[16,1792]{1,0:T(8,128)(2,1)S(1)}, u32[]{:S(2)}, u32[]{:S(2)}) collective-permute-start(bf16[16,1792]{1,0:T(8,128)(2,1)S(1)} %get-tuple-element.39), channel_id=1, source_target_pairs={{0,12},{4,8},{8,4},{12,0},{1,13},{5,9},{9,5},{13,1},{2,14},{6,10},... | collective-permute-start | bytes 172040 | tf_op jit(solution)/shard_map/ppermute | solution.py:463
  25.2 0.0 copy-done.2
  25.2 0.0 copy-done.3
  25.2 0.1 sine_multiply_fusion
  25.2 1.7 %collective-permute-done.rest_2_ = bf16[16,1792]{1,0:T(8,128)(2,1)S(1)} collective-permute-done((bf16[16,1792]{1,0:T(8,128)(2,1)S(1)}, bf16[16,1792]{1,0:T(8,128)(2,1)S(1)}, u32[]{:S(2)}, u32[]{:S(2)}) %collective-permute-start) | collective-permute-done | bytes 57376 | tf_op jit(solution)/shard_map/ppermute | solution.py:463
  27.0 2.8 %collective-permute-done.3.rest_3_ = bf16[16,1792]{1,0:T(8,128)(2,1)S(1)} collective-permute-done((bf16[16,1792]{1,0:T(8,128)(2,1)S(1)}, bf16[16,1792]{1,0:T(8,128)(2,1)S(1)}, u32[]{:S(2)}, u32[]{:S(2)}) %collective-permute-start.3) | collective-permute-done | bytes 57376 | tf_op jit(solution)/shard_map/ppermute | solution.py:463
  29.8 0.0 collective-permute-done.4.rest_6_
  29.8 0.0 copy-done
  29.8 0.0 copy-done.1
  29.8 1.1 %attend.1 = (bf16[144,128]{1,0:T(8,128)(2,1)S(1)}, bf16[144,128]{1,0:T(8,128)(2,1)S(1)}, bf16[144,128]{1,0:T(8,128)(2,1)S(1)}, bf16[144,128]{1,0:T(8,128)(2,1)S(1)}) custom-call(s32[1]{0:T(128)} %bitcast.me_ref, bf16[16,2944]{1,0:T(8,128)(2,1)S(1)} %get-tuple-element.29.rest_0_, bf16[16,1792]{1,0:T(8,128)(2,1)S(1)} %get-tuple-element.34.rest_1_, ...), custom_call_target="tpu_custom_call" | custom-call | tf_op jit(solution)/shard_map/attend/pallas_call | solution.py:581
  30.9 1.4 %collective-permute-start.5 = (bf16[144,128]{1,0:T(8,128)(2,1)S(1)}, bf16[144,128]{1,0:T(8,128)(2,1)S(1)}, u32[]{:S(2)}, u32[]{:S(2)}) collective-permute-start(bf16[144,128]{1,0:T(8,128)(2,1)S(1)} %get-tuple-element.46), channel_id=1, source_target_pairs={{0,8},{4,12},{8,0},{12,4},{1,9},{5,13},{9,1},{13,5},{2,10},{6,14},... | collective-permute-start | bytes 110600 | tf_op jit(solution)/shard_map/ppermute | solution.py:463
  32.3 0.8 %collective-permute-start.6 = (bf16[144,128]{1,0:T(8,128)(2,1)S(1)}, bf16[144,128]{1,0:T(8,128)(2,1)S(1)}, u32[]{:S(2)}, u32[]{:S(2)}) collective-permute-start(bf16[144,128]{1,0:T(8,128)(2,1)S(1)} %get-tuple-element.47), channel_id=1, source_target_pairs={{0,12},{4,8},{8,4},{12,0},{1,13},{5,9},{9,5},{13,1},{2,14},{6,10},... | collective-permute-start | bytes 110600 | tf_op jit(solution)/shard_map/ppermute | solution.py:463
  33.1 1.3 %collective-permute-start.7 = (bf16[144,128]{1,0:T(8,128)(2,1)S(1)}, bf16[144,128]{1,0:T(8,128)(2,1)S(1)}, u32[]{:S(2)}, u32[]{:S(2)}) collective-permute-start(bf16[144,128]{1,0:T(8,128)(2,1)S(1)} %get-tuple-element.48), channel_id=1, source_target_pairs={{0,4},{4,0},{8,12},{12,8},{1,5},{5,1},{9,13},{13,9},{2,6},{6,2},{1... | collective-permute-start | bytes 110600 | tf_op jit(solution)/shard_map/ppermute | solution.py:463
  34.4 1.4 %collective-permute-done.5.rest_0_ = bf16[144,128]{1,0:T(8,128)(2,1)S(1)} collective-permute-done((bf16[144,128]{1,0:T(8,128)(2,1)S(1)}, bf16[144,128]{1,0:T(8,128)(2,1)S(1)}, u32[]{:S(2)}, u32[]{:S(2)}) %collective-permute-start.5) | collective-permute-done | bytes 36896 | tf_op jit(solution)/shard_map/ppermute | solution.py:463
  35.8 2.3 %collective-permute-done.6.rest_1_ = bf16[144,128]{1,0:T(8,128)(2,1)S(1)} collective-permute-done((bf16[144,128]{1,0:T(8,128)(2,1)S(1)}, bf16[144,128]{1,0:T(8,128)(2,1)S(1)}, u32[]{:S(2)}, u32[]{:S(2)}) %collective-permute-start.6) | collective-permute-done | bytes 36896 | tf_op jit(solution)/shard_map/ppermute | solution.py:463
  38.1 0.0 collective-permute-done.7.rest_2_
  38.1 1.3 %merge.1 = bf16[16,4096]{1,0:T(8,128)(2,1)} custom-call(s32[1,128]{1,0:T(1,128)S(1)} %get-tuple-element.27.slots_ref, s32[4,128]{1,0:T(4,128)S(1)} %get-tuple-element.28.rows_ref, bf16[144,128]{1,0:T(8,128)(2,1)S(1)} %get-tuple-element.45.own, bf16[144,128]{1,0:T(8,128)(2,1)S(1)} %collective-permute-done.5.rest_0_, ...), custom_call_target="tpu_custom_call" | custom-call | tf_op jit(solution)/shard_map/merge/pallas_call | solution.py:593
Async XLA Ops:
  9.7 14.1 %collective-permute-start.1 = (bf16[16,2944]{1,0:T(8,128)(2,1)S(1)}, bf16[16,2944]{1,0:T(8,128)(2,1)S(1)}, u32[]{:S(2)}, u32[]{:S(2)}) collective-permute-start(bf16[16,2944]{1,0:T(8,128)(2,1)S(1)} %get-tuple-element.36), channel_id=1, source_target_pairs={{0,8},{4,12},{8,0},{12,4},{1,9},{5,13},{9,1},{13,5},{2,10},{6,14},... | collective-permute-start | bytes 282632 | tf_op jit(solution)/shard_map/ppermute | solution.py:463
  13.8 10.0 %collective-permute-start.2 = (bf16[16,2944]{1,0:T(8,128)(2,1)S(1)}, bf16[16,2944]{1,0:T(8,128)(2,1)S(1)}, u32[]{:S(2)}, u32[]{:S(2)}) collective-permute-start(bf16[16,2944]{1,0:T(8,128)(2,1)S(1)} %get-tuple-element.37), channel_id=1, source_target_pairs={{0,12},{4,8},{8,4},{12,0},{1,13},{5,9},{9,5},{13,1},{2,14},{6,10},... | collective-permute-start | bytes 282632 | tf_op jit(solution)/shard_map/ppermute | solution.py:463
  15.1 10.1 %copy-start.2 = (f32[128]{0:T(128)S(1)}, f32[128]{0:T(128)}, u32[]{:S(2)}) copy-start(f32[128]{0:T(128)} %constant.12) | copy-start | bytes 1540
  15.1 10.1 %copy-start.3 = (f32[128]{0:T(128)S(1)}, f32[128]{0:T(128)}, u32[]{:S(2)}) copy-start(f32[128]{0:T(128)} %constant.13) | copy-start | bytes 1540
  15.1 14.7 %copy-start = (bf16[1024,256]{1,0:T(8,128)(2,1)S(1)}, bf16[1024,256]{1,0:T(8,128)(2,1)}, u32[]{:S(2)}) copy-start(bf16[1024,256]{1,0:T(8,128)(2,1)} %rest_10_.1) | copy-start | bytes 1572868
  15.1 14.7 %copy-start.1 = (bf16[1024,256]{1,0:T(8,128)(2,1)S(1)}, bf16[1024,256]{1,0:T(8,128)(2,1)}, u32[]{:S(2)}) copy-start(bf16[1024,256]{1,0:T(8,128)(2,1)} %rest_11_.1) | copy-start | bytes 1572868
  20.7 9.1 %collective-permute-start.4 = (bf16[16,4736]{1,0:T(8,128)(2,1)S(1)}, bf16[16,4736]{1,0:T(8,128)(2,1)S(1)}, u32[]{:S(2)}, u32[]{:S(2)}) collective-permute-start(bf16[16,4736]{1,0:T(8,128)(2,1)S(1)} %get-tuple-element.42), channel_id=1, source_target_pairs={{0,4},{4,0},{8,12},{12,8},{1,5},{5,1},{9,13},{13,9},{2,6},{6,2},{1... | collective-permute-start | bytes 454664 | tf_op jit(solution)/shard_map/ppermute | solution.py:463
  21.0 6.0 %collective-permute-start = (bf16[16,1792]{1,0:T(8,128)(2,1)S(1)}, bf16[16,1792]{1,0:T(8,128)(2,1)S(1)}, u32[]{:S(2)}, u32[]{:S(2)}) collective-permute-start(bf16[16,1792]{1,0:T(8,128)(2,1)S(1)} %get-tuple-element.35), channel_id=1, source_target_pairs={{0,8},{4,12},{8,0},{12,4},{1,9},{5,13},{9,1},{13,5},{2,10},{6,14},... | collective-permute-start | bytes 172040 | tf_op jit(solution)/shard_map/ppermute | solution.py:463
  23.8 6.0 %collective-permute-start.3 = (bf16[16,1792]{1,0:T(8,128)(2,1)S(1)}, bf16[16,1792]{1,0:T(8,128)(2,1)S(1)}, u32[]{:S(2)}, u32[]{:S(2)}) collective-permute-start(bf16[16,1792]{1,0:T(8,128)(2,1)S(1)} %get-tuple-element.39), channel_id=1, source_target_pairs={{0,12},{4,8},{8,4},{12,0},{1,13},{5,9},{9,5},{13,1},{2,14},{6,10},... | collective-permute-start | bytes 172040 | tf_op jit(solution)/shard_map/ppermute | solution.py:463
  30.9 4.9 %collective-permute-start.5 = (bf16[144,128]{1,0:T(8,128)(2,1)S(1)}, bf16[144,128]{1,0:T(8,128)(2,1)S(1)}, u32[]{:S(2)}, u32[]{:S(2)}) collective-permute-start(bf16[144,128]{1,0:T(8,128)(2,1)S(1)} %get-tuple-element.46), channel_id=1, source_target_pairs={{0,8},{4,12},{8,0},{12,4},{1,9},{5,13},{9,1},{13,5},{2,10},{6,14},... | collective-permute-start | bytes 110600 | tf_op jit(solution)/shard_map/ppermute | solution.py:463
  32.3 5.8 %collective-permute-start.6 = (bf16[144,128]{1,0:T(8,128)(2,1)S(1)}, bf16[144,128]{1,0:T(8,128)(2,1)S(1)}, u32[]{:S(2)}, u32[]{:S(2)}) collective-permute-start(bf16[144,128]{1,0:T(8,128)(2,1)S(1)} %get-tuple-element.47), channel_id=1, source_target_pairs={{0,12},{4,8},{8,4},{12,0},{1,13},{5,9},{9,5},{13,1},{2,14},{6,10},... | collective-permute-start | bytes 110600 | tf_op jit(solution)/shard_map/ppermute | solution.py:463
  33.1 4.9 %collective-permute-start.7 = (bf16[144,128]{1,0:T(8,128)(2,1)S(1)}, bf16[144,128]{1,0:T(8,128)(2,1)S(1)}, u32[]{:S(2)}, u32[]{:S(2)}) collective-permute-start(bf16[144,128]{1,0:T(8,128)(2,1)S(1)} %get-tuple-element.48), channel_id=1, source_target_pairs={{0,4},{4,0},{8,12},{12,8},{1,5},{5,1},{9,13},{13,9},{2,6},{6,2},{1... | collective-permute-start | bytes 110600 | tf_op jit(solution)/shard_map/ppermute | solution.py:463

commit v15 on v11

--- a/solution.py
+++ b/solution.py
@@ -14,7 +14,7 @@
 LOW = -1e30
 DEEP = 512
 LEVELS = 16
-TILE = 1536
+TILE = 3072
 
 
 def divides(width, limit):

time: 39.1 us -> 39.1 us (level)
  no operation moved by 1% of the time
where the time goes in v15:
time: 39.1 us; the launch traced here: 38.9 us
  Pallas kernels  17.1 us (44%)
  starting transfers between devices  13.5 us (35%)
  waiting for transfers between devices  8.23 us (21%)
    ppermute x8, starting transfers between devices, exchange(): lax.ppermute(parts[k], 'pool', [(i, i ^ k) for i in range(len(parts))])  13.5 us
    pallas_call x1, Pallas kernels, body(): pl.pallas_call(functools.partial(project_kernel, pool, slots, rows_local)...  9.39 us
    ppermute x8, waiting for transfers between devices, exchange(): lax.ppermute(parts[k], 'pool', [(i, i ^ k) for i in range(len(parts))])  8.23 us
    pallas_call x1, Pallas kernels, body(): pl.pallas_call(functools.partial(project_rest_kernel, pool, widths[0]), o...  5.33 us
    pallas_call x1, Pallas kernels, body(): pl.pallas_call(functools.partial(merge_kernel, pool, slots, rows_local, q...  1.33 us
    pallas_call x1, Pallas kernels, body(): pl.pallas_call(functools.partial(attend_kernel, pool, slots, seg, width_d...  1.06 us
  transfers between devices with their start and end apart: 8, of which 4 were waited for; matrix products, arithmetic and copies ran while one was open for 0% of the time, Pallas kernels for 14%

profile of v15, /device:TPU:0, one launch (start us, length us, event | category | flops | bytes accessed | tf_op | source)
XLA Modules:
  0.0 38.9 jit_solution(5876870027152052475)
XLA Ops:
  0.0 9.4 %project.1 = (bf16[16,2944]{1,0:T(8,128)(2,1)S(1)}, bf16[16,2944]{1,0:T(8,128)(2,1)S(1)}, bf16[16,2944]{1,0:T(8,128)(2,1)S(1)}, bf16[16,2944]{1,0:T(8,128)(2,1)S...) custom-call(s32[1]{0:T(128)} %bitcast.me_ref, ...), custom_call_target="tpu_custom_call" | custom-call | tf_op jit(solution)/shard_map/project/pallas_call | solution.py:515
  9.4 4.1 %collective-permute-start.1 = (bf16[16,2944]{1,0:T(8,128)(2,1)S(1)}, bf16[16,2944]{1,0:T(8,128)(2,1)S(1)}, u32[]{:S(2)}, u32[]{:S(2)}) collective-permute-start(bf16[16,2944]{1,0:T(8,128)(2,1)S(1)} %get-tuple-element.36), channel_id=1, source_target_pairs={{0,8},{4,12},{8,0},{12,4},{1,9},{5,13},{9,1},{13,5},{2,10},{6,14},... | collective-permute-start | bytes 282632 | tf_op jit(solution)/shard_map/ppermute | solution.py:464
  13.5 1.3 %collective-permute-start.2 = (bf16[16,2944]{1,0:T(8,128)(2,1)S(1)}, bf16[16,2944]{1,0:T(8,128)(2,1)S(1)}, u32[]{:S(2)}, u32[]{:S(2)}) collective-permute-start(bf16[16,2944]{1,0:T(8,128)(2,1)S(1)} %get-tuple-element.37), channel_id=1, source_target_pairs={{0,12},{4,8},{8,4},{12,0},{1,13},{5,9},{9,5},{13,1},{2,14},{6,10},... | collective-permute-start | bytes 282632 | tf_op jit(solution)/shard_map/ppermute | solution.py:464
  14.8 0.0 copy-start.2
  14.9 0.0 copy-start.3
  14.9 0.0 copy-start
  14.9 0.0 copy-start.1
  14.9 5.3 %project_rest.1 = (bf16[16,1792]{1,0:T(8,128)(2,1)S(1)}, bf16[16,4736]{1,0:T(8,128)(2,1)S(1)}, bf16[16,1792]{1,0:T(8,128)(2,1)S(1)}, bf16[16,1792]{1,0:T(8,128)(2,1)S(1)}) custom-call(bf16[64,4096]{1,0:T(8,128)(2,1)S(1)} %get-tuple-element.30.lhs, f32[64,64]{1,0:T(8,128)S(1)} %get-tuple-element.31.pick, bf16[16,2944]{1,0:T(8,128)(2,1)S(1)} %get-tuple-element.32.near, ...), custom_call_target="tpu_custom_call" | custom-call | flops 939524096 | bytes 15204352 | tf_op jit(solution)/shard_map/project_rest/pallas_call | solution.py:545
  20.2 0.3 collective-permute-start.4
  20.5 2.8 %collective-permute-start = (bf16[16,1792]{1,0:T(8,128)(2,1)S(1)}, bf16[16,1792]{1,0:T(8,128)(2,1)S(1)}, u32[]{:S(2)}, u32[]{:S(2)}) collective-permute-start(bf16[16,1792]{1,0:T(8,128)(2,1)S(1)} %get-tuple-element.35), channel_id=1, source_target_pairs={{0,8},{4,12},{8,0},{12,4},{1,9},{5,13},{9,1},{13,5},{2,10},{6,14},... | collective-permute-start | bytes 172040 | tf_op jit(solution)/shard_map/ppermute | solution.py:464
  23.3 0.0 collective-permute-done.1.rest_4_
  23.3 0.0 collective-permute-done.2.rest_5_
  23.3 1.3 %collective-permute-start.3 = (bf16[16,1792]{1,0:T(8,128)(2,1)S(1)}, bf16[16,1792]{1,0:T(8,128)(2,1)S(1)}, u32[]{:S(2)}, u32[]{:S(2)}) collective-permute-start(bf16[16,1792]{1,0:T(8,128)(2,1)S(1)} %get-tuple-element.39), channel_id=1, source_target_pairs={{0,12},{4,8},{8,4},{12,0},{1,13},{5,9},{9,5},{13,1},{2,14},{6,10},... | collective-permute-start | bytes 172040 | tf_op jit(solution)/shard_map/ppermute | solution.py:464
  24.7 0.0 copy-done.2
  24.7 0.0 copy-done.3
  24.7 0.1 sine_multiply_fusion
  24.7 1.7 %collective-permute-done.rest_2_ = bf16[16,1792]{1,0:T(8,128)(2,1)S(1)} collective-permute-done((bf16[16,1792]{1,0:T(8,128)(2,1)S(1)}, bf16[16,1792]{1,0:T(8,128)(2,1)S(1)}, u32[]{:S(2)}, u32[]{:S(2)}) %collective-permute-start) | collective-permute-done | bytes 57376 | tf_op jit(solution)/shard_map/ppermute | solution.py:464
  26.4 2.9 %collective-permute-done.3.rest_3_ = bf16[16,1792]{1,0:T(8,128)(2,1)S(1)} collective-permute-done((bf16[16,1792]{1,0:T(8,128)(2,1)S(1)}, bf16[16,1792]{1,0:T(8,128)(2,1)S(1)}, u32[]{:S(2)}, u32[]{:S(2)}) %collective-permute-start.3) | collective-permute-done | bytes 57376 | tf_op jit(solution)/shard_map/ppermute | solution.py:464
  29.3 0.0 collective-permute-done.4.rest_6_
  29.3 0.0 copy-done
  29.3 0.0 copy-done.1
  29.3 1.1 %attend.1 = (bf16[144,128]{1,0:T(8,128)(2,1)S(1)}, bf16[144,128]{1,0:T(8,128)(2,1)S(1)}, bf16[144,128]{1,0:T(8,128)(2,1)S(1)}, bf16[144,128]{1,0:T(8,128)(2,1)S(1)}) custom-call(s32[1]{0:T(128)} %bitcast.me_ref, bf16[16,2944]{1,0:T(8,128)(2,1)S(1)} %get-tuple-element.29.rest_0_, bf16[16,1792]{1,0:T(8,128)(2,1)S(1)} %get-tuple-element.34.rest_1_, ...), custom_call_target="tpu_custom_call" | custom-call | tf_op jit(solution)/shard_map/attend/pallas_call | solution.py:582
  30.4 1.4 %collective-permute-start.5 = (bf16[144,128]{1,0:T(8,128)(2,1)S(1)}, bf16[144,128]{1,0:T(8,128)(2,1)S(1)}, u32[]{:S(2)}, u32[]{:S(2)}) collective-permute-start(bf16[144,128]{1,0:T(8,128)(2,1)S(1)} %get-tuple-element.46), channel_id=1, source_target_pairs={{0,8},{4,12},{8,0},{12,4},{1,9},{5,13},{9,1},{13,5},{2,10},{6,14},... | collective-permute-start | bytes 110600 | tf_op jit(solution)/shard_map/ppermute | solution.py:464
  31.8 0.8 %collective-permute-start.6 = (bf16[144,128]{1,0:T(8,128)(2,1)S(1)}, bf16[144,128]{1,0:T(8,128)(2,1)S(1)}, u32[]{:S(2)}, u32[]{:S(2)}) collective-permute-start(bf16[144,128]{1,0:T(8,128)(2,1)S(1)} %get-tuple-element.47), channel_id=1, source_target_pairs={{0,12},{4,8},{8,4},{12,0},{1,13},{5,9},{9,5},{13,1},{2,14},{6,10},... | collective-permute-start | bytes 110600 | tf_op jit(solution)/shard_map/ppermute | solution.py:464
  32.6 1.3 %collective-permute-start.7 = (bf16[144,128]{1,0:T(8,128)(2,1)S(1)}, bf16[144,128]{1,0:T(8,128)(2,1)S(1)}, u32[]{:S(2)}, u32[]{:S(2)}) collective-permute-start(bf16[144,128]{1,0:T(8,128)(2,1)S(1)} %get-tuple-element.48), channel_id=1, source_target_pairs={{0,4},{4,0},{8,12},{12,8},{1,5},{5,1},{9,13},{13,9},{2,6},{6,2},{1... | collective-permute-start | bytes 110600 | tf_op jit(solution)/shard_map/ppermute | solution.py:464
  33.9 1.4 %collective-permute-done.5.rest_0_ = bf16[144,128]{1,0:T(8,128)(2,1)S(1)} collective-permute-done((bf16[144,128]{1,0:T(8,128)(2,1)S(1)}, bf16[144,128]{1,0:T(8,128)(2,1)S(1)}, u32[]{:S(2)}, u32[]{:S(2)}) %collective-permute-start.5) | collective-permute-done | bytes 36896 | tf_op jit(solution)/shard_map/ppermute | solution.py:464
  35.3 2.3 %collective-permute-done.6.rest_1_ = bf16[144,128]{1,0:T(8,128)(2,1)S(1)} collective-permute-done((bf16[144,128]{1,0:T(8,128)(2,1)S(1)}, bf16[144,128]{1,0:T(8,128)(2,1)S(1)}, u32[]{:S(2)}, u32[]{:S(2)}) %collective-permute-start.6) | collective-permute-done | bytes 36896 | tf_op jit(solution)/shard_map/ppermute | solution.py:464
  37.6 0.0 collective-permute-done.7.rest_2_
  37.6 1.3 %merge.1 = bf16[16,4096]{1,0:T(8,128)(2,1)} custom-call(s32[1,128]{1,0:T(1,128)S(1)} %get-tuple-element.27.slots_ref, s32[4,128]{1,0:T(4,128)S(1)} %get-tuple-element.28.rows_ref, bf16[144,128]{1,0:T(8,128)(2,1)S(1)} %get-tuple-element.45.own, bf16[144,128]{1,0:T(8,128)(2,1)S(1)} %collective-permute-done.5.rest_0_, ...), custom_call_target="tpu_custom_call" | custom-call | tf_op jit(solution)/shard_map/merge/pallas_call | solution.py:594
Async XLA Ops:
  9.4 13.9 %collective-permute-start.1 = (bf16[16,2944]{1,0:T(8,128)(2,1)S(1)}, bf16[16,2944]{1,0:T(8,128)(2,1)S(1)}, u32[]{:S(2)}, u32[]{:S(2)}) collective-permute-start(bf16[16,2944]{1,0:T(8,128)(2,1)S(1)} %get-tuple-element.36), channel_id=1, source_target_pairs={{0,8},{4,12},{8,0},{12,4},{1,9},{5,13},{9,1},{13,5},{2,10},{6,14},... | collective-permute-start | bytes 282632 | tf_op jit(solution)/shard_map/ppermute | solution.py:464
  13.5 9.8 %collective-permute-start.2 = (bf16[16,2944]{1,0:T(8,128)(2,1)S(1)}, bf16[16,2944]{1,0:T(8,128)(2,1)S(1)}, u32[]{:S(2)}, u32[]{:S(2)}) collective-permute-start(bf16[16,2944]{1,0:T(8,128)(2,1)S(1)} %get-tuple-element.37), channel_id=1, source_target_pairs={{0,12},{4,8},{8,4},{12,0},{1,13},{5,9},{9,5},{13,1},{2,14},{6,10},... | collective-permute-start | bytes 282632 | tf_op jit(solution)/shard_map/ppermute | solution.py:464
  14.8 9.8 %copy-start.2 = (f32[128]{0:T(128)S(1)}, f32[128]{0:T(128)}, u32[]{:S(2)}) copy-start(f32[128]{0:T(128)} %constant.12) | copy-start | bytes 1540
  14.9 9.8 %copy-start.3 = (f32[128]{0:T(128)S(1)}, f32[128]{0:T(128)}, u32[]{:S(2)}) copy-start(f32[128]{0:T(128)} %constant.13) | copy-start | bytes 1540
  14.9 14.4 %copy-start = (bf16[1024,256]{1,0:T(8,128)(2,1)S(1)}, bf16[1024,256]{1,0:T(8,128)(2,1)}, u32[]{:S(2)}) copy-start(bf16[1024,256]{1,0:T(8,128)(2,1)} %rest_10_.1) | copy-start | bytes 1572868
  14.9 14.4 %copy-start.1 = (bf16[1024,256]{1,0:T(8,128)(2,1)S(1)}, bf16[1024,256]{1,0:T(8,128)(2,1)}, u32[]{:S(2)}) copy-start(bf16[1024,256]{1,0:T(8,128)(2,1)} %rest_11_.1) | copy-start | bytes 1572868
  20.2 9.1 %collective-permute-start.4 = (bf16[16,4736]{1,0:T(8,128)(2,1)S(1)}, bf16[16,4736]{1,0:T(8,128)(2,1)S(1)}, u32[]{:S(2)}, u32[]{:S(2)}) collective-permute-start(bf16[16,4736]{1,0:T(8,128)(2,1)S(1)} %get-tuple-element.42), channel_id=1, source_target_pairs={{0,4},{4,0},{8,12},{12,8},{1,5},{5,1},{9,13},{13,9},{2,6},{6,2},{1... | collective-permute-start | bytes 454664 | tf_op jit(solution)/shard_map/ppermute | solution.py:464
  20.5 5.9 %collective-permute-start = (bf16[16,1792]{1,0:T(8,128)(2,1)S(1)}, bf16[16,1792]{1,0:T(8,128)(2,1)S(1)}, u32[]{:S(2)}, u32[]{:S(2)}) collective-permute-start(bf16[16,1792]{1,0:T(8,128)(2,1)S(1)} %get-tuple-element.35), channel_id=1, source_target_pairs={{0,8},{4,12},{8,0},{12,4},{1,9},{5,13},{9,1},{13,5},{2,10},{6,14},... | collective-permute-start | bytes 172040 | tf_op jit(solution)/shard_map/ppermute | solution.py:464
  23.3 6.0 %collective-permute-start.3 = (bf16[16,1792]{1,0:T(8,128)(2,1)S(1)}, bf16[16,1792]{1,0:T(8,128)(2,1)S(1)}, u32[]{:S(2)}, u32[]{:S(2)}) collective-permute-start(bf16[16,1792]{1,0:T(8,128)(2,1)S(1)} %get-tuple-element.39), channel_id=1, source_target_pairs={{0,12},{4,8},{8,4},{12,0},{1,13},{5,9},{9,5},{13,1},{2,14},{6,10},... | collective-permute-start | bytes 172040 | tf_op jit(solution)/shard_map/ppermute | solution.py:464
  30.4 4.9 %collective-permute-start.5 = (bf16[144,128]{1,0:T(8,128)(2,1)S(1)}, bf16[144,128]{1,0:T(8,128)(2,1)S(1)}, u32[]{:S(2)}, u32[]{:S(2)}) collective-permute-start(bf16[144,128]{1,0:T(8,128)(2,1)S(1)} %get-tuple-element.46), channel_id=1, source_target_pairs={{0,8},{4,12},{8,0},{12,4},{1,9},{5,13},{9,1},{13,5},{2,10},{6,14},... | collective-permute-start | bytes 110600 | tf_op jit(solution)/shard_map/ppermute | solution.py:464
  31.8 5.8 %collective-permute-start.6 = (bf16[144,128]{1,0:T(8,128)(2,1)S(1)}, bf16[144,128]{1,0:T(8,128)(2,1)S(1)}, u32[]{:S(2)}, u32[]{:S(2)}) collective-permute-start(bf16[144,128]{1,0:T(8,128)(2,1)S(1)} %get-tuple-element.47), channel_id=1, source_target_pairs={{0,12},{4,8},{8,4},{12,0},{1,13},{5,9},{9,5},{13,1},{2,14},{6,10},... | collective-permute-start | bytes 110600 | tf_op jit(solution)/shard_map/ppermute | solution.py:464
  32.6 4.9 %collective-permute-start.7 = (bf16[144,128]{1,0:T(8,128)(2,1)S(1)}, bf16[144,128]{1,0:T(8,128)(2,1)S(1)}, u32[]{:S(2)}, u32[]{:S(2)}) collective-permute-start(bf16[144,128]{1,0:T(8,128)(2,1)S(1)} %get-tuple-element.48), channel_id=1, source_target_pairs={{0,4},{4,0},{8,12},{12,8},{1,5},{5,1},{9,13},{13,9},{2,6},{6,2},{1... | collective-permute-start | bytes 110600 | tf_op jit(solution)/shard_map/ppermute | solution.py:464
